TPU v7x, 512 devices: a whole 4x4x16 slice. The times are simulated.
512 devices in a mesh: gy: 32 (over z, core), gz: 16 (over y, x).
Axes of the slice: x: 4, y: 4, z: 16, core: 2. Of those that a mesh axis runs over, the one named last changes fastest.
Arguments:
- measured: float32 [16, 1024, 1024], P('gz', 'gy'), may hold values from -20 to 20
- point_spread: float32 [1024, 1024], P('gy'), may hold values from -0.005859375 to 0.005859375
- stencil_weights: float32 [3, 3, 3], replicated, may hold values from -0.9 to 0.9
- upstream: float32 [16, 1024, 1024], P('gz', 'gy'), may hold values from -6 to 6
Outputs:
- grad_measured: float32 [16, 1024, 1024], P('gz', 'gy')
- grad_stencil: float32 [3, 3, 3], replicated
All inputs are finite; a program needn't handle non-finite values.
Results may differ from a plain program's by a relative error of at most 0.00021.
Values sent between devices are 32-bit elements; how exact they have to be, the bound alone decides.
No kernel may reach another device: no remote copies, remote signals or barrier semaphores. Data moves between devices by JAX's collectives and lax.ppermute only.
A program may use at most 64 MiB of HBM per device.

v0:
```python
import math

import jax
import jax.numpy as jnp
from jax import lax
from jax.sharding import Mesh
from jax.sharding import PartitionSpec as P

ITERS = 2
GY = ("gy_0", "gy_1")
GY_GZ = ("gy_0", "gy_1", "gz_0", "gz_1")
GZ = ("gz_0", "gz_1")


highest = lax.Precision.HIGHEST


def extended(value, sides, width):
    for axis, dim in sides:
        size, length = (lax.axis_size(axis), value.shape[dim])
        up = [(i, (i + 1) % size) for i in range(size - 1)]
        down = [(j, i) for i, j in up]
        last = lax.slice_in_dim(value, length - width, length, axis=dim)
        first = lax.slice_in_dim(value, 0, width, axis=dim)
        before = lax.ppermute(last, axis, up)
        after = lax.ppermute(first, axis, down)
        value = jnp.concatenate([before, value, after], axis=dim)
    return value


def by_axis(value, axes):
    for axis in axes:
        value = lax.psum(value, axis)
    return value


def waves(count_first, count_second, length):
    product = (
        jnp.arange(count_first, dtype=jnp.int32)[:, None]
        * jnp.arange(count_second, dtype=jnp.int32)[None, :]
        % length
    )
    angle = product.astype(jnp.float32) * (2.0 * math.pi / length)
    return (jnp.cos(angle), jnp.sin(angle))


def contract(form, left, table):
    return jnp.einsum(form, left, table, precision=highest)


def forward_block(cosine, sine):
    return jnp.stack([jnp.stack([cosine, -sine], 1), jnp.stack([sine, cosine], 1)], 0)


def inverse_block(cosine, sine):
    return jnp.stack([jnp.stack([cosine, sine], 1), jnp.stack([-sine, cosine], 1)], 0)


def build_tables(columns, row_total):
    radix_cols = columns // 128
    radix_rows = row_total // 128
    first_cos, first_sin = waves(radix_cols, radix_cols, radix_cols)
    turn_cos, turn_sin = waves(radix_cols, 128, columns)
    inner_cos, inner_sin = waves(128, 128, 128)
    second_cos, second_sin = waves(radix_rows, radix_rows, radix_rows)
    spin_cos, spin_sin = waves(radix_rows, 128, row_total)
    first_start = jnp.stack([first_cos, -first_sin], 1)
    first_final = jnp.stack([first_cos, -first_sin], 0)
    return (
        first_start,
        first_final,
        turn_cos,
        turn_sin,
        forward_block(inner_cos, inner_sin),
        inverse_block(inner_cos, inner_sin),
        forward_block(second_cos, second_sin),
        inverse_block(second_cos, second_sin),
        spin_cos,
        spin_sin,
    )


def forward_fourier_map(volume, twiddle_tables):
    (
        first_start,
        first_final,
        turn_cos,
        turn_sin,
        inner_fwd,
        inner_inv,
        second_fwd,
        second_inv,
        spin_cos,
        spin_sin,
    ) = twiddle_tables
    batches, planes, row_count, columns = volume.shape
    groups = lax.axis_size(GY)
    per_group = 128 // row_count
    bins_here = columns // groups
    radix_cols = first_start.shape[0]
    radix_rows = second_fwd.shape[1]
    blocked = volume.reshape(batches, planes, row_count, radix_cols, 128)
    parts = contract("bzyan,adk->dbzykn", blocked, first_start)
    twisted = jnp.stack(
        [parts[0] * turn_cos + parts[1] * turn_sin, parts[1] * turn_cos - parts[0] * turn_sin], 0
    )
    across = contract("cbzykn,cndq->dbkqzy", twisted, inner_fwd)
    arrived = lax.all_to_all(
        across.reshape(2, batches, columns, planes * row_count),
        GY,
        split_axis=2,
        concat_axis=3,
        tiled=True,
    )
    arrived = arrived.reshape(2, batches, bins_here, radix_rows, per_group, planes, row_count)
    down = contract("cbpajzy,cadk->dbpkzjy", arrived, second_fwd)
    down = down.reshape(2, batches, bins_here, radix_rows, planes, 128)
    spin_real = spin_cos[:, None, :]
    spin_imaginary = spin_sin[:, None, :]
    spun = jnp.stack(
        [
            down[0] * spin_real + down[1] * spin_imaginary,
            down[1] * spin_real - down[0] * spin_imaginary,
        ],
        0,
    )
    return contract("cbpkzm,cmdq->dbpkzq", spun, inner_fwd)


def inverse_transform(spectrum, twiddle_tables):
    (
        first_start,
        first_final,
        turn_cos,
        turn_sin,
        inner_fwd,
        inner_inv,
        second_fwd,
        second_inv,
        spin_cos,
        spin_sin,
    ) = twiddle_tables
    unused, batches, bins_here, radix_rows, planes, width = spectrum.shape
    groups = lax.axis_size(GY)
    columns = bins_here * groups
    radix_cols = first_start.shape[0]
    row_count = radix_rows * 128 // groups
    per_group = 128 // row_count
    down = contract("cbpkzq,cqdm->dbpkzm", spectrum, inner_inv)
    spin_real = spin_cos[:, None, :]
    spin_imaginary = spin_sin[:, None, :]
    twist = jnp.stack(
        [
            down[0] * spin_real - down[1] * spin_imaginary,
            down[1] * spin_real + down[0] * spin_imaginary,
        ],
        0,
    )
    twist = twist.reshape(2, batches, bins_here, radix_rows, planes, per_group, row_count)
    rows_part = contract("cbpkzjy,ckda->dbpajzy", twist, second_inv)
    arrived = lax.all_to_all(
        rows_part.reshape(2, batches, bins_here, groups * planes * row_count),
        GY,
        split_axis=3,
        concat_axis=2,
        tiled=True,
    )
    arrived = arrived.reshape(2, batches, radix_cols, 128, planes, row_count)
    inner = contract("cbkqzy,cqdn->dbzykn", arrived, inner_inv)
    turned = jnp.stack(
        [inner[0] * turn_cos - inner[1] * turn_sin, inner[1] * turn_cos + inner[0] * turn_sin], 0
    )
    volume = contract("cbzykn,cka->bzyan", turned, first_final)
    return volume.reshape(batches, planes, row_count, columns) / float(columns * radix_rows * 128)


def filtered(volume, power_gain, twiddle_tables):
    spectrum = forward_fourier_map(volume[None], twiddle_tables)
    return inverse_transform(spectrum * power_gain, twiddle_tables)[0]


def extend(volume):
    grown = extended(volume, ((GY, 1), (GZ, 0)), 1)
    return jnp.pad(grown, ((0, 0), (0, 0), (1, 1)))


def stencil(grown, kernel, planes, row_count, columns):
    summed = jnp.zeros((planes, row_count, columns), jnp.float32)
    for shift_z in range(3):
        for shift_y in range(3):
            for shift_x in range(3):
                summed = (
                    summed
                    + kernel[shift_z, shift_y, shift_x]
                    * grown[
                        shift_z : shift_z + planes,
                        shift_y : shift_y + row_count,
                        shift_x : shift_x + columns,
                    ]
                )
    return summed


def correlate(values, grown):
    planes, row_count, columns = values.shape
    pieces = []
    for shift_z in range(3):
        for shift_y in range(3):
            for shift_x in range(3):
                pieces.append(
                    jnp.sum(
                        values
                        * grown[
                            shift_z : shift_z + planes,
                            shift_y : shift_y + row_count,
                            shift_x : shift_x + columns,
                        ]
                    )
                )
    return jnp.stack(pieces)


def regular(volume, kernel, flipped):
    planes, row_count, columns = volume.shape
    grown = extend(volume)
    mapped = stencil(grown, kernel, planes, row_count, columns)
    back = stencil(extend(mapped), flipped, planes, row_count, columns)
    return (back, grown, mapped)


def local(measured, point_spread, stencil_weights, upstream):
    planes, row_count, columns = measured.shape
    groups = lax.axis_size(GY)
    cells = planes * row_count * columns * groups * lax.axis_size(GZ)
    twiddle_tables = build_tables(columns, row_count * groups)
    flipped = stencil_weights[::-1, ::-1, ::-1]
    optical = forward_fourier_map(point_spread[None, None], twiddle_tables)
    optical_real = optical[0]
    optical_imaginary = optical[1]
    power_gain = optical_real * optical_real + optical_imaginary * optical_imaginary
    observed = forward_fourier_map(measured[None], twiddle_tables)
    adjoint_spectrum = jnp.stack(
        [
            observed[0] * optical_real + observed[1] * optical_imaginary,
            observed[1] * optical_real - observed[0] * optical_imaginary,
        ],
        0,
    )
    early_blur = None
    stacked = inverse_transform(
        jnp.concatenate([adjoint_spectrum, adjoint_spectrum * power_gain], axis=1), twiddle_tables
    )
    right_side = stacked[0]
    early_blur = stacked[1]
    directions = [right_side]
    residuals = [right_side]
    images = []
    norms = []
    curvatures = []
    step_sizes = []
    ratios = []
    grown_list = []
    mapped_list = []
    upward = []
    crossed = []
    norm_now = by_axis(jnp.sum(right_side * right_side), GY_GZ)
    for iteration in range(ITERS):
        direction = directions[iteration]
        back, grown, mapped = regular(direction, stencil_weights, flipped)
        if iteration == 0 and early_blur is not None:
            blurred = early_blur
        else:
            blurred = filtered(direction, power_gain, twiddle_tables)
        applied = blurred + back
        curvature, along = (
            by_axis(jnp.sum(direction * applied), GY_GZ),
            by_axis(jnp.sum(upstream * direction), GY_GZ),
        )
        upward.append(along)
        step_size = norm_now / curvature
        images.append(applied)
        norms.append(norm_now)
        curvatures.append(curvature)
        step_sizes.append(step_size)
        grown_list.append(grown)
        mapped_list.append(mapped)
        if iteration + 1 < ITERS:
            residual = residuals[iteration] - step_size * applied
            norm_next, cross = (
                by_axis(jnp.sum(residual * residual), GY_GZ),
                by_axis(jnp.sum(residual * applied), GY_GZ),
            )
            crossed.append(cross)
            ratio = norm_next / norm_now
            ratios.append(ratio)
            residuals.append(residual)
            directions.append(residual + ratio * direction)
            norm_now = norm_next
    grad_direction = None
    grad_residual = None
    grad_norm = 0.0
    stencil_terms = jnp.zeros((27,), jnp.float32)
    for iteration in reversed(range(ITERS)):
        direction = directions[iteration]
        applied = images[iteration]
        step_size = step_sizes[iteration]
        grad_step = upward[iteration]
        grad_new = step_size * upstream
        grad_norm_here = 0.0
        grad_residual_next = None
        if iteration + 1 < ITERS:
            grad_ratio, known_image = (
                by_axis(jnp.sum(grad_direction * direction), GY_GZ),
                by_axis(jnp.sum(grad_direction * applied), GY_GZ),
            )
            grad_norm = grad_norm + grad_ratio / norms[iteration]
            grad_image = known_image + 2.0 * grad_norm * crossed[iteration]
            grad_residual_next = grad_direction + 2.0 * grad_norm * residuals[iteration + 1]
            grad_step = grad_step - grad_image
            grad_new = grad_new + ratios[iteration] * grad_direction
            grad_norm_here = -grad_ratio * ratios[iteration] / norms[iteration]
        grad_norm_step = grad_norm_here + grad_step / curvatures[iteration]
        grad_curve = -grad_step * step_size / curvatures[iteration]
        grad_new = grad_new + 2.0 * grad_curve * applied
        mapped = mapped_list[iteration]
        grown = grown_list[iteration]
        if grad_residual_next is not None:
            back_other, grown_other, mapped_other = regular(
                grad_residual_next, stencil_weights, flipped
            )
            blurred_other = filtered(grad_residual_next, power_gain, twiddle_tables)
            grad_new = grad_new - step_size * (blurred_other + back_other)
            local_terms = correlate(
                2.0 * grad_curve * mapped - step_size * mapped_other, grown
            ) - step_size * correlate(mapped, grown_other)
        else:
            local_terms = correlate(2.0 * grad_curve * mapped, grown)
        stencil_terms = stencil_terms + local_terms
        grad_direction = grad_new
        grad_residual = grad_residual_next
        grad_norm = grad_norm_step
    stencil_terms = by_axis(stencil_terms, GY_GZ)
    grad_right = grad_direction + 2.0 * grad_norm * right_side
    grad_right = grad_right + grad_residual
    right_spectrum = forward_fourier_map(grad_right[None], twiddle_tables)
    product = jnp.stack(
        [
            right_spectrum[0] * optical_real - right_spectrum[1] * optical_imaginary,
            right_spectrum[1] * optical_real + right_spectrum[0] * optical_imaginary,
        ],
        0,
    )
    grad_measured = inverse_transform(product, twiddle_tables)[0]
    grad_stencil = stencil_terms.reshape(3, 3, 3) / math.sqrt(cells)
    return (grad_measured, grad_stencil)


def solution(mesh):
    finer = Mesh(mesh.devices.reshape(16, 2, 4, 4), ("gy_0", "gy_1", "gz_0", "gz_1"))
    return jax.shard_map(
        local,
        mesh=finer,
        in_specs=(P(GZ, GY, None), P(GY, None), P(), P(GZ, GY, None)),
        out_specs=(P(GZ, GY, None), P()),
        check_vma=False,
    )
```

profile of v0, /device:TPU:1, one launch (start us, length us, event | category | flops | bytes accessed | tf_op | source)
XLA Modules:
  0.0 899.0 jit_solution(1123461139081819542)
XLA Ops:
  6.9 16.7 %all-to-all-start.1 = ((f32[32,1,2048]{2,1,0:T(1,128)}), f32[32,1,2048]{2,1,0:T(1,128)S(1)}, u32[]{:S(2)}, u32[]{:S(2)}) async-start(f32[32,1,2048]{2,1,0:T(1,128)} %reshape.1333), calls=%async_computation.1 | async-start | bytes 524288 | tf_op jit(solution)/shard_map/all_to_all | solution.py:108
  26.6 19.1 %all-to-all-done.1 = f32[32,1,2048]{2,1,0:T(1,128)S(1)} async-done(((f32[32,1,2048]{2,1,0:T(1,128)}), f32[32,1,2048]{2,1,0:T(1,128)S(1)}, u32[]{:S(2)}, u32[]{:S(2)}) %all-to-all-start.1) | async-done | bytes 262176 | tf_op jit(solution)/shard_map/all_to_all | solution.py:108
  45.7 4.7 all-to-all-start
  56.8 15.4 %all-to-all-done = f32[32,1,2048]{2,1,0:T(1,128)S(1)} async-done(((f32[32,1,2048]{2,1,0:T(1,128)}), f32[32,1,2048]{2,1,0:T(1,128)S(1)}, u32[]{:S(2)}, u32[]{:S(2)}) %all-to-all-start) | async-done | bytes 262176 | tf_op jit(solution)/shard_map/all_to_all | solution.py:108
  92.3 4.7 all-to-all-start.2
  97.1 33.5 %all-to-all-done.2 = f32[32,1,4096]{2,1,0:T(1,128)S(1)} async-done(((f32[32,1,4096]{2,1,0:T(1,128)}), f32[32,1,4096]{2,1,0:T(1,128)S(1)}, u32[]{:S(2)}, u32[]{:S(2)}) %all-to-all-start.2) | async-done | bytes 524320 | tf_op jit(solution)/shard_map/all_to_all | solution.py:161
  157.9 17.3 %multiply_add_fusion.20 = f32[1,32,1024]{2,1,0:T(8,128)S(1)} fusion(f32[1,32,1024]{2,1,0:T(8,128)S(1)} %squeeze.82, f32[3,34,1026]{2,1,0:T(8,128)S(1)} %select_maximum_fusion.20, f32[1,34,1024]{2,1,0:T(8,128)S(1)} %collective-permute-done.3, f32[1,34,1024]{2,1,0:T(8,128)S(1)} %collective-permute-done.2, f32[1,1,1024]{2,1,0:T(1,128)S(1)} %collective-permute-done, ...), kind=kLoop, calls=%fused_computation.485 | loop fusion | flops 1802240 | bytes 3416172 | tf_op jit(solution)/shard_map/add | solution.py:193
  183.1 4.7 collective-permute-start.6
  191.8 18.0 %multiply_reduce_fusion.88 = (f32[]{:T(128)}, f32[]{:T(128)}, f32[1,32,1024]{2,1,0:T(8,128)S(1)}) fusion(f32[1,32,1024]{2,1,0:T(8,128)S(1)} %squeeze.82, f32[1,32,1024]{2,1,0:T(8,128)S(1)} %squeeze.83, f32[3,34,1026]{2,1,0:T(8,128)S(1)} %select_maximum_fusion.16, f32[]{:T(128)} %bitcast.113, f32[1,34,1024]{2,1,0:T(8,128)S(1)} %collective-permute-done.7, ...), kind=kLoop, calls=%fused_computation.484 | loop fusion | flops 1966078 | bytes 3678324 | tf_op jit(solution)/shard_map/reduce_sum | solution.py:276
  209.8 20.7 %all-reduce.8 = (f32[]{:T(128)}, f32[]{:T(128)}) all-reduce(f32[]{:T(128)} %get-tuple-element.109, f32[]{:T(128)} %get-tuple-element.108), channel_id=1, replica_groups=mesh['gy_0'=16,'gy_1'=2,'gz_0'=4,'gz_1'=4] {'gy_0'}, use_global_device_ids=true, to_apply=%region_1.2 | all-reduce | flops 2 | bytes 16 | tf_op jit(solution)/shard_map/psum | solution.py:33
  230.6 11.7 %all-reduce.17 = (f32[]{:T(128)}, f32[]{:T(128)}) all-reduce(f32[]{:T(128)} %get-tuple-element.116, f32[]{:T(128)} %get-tuple-element.117), channel_id=1, replica_groups=mesh['gy_0'=16,'gy_1'=2,'gz_0'=4,'gz_1'=4] {'gy_1'}, use_global_device_ids=true, to_apply=%region_2.3 | all-reduce | flops 2 | bytes 16 | tf_op jit(solution)/shard_map/psum | solution.py:33
  242.3 17.0 %all-reduce.14 = (f32[]{:T(128)}, f32[]{:T(128)}) all-reduce(f32[]{:T(128)} %get-tuple-element.140, f32[]{:T(128)} %get-tuple-element.141), channel_id=1, replica_groups=mesh['gy_0'=16,'gy_1'=2,'gz_0'=4,'gz_1'=4] {'gz_0'}, use_global_device_ids=true, to_apply=%region_3.4 | all-reduce | flops 2 | bytes 16 | tf_op jit(solution)/shard_map/psum | solution.py:33
  259.3 6.7 all-reduce.11
  268.1 20.8 %psum.288 = f32[]{:T(128)} all-reduce(f32[]{:T(128)} %get-tuple-element.83), channel_id=1, replica_groups=mesh['gy_0'=16,'gy_1'=2,'gz_0'=4,'gz_1'=4] {'gy_0'}, use_global_device_ids=true, to_apply=%region_11.12 | all-reduce | flops 1 | bytes 8 | tf_op jit(solution)/shard_map/psum | solution.py:33
  288.9 13.9 %psum.289 = f32[]{:T(128)} all-reduce(f32[]{:T(128)} %psum.288), channel_id=1, replica_groups=mesh['gy_0'=16,'gy_1'=2,'gz_0'=4,'gz_1'=4] {'gy_1'}, use_global_device_ids=true, to_apply=%region_12.13 | all-reduce | flops 1 | bytes 8 | tf_op jit(solution)/shard_map/psum | solution.py:33
  302.8 6.7 psum.290
  309.5 8.4 psum.291
  324.2 11.8 %all-to-all-start.3 = ((f32[32,1,2048]{2,1,0:T(1,128)}), f32[32,1,2048]{2,1,0:T(1,128)S(1)}, u32[]{:S(2)}, u32[]{:S(2)}) async-start(f32[32,1,2048]{2,1,0:T(1,128)} %reshape.1337), calls=%async_computation.3 | async-start | bytes 524288 | tf_op jit(solution)/shard_map/all_to_all | solution.py:108
  341.5 6.9 collective-permute-done.9
  373.7 9.7 %all-to-all-start.4 = ((f32[32,1,2048]{2,1,0:T(1,128)}), f32[32,1,2048]{2,1,0:T(1,128)}, u32[]{:S(2)}, u32[]{:S(2)}) async-start(f32[32,1,2048]{2,1,0:T(1,128)} %reshape.1339), calls=%async_computation.4 | async-start | bytes 524288 | tf_op jit(solution)/shard_map/all_to_all | solution.py:161
  383.7 17.3 %multiply_add_fusion.14 = f32[1,32,1024]{2,1,0:T(8,128)S(1)} fusion(f32[1,32,1024]{2,1,0:T(8,128)S(1)} %multiply_add_fusion.19, f32[3,34,1026]{2,1,0:T(8,128)S(1)} %select_maximum_fusion.12, f32[1,34,1024]{2,1,0:T(8,128)S(1)} %collective-permute-done.11, f32[1,34,1024]{2,1,0:T(8,128)S(1)} %collective-permute-done.10, ...), kind=kLoop, calls=%fused_computation.472 | loop fusion | flops 1802240 | bytes 3416172 | tf_op jit(solution)/shard_map/add | solution.py:193
  408.6 4.2 collective-permute-start.14
  432.3 19.8 %multiply_reduce_fusion.86 = (f32[]{:T(128)}, f32[]{:T(128)}, f32[1,32,1024]{2,1,0:T(8,128)}) fusion(f32[1,32,1024]{2,1,0:T(8,128)S(1)} %multiply_add_fusion.19, f32[1,32,1024]{2,1,0:T(8,128)S(1)} %copy-done.11, f32[1,32,1024]{2,1,0:T(8,128)} %div.78, f32[3,34,1026]{2,1,0:T(8,128)S(1)} %select_maximum_fusion.8, f32[]{:T(128)} %bitcast.113, ...), kind=kLoop, calls=%fused_computation.471 | loop fusion | flops 1966078 | bytes 3809396 | tf_op jit(solution)/shard_map/reduce_sum | solution.py:276
  452.2 23.7 %all-reduce.7 = (f32[]{:T(128)}, f32[]{:T(128)}) all-reduce(f32[]{:T(128)} %get-tuple-element.107, f32[]{:T(128)} %get-tuple-element.106), channel_id=1, replica_groups=mesh['gy_0'=16,'gy_1'=2,'gz_0'=4,'gz_1'=4] {'gy_0'}, use_global_device_ids=true, to_apply=%region_21.22 | all-reduce | flops 2 | bytes 16 | tf_op jit(solution)/shard_map/psum | solution.py:33
  475.9 11.9 %all-reduce.16 = (f32[]{:T(128)}, f32[]{:T(128)}) all-reduce(f32[]{:T(128)} %get-tuple-element.114, f32[]{:T(128)} %get-tuple-element.115), channel_id=1, replica_groups=mesh['gy_0'=16,'gy_1'=2,'gz_0'=4,'gz_1'=4] {'gy_1'}, use_global_device_ids=true, to_apply=%region_22.23 | all-reduce | flops 2 | bytes 16 | tf_op jit(solution)/shard_map/psum | solution.py:33
  487.8 13.1 %all-reduce.13 = (f32[]{:T(128)}, f32[]{:T(128)}) all-reduce(f32[]{:T(128)} %get-tuple-element.138, f32[]{:T(128)} %get-tuple-element.139), channel_id=1, replica_groups=mesh['gy_0'=16,'gy_1'=2,'gz_0'=4,'gz_1'=4] {'gz_0'}, use_global_device_ids=true, to_apply=%region_23.24 | all-reduce | flops 2 | bytes 16 | tf_op jit(solution)/shard_map/psum | solution.py:33
  500.9 6.7 all-reduce.10
  513.4 23.5 %all-reduce.6 = (f32[]{:T(128)}, f32[]{:T(128)}, f32[]{:T(128)}, f32[]{:T(128)}) all-reduce(f32[]{:T(128)} %get-tuple-element.105, f32[]{:T(128)} %get-tuple-element.103, f32[]{:T(128)} %get-tuple-element.104, f32[]{:T(128)} %get-tuple-element.82), channel_id=1, replica_groups=mesh['gy_0'=16,'gy_1'=2,'gz_0'=4,'gz_1'=4] {'gy_0'}, use_global_device_ids=true, to_apply=%region_36.37 | all-reduce | flops 4 | bytes 32 | tf_op jit(solution)/shard_map/psum | solution.py:33
  537.0 14.0 %all-reduce.15 = (f32[]{:T(128)}, f32[]{:T(128)}, f32[]{:T(128)}, f32[]{:T(128)}) all-reduce(f32[]{:T(128)} %get-tuple-element.110, f32[]{:T(128)} %get-tuple-element.111, f32[]{:T(128)} %get-tuple-element.112, f32[]{:T(128)} %get-tuple-element.113), channel_id=1, replica_groups=mesh['gy_0'=16,'gy_1'=2,'gz_0'=4,'gz_1'=4] {'gy_1'}, use_global_device_ids=true, to_apply=%region_37.38 | all-reduce | flops 4 | bytes 32 | tf_op jit(solution)/shard_map/psum | solution.py:33
  550.9 7.3 all-reduce.12
  558.2 8.4 all-reduce.9
  573.2 12.1 %all-to-all-start.5 = ((f32[32,1,2048]{2,1,0:T(1,128)}), f32[32,1,2048]{2,1,0:T(1,128)S(1)}, u32[]{:S(2)}, u32[]{:S(2)}) async-start(f32[32,1,2048]{2,1,0:T(1,128)} %reshape.1341), calls=%async_computation.5 | async-start | bytes 524288 | tf_op jit(solution)/shard_map/all_to_all | solution.py:108
  593.6 4.2 collective-permute-done.17
  599.8 4.4 collective-permute-start.18
  632.7 10.1 %all-to-all-start.6 = ((f32[32,1,2048]{2,1,0:T(1,128)}), f32[32,1,2048]{2,1,0:T(1,128)}, u32[]{:S(2)}, u32[]{:S(2)}) async-start(f32[32,1,2048]{2,1,0:T(1,128)} %reshape.1343), calls=%async_computation.6 | async-start | bytes 524288 | tf_op jit(solution)/shard_map/all_to_all | solution.py:161
  643.2 18.8 %multiply_reduce_fusion.28 = (f32[]{:T(128)}, f32[]{:T(128)}, f32[]{:T(128)}, f32[]{:T(128)}, f32[]{:T(128)}, /*index=5*/f32[]{:T(128)}, f32[]{:T(128)}, f32[]{:...) fusion(f32[1,34,1024]{2,1,0:T(8,128)S(1)} %collective-permute-done.3, ...), kind=kLoop, calls=%fused_computation.391 | loop fusion | flops 2555895 | bytes 4604056 | tf_op jit(solution)/shard_map/reduce_sum | solution.py:211
  669.6 4.8 collective-permute-start.22
  693.7 18.9 %fusion.91 = f32[4,8,8,128]{3,1,2,0:T(8,128)S(1)} fusion(f32[1,32,1024]{2,1,0:T(8,128)S(1)} %multiply_add_fusion.12, f32[1,32,1024]{2,1,0:T(8,128)} %div.87, f32[3,34,1026]{2,1,0:T(8,128)S(1)} %select_maximum_fusion, f32[1,34,1024]{2,1,0:T(8,128)} %copy-done.15, f32[1,1,1024]{2,1,0:T(1,128)} %copy-done.27, f32[1,32,1024]{2,1,0:T(8,128)} %copy-done.10, ...), kind=kLoop, calls=%fused_computation.194 | loop fusion | flops 2162688 | bytes 4202620
  718.0 14.6 %all-to-all-start.7 = ((f32[32,1,2048]{2,1,0:T(1,128)}), f32[32,1,2048]{2,1,0:T(1,128)S(1)}, u32[]{:S(2)}, u32[]{:S(2)}) async-start(f32[32,1,2048]{2,1,0:T(1,128)} %reshape.1345), calls=%async_computation.7 | async-start | bytes 524288 | tf_op jit(solution)/shard_map/all_to_all | solution.py:108
  733.8 20.7 %all-to-all-done.7 = f32[32,1,2048]{2,1,0:T(1,128)S(1)} async-done(((f32[32,1,2048]{2,1,0:T(1,128)}), f32[32,1,2048]{2,1,0:T(1,128)S(1)}, u32[]{:S(2)}, u32[]{:S(2)}) %all-to-all-start.7) | async-done | bytes 262176 | tf_op jit(solution)/shard_map/all_to_all | solution.py:108
  783.5 4.5 all-to-all-start.8
  788.9 16.7 %stack.528 = f32[27]{0:T(128)S(1)} concatenate(f32[1]{0:T(128)} %bitcast.305, f32[1]{0:T(128)} %bitcast.306, f32[1]{0:T(128)} %bitcast.307, f32[1]{0:T(128)} %bitcast.308, f32[1]{0:T(128)} %bitcast.309, f32[1]{0:T(128)} %bitcast.310, f32[1]{0:T(128)} %bitcast.311, f32[1]{0:T(128)} %bitcast.312, f32[1]{0:T(128)} %bitcast.313, f32[1]{0:T(128)} %bitcast.314, f32[1]{0:T(128)} %bitcast.315, ...), dimensions={0} | concatenate | bytes 216 | tf_op jit(solution)/shard_map/stack | solution.py:220
  806.7 17.0 %stack.556 = f32[27]{0:T(128)S(1)} concatenate(f32[1]{0:T(128)} %bitcast.332, f32[1]{0:T(128)} %bitcast.333, f32[1]{0:T(128)} %bitcast.334, f32[1]{0:T(128)} %bitcast.335, f32[1]{0:T(128)} %bitcast.336, f32[1]{0:T(128)} %bitcast.337, f32[1]{0:T(128)} %bitcast.338, f32[1]{0:T(128)} %bitcast.339, f32[1]{0:T(128)} %bitcast.340, f32[1]{0:T(128)} %bitcast.341, f32[1]{0:T(128)} %bitcast.342, ...), dimensions={0} | concatenate | bytes 216 | tf_op jit(solution)/shard_map/stack | solution.py:220
  825.7 17.2 %stack.584 = f32[27]{0:T(128)S(1)} concatenate(f32[1]{0:T(128)} %bitcast.359, f32[1]{0:T(128)} %bitcast.360, f32[1]{0:T(128)} %bitcast.361, f32[1]{0:T(128)} %bitcast.362, f32[1]{0:T(128)} %bitcast.363, f32[1]{0:T(128)} %bitcast.364, f32[1]{0:T(128)} %bitcast.365, f32[1]{0:T(128)} %bitcast.366, f32[1]{0:T(128)} %bitcast.367, f32[1]{0:T(128)} %bitcast.368, f32[1]{0:T(128)} %bitcast.369, ...), dimensions={0} | concatenate | bytes 216 | tf_op jit(solution)/shard_map/stack | solution.py:220
  842.9 23.7 %psum.316 = f32[27]{0:T(128)S(1)} all-reduce(f32[27]{0:T(128)S(1)} %subtract_add_fusion), channel_id=1, replica_groups=mesh['gy_0'=16,'gy_1'=2,'gz_0'=4,'gz_1'=4] {'gy_0'}, use_global_device_ids=true, to_apply=%region_126.127 | all-reduce | flops 27 | bytes 216 | tf_op jit(solution)/shard_map/psum | solution.py:33
  866.6 9.4 %psum.317 = f32[27]{0:T(128)S(1)} all-reduce(f32[27]{0:T(128)S(1)} %psum.316), channel_id=1, replica_groups=mesh['gy_0'=16,'gy_1'=2,'gz_0'=4,'gz_1'=4] {'gy_1'}, use_global_device_ids=true, to_apply=%region_127.128 | all-reduce | flops 27 | bytes 216 | tf_op jit(solution)/shard_map/psum | solution.py:33
  876.0 11.3 %psum.318 = f32[27]{0:T(128)S(1)} all-reduce(f32[27]{0:T(128)S(1)} %psum.317), channel_id=1, replica_groups=mesh['gy_0'=16,'gy_1'=2,'gz_0'=4,'gz_1'=4] {'gz_0'}, use_global_device_ids=true, to_apply=%region_128.129 | all-reduce | flops 27 | bytes 216 | tf_op jit(solution)/shard_map/psum | solution.py:33
  887.3 6.2 psum.319
  (316 shorter events, 250.5 us)
Async XLA Ops:
  6.9 38.7 %all-to-all-start.1 = ((f32[32,1,2048]{2,1,0:T(1,128)}), f32[32,1,2048]{2,1,0:T(1,128)S(1)}, u32[]{:S(2)}, u32[]{:S(2)}) async-start(f32[32,1,2048]{2,1,0:T(1,128)} %reshape.1333), calls=%async_computation.1 | async-start | bytes 524288 | tf_op jit(solution)/shard_map/all_to_all | solution.py:108
  45.7 26.5 %all-to-all-start = ((f32[32,1,2048]{2,1,0:T(1,128)}), f32[32,1,2048]{2,1,0:T(1,128)S(1)}, u32[]{:S(2)}, u32[]{:S(2)}) async-start(f32[32,1,2048]{2,1,0:T(1,128)} %reshape.1331), calls=%async_computation | async-start | bytes 524288 | tf_op jit(solution)/shard_map/all_to_all | solution.py:108
  78.1 288.1 %copy-start.12 = (f32[32,8,128]{2,0,1:T(8,128)}, f32[32,8,128]{2,0,1:T(8,128)S(1)}, u32[]{:S(2)}) copy-start(f32[32,8,128]{2,0,1:T(8,128)S(1)} %get-tuple-element.202) | copy-start | bytes 393220
  92.3 38.2 %all-to-all-start.2 = ((f32[32,1,4096]{2,1,0:T(1,128)}), f32[32,1,4096]{2,1,0:T(1,128)S(1)}, u32[]{:S(2)}, u32[]{:S(2)}) async-start(f32[32,1,4096]{2,1,0:T(1,128)} %reshape.1335), calls=%async_computation.2 | async-start | bytes 1048576 | tf_op jit(solution)/shard_map/all_to_all | solution.py:161
  142.3 5.6 collective-permute-start.1
  145.0 3.6 collective-permute-start
  147.9 27.3 %copy-start.19 = (f32[1,1,1024]{2,1,0:T(1,128)}, f32[1,1,1024]{2,1,0:T(1,128)S(1)}, u32[]{:S(2)}) copy-start(f32[1,1,1024]{2,1,0:T(1,128)S(1)} %collective-permute-done.1) | copy-start | bytes 12292
  148.6 26.6 %copy-start.21 = (f32[1,1,1024]{2,1,0:T(1,128)}, f32[1,1,1024]{2,1,0:T(1,128)S(1)}, u32[]{:S(2)}) copy-start(f32[1,1,1024]{2,1,0:T(1,128)S(1)} %collective-permute-done) | copy-start | bytes 12292
  148.6 8.0 collective-permute-start.3
  149.9 7.7 collective-permute-start.2
  175.2 5.8 collective-permute-start.5
  177.8 3.9 collective-permute-start.4
  181.8 8.1 collective-permute-start.7
  183.1 8.5 collective-permute-start.6
  191.8 75.5 %copy-start.11 = (f32[1,32,1024]{2,1,0:T(8,128)S(1)}, f32[1,32,1024]{2,1,0:T(8,128)}, u32[]{:S(2)}) copy-start(f32[1,32,1024]{2,1,0:T(8,128)} %param.7) | copy-start | bytes 393220
  209.8 358.0 %copy-start.4 = (f32[1,32,1024]{2,1,0:T(8,128)}, f32[1,32,1024]{2,1,0:T(8,128)S(1)}, u32[]{:S(2)}) copy-start(f32[1,32,1024]{2,1,0:T(8,128)S(1)} %get-tuple-element.146) | copy-start | bytes 393220
  324.2 33.6 %all-to-all-start.3 = ((f32[32,1,2048]{2,1,0:T(1,128)}), f32[32,1,2048]{2,1,0:T(1,128)S(1)}, u32[]{:S(2)}, u32[]{:S(2)}) async-start(f32[32,1,2048]{2,1,0:T(1,128)} %reshape.1337), calls=%async_computation.3 | async-start | bytes 524288 | tf_op jit(solution)/shard_map/all_to_all | solution.py:108
  336.0 12.5 %collective-permute-start.9 = (f32[1,1,1024]{2,1,0:T(1,128)S(1)}, f32[1,1,1024]{2,1,0:T(1,128)S(1)}, u32[]{:S(2)}, u32[]{:S(2)}) collective-permute-start(f32[1,1,1024]{2,1,0:T(1,128)S(1)} %get-tuple-element.210), channel_id=1, source_target_pairs={{16,0},{32,16},{48,32},{64,48},{80,64},{96,80},{112,96},{128,112},... | collective-permute-start | bytes 12296 | tf_op jit(solution)/shard_map/ppermute | solution.py:26
  338.1 10.3 %collective-permute-start.8 = (f32[1,1,1024]{2,1,0:T(1,128)S(1)}, f32[1,1,1024]{2,1,0:T(1,128)S(1)}, u32[]{:S(2)}, u32[]{:S(2)}) collective-permute-start(f32[1,1,1024]{2,1,0:T(1,128)S(1)} %get-tuple-element.209), channel_id=1, source_target_pairs={{0,16},{16,32},{32,48},{48,64},{64,80},{80,96},{96,112},{112,128},... | collective-permute-start | bytes 12296 | tf_op jit(solution)/shard_map/ppermute | solution.py:25
  349.1 34.3 %collective-permute-start.11 = (f32[1,34,1024]{2,1,0:T(8,128)}, f32[1,34,1024]{2,1,0:T(8,128)S(1)}, u32[]{:S(2)}, u32[]{:S(2)}) collective-permute-start(f32[1,34,1024]{2,1,0:T(8,128)} %pad_maximum_fusion.3), channel_id=1, source_target_pairs={{1,0},{2,1},{3,2},{4,3},{5,4},{6,5},{7,6},{8,7},{9,8},{10,9},{11,1... | collective-permute-start | bytes 417800 | tf_op jit(solution)/shard_map/ppermute | solution.py:26
  350.4 33.0 %collective-permute-start.10 = (f32[1,34,1024]{2,1,0:T(8,128)}, f32[1,34,1024]{2,1,0:T(8,128)S(1)}, u32[]{:S(2)}, u32[]{:S(2)}) collective-permute-start(f32[1,34,1024]{2,1,0:T(8,128)} %pad_maximum_fusion.3), channel_id=1, source_target_pairs={{0,1},{1,2},{2,3},{3,4},{4,5},{5,6},{6,7},{7,8},{8,9},{9,10},{10,1... | collective-permute-start | bytes 417800 | tf_op jit(solution)/shard_map/ppermute | solution.py:25
  373.7 43.8 %all-to-all-start.4 = ((f32[32,1,2048]{2,1,0:T(1,128)}), f32[32,1,2048]{2,1,0:T(1,128)}, u32[]{:S(2)}, u32[]{:S(2)}) async-start(f32[32,1,2048]{2,1,0:T(1,128)} %reshape.1339), calls=%async_computation.4 | async-start | bytes 524288 | tf_op jit(solution)/shard_map/all_to_all | solution.py:161
  383.4 17.6 %copy-start = (f32[1,34,1024]{2,1,0:T(8,128)}, f32[1,34,1024]{2,1,0:T(8,128)S(1)}, u32[]{:S(2)}) copy-start(f32[1,34,1024]{2,1,0:T(8,128)S(1)} %collective-permute-done.10) | copy-start | bytes 417796
  401.0 31.4 %copy-start.2 = (f32[1,32,1024]{2,1,0:T(8,128)}, f32[1,32,1024]{2,1,0:T(8,128)S(1)}, u32[]{:S(2)}) copy-start(f32[1,32,1024]{2,1,0:T(8,128)S(1)} %multiply_add_fusion.14) | copy-start | bytes 393220
  401.0 5.6 collective-permute-start.13
  403.2 4.1 collective-permute-start.12
  407.3 7.4 collective-permute-start.15
  408.6 8.0 collective-permute-start.14
  513.4 56.8 %copy-start.16 = (f32[1,32,1024]{2,1,0:T(8,128)}, f32[1,32,1024]{2,1,0:T(8,128)S(1)}, u32[]{:S(2)}) copy-start(f32[1,32,1024]{2,1,0:T(8,128)S(1)} %get-tuple-element.144) | copy-start | bytes 393220
  573.2 33.9 %all-to-all-start.5 = ((f32[32,1,2048]{2,1,0:T(1,128)}), f32[32,1,2048]{2,1,0:T(1,128)S(1)}, u32[]{:S(2)}, u32[]{:S(2)}) async-start(f32[32,1,2048]{2,1,0:T(1,128)} %reshape.1341), calls=%async_computation.5 | async-start | bytes 524288 | tf_op jit(solution)/shard_map/all_to_all | solution.py:108
  585.3 12.5 %collective-permute-start.17 = (f32[1,1,1024]{2,1,0:T(1,128)S(1)}, f32[1,1,1024]{2,1,0:T(1,128)S(1)}, u32[]{:S(2)}, u32[]{:S(2)}) collective-permute-start(f32[1,1,1024]{2,1,0:T(1,128)S(1)} %get-tuple-element.206), channel_id=1, source_target_pairs={{16,0},{32,16},{48,32},{64,48},{80,64},{96,80},{112,96},{128,112},... | collective-permute-start | bytes 12296 | tf_op jit(solution)/shard_map/ppermute | solution.py:26
  587.5 10.3 %collective-permute-start.16 = (f32[1,1,1024]{2,1,0:T(1,128)S(1)}, f32[1,1,1024]{2,1,0:T(1,128)S(1)}, u32[]{:S(2)}, u32[]{:S(2)}) collective-permute-start(f32[1,1,1024]{2,1,0:T(1,128)S(1)} %get-tuple-element.205), channel_id=1, source_target_pairs={{0,16},{16,32},{32,48},{48,64},{64,80},{80,96},{96,112},{112,128},... | collective-permute-start | bytes 12296 | tf_op jit(solution)/shard_map/ppermute | solution.py:25
  597.8 45.3 %copy-start.23 = (f32[1,1,1024]{2,1,0:T(1,128)}, f32[1,1,1024]{2,1,0:T(1,128)S(1)}, u32[]{:S(2)}) copy-start(f32[1,1,1024]{2,1,0:T(1,128)S(1)} %collective-permute-done.17) | copy-start | bytes 12292
  597.8 45.3 %copy-start.25 = (f32[1,1,1024]{2,1,0:T(1,128)}, f32[1,1,1024]{2,1,0:T(1,128)S(1)}, u32[]{:S(2)}) copy-start(f32[1,1,1024]{2,1,0:T(1,128)S(1)} %collective-permute-done.16) | copy-start | bytes 12292
  598.5 44.4 %collective-permute-start.19 = (f32[1,34,1024]{2,1,0:T(8,128)}, f32[1,34,1024]{2,1,0:T(8,128)S(1)}, u32[]{:S(2)}, u32[]{:S(2)}) collective-permute-start(f32[1,34,1024]{2,1,0:T(8,128)} %pad_maximum_fusion.5), channel_id=1, source_target_pairs={{1,0},{2,1},{3,2},{4,3},{5,4},{6,5},{7,6},{8,7},{9,8},{10,9},{11,1... | collective-permute-start | bytes 417800 | tf_op jit(solution)/shard_map/ppermute | solution.py:26
  599.8 43.1 %collective-permute-start.18 = (f32[1,34,1024]{2,1,0:T(8,128)}, f32[1,34,1024]{2,1,0:T(8,128)S(1)}, u32[]{:S(2)}, u32[]{:S(2)}) collective-permute-start(f32[1,34,1024]{2,1,0:T(8,128)} %pad_maximum_fusion.5), channel_id=1, source_target_pairs={{0,1},{1,2},{2,3},{3,4},{4,5},{5,6},{6,7},{7,8},{8,9},{9,10},{10,1... | collective-permute-start | bytes 417800 | tf_op jit(solution)/shard_map/ppermute | solution.py:25
  627.3 15.8 %copy-start.22 = (f32[1,1,1024]{2,1,0:T(1,128)S(1)}, f32[1,1,1024]{2,1,0:T(1,128)}, u32[]{:S(2)}) copy-start(f32[1,1,1024]{2,1,0:T(1,128)} %copy-done.21) | copy-start | bytes 12292
  632.7 46.1 %all-to-all-start.6 = ((f32[32,1,2048]{2,1,0:T(1,128)}), f32[32,1,2048]{2,1,0:T(1,128)}, u32[]{:S(2)}, u32[]{:S(2)}) async-start(f32[32,1,2048]{2,1,0:T(1,128)} %reshape.1343), calls=%async_computation.6 | async-start | bytes 524288 | tf_op jit(solution)/shard_map/all_to_all | solution.py:161
  662.0 5.6 collective-permute-start.21
  664.2 4.1 collective-permute-start.20
  668.3 8.1 collective-permute-start.23
  669.6 8.0 collective-permute-start.22
  713.2 19.5 %copy-start.3 = (f32[1,32,1024]{2,1,0:T(8,128)S(1)}, f32[1,32,1024]{2,1,0:T(8,128)}, u32[]{:S(2)}) copy-start(f32[1,32,1024]{2,1,0:T(8,128)} %copy-done.2) | copy-start | bytes 393220
  718.0 36.5 %all-to-all-start.7 = ((f32[32,1,2048]{2,1,0:T(1,128)}), f32[32,1,2048]{2,1,0:T(1,128)S(1)}, u32[]{:S(2)}, u32[]{:S(2)}) async-start(f32[32,1,2048]{2,1,0:T(1,128)} %reshape.1345), calls=%async_computation.7 | async-start | bytes 524288 | tf_op jit(solution)/shard_map/all_to_all | solution.py:108
  780.5 25.1 %copy-start.17 = (f32[1,32,1024]{2,1,0:T(8,128)S(1)}, f32[1,32,1024]{2,1,0:T(8,128)}, u32[]{:S(2)}) copy-start(f32[1,32,1024]{2,1,0:T(8,128)} %get-tuple-element.142) | copy-start | bytes 393220
  783.5 110.7 %all-to-all-start.8 = ((f32[32,1,2048]{2,1,0:T(1,128)}), f32[32,1,2048]{2,1,0:T(1,128)S(1)}, u32[]{:S(2)}, u32[]{:S(2)}) async-start(f32[32,1,2048]{2,1,0:T(1,128)} %reshape.1347), calls=%async_computation.8 | async-start | bytes 524288 | tf_op jit(solution)/shard_map/all_to_all | solution.py:161
  788.0 35.7 %copy-start.24 = (f32[1,1,1024]{2,1,0:T(1,128)S(1)}, f32[1,1,1024]{2,1,0:T(1,128)}, u32[]{:S(2)}) copy-start(f32[1,1,1024]{2,1,0:T(1,128)} %copy-done.23) | copy-start | bytes 12292
  788.0 35.7 %copy-start.26 = (f32[1,1,1024]{2,1,0:T(1,128)S(1)}, f32[1,1,1024]{2,1,0:T(1,128)}, u32[]{:S(2)}) copy-start(f32[1,1,1024]{2,1,0:T(1,128)} %copy-done.25) | copy-start | bytes 12292
  (15 other events, 102.6 us)
where the time goes:
time: 912 us; the launch traced here: 899 us
  blocking collectives  265 us (29%)
  local copies, waits for them, and re-layouts  164 us (18%)
  starting transfers between devices  157 us (17%)
  other arithmetic  144 us (16%)
  waiting for transfers between devices  119 us (13%)
  matrix products  34.8 us (4%)
  between operations  15.3 us (2%)
    psum x20, blocking collectives, by_axis(): value = lax.psum(value, axis)  265 us
    all_to_all x5, waiting for transfers between devices, forward_fourier_map(): lax.all_to_all(across.reshape(2, batches, columns, planes * row_count), G...  61.5 us
    all_to_all x5, starting transfers between devices, forward_fourier_map(): lax.all_to_all(across.reshape(2, batches, columns, planes * row_count), G...  59.9 us
    another operation x3, local copies, waits for them, and re-layouts, correlate(): return jnp.stack(pieces)  50.9 us
    ppermute x12, starting transfers between devices, extended(): before = lax.ppermute(last, axis, up)  45.9 us
    unnamed x83, local copies, waits for them, and re-layouts  42.1 us
    reduce_sum x2, other arithmetic, local(): jnp.sum(direction * applied)  37.8 us
    dot_general x36, matrix products, contract(): return jnp.einsum(form, left, table, precision=highest)  34.8 us
  transfers between devices with their start and end apart: 33, of which 19 were waited for; matrix products, arithmetic and copies ran while one was open for 16% of the time, Pallas kernels for 0%

commit v1 on v0

v1 whole, which is shorter than its diff:
```python
import functools
import math

import jax
import jax.numpy as jnp
import ml_dtypes
import numpy as np
from jax import lax
from jax.experimental import pallas as pl
from jax.experimental.pallas import tpu as pltpu
from jax.sharding import PartitionSpec as P

ROWS = 32
COLS = 1024
FRAME = 48
BLOCKS = 9
F32 = jnp.float32
BF16 = jnp.bfloat16
VMEM = 40 * 1024 * 1024


def split_table(table):
    high = table.astype(ml_dtypes.bfloat16)
    low = (table - high.astype(np.float64)).astype(ml_dtypes.bfloat16)
    return high, low


def x_tables():
    part, half, device, i = np.meshgrid(
        np.arange(2), np.arange(2), np.arange(32), np.arange(8), indexing="ij"
    )
    part, kx = part.reshape(-1, 1), (16 * device + 8 * half + i).reshape(-1, 1)
    x = np.arange(COLS)[None, :]
    angle = 2.0 * np.pi * ((kx * x) % COLS) / COLS
    flip = 1.0 - 2.0 * (x % 2)
    nyquist = (kx == 0) & (part == 1)
    wave = np.where(part == 0, np.cos(angle), -np.sin(angle))
    forward = np.where(nyquist, flip, wave)
    weight = np.where(kx == 0, 1.0, 2.0) / (COLS * 1024.0)
    return forward, forward * weight


def y_tables():
    q = np.arange(32)[:, None]
    s = np.arange(32)[None, :]
    angle = 2.0 * np.pi * ((q * s) % 32) / 32
    first = np.concatenate([np.cos(angle), np.sin(angle)], 0)
    lane = np.arange(128)
    part, half, t = lane // 64, lane // 32 % 2, lane % 32
    turn = 2.0 * np.pi * q * t[None, :] / 1024
    sign = np.where(part == 0, 1.0, -1.0)[None, :]
    turn_cos, turn_sin = np.cos(turn), np.sin(turn) * sign
    angle = 2.0 * np.pi * ((t[:, None] * t[None, :]) % 32) / 32
    pi, po = part[:, None], part[None, :]
    block = np.where(pi == po, np.cos(angle), np.where(pi > po, np.sin(angle), -np.sin(angle)))
    second = np.where(half[:, None] == half[None, :], block, 0.0)
    return first, turn_cos, turn_sin, second


X_FORWARD, X_INVERSE = x_tables()
Y_FIRST, TURN_COS, TURN_SIN, Y_SECOND = y_tables()


def halves(value):
    high = value.astype(BF16)
    return high, (value - high.astype(F32)).astype(BF16)


def dot(left, right):
    return lax.dot_general(left, right, (((1,), (0,)), ((), ())), preferred_element_type=F32)


def dot_nt(left, right):
    return lax.dot_general(left, right, (((1,), (1,)), ((), ())), preferred_element_type=F32)


def swap(value):
    return pltpu.roll(value, 64, 1)


def lanes(shape):
    return lax.broadcasted_iota(jnp.int32, shape, 1)


def sublanes(shape):
    return lax.broadcasted_iota(jnp.int32, shape, 0)


def x_forward(value, high_ref, low_ref):
    high, low = halves(value)
    both = jnp.concatenate([high] * 4 + [low] * 4, 0)
    group = lanes((256, 128)) // 32
    out = None
    for h in range(4):
        rows = slice(256 * h, 256 * h + 256)
        first = dot_nt(high_ref[rows, :], both)
        piece = first[:, :128] + first[:, 128:] + dot_nt(low_ref[rows, :], both[:128])
        out = piece if out is None else jnp.where(group == h, piece, out)
    return out


def x_inverse(spectra, high_ref, low_ref):
    lefts = []
    for value in spectra:
        turned = value.T
        lefts.append(jnp.concatenate([turned[32 * h : 32 * h + 32] for h in range(4)], 1))
    left = lefts[0] if len(lefts) == 1 else jnp.concatenate(lefts, 0)
    count = left.shape[0]
    high, low = halves(left)
    first = dot(jnp.concatenate([high, low], 0), high_ref[...])
    return first[:count] + first[count:] + dot(high, low_ref[...])


class Lateral:
    def __init__(self, refs):
        self.first_high, self.first_low, self.cos, self.sin, second_high, second_low, back_high, back_low = refs
        self.second = (second_high, second_low)
        self.back = (back_high, back_low)
        self.sign = jnp.where(lanes((32, 128)) < 64, 1.0, -1.0)

    def over_s(self, blocks, direction):
        high, low = halves(jnp.concatenate(blocks, 1))
        first_high, first_low = self.first_high[...], self.first_low[...]
        both = dot(first_high, high) + dot(first_high, low) + dot(first_low, high)
        out = []
        for i in range(len(blocks)):
            cols = slice(128 * i, 128 * i + 128)
            out.append(both[:32, cols] + direction * self.sign * swap(both[32:, cols]))
        return out

    def over_t(self, blocks, tables):
        high, low = halves(jnp.concatenate(blocks, 0))
        table_high, table_low = tables[0][...], tables[1][...]
        return dot(high, table_high) + dot(low, table_high) + dot(high, table_low)

    def forward(self, ref, offset, is_first):
        blocks = [ref[:, offset + i, :] for i in range(8)]
        lane = lanes((32, 128))
        nyquist = (lane >= 64) & (lane < 96)
        blocks.append(jnp.where(lane < 32, swap(blocks[0]), 0.0) * is_first)
        blocks[0] = jnp.where(nyquist, blocks[0] * (1.0 - is_first), blocks[0])
        blocks = self.over_s(blocks, 1.0)
        blocks = [z * self.cos[...] + swap(z) * self.sin[...] for z in blocks]
        return self.over_t(blocks, self.second)

    def inverse(self, spectrum, ref, offset, halo):
        all_rows = self.over_t([spectrum], self.back)
        blocks = [all_rows[32 * i : 32 * i + 32] for i in range(BLOCKS)]
        blocks = [z * self.cos[...] - swap(z) * self.sin[...] for z in blocks]
        blocks = self.over_s(blocks, -1.0)
        lane = lanes((32, 128))
        nyquist = (lane >= 64) & (lane < 96)
        blocks[0] = blocks[0] + jnp.where(nyquist, swap(blocks[8]), 0.0)
        t = lane % 32
        row = sublanes((32, 128))
        for i in range(8):
            ref[:, offset + i, :] = blocks[i]
            if halo:
                after = jnp.where((t < 8) & (row < 31), pltpu.roll(blocks[i], 31, 0), 0.0)
                before = jnp.where((t >= 24) & (row > 0), pltpu.roll(blocks[i], 1, 0), 0.0)
                ref[:, offset + 8 + i, :] = after + before


def product(real, imaginary, value):
    return real * value + imaginary * swap(value)


def spread_kernel(fields, high_ref, low_ref, *refs):
    out_ref = refs[fields]
    for f in range(fields):
        out_ref[:, 8 * f : 8 * f + 8, :] = x_forward(refs[f][...], high_ref, low_ref).reshape(32, 8, 128)


def first_filter_kernel(*refs):
    lateral = Lateral(refs[:8])
    is_first_ref, arrived, right, image, real_ref, imaginary_ref, power_ref, spectrum_ref = refs[8:]
    is_first = is_first_ref[0]
    transfer = lateral.forward(arrived, 8, is_first)
    observed = lateral.forward(arrived, 0, is_first)
    turned = swap(transfer)
    left = lanes(transfer.shape) < 64
    real = jnp.where(left, transfer, turned)
    imaginary = jnp.where(left, turned, -transfer)
    power = real * real + imaginary * imaginary
    spectrum = product(real, imaginary, observed)
    lateral.inverse(spectrum, right, 0, True)
    lateral.inverse(spectrum * power, image, 0, True)
    real_ref[...] = real
    imaginary_ref[...] = imaginary
    power_ref[...] = power
    spectrum_ref[...] = spectrum


def second_filter_kernel(*refs):
    lateral = Lateral(refs[:8])
    is_first_ref, arrived, power_ref, spectrum_ref, out_ref, image_ref = refs[8:]
    power = power_ref[...]
    image = power * spectrum_ref[...] + lateral.forward(arrived, 0, is_first_ref[0])
    lateral.inverse(power * image, out_ref, 0, True)
    image_ref[...] = image


def last_filter_kernel(*refs):
    lateral = Lateral(refs[:8])
    (is_first_ref, factor_ref, third, second, upstream, real_ref, imaginary_ref, power_ref, spectrum_ref, image_ref, out_ref) = refs[8:]
    is_first = is_first_ref[0]
    power = power_ref[...]
    image = image_ref[...]
    further = power * image + lateral.forward(second, 0, is_first)
    last = power * further + lateral.forward(third, 0, is_first)
    weights = lateral.forward(upstream, 0, is_first)
    total = factor_ref[0] * weights + factor_ref[1] * (power * weights + lateral.forward(upstream, 8, is_first))
    total = total + factor_ref[2] * spectrum_ref[...] + factor_ref[3] * image
    total = total + factor_ref[4] * further + factor_ref[5] * last
    lateral.inverse(product(real_ref[...], -imaginary_ref[...], total), out_ref, 0, False)


def gather_kernel(high_ref, low_ref, arrived, out_ref):
    main = arrived[:, 0:8, :].reshape(256, 128)
    halo = arrived[:, 8:16, :].reshape(256, 128)
    value = x_inverse([main, halo], high_ref, low_ref)
    out_ref[0:8, :] = value[56:64]
    out_ref[8:40, :] = value[0:32]
    out_ref[40:48, :] = value[32:40]


def final_kernel(high_ref, low_ref, arrived, out_ref):
    out_ref[...] = x_inverse([arrived[...].reshape(256, 128)], high_ref, low_ref)


def shifted_columns(value):
    column = lanes(value.shape)
    left = jnp.where(column >= 1, pltpu.roll(value, 1, 1), 0.0)
    right = jnp.where(column < COLS - 1, pltpu.roll(value, COLS - 1, 1), 0.0)
    return left, right


def stencil_sum(weight, source, start, cols):
    total = None
    for b in range(3):
        part = None
        for a in range(3):
            for c in range(3):
                term = weight(a, b, c) * source[c, start + a, :, cols]
                part = term if part is None else part + term
        if b == 0:
            part = pltpu.roll(part, 1, 0)
        elif b == 2:
            part = pltpu.roll(part, FRAME - 1, 0)
        total = part if total is None else total + part
    return total


def stencil_kernel(mode, place_ref, weights_ref, high_ref, low_ref, own, up1, up2, down1, down2, *refs):
    refs = list(refs)
    base = refs.pop(0) if mode == "add" else None
    back_ref = None if mode == "both" else refs.pop(0)
    mapped_ref, out_ref, source, middle = refs
    device, plane, planes = place_ref[0], place_ref[1], place_ref[2]
    for p, ref in enumerate((up2, up1, own, down1, down2)):
        value = ref[...]
        left, right = shifted_columns(value)
        source[0, p], source[1, p], source[2, p] = left, value, right
    row = sublanes((FRAME, 128))
    lowest = jnp.where(device > 0, 0, 8)
    highest = jnp.where(device < 31, FRAME, 40)
    inside = (row >= lowest) & (row < highest)

    def weight(a, b, c):
        return weights_ref[9 * a + 3 * b + c]

    def flipped(a, b, c):
        return weights_ref[26 - 9 * a - 3 * b - c]

    for p in range(3):
        here = plane + (p - 1)
        end = jnp.where((here >= 0) & (here < planes), highest, 0)
        valid = (row >= lowest) & (row < end)
        for k in range(8):
            cols = slice(128 * k, 128 * k + 128)
            value = stencil_sum(weight, source, p, cols)
            middle[1, p, :, cols] = jnp.where(valid, value, 0.0)
    for p in range(3):
        value = middle[1, p]
        left, right = shifted_columns(value)
        middle[0, p], middle[2, p] = left, right
    mapped_ref[...] = middle[1, 1]
    for k in range(8):
        cols = slice(128 * k, 128 * k + 128)
        value = jnp.where(inside, stencil_sum(flipped, middle, 0, cols), 0.0)
        source[1, 0, :, cols] = value
        if mode == "add":
            back_ref[:, cols] = base[:, cols] + value
    if mode == "both":
        out_ref[:, 0:8, :] = x_forward(own[8:40, :], high_ref, low_ref).reshape(32, 8, 128)
        out_ref[:, 8:16, :] = x_forward(source[1, 0, 8:40, :], high_ref, low_ref).reshape(32, 8, 128)
    else:
        out_ref[...] = x_forward(source[1, 0, 8:40, :], high_ref, low_ref).reshape(32, 8, 128)
    if mode == "plain":
        back_ref[...] = source[1, 0]


def moments_kernel(right, image, further, upstream, out_ref):
    b, ab, aab, u = (ref[8:40, :] for ref in (right, image, further, upstream))
    lane = lanes((1, 128))
    out = jnp.zeros((1, 128), F32)
    for k, value in enumerate((b * b, b * ab, ab * ab, ab * aab, u * b, u * ab)):
        out = jnp.where(lane == k, jnp.sum(value), out)
    out_ref[...] = out


def correlate_kernel(factor_ref, *refs):
    out_ref, scaled, mapped = refs[-3:]
    right, image, further, upstream = refs[0:3], refs[3:6], refs[6:9], refs[9:12]
    right_map, image_map, further_map, upstream_map = refs[12:16]
    f = [factor_ref[k] for k in range(6)]
    for p in range(3):
        scaled[p] = f[0] * upstream[p][...] + f[1] * right[p][...] + f[2] * image[p][...] + f[3] * further[p][...]
    mapped[0] = (
        f[0] * upstream_map[8:40, :] + f[1] * right_map[8:40, :] + f[2] * image_map[8:40, :] + f[3] * further_map[8:40, :]
    )
    mapped[1] = right_map[8:40, :]
    mapped[2] = f[4] * image_map[8:40, :]
    lane = lanes((1, 128))
    out = jnp.zeros((1, 128), F32)
    column = lanes((ROWS, COLS))
    left_edge, right_edge = column < COLS - 1, column >= 1
    for c in range(3):
        parts = []
        for k in range(3):
            value = mapped[k]
            if c == 0:
                value = jnp.where(left_edge, pltpu.roll(value, COLS - 1, 1), 0.0)
            elif c == 2:
                value = jnp.where(right_edge, pltpu.roll(value, 1, 1), 0.0)
            parts.append(value)
        for a in range(3):
            for b in range(3):
                rows = slice(7 + b, 39 + b)
                total = parts[0] * right[a][rows, :] + parts[1] * scaled[a, rows, :] + parts[2] * image[a][rows, :]
                out = jnp.where(lane == 9 * a + 3 * b + c, jnp.sum(total), out)
    out_ref[...] = out


def shape(*dims):
    return jax.ShapeDtypeStruct(dims, F32)


def call(body, out_shape, operands, scalars=0, scratch=(), flops=200_000_000):
    memory = [pl.BlockSpec(memory_space=pltpu.SMEM)] * scalars
    memory = memory + [pl.BlockSpec(memory_space=pltpu.VMEM)] * (len(operands) - scalars)
    return pl.pallas_call(
        body,
        out_shape=out_shape,
        in_specs=memory,
        out_specs=jax.tree.map(lambda _: pl.BlockSpec(memory_space=pltpu.VMEM), out_shape),
        scratch_shapes=list(scratch),
        compiler_params=pltpu.CompilerParams(vmem_limit_bytes=VMEM),
        cost_estimate=pl.CostEstimate(flops=flops, bytes_accessed=8_000_000, transcendentals=0),
    )(*operands)


def exchange(value):
    return lax.all_to_all(value, "gy", 0, 0, tiled=True)


def neighbours(value):
    size = lax.axis_size("gz")

    def moved(by):
        pairs = [(i, i + by) for i in range(size) if 0 <= i + by < size]
        return lax.ppermute(value, "gz", pairs)

    return value, moved(1), moved(2), moved(-1), moved(-2)


def summed(row):
    for axis in ("gy", "gz"):
        size = lax.axis_size(axis)
        copies = jnp.broadcast_to(row[None], (size, 1, 128))
        row = jnp.sum(lax.all_to_all(copies, axis, 0, 0, tiled=True), 0)
    return row[0]


def factors(m0, m1, m2, m3, u0, u1):
    def pair(m0, m1, m2, m3):
        step0 = m0 / m1
        norm1 = m0 - 2.0 * step0 * m1 + step0 * step0 * m2
        ratio = norm1 / m0
        keep = 1.0 + ratio
        curvature = keep * keep * m1 - 2.0 * keep * step0 * m2 + step0 * step0 * m3
        step1 = norm1 / curvature
        return step0 + step1 * keep, -step1 * step0

    (alpha, gamma), back = jax.vjp(pair, m0, m1, m2, m3)
    return (alpha, gamma, *back((u0, u1)))


def local(measured, point_spread, stencil_weights, upstream):
    cells = measured.size * lax.axis_size("gy") * lax.axis_size("gz")
    device, plane = lax.axis_index("gy"), lax.axis_index("gz")
    is_first = jnp.where(device == 0, 1.0, 0.0).astype(F32).reshape(1)
    place = jnp.stack([device, plane, jnp.int32(lax.axis_size("gz"))]).astype(jnp.int32)
    weights = stencil_weights.reshape(27)
    to_x = [jnp.asarray(table) for table in split_table(X_FORWARD)]
    from_x = [jnp.asarray(table) for table in split_table(X_INVERSE)]
    along_y = [jnp.asarray(table) for table in split_table(Y_FIRST)]
    along_y += [jnp.asarray(TURN_COS, F32), jnp.asarray(TURN_SIN, F32)]
    along_y += [jnp.asarray(table) for table in split_table(Y_SECOND)]
    along_y += [jnp.asarray(table) for table in split_table(Y_SECOND.T)]
    measured, upstream = measured[0], upstream[0]
    tile = (32, 8, 128)
    tiles = (32, 16, 128)
    spectral = (32 * BLOCKS, 128)
    frame = (FRAME, COLS)

    def stencil(mode, parts, *base):
        frames = (shape(*frame), shape(*frame)) if mode != "both" else (shape(*frame),)
        outs = (*frames, shape(*(tiles if mode == "both" else tile)))
        scratch = (pltpu.VMEM((3, 5, FRAME, COLS), F32), pltpu.VMEM((3, 3, FRAME, COLS), F32))
        operands = [place, weights, *to_x, *parts, *base]
        return call(functools.partial(stencil_kernel, mode), outs, operands, 2, scratch)

    def filter_call(body, outs, scalars, operands):
        count, end = len(scalars), len(scalars) + len(along_y)

        def ordered(*refs):
            body(*refs[count:end], *refs[:count], *refs[end:])

        return call(ordered, outs, [*scalars, *along_y, *operands], count)

    first = exchange(
        call(functools.partial(spread_kernel, 2), shape(*tiles), [*to_x, measured, point_spread])
    )

    size = lax.axis_size("gy")
    below = lax.ppermute(upstream[24:32], "gy", [(i, i + 1) for i in range(size - 1)])
    above = lax.ppermute(upstream[0:8], "gy", [(i + 1, i) for i in range(size - 1)])
    loss_parts = neighbours(jnp.concatenate([below, upstream, above], 0))
    loss_map, loss_out = stencil("both", loss_parts)
    loss_arrived = exchange(loss_out)

    right_out, image_out, real, imaginary, power, spectrum = filter_call(
        first_filter_kernel,
        (shape(*tiles), shape(*tiles), shape(*spectral), shape(*spectral), shape(*spectral), shape(*spectral)),
        [is_first],
        [first],
    )
    right = call(gather_kernel, shape(*frame), [*from_x, exchange(right_out)])
    blurred = call(gather_kernel, shape(*frame), [*from_x, exchange(image_out)])
    right_parts = neighbours(right)
    image, right_map, image_send = stencil("add", right_parts, blurred)
    further_out, image_spectrum = filter_call(
        second_filter_kernel,
        (shape(*tiles), shape(*spectral)),
        [is_first],
        [exchange(image_send), power, spectrum],
    )
    image_parts = neighbours(image)
    image_back, image_map, further_send = stencil("plain", image_parts)
    further_arrived = exchange(further_send)
    further = call(gather_kernel, shape(*frame), [*from_x, exchange(further_out)]) + image_back
    further_parts = neighbours(further)
    unused, further_map, last_send = stencil("plain", further_parts)
    last_arrived = exchange(last_send)

    moments = summed(call(moments_kernel, shape(1, 128), [right, image, further, loss_parts[0]]))
    alpha, gamma, g0, g1, g2, g3 = factors(*(moments[k] for k in range(6)))
    filter_factors = jnp.stack([alpha, gamma, 2.0 * g0, 2.0 * g1, 2.0 * g2, 2.0 * g3])
    result_out = filter_call(
        last_filter_kernel,
        shape(*tile),
        [is_first, filter_factors],
        [last_arrived, further_arrived, loss_arrived, real, imaginary, power, spectrum, image_spectrum],
    )
    grad_measured = call(final_kernel, shape(ROWS, COLS), [*from_x, exchange(result_out)])

    stencil_factors = jnp.stack([gamma, g1, 2.0 * g2, 2.0 * g3, 2.0 * g3, g3])
    operands = [stencil_factors]
    for parts in (right_parts, image_parts, further_parts, loss_parts):
        operands += [parts[1], parts[0], parts[3]]
    operands += [right_map, image_map, further_map, loss_map]
    scratch = (pltpu.VMEM((3, FRAME, COLS), F32), pltpu.VMEM((3, ROWS, COLS), F32))
    terms = summed(call(correlate_kernel, shape(1, 128), operands, 1, scratch))
    grad_stencil = terms[:27].reshape(3, 3, 3) / math.sqrt(cells)
    return grad_measured[None], grad_stencil


def solution(mesh):
    return jax.shard_map(
        local,
        mesh=mesh,
        in_specs=(P("gz", "gy", None), P("gy", None), P(), P("gz", "gy", None)),
        out_specs=(P("gz", "gy", None), P()),
        check_vma=False,
    )
```

time: 912 us -> 407 us (0.45); the launches traced: 899 us -> 403 us
  blocking collectives: 265 us -> 88.7 us
  other arithmetic: 144 us -> 4.06 us
  local copies, waits for them, and re-layouts: 164 us -> 47.5 us
  waiting for transfers between devices: 119 us -> 83.1 us
  Pallas kernels: 0 us -> 35.8 us
  matrix products: 34.8 us -> 0 us
  starting transfers between devices: 157 us -> 126 us
    psum x20 -> x0, blocking collectives: 265 us -> none  [by_axis(): value = lax.psum(value, axis)]
    all_to_all x0 -> x4, blocking collectives: none -> 88.7 us  [the longest x2 48.7 us: exchange(): return lax.all_to_all(value, 'gy', 0, 0, tiled=True)]
    another operation x23 -> x2, local copies, waits for them, and re-layouts: 68.8 us -> 0.74 us  [the longest x1 0.66 us: local(): stencil_factors = jnp.stack([gamma, g1, 2.0 * g2, 2.0 * g3, 2.0 * g3, g3])]
    reduce_sum x10 -> x4, other arithmetic: 64.1 us -> 2.51 us  [summed(): row = jnp.sum(lax.all_to_all(copies, axis, 0, 0, tiled=True), 0)]
    add x14 -> x1, other arithmetic: 36 us -> 0.02 us  [local(): call(gather_kernel, shape(*frame), [*from_x, exchange(further_out)])]
    pallas_call x0 -> x14, Pallas kernels: none -> 35.8 us  [call(): pl.pallas_call(body, out_shape=out_shape, in_specs=memory, out_specs=jax....]
    dot_general x36 -> x0, matrix products: 34.8 us -> none  [contract(): return jnp.einsum(form, left, table, precision=highest)]
    ppermute x24 -> x18, waiting for transfers between devices: 24.1 us -> 0.05 us  [the longest x16 0.04 us: moved(): return lax.ppermute(value, 'gz', pairs)]
  transfers between devices with their start and end apart: 33 -> 27, of which waited for: 19 -> 6; matrix products, arithmetic and copies ran while one was open for 16% -> 2% of each run, Pallas kernels for 0% -> 6%
where the time goes in v1:
time: 407 us; the launch traced here: 403 us
  starting transfers between devices  126 us (31%)
  blocking collectives  88.7 us (22%)
  waiting for transfers between devices  83.1 us (20%)
  local copies, waits for them, and re-layouts  47.5 us (12%)
  Pallas kernels  35.8 us (9%)
  between operations  18.4 us (5%)
    all_to_all x7, waiting for transfers between devices, exchange(): return lax.all_to_all(value, 'gy', 0, 0, tiled=True)  80.5 us
    all_to_all x7, starting transfers between devices, exchange(): return lax.all_to_all(value, 'gy', 0, 0, tiled=True)  52.4 us
    all_to_all x2, blocking collectives, exchange(): return lax.all_to_all(value, 'gy', 0, 0, tiled=True)  48.7 us
    ppermute x16, starting transfers between devices, moved(): return lax.ppermute(value, 'gz', pairs)  46.9 us
    unnamed x154, local copies, waits for them, and re-layouts  40.7 us
    all_to_all x2, blocking collectives, summed(): row = jnp.sum(lax.all_to_all(copies, axis, 0, 0, tiled=True), 0)  40 us
    pallas_call x14, Pallas kernels, call(): pl.pallas_call(body, out_shape=out_shape, in_specs=memory, out_specs=jax....  35.8 us
    all_to_all x2, starting transfers between devices, summed(): row = jnp.sum(lax.all_to_all(copies, axis, 0, 0, tiled=True), 0)  20.5 us
  transfers between devices with their start and end apart: 27, of which 6 were waited for; matrix products, arithmetic and copies ran while one was open for 2% of the time, Pallas kernels for 6%

profile of v1, /device:TPU:1, one launch (start us, length us, event | category | flops | bytes accessed | tf_op | source)
XLA Modules:
  0.0 403.5 jit_solution(17675710800775582068)
XLA Ops:
  0.6 1.6 copy-done
  2.2 1.6 copy-done.2
  5.7 3.1 shard_map.167
  8.8 16.9 %all-to-all-start = ((f32[32,16,128]{2,1,0:T(8,128)}), f32[32,16,128]{2,1,0:T(8,128)S(1)}, u32[]{:S(2)}, u32[]{:S(2)}) async-start(f32[32,16,128]{2,1,0:T(8,128)} %shard_map.167), calls=%async_computation | async-start | bytes 524288 | tf_op jit(solution)/shard_map/all_to_all | solution.py:364
  25.7 22.0 %all-to-all-done.refs_9_ = f32[32,16,128]{2,1,0:T(8,128)S(1)} async-done(((f32[32,16,128]{2,1,0:T(8,128)}), f32[32,16,128]{2,1,0:T(8,128)S(1)}, u32[]{:S(2)}, u32[]{:S(2)}) %all-to-all-start) | async-done | bytes 262176 | tf_op jit(solution)/shard_map/all_to_all | solution.py:364
  47.7 2.9 shard_map.168
  51.3 25.6 %all_to_all.65.arrived = f32[32,16,128]{2,1,0:T(8,128)S(1)} all-to-all(f32[32,16,128]{2,1,0:T(8,128)S(1)} %get-tuple-element.20), channel_id=1, replica_groups=mesh['gy'=32,'gz'=16] {'gy'}, dimensions={0} | all-to-all | bytes 524288 | tf_op jit(solution)/shard_map/all_to_all | solution.py:364
  76.9 4.7 %all-to-all-start.2 = ((f32[32,16,128]{2,1,0:T(8,128)}), f32[32,16,128]{2,1,0:T(8,128)S(1)}, u32[]{:S(2)}, u32[]{:S(2)}) async-start(f32[32,16,128]{2,1,0:T(8,128)} %get-tuple-element.21), calls=%async_computation.2 | async-start | bytes 524288 | tf_op jit(solution)/shard_map/all_to_all | solution.py:364
  81.6 1.6 copy-done.11
  84.0 3.1 collective-permute-start
  87.2 4.3 %collective-permute-start.1 = (f32[48,1024]{1,0:T(8,128)S(1)}, f32[48,1024]{1,0:T(8,128)S(1)}, u32[]{:S(2)}, u32[]{:S(2)}) collective-permute-start(f32[48,1024]{1,0:T(8,128)S(1)} %shard_map.169.own.right.refs_1_), channel_id=1, source_target_pairs={{0,2},{1,3},{2,4},{3,5},{4,6},{5,7},{6,8},{7,9},{8,10},{9,11},{10,... | collective-permute-start | bytes 589832 | tf_op jit(solution)/shard_map/ppermute | solution.py:372
  95.4 8.2 %all-to-all-done.2.arrived = f32[32,16,128]{2,1,0:T(8,128)S(1)} async-done(((f32[32,16,128]{2,1,0:T(8,128)}), f32[32,16,128]{2,1,0:T(8,128)S(1)}, u32[]{:S(2)}, u32[]{:S(2)}) %all-to-all-start.2) | async-done | bytes 262176 | tf_op jit(solution)/shard_map/all_to_all | solution.py:364
  103.6 1.6 copy-done.8
  105.2 1.6 copy-done.12
  108.4 3.6 shard_map.171
  112.6 23.1 %all_to_all.66.refs_9_ = f32[32,8,128]{2,1,0:T(8,128)S(1)} all-to-all(f32[32,8,128]{2,1,0:T(8,128)S(1)} %get-tuple-element.23), channel_id=1, replica_groups=mesh['gy'=32,'gz'=16] {'gy'}, dimensions={0} | all-to-all | bytes 262144 | tf_op jit(solution)/shard_map/all_to_all | solution.py:364
  135.8 2.1 shard_map.172
  137.9 5.3 %all-to-all-start.4 = ((f32[32,16,128]{2,1,0:T(8,128)}), f32[32,16,128]{2,1,0:T(8,128)S(1)}, u32[]{:S(2)}, u32[]{:S(2)}) async-start(f32[32,16,128]{2,1,0:T(8,128)} %get-tuple-element.26), calls=%async_computation.4 | async-start | bytes 524288 | tf_op jit(solution)/shard_map/all_to_all | solution.py:364
  143.2 6.6 %collective-permute-start.4 = (f32[48,1024]{1,0:T(8,128)S(1)}, f32[48,1024]{1,0:T(8,128)S(1)}, u32[]{:S(2)}, u32[]{:S(2)}) collective-permute-start(f32[48,1024]{1,0:T(8,128)S(1)} %get-tuple-element.22.own.image.refs_4_), channel_id=1, source_target_pairs={{0,1},{1,2},{2,3},{3,4},{4,5},{5,6},{6,7},{7,8},{8,9},{9,10},{10,1... | collective-permute-start | bytes 589832 | tf_op jit(solution)/shard_map/ppermute | solution.py:372
  149.9 4.6 %collective-permute-start.5 = (f32[48,1024]{1,0:T(8,128)S(1)}, f32[48,1024]{1,0:T(8,128)S(1)}, u32[]{:S(2)}, u32[]{:S(2)}) collective-permute-start(f32[48,1024]{1,0:T(8,128)S(1)} %get-tuple-element.22.own.image.refs_4_), channel_id=1, source_target_pairs={{0,2},{1,3},{2,4},{3,5},{4,6},{5,7},{6,8},{7,9},{8,10},{9,11},{10,... | collective-permute-start | bytes 589832 | tf_op jit(solution)/shard_map/ppermute | solution.py:372
  156.5 2.8 collective-permute-start.9
  159.3 3.2 collective-permute-start.8
  164.8 5.0 %collective-permute-start.14 = (f32[48,1024]{1,0:T(8,128)S(1)}, f32[48,1024]{1,0:T(8,128)}, u32[]{:S(2)}, u32[]{:S(2)}) collective-permute-start(f32[48,1024]{1,0:T(8,128)S(1)} %pad_maximum_fusion.upstream.own.refs_10_), channel_id=1, source_target_pairs={{0,1},{1,2},{2,3},{3,4},{4,5},{5,6},{6,7},{7,8},{8,9},{9,10},{10,1... | collective-permute-start | bytes 589832 | tf_op jit(solution)/shard_map/ppermute | solution.py:372
  169.8 6.1 %collective-permute-start.15 = (f32[48,1024]{1,0:T(8,128)S(1)}, f32[48,1024]{1,0:T(8,128)}, u32[]{:S(2)}, u32[]{:S(2)}) collective-permute-start(f32[48,1024]{1,0:T(8,128)S(1)} %pad_maximum_fusion.upstream.own.refs_10_), channel_id=1, source_target_pairs={{0,2},{1,3},{2,4},{3,5},{4,6},{5,7},{6,8},{7,9},{8,10},{9,11},{10,... | collective-permute-start | bytes 589832 | tf_op jit(solution)/shard_map/ppermute | solution.py:372
  178.5 1.6 copy-done.4
  181.3 3.6 shard_map.174
  188.3 1.6 copy-done.9
  189.9 1.6 copy-done.13
  193.2 12.0 %all-to-all-start.5 = ((f32[32,1,128]{2,1,0:T(1,128)}), f32[32,1,128]{2,1,0:T(1,128)}, u32[]{:S(2)}, u32[]{:S(2)}) async-start(f32[32,1,128]{2,1,0:T(1,128)} %broadcast_in_dim.15), calls=%async_computation.5 | async-start | bytes 32768 | tf_op jit(solution)/shard_map/all_to_all | solution.py:381
  205.3 1.6 copy-done.5
  208.1 4.8 %shard_map.177 = (f32[48,1024]{1,0:T(8,128)S(1)}, f32[32,16,128]{2,1,0:T(8,128)S(1)}) custom-call(s32[3]{0:T(128)S(1)} %copy-done.68, f32[27]{0:T(128)S(1)} %copy-done.72, bf16[1024,1024]{1,0:T(8,128)(2,1)S(1)} %copy-done.1, bf16[1024,1024]{1,0:T(8,128)(2,1)S(1)} %copy-done.5, f32[48,1024]{1,0:T(8,128)S(1)} %pad_maximum_fusion.upstream.own.refs_10_, ...), custom_call_target="tpu_custom_call" | custom-call | flops 200000000 | bytes 8000000 | tf_op jit(solution)/shard_map/pallas_call | solution.py:352
  214.3 2.6 all-to-all-done.5
  216.9 9.6 %all-to-all-start.9 = ((f32[32,16,128]{2,1,0:T(8,128)}), f32[32,16,128]{2,1,0:T(8,128)S(1)}, u32[]{:S(2)}, u32[]{:S(2)}) async-start(f32[32,16,128]{2,1,0:T(8,128)} %copy-done.19), calls=%async_computation.9 | async-start | bytes 524288 | tf_op jit(solution)/shard_map/all_to_all | solution.py:364
  227.7 20.7 %all-to-all-done.9.refs_12_ = f32[32,16,128]{2,1,0:T(8,128)S(1)} async-done(((f32[32,16,128]{2,1,0:T(8,128)}), f32[32,16,128]{2,1,0:T(8,128)S(1)}, u32[]{:S(2)}, u32[]{:S(2)}) %all-to-all-start.9) | async-done | bytes 262176 | tf_op jit(solution)/shard_map/all_to_all | solution.py:364
  249.1 15.5 %all_to_all.67 = f32[16,1,128]{2,1,0:T(1,128)} all-to-all(f32[16,1,128]{2,1,0:T(1,128)S(1)} %broadcast_in_dim.16), channel_id=1, replica_groups=mesh['gy'=32,'gz'=16] {'gz'}, dimensions={0} | all-to-all | bytes 16384 | tf_op jit(solution)/shard_map/all_to_all | solution.py:381
  264.7 6.4 %all-to-all-start.8 = ((f32[32,8,128]{2,1,0:T(8,128)}), f32[32,8,128]{2,1,0:T(8,128)}, u32[]{:S(2)}, u32[]{:S(2)}) async-start(f32[32,8,128]{2,1,0:T(8,128)} %copy-done.42), calls=%async_computation.8 | async-start | bytes 262144 | tf_op jit(solution)/shard_map/all_to_all | solution.py:364
  271.1 3.0 collective-permute-start.10
  274.1 3.6 collective-permute-start.11
  301.7 4.4 %shard_map.176 = (f32[48,1024]{1,0:T(8,128)}, f32[48,1024]{1,0:T(8,128)S(1)}, f32[32,8,128]{2,1,0:T(8,128)S(1)}) custom-call(s32[3]{0:T(128)S(1)} %copy-done.69, f32[27]{0:T(128)S(1)} %copy-done.73, bf16[1024,1024]{1,0:T(8,128)(2,1)S(1)} %copy-done.1, bf16[1024,1024]{1,0:T(8,128)(2,1)S(1)} %copy-done.6, f32[48,1024]{1,0:T(8,128)S(1)} %add.15.further.own.refs_7_, ...), custom_call_target="tpu_custom_call" | custom-call | flops 200000000 | bytes 8000000 | tf_op jit(solution)/shard_map/pallas_call | solution.py:352
  306.8 2.9 shard_map.180
  310.8 24.4 %all_to_all.68 = f32[32,1,128]{2,1,0:T(1,128)S(1)} all-to-all(f32[32,1,128]{2,1,0:T(1,128)S(1)} %broadcast_in_dim.36), channel_id=1, replica_groups=mesh['gy'=32,'gz'=16] {'gy'}, dimensions={0} | all-to-all | bytes 32768 | tf_op jit(solution)/shard_map/all_to_all | solution.py:381
  335.2 4.4 %all-to-all-start.7 = ((f32[32,8,128]{2,1,0:T(8,128)}), f32[32,8,128]{2,1,0:T(8,128)S(1)}, u32[]{:S(2)}, u32[]{:S(2)}) async-start(f32[32,8,128]{2,1,0:T(8,128)} %copy-done.43), calls=%async_computation.7 | async-start | bytes 262144 | tf_op jit(solution)/shard_map/all_to_all | solution.py:364
  341.7 14.1 %all-to-all-done.7.refs_10_ = f32[32,8,128]{2,1,0:T(8,128)S(1)} async-done(((f32[32,8,128]{2,1,0:T(8,128)}), f32[32,8,128]{2,1,0:T(8,128)S(1)}, u32[]{:S(2)}, u32[]{:S(2)}) %all-to-all-start.7) | async-done | bytes 131104 | tf_op jit(solution)/shard_map/all_to_all | solution.py:364
  356.4 8.5 %all-to-all-start.12 = ((f32[16,1,128]{2,1,0:T(1,128)}), f32[16,1,128]{2,1,0:T(1,128)S(1)}, u32[]{:S(2)}, u32[]{:S(2)}) async-start(f32[16,1,128]{2,1,0:T(1,128)} %broadcast_in_dim.37), calls=%async_computation.12 | async-start | bytes 16384 | tf_op jit(solution)/shard_map/all_to_all | solution.py:381
  374.7 4.3 %shard_map.178 = f32[32,8,128]{2,1,0:T(8,128)} custom-call(f32[1]{0:T(128)} %bitcast.refs_0_, f32[6]{0:T(128)S(1)} %stack.52.refs_1_, bf16[64,32]{1,0:T(8,128)(2,1)S(1)} %copy-done.56, bf16[64,32]{1,0:T(8,128)(2,1)S(1)} %copy-done.59, f32[32,128]{1,0:T(8,128)S(1)} %copy-done.62, f32[32,128]{1,0:T(8,128)S(1)} %copy-done.65, bf16[128,128]{1,0:T(8,128)(2,1)S(1)} %copy-done.46, ...), custom_call_target="tpu_custom_call" | custom-call | flops 200000000 | bytes 8000000 | tf_op jit(solution)/shard_map/pallas_call | solution.py:352
  379.0 5.1 %all-to-all-start.10 = ((f32[32,8,128]{2,1,0:T(8,128)}), f32[32,8,128]{2,1,0:T(8,128)S(1)}, u32[]{:S(2)}, u32[]{:S(2)}) async-start(f32[32,8,128]{2,1,0:T(8,128)} %shard_map.178), calls=%async_computation.10 | async-start | bytes 262144 | tf_op jit(solution)/shard_map/all_to_all | solution.py:364
  384.9 15.5 %all-to-all-done.10.arrived = f32[32,8,128]{2,1,0:T(8,128)S(1)} async-done(((f32[32,8,128]{2,1,0:T(8,128)}), f32[32,8,128]{2,1,0:T(8,128)S(1)}, u32[]{:S(2)}, u32[]{:S(2)}) %all-to-all-start.10) | async-done | bytes 131104 | tf_op jit(solution)/shard_map/all_to_all | solution.py:364
  400.4 1.6 copy-done.14
  (196 shorter events, 50.5 us)
Async XLA Ops:
  5.6 42.0 %copy-start.44 = (bf16[128,128]{1,0:T(8,128)(2,1)S(1)}, bf16[128,128]{1,0:T(8,128)(2,1)}, u32[]{:S(2)}) copy-start(bf16[128,128]{1,0:T(8,128)(2,1)} %constant.54.clone.refs_5_.refs_6_) | copy-start | bytes 98308
  5.6 42.0 %copy-start.47 = (bf16[128,128]{1,0:T(8,128)(2,1)S(1)}, bf16[128,128]{1,0:T(8,128)(2,1)}, u32[]{:S(2)}) copy-start(bf16[128,128]{1,0:T(8,128)(2,1)} %constant.55.clone.refs_6_.refs_7_) | copy-start | bytes 98308
  5.6 42.0 %copy-start.50 = (bf16[128,128]{1,0:T(8,128)(2,1)S(1)}, bf16[128,128]{1,0:T(8,128)(2,1)}, u32[]{:S(2)}) copy-start(bf16[128,128]{1,0:T(8,128)(2,1)} %constant.56.clone.refs_7_.refs_8_) | copy-start | bytes 98308
  5.6 42.0 %copy-start.53 = (bf16[128,128]{1,0:T(8,128)(2,1)S(1)}, bf16[128,128]{1,0:T(8,128)(2,1)}, u32[]{:S(2)}) copy-start(bf16[128,128]{1,0:T(8,128)(2,1)} %constant.57.clone.refs_8_.refs_9_) | copy-start | bytes 98308
  5.6 42.0 %copy-start.56 = (bf16[64,32]{1,0:T(8,128)(2,1)S(1)}, bf16[64,32]{1,0:T(8,128)(2,1)}, u32[]{:S(2)}) copy-start(bf16[64,32]{1,0:T(8,128)(2,1)} %constant.50.clone.refs_1_.refs_2_) | copy-start | bytes 12292
  5.6 42.0 %copy-start.57 = (bf16[64,32]{1,0:T(8,128)(2,1)S(1)}, bf16[64,32]{1,0:T(8,128)(2,1)}, u32[]{:S(2)}) copy-start(bf16[64,32]{1,0:T(8,128)(2,1)} %constant.51.clone.refs_2_.refs_3_) | copy-start | bytes 12292
  5.7 42.0 %copy-start.60 = (f32[32,128]{1,0:T(8,128)S(1)}, f32[32,128]{1,0:T(8,128)}, u32[]{:S(2)}) copy-start(f32[32,128]{1,0:T(8,128)} %constant.52.clone.refs_3_.refs_4_) | copy-start | bytes 49156
  5.7 42.0 %copy-start.63 = (f32[32,128]{1,0:T(8,128)S(1)}, f32[32,128]{1,0:T(8,128)}, u32[]{:S(2)}) copy-start(f32[32,128]{1,0:T(8,128)} %constant.53.clone.refs_4_.refs_5_) | copy-start | bytes 49156
  8.8 72.8 %copy-start.7 = (bf16[1024,1024]{1,0:T(8,128)(2,1)S(1)}, bf16[1024,1024]{1,0:T(8,128)(2,1)}, u32[]{:S(2)}) copy-start(bf16[1024,1024]{1,0:T(8,128)(2,1)} %constant.48.clone.high_ref) | copy-start | bytes 6291460
  8.8 38.9 %all-to-all-start = ((f32[32,16,128]{2,1,0:T(8,128)}), f32[32,16,128]{2,1,0:T(8,128)S(1)}, u32[]{:S(2)}, u32[]{:S(2)}) async-start(f32[32,16,128]{2,1,0:T(8,128)} %shard_map.167), calls=%async_computation | async-start | bytes 524288 | tf_op jit(solution)/shard_map/all_to_all | solution.py:364
  51.3 32.8 %copy-start.30 = (f32[288,128]{1,0:T(8,128)}, f32[288,128]{1,0:T(8,128)S(1)}, u32[]{:S(2)}) copy-start(f32[288,128]{1,0:T(8,128)S(1)} %get-tuple-element.32.refs_14_) | copy-start | bytes 442372
  76.9 26.7 %all-to-all-start.2 = ((f32[32,16,128]{2,1,0:T(8,128)}), f32[32,16,128]{2,1,0:T(8,128)S(1)}, u32[]{:S(2)}, u32[]{:S(2)}) async-start(f32[32,16,128]{2,1,0:T(8,128)} %get-tuple-element.21), calls=%async_computation.2 | async-start | bytes 524288 | tf_op jit(solution)/shard_map/all_to_all | solution.py:364
  84.0 23.7 %collective-permute-start = (f32[48,1024]{1,0:T(8,128)S(1)}, f32[48,1024]{1,0:T(8,128)S(1)}, u32[]{:S(2)}, u32[]{:S(2)}) collective-permute-start(f32[48,1024]{1,0:T(8,128)S(1)} %shard_map.169.own.right.refs_1_), channel_id=1, source_target_pairs={{0,1},{1,2},{2,3},{3,4},{4,5},{5,6},{6,7},{7,8},{8,9},{9,10},{10,1... | collective-permute-start | bytes 589832 | tf_op jit(solution)/shard_map/ppermute | solution.py:372
  87.2 20.6 %collective-permute-start.1 = (f32[48,1024]{1,0:T(8,128)S(1)}, f32[48,1024]{1,0:T(8,128)S(1)}, u32[]{:S(2)}, u32[]{:S(2)}) collective-permute-start(f32[48,1024]{1,0:T(8,128)S(1)} %shard_map.169.own.right.refs_1_), channel_id=1, source_target_pairs={{0,2},{1,3},{2,4},{3,5},{4,6},{5,7},{6,8},{7,9},{8,10},{9,11},{10,... | collective-permute-start | bytes 589832 | tf_op jit(solution)/shard_map/ppermute | solution.py:372
  91.5 16.2 %collective-permute-start.2 = (f32[48,1024]{1,0:T(8,128)S(1)}, f32[48,1024]{1,0:T(8,128)S(1)}, u32[]{:S(2)}, u32[]{:S(2)}) collective-permute-start(f32[48,1024]{1,0:T(8,128)S(1)} %shard_map.169.own.right.refs_1_), channel_id=1, source_target_pairs={{1,0},{2,1},{3,2},{4,3},{5,4},{6,5},{7,6},{8,7},{9,8},{10,9},{11,1... | collective-permute-start | bytes 589832 | tf_op jit(solution)/shard_map/ppermute | solution.py:372
  92.8 14.9 %collective-permute-start.3 = (f32[48,1024]{1,0:T(8,128)S(1)}, f32[48,1024]{1,0:T(8,128)S(1)}, u32[]{:S(2)}, u32[]{:S(2)}) collective-permute-start(f32[48,1024]{1,0:T(8,128)S(1)} %shard_map.169.own.right.refs_1_), channel_id=1, source_target_pairs={{2,0},{3,1},{4,2},{5,3},{6,4},{7,5},{8,6},{9,7},{10,8},{11,9},{12,... | collective-permute-start | bytes 589832 | tf_op jit(solution)/shard_map/ppermute | solution.py:372
  107.6 28.1 %copy-start.33 = (f32[288,128]{1,0:T(8,128)S(1)}, f32[288,128]{1,0:T(8,128)}, u32[]{:S(2)}) copy-start(f32[288,128]{1,0:T(8,128)} %copy-done.32) | copy-start | bytes 442372
  107.6 28.1 %copy-start.36 = (f32[288,128]{1,0:T(8,128)S(1)}, f32[288,128]{1,0:T(8,128)}, u32[]{:S(2)}) copy-start(f32[288,128]{1,0:T(8,128)} %copy-done.35) | copy-start | bytes 442372
  107.6 28.1 %copy-start.45 = (bf16[128,128]{1,0:T(8,128)(2,1)S(1)}, bf16[128,128]{1,0:T(8,128)(2,1)}, u32[]{:S(2)}) copy-start(bf16[128,128]{1,0:T(8,128)(2,1)} %constant.54.clone.refs_5_.refs_6_) | copy-start | bytes 98308
  107.7 28.1 %copy-start.48 = (bf16[128,128]{1,0:T(8,128)(2,1)S(1)}, bf16[128,128]{1,0:T(8,128)(2,1)}, u32[]{:S(2)}) copy-start(bf16[128,128]{1,0:T(8,128)(2,1)} %constant.55.clone.refs_6_.refs_7_) | copy-start | bytes 98308
  107.7 28.1 %copy-start.51 = (bf16[128,128]{1,0:T(8,128)(2,1)S(1)}, bf16[128,128]{1,0:T(8,128)(2,1)}, u32[]{:S(2)}) copy-start(bf16[128,128]{1,0:T(8,128)(2,1)} %constant.56.clone.refs_7_.refs_8_) | copy-start | bytes 98308
  107.7 28.1 %copy-start.54 = (bf16[128,128]{1,0:T(8,128)(2,1)S(1)}, bf16[128,128]{1,0:T(8,128)(2,1)}, u32[]{:S(2)}) copy-start(bf16[128,128]{1,0:T(8,128)(2,1)} %constant.57.clone.refs_8_.refs_9_) | copy-start | bytes 98308
  107.7 28.1 %copy-start.58 = (bf16[64,32]{1,0:T(8,128)(2,1)S(1)}, bf16[64,32]{1,0:T(8,128)(2,1)}, u32[]{:S(2)}) copy-start(bf16[64,32]{1,0:T(8,128)(2,1)} %constant.51.clone.refs_2_.refs_3_) | copy-start | bytes 12292
  107.7 28.1 %copy-start.61 = (f32[32,128]{1,0:T(8,128)S(1)}, f32[32,128]{1,0:T(8,128)}, u32[]{:S(2)}) copy-start(f32[32,128]{1,0:T(8,128)} %constant.52.clone.refs_3_.refs_4_) | copy-start | bytes 49156
  107.7 28.1 %copy-start.64 = (f32[32,128]{1,0:T(8,128)S(1)}, f32[32,128]{1,0:T(8,128)}, u32[]{:S(2)}) copy-start(f32[32,128]{1,0:T(8,128)} %constant.53.clone.refs_4_.refs_5_) | copy-start | bytes 49156
  137.9 26.0 %copy-start.38 = (f32[288,128]{1,0:T(8,128)}, f32[288,128]{1,0:T(8,128)S(1)}, u32[]{:S(2)}) copy-start(f32[288,128]{1,0:T(8,128)S(1)} %get-tuple-element.33.refs_17_) | copy-start | bytes 442372
  137.9 50.4 %all-to-all-start.4 = ((f32[32,16,128]{2,1,0:T(8,128)}), f32[32,16,128]{2,1,0:T(8,128)S(1)}, u32[]{:S(2)}, u32[]{:S(2)}) async-start(f32[32,16,128]{2,1,0:T(8,128)} %get-tuple-element.26), calls=%async_computation.4 | async-start | bytes 524288 | tf_op jit(solution)/shard_map/all_to_all | solution.py:364
  143.2 26.5 %collective-permute-start.4 = (f32[48,1024]{1,0:T(8,128)S(1)}, f32[48,1024]{1,0:T(8,128)S(1)}, u32[]{:S(2)}, u32[]{:S(2)}) collective-permute-start(f32[48,1024]{1,0:T(8,128)S(1)} %get-tuple-element.22.own.image.refs_4_), channel_id=1, source_target_pairs={{0,1},{1,2},{2,3},{3,4},{4,5},{5,6},{6,7},{7,8},{8,9},{9,10},{10,1... | collective-permute-start | bytes 589832 | tf_op jit(solution)/shard_map/ppermute | solution.py:372
  149.9 26.0 %collective-permute-start.5 = (f32[48,1024]{1,0:T(8,128)S(1)}, f32[48,1024]{1,0:T(8,128)S(1)}, u32[]{:S(2)}, u32[]{:S(2)}) collective-permute-start(f32[48,1024]{1,0:T(8,128)S(1)} %get-tuple-element.22.own.image.refs_4_), channel_id=1, source_target_pairs={{0,2},{1,3},{2,4},{3,5},{4,6},{5,7},{6,8},{7,9},{8,10},{9,11},{10,... | collective-permute-start | bytes 589832 | tf_op jit(solution)/shard_map/ppermute | solution.py:372
  154.4 22.7 %collective-permute-start.6 = (f32[48,1024]{1,0:T(8,128)S(1)}, f32[48,1024]{1,0:T(8,128)S(1)}, u32[]{:S(2)}, u32[]{:S(2)}) collective-permute-start(f32[48,1024]{1,0:T(8,128)S(1)} %get-tuple-element.22.own.image.refs_4_), channel_id=1, source_target_pairs={{1,0},{2,1},{3,2},{4,3},{5,4},{6,5},{7,6},{8,7},{9,8},{10,9},{11,1... | collective-permute-start | bytes 589832 | tf_op jit(solution)/shard_map/ppermute | solution.py:372
  156.5 6.0 %collective-permute-start.9 = (f32[8,1024]{1,0:T(8,128)S(1)}, f32[8,1024]{1,0:T(8,128)S(1)}, u32[]{:S(2)}, u32[]{:S(2)}) collective-permute-start(f32[8,1024]{1,0:T(8,128)S(1)} %get-tuple-element.39), channel_id=1, source_target_pairs={{16,0},{32,16},{48,32},{64,48},{80,64},{96,80},{112,96},{128,112},... | collective-permute-start | bytes 98312 | tf_op jit(solution)/shard_map/ppermute | solution.py:438
  159.3 4.5 %collective-permute-start.8 = (f32[8,1024]{1,0:T(8,128)S(1)}, f32[8,1024]{1,0:T(8,128)S(1)}, u32[]{:S(2)}, u32[]{:S(2)}) collective-permute-start(f32[8,1024]{1,0:T(8,128)S(1)} %get-tuple-element.38), channel_id=1, source_target_pairs={{0,16},{16,32},{32,48},{48,64},{64,80},{80,96},{96,112},{112,128},... | collective-permute-start | bytes 98312 | tf_op jit(solution)/shard_map/ppermute | solution.py:437
  162.6 15.9 %collective-permute-start.7 = (f32[48,1024]{1,0:T(8,128)S(1)}, f32[48,1024]{1,0:T(8,128)S(1)}, u32[]{:S(2)}, u32[]{:S(2)}) collective-permute-start(f32[48,1024]{1,0:T(8,128)S(1)} %get-tuple-element.22.own.image.refs_4_), channel_id=1, source_target_pairs={{2,0},{3,1},{4,2},{5,3},{6,4},{7,5},{8,6},{9,7},{10,8},{11,9},{12,... | collective-permute-start | bytes 589832 | tf_op jit(solution)/shard_map/ppermute | solution.py:372
  164.8 40.5 %collective-permute-start.14 = (f32[48,1024]{1,0:T(8,128)S(1)}, f32[48,1024]{1,0:T(8,128)}, u32[]{:S(2)}, u32[]{:S(2)}) collective-permute-start(f32[48,1024]{1,0:T(8,128)S(1)} %pad_maximum_fusion.upstream.own.refs_10_), channel_id=1, source_target_pairs={{0,1},{1,2},{2,3},{3,4},{4,5},{5,6},{6,7},{7,8},{8,9},{9,10},{10,1... | collective-permute-start | bytes 589832 | tf_op jit(solution)/shard_map/ppermute | solution.py:372
  169.8 35.5 %collective-permute-start.15 = (f32[48,1024]{1,0:T(8,128)S(1)}, f32[48,1024]{1,0:T(8,128)}, u32[]{:S(2)}, u32[]{:S(2)}) collective-permute-start(f32[48,1024]{1,0:T(8,128)S(1)} %pad_maximum_fusion.upstream.own.refs_10_), channel_id=1, source_target_pairs={{0,2},{1,3},{2,4},{3,5},{4,6},{5,7},{6,8},{7,9},{8,10},{9,11},{10,... | collective-permute-start | bytes 589832 | tf_op jit(solution)/shard_map/ppermute | solution.py:372
  175.9 29.4 %collective-permute-start.16 = (f32[48,1024]{1,0:T(8,128)S(1)}, f32[48,1024]{1,0:T(8,128)}, u32[]{:S(2)}, u32[]{:S(2)}) collective-permute-start(f32[48,1024]{1,0:T(8,128)S(1)} %pad_maximum_fusion.upstream.own.refs_10_), channel_id=1, source_target_pairs={{1,0},{2,1},{3,2},{4,3},{5,4},{6,5},{7,6},{8,7},{9,8},{10,9},{11,1... | collective-permute-start | bytes 589832 | tf_op jit(solution)/shard_map/ppermute | solution.py:372
  177.2 28.1 %collective-permute-start.17 = (f32[48,1024]{1,0:T(8,128)S(1)}, f32[48,1024]{1,0:T(8,128)}, u32[]{:S(2)}, u32[]{:S(2)}) collective-permute-start(f32[48,1024]{1,0:T(8,128)S(1)} %pad_maximum_fusion.upstream.own.refs_10_), channel_id=1, source_target_pairs={{2,0},{3,1},{4,2},{5,3},{6,4},{7,5},{8,6},{9,7},{10,8},{11,9},{12,... | collective-permute-start | bytes 589832 | tf_op jit(solution)/shard_map/ppermute | solution.py:372
  193.2 23.6 %all-to-all-start.5 = ((f32[32,1,128]{2,1,0:T(1,128)}), f32[32,1,128]{2,1,0:T(1,128)}, u32[]{:S(2)}, u32[]{:S(2)}) async-start(f32[32,1,128]{2,1,0:T(1,128)} %broadcast_in_dim.15), calls=%async_computation.5 | async-start | bytes 32768 | tf_op jit(solution)/shard_map/all_to_all | solution.py:381
  216.9 31.6 %all-to-all-start.9 = ((f32[32,16,128]{2,1,0:T(8,128)}), f32[32,16,128]{2,1,0:T(8,128)S(1)}, u32[]{:S(2)}, u32[]{:S(2)}) async-start(f32[32,16,128]{2,1,0:T(8,128)} %copy-done.19), calls=%async_computation.9 | async-start | bytes 524288 | tf_op jit(solution)/shard_map/all_to_all | solution.py:364
  264.7 45.5 %all-to-all-start.8 = ((f32[32,8,128]{2,1,0:T(8,128)}), f32[32,8,128]{2,1,0:T(8,128)}, u32[]{:S(2)}, u32[]{:S(2)}) async-start(f32[32,8,128]{2,1,0:T(8,128)} %copy-done.42), calls=%async_computation.8 | async-start | bytes 262144 | tf_op jit(solution)/shard_map/all_to_all | solution.py:364
  271.1 27.8 %collective-permute-start.10 = (f32[48,1024]{1,0:T(8,128)S(1)}, f32[48,1024]{1,0:T(8,128)}, u32[]{:S(2)}, u32[]{:S(2)}) collective-permute-start(f32[48,1024]{1,0:T(8,128)S(1)} %add.15.further.own.refs_7_), channel_id=1, source_target_pairs={{0,1},{1,2},{2,3},{3,4},{4,5},{5,6},{6,7},{7,8},{8,9},{9,10},{10,1... | collective-permute-start | bytes 589832 | tf_op jit(solution)/shard_map/ppermute | solution.py:372
  274.1 24.7 %collective-permute-start.11 = (f32[48,1024]{1,0:T(8,128)S(1)}, f32[48,1024]{1,0:T(8,128)}, u32[]{:S(2)}, u32[]{:S(2)}) collective-permute-start(f32[48,1024]{1,0:T(8,128)S(1)} %add.15.further.own.refs_7_), channel_id=1, source_target_pairs={{0,2},{1,3},{2,4},{3,5},{4,6},{5,7},{6,8},{7,9},{8,10},{9,11},{10,... | collective-permute-start | bytes 589832 | tf_op jit(solution)/shard_map/ppermute | solution.py:372
  277.7 21.2 %collective-permute-start.12 = (f32[48,1024]{1,0:T(8,128)S(1)}, f32[48,1024]{1,0:T(8,128)}, u32[]{:S(2)}, u32[]{:S(2)}) collective-permute-start(f32[48,1024]{1,0:T(8,128)S(1)} %add.15.further.own.refs_7_), channel_id=1, source_target_pairs={{1,0},{2,1},{3,2},{4,3},{5,4},{6,5},{7,6},{8,7},{9,8},{10,9},{11,1... | collective-permute-start | bytes 589832 | tf_op jit(solution)/shard_map/ppermute | solution.py:372
  279.0 19.9 %collective-permute-start.13 = (f32[48,1024]{1,0:T(8,128)S(1)}, f32[48,1024]{1,0:T(8,128)}, u32[]{:S(2)}, u32[]{:S(2)}) collective-permute-start(f32[48,1024]{1,0:T(8,128)S(1)} %add.15.further.own.refs_7_), channel_id=1, source_target_pairs={{2,0},{3,1},{4,2},{5,3},{6,4},{7,5},{8,6},{9,7},{10,8},{11,9},{12,... | collective-permute-start | bytes 589832 | tf_op jit(solution)/shard_map/ppermute | solution.py:372
  306.8 93.6 %copy-start.10 = (bf16[1024,1024]{1,0:T(8,128)(2,1)S(1)}, bf16[1024,1024]{1,0:T(8,128)(2,1)}, u32[]{:S(2)}) copy-start(bf16[1024,1024]{1,0:T(8,128)(2,1)} %constant.48.clone.high_ref) | copy-start | bytes 6291460
  335.2 20.6 %all-to-all-start.7 = ((f32[32,8,128]{2,1,0:T(8,128)}), f32[32,8,128]{2,1,0:T(8,128)S(1)}, u32[]{:S(2)}, u32[]{:S(2)}) async-start(f32[32,8,128]{2,1,0:T(8,128)} %copy-done.43), calls=%async_computation.7 | async-start | bytes 262144 | tf_op jit(solution)/shard_map/all_to_all | solution.py:364
  356.4 22.6 %all-to-all-start.12 = ((f32[16,1,128]{2,1,0:T(1,128)}), f32[16,1,128]{2,1,0:T(1,128)S(1)}, u32[]{:S(2)}, u32[]{:S(2)}) async-start(f32[16,1,128]{2,1,0:T(1,128)} %broadcast_in_dim.37), calls=%async_computation.12 | async-start | bytes 16384 | tf_op jit(solution)/shard_map/all_to_all | solution.py:381
  379.0 21.3 %all-to-all-start.10 = ((f32[32,8,128]{2,1,0:T(8,128)}), f32[32,8,128]{2,1,0:T(8,128)S(1)}, u32[]{:S(2)}, u32[]{:S(2)}) async-start(f32[32,8,128]{2,1,0:T(8,128)} %shard_map.178), calls=%async_computation.10 | async-start | bytes 262144 | tf_op jit(solution)/shard_map/all_to_all | solution.py:364
  (56 other events, 150.6 us)

commit v2 on v1

v2 whole, which is shorter than its diff:
```python
import functools
import math

import jax
import jax.numpy as jnp
import ml_dtypes
import numpy as np
from jax import lax
from jax.experimental import pallas as pl
from jax.experimental.pallas import tpu as pltpu
from jax.sharding import Mesh
from jax.sharding import PartitionSpec as P

GY = ("gy_0", "gy_1")
GZ = ("gz_0", "gz_1")
ROWS = 32
COLS = 1024
FRAME = 48
BLOCKS = 9
F32 = jnp.float32
BF16 = jnp.bfloat16
VMEM = 14 * 1024 * 1024


def split_table(table):
    high = table.astype(ml_dtypes.bfloat16)
    low = (table - high.astype(np.float64)).astype(ml_dtypes.bfloat16)
    return high, low


def x_table():
    part, half, device, i = np.meshgrid(
        np.arange(2), np.arange(2), np.arange(32), np.arange(8), indexing="ij"
    )
    kx = 2 * (16 * (device % 16) + 8 * half + i) + device // 16
    part, kx = part.reshape(-1, 1), kx.reshape(-1, 1)
    x = np.arange(COLS // 2)[None, :]
    angle = 2.0 * np.pi * ((kx * x) % COLS) / COLS
    flip = 1.0 - 2.0 * (x % 2)
    wave = np.where(part == 0, np.cos(angle), -np.sin(angle))
    return np.where((kx == 0) & (part == 1), flip, wave)


def y_tables():
    q = np.arange(32)[:, None]
    s = np.arange(32)[None, :]
    angle = 2.0 * np.pi * ((q * s) % 32) / 32
    first = np.concatenate([np.cos(angle), np.sin(angle)], 0)
    lane = np.arange(128)
    part, half, t = lane // 64, lane // 32 % 2, lane % 32
    turn = 2.0 * np.pi * q * t[None, :] / 1024
    sign = np.where(part == 0, 1.0, -1.0)[None, :]
    turn_cos, turn_sin = np.cos(turn), np.sin(turn) * sign
    angle = 2.0 * np.pi * ((t[:, None] * t[None, :]) % 32) / 32
    pi, po = part[:, None], part[None, :]
    block = np.where(pi == po, np.cos(angle), np.where(pi > po, np.sin(angle), -np.sin(angle)))
    second = np.where(half[:, None] == half[None, :], block, 0.0)
    return first, turn_cos, turn_sin, second


def packed_tables():
    first, turn_cos, turn_sin, second = y_tables()
    first = np.pad(first, ((0, 0), (0, 96)))
    tables = [*split_table(second), *split_table(second.T), *split_table(first)]
    turns = np.concatenate([turn_cos, turn_sin], 0).astype(np.float32)
    return np.concatenate(tables, 0), turns


X_TABLE = np.concatenate(split_table(x_table()), 0)
Y_TABLE, Y_TURNS = packed_tables()
SCALE = 2.0 / (COLS * 1024.0)


def halves(value):
    high = value.astype(BF16)
    return high, (value - high.astype(F32)).astype(BF16)


def dot(left, right):
    return lax.dot_general(left, right, (((1,), (0,)), ((), ())), preferred_element_type=F32)


def dot_nt(left, right):
    return lax.dot_general(left, right, (((1,), (1,)), ((), ())), preferred_element_type=F32)


def swap(value):
    return pltpu.roll(value, 64, 1)


def lanes(shape):
    return lax.broadcasted_iota(jnp.int32, shape, 1)


def sublanes(shape):
    return lax.broadcasted_iota(jnp.int32, shape, 0)


def x_forward(value, table_ref):
    left, right = value[:, : COLS // 2], value[:, COLS // 2 :]
    group = lanes((128, 128)) // 32
    outs = []
    for parity, folded in enumerate((left + right, left - right)):
        high, low = halves(folded)
        both = jnp.concatenate([high] * 4 + [low] * 4, 0)
        out = None
        for h in range(4):
            start = 256 * h + 128 * parity
            first = dot_nt(table_ref[start : start + 128, :], both)
            piece = first[:, :128] + first[:, 128:]
            piece = piece + dot_nt(table_ref[1024 + start : 1152 + start, :], both[:128])
            out = piece if out is None else jnp.where(group == h, piece, out)
        outs.append(out)
    return jnp.concatenate(outs, 0)


def x_inverse(spectra, table_ref):
    turned = [value.T for value in spectra]
    sums = []
    for parity in range(2):
        cols = slice(128 * parity, 128 * parity + 128)
        rows = [jnp.concatenate([v[32 * h : 32 * h + 32, cols] for h in range(4)], 1) for v in turned]
        left = rows[0] if len(rows) == 1 else jnp.concatenate(rows, 0)
        count = left.shape[0]
        high, low = halves(left)
        both = jnp.concatenate([high, low], 0)
        total = None
        for h in range(4):
            start = 256 * h + 128 * parity
            k = slice(128 * h, 128 * h + 128)
            first = dot(both[:, k], table_ref[start : start + 128, :])
            piece = first[:count] + first[count:] + dot(high[:, k], table_ref[1024 + start : 1152 + start, :])
            total = piece if total is None else total + piece
        sums.append(total)
    return jnp.concatenate([sums[0] + sums[1], sums[0] - sums[1]], 1)


class Lateral:
    def __init__(self, table, turns, is_first):
        self.second = (table[0:128, :], table[128:256, :])
        self.back = (table[256:384, :], table[384:512, :])
        self.first = (table[512:576, 0:32], table[576:640, 0:32])
        self.cos, self.sin = turns[0:32, :], turns[32:64, :]
        self.is_first = is_first
        self.sign = jnp.where(lanes((32, 128)) < 64, 1.0, -1.0)

    def over_s(self, blocks, direction):
        high, low = halves(jnp.concatenate(blocks, 1))
        both = dot(self.first[0], high) + dot(self.first[0], low) + dot(self.first[1], high)
        out = []
        for i in range(len(blocks)):
            cols = slice(128 * i, 128 * i + 128)
            out.append(both[:32, cols] + direction * self.sign * swap(both[32:, cols]))
        return out

    def over_t(self, value, tables):
        high, low = halves(value)
        return dot(high, tables[0]) + dot(low, tables[0]) + dot(high, tables[1])

    def forward(self, ref, offset):
        blocks = [ref[:, offset + i, :] for i in range(8)]
        lane = lanes((32, 128))
        nyquist = (lane >= 64) & (lane < 96)
        blocks.append(jnp.where(lane < 32, swap(blocks[0]), 0.0) * self.is_first)
        blocks[0] = jnp.where(nyquist, blocks[0] * (1.0 - self.is_first), blocks[0])
        blocks = self.over_s(blocks, 1.0)
        blocks = [z * self.cos + swap(z) * self.sin for z in blocks]
        return self.over_t(jnp.concatenate(blocks, 0), self.second)

    def inverse(self, spectrum):
        all_rows = self.over_t(spectrum, self.back)
        blocks = [all_rows[32 * i : 32 * i + 32] for i in range(BLOCKS)]
        blocks = [z * self.cos - swap(z) * self.sin for z in blocks]
        blocks = self.over_s(blocks, -1.0)
        lane = lanes((32, 128))
        nyquist = (lane >= 64) & (lane < 96)
        own = jnp.where(lane // 32 % 2 == 0, SCALE * (1.0 - 0.5 * self.is_first), SCALE)
        blocks[0] = (blocks[0] + jnp.where(nyquist, swap(blocks[8]), 0.0)) * own
        return [blocks[0]] + [z * SCALE for z in blocks[1:8]]

    def weighted_sum(self, value):
        lane, row = lanes(value.shape), sublanes(value.shape)
        weight = jnp.where((row < 32) & (lane // 32 % 2 == 0), 2.0 - self.is_first, 2.0)
        weight = jnp.where(row >= 256, 1.0, weight)
        return jnp.sum(value * weight) * (1.0 / (COLS * 1024.0))


def halo_rows(block):
    lane, row = lanes((32, 128)) % 32, sublanes((32, 128))
    after = jnp.where((lane < 8) & (row < 31), pltpu.roll(block, 31, 0), 0.0)
    before = jnp.where((lane >= 24) & (row > 0), pltpu.roll(block, 1, 0), 0.0)
    return after, before


def product(real, imaginary, value):
    return real * value + imaginary * swap(value)


def spread_kernel(table_ref, measured, point_spread, out_ref):
    for f, ref in enumerate((measured, point_spread)):
        out_ref[:, 8 * f : 8 * f + 8, :] = x_forward(ref[...], table_ref).reshape(32, 8, 128)


def first_filter_kernel(is_first_ref, table, turns, arrived, out_ref, real_ref, imaginary_ref, power_ref, spectrum_ref):
    lateral = Lateral(table, turns, is_first_ref[0])
    transfer = lateral.forward(arrived, 8)
    observed = lateral.forward(arrived, 0)
    turned = swap(transfer)
    left = lanes(transfer.shape) < 64
    real = jnp.where(left, transfer, turned)
    imaginary = jnp.where(left, turned, -transfer)
    power = real * real + imaginary * imaginary
    spectrum = product(real, imaginary, observed)
    right = lateral.inverse(spectrum)
    image = lateral.inverse(spectrum * power)
    for i in range(8):
        out_ref[:, i, :] = right[i]
        out_ref[:, 8 + i, :] = image[i]
        after, before = halo_rows(right[i])
        image_after, image_before = halo_rows(image[i])
        image_after, image_before = pltpu.roll(image_after, 8, 1), pltpu.roll(image_before, 120, 1)
        out_ref[:, 16 + i, :] = after + before + image_after + image_before
    real_ref[...] = real
    imaginary_ref[...] = imaginary
    power_ref[...] = power
    spectrum_ref[...] = spectrum


def second_filter_kernel(is_first_ref, table, turns, arrived, power_ref, spectrum_ref, row_b, row_ab, out_ref, image_ref):
    lateral = Lateral(table, turns, is_first_ref[0])
    power = power_ref[...]
    image = power * spectrum_ref[...] + lateral.forward(arrived, 0)
    filtered = power * image
    blocks = lateral.inverse(filtered)
    for i in range(8):
        out_ref[:, i, :] = blocks[i]
        after, before = halo_rows(blocks[i])
        out_ref[:, 8 + i, :] = after + before
    image_ref[...] = image
    row = row_b[...] + row_ab[...]
    row = row + jnp.where(lanes((1, 128)) == 3, lateral.weighted_sum(image * filtered), 0.0)
    out_ref[:, 8, :] = out_ref[:, 8, :] + pltpu.roll(jnp.broadcast_to(row, (32, 128)), 8, 1)


def last_filter_kernel(
    is_first_ref, factor_ref, table, turns, arrived, real_ref, imaginary_ref, power_ref, spectrum_ref, image_ref, out_ref
):
    lateral = Lateral(table, turns, is_first_ref[0])
    power = power_ref[...]
    image = image_ref[...]
    total = factor_ref[4] * image + factor_ref[5] * (power * image) + lateral.forward(arrived, 8)
    total = power * total + factor_ref[2] * spectrum_ref[...] + factor_ref[3] * image
    total = total + lateral.forward(arrived, 0)
    blocks = lateral.inverse(product(real_ref[...], -imaginary_ref[...], total))
    for i in range(8):
        out_ref[:, i, :] = blocks[i]


def gather_two_kernel(table_ref, arrived, right_ref, image_ref):
    tiles = [arrived[:, 8 * f : 8 * f + 8, :].reshape(256, 128) for f in range(3)]
    value = x_inverse(tiles, table_ref)
    right_ref[0:8, :] = value[88:96]
    right_ref[8:40, :] = value[0:32]
    right_ref[40:48, :] = value[64:72]
    image_ref[0:8, :] = value[80:88]
    image_ref[8:40, :] = value[32:64]
    image_ref[40:48, :] = value[72:80]


def gather_sum_kernel(table_ref, arrived, base, out_ref, row_ref):
    row = pltpu.roll(jnp.broadcast_to(jnp.sum(arrived[:, 8, :], 0, keepdims=True), (8, 128)), 120, 1)
    row_ref[...] = jnp.where(lanes((1, 128)) < 6, row[0:1], 0.0)
    tiles = [arrived[:, 8 * f : 8 * f + 8, :].reshape(256, 128) for f in range(2)]
    value = x_inverse(tiles, table_ref)
    out_ref[0:8, :] = base[0:8, :] + value[56:64]
    out_ref[8:40, :] = base[8:40, :] + value[0:32]
    out_ref[40:48, :] = base[40:48, :] + value[32:40]


def final_kernel(table_ref, arrived, out_ref):
    out_ref[...] = x_inverse([arrived[...].reshape(256, 128)], table_ref)


def shifted_columns(value):
    column = lanes(value.shape)
    left = jnp.where(column >= 1, pltpu.roll(value, 1, 1), 0.0)
    right = jnp.where(column < COLS - 1, pltpu.roll(value, COLS - 1, 1), 0.0)
    return left, right


def stencil_sum(weight, source, start, cols):
    total = None
    for b in range(3):
        part = None
        for a in range(3):
            for c in range(3):
                term = weight(a, b, c) * source[c, start + a, :, cols]
                part = term if part is None else part + term
        if b == 0:
            part = pltpu.roll(part, 1, 0)
        elif b == 2:
            part = pltpu.roll(part, FRAME - 1, 0)
        total = part if total is None else total + part
    return total


def apply_stencils(place_ref, weights_ref, parts, source, middle, back_ref):
    device, plane, planes = place_ref[0], place_ref[1], place_ref[2]
    own, up1, up2, down1, down2 = parts
    for p, ref in enumerate((up2, up1, own, down1, down2)):
        value = ref[...]
        left, right = shifted_columns(value)
        source[0, p], source[1, p], source[2, p] = left, value, right
    row = sublanes((FRAME, 128))
    lowest = jnp.where(device > 0, 0, 8)
    highest = jnp.where(device < 31, FRAME, 40)

    def weight(a, b, c):
        return weights_ref[9 * a + 3 * b + c]

    def flipped(a, b, c):
        return weights_ref[26 - 9 * a - 3 * b - c]

    for p in range(3):
        here = plane + (p - 1)
        end = jnp.where((here >= 0) & (here < planes), highest, 0)
        valid = (row >= lowest) & (row < end)
        for k in range(8):
            cols = slice(128 * k, 128 * k + 128)
            value = stencil_sum(weight, source, p, cols)
            middle[1, p, :, cols] = jnp.where(valid, value, 0.0)
    for p in range(3):
        value = middle[1, p]
        left, right = shifted_columns(value)
        middle[0, p], middle[2, p] = left, right
    inside = (row >= lowest) & (row < highest)
    for k in range(8):
        cols = slice(128 * k, 128 * k + 128)
        back_ref[:, cols] = jnp.where(inside, stencil_sum(flipped, middle, 0, cols), 0.0)


def row_of(values):
    lane = lanes((1, 128))
    out = jnp.zeros((1, 128), F32)
    for k, value in values:
        out = jnp.where(lane == k, jnp.sum(value), out)
    return out


def image_kernel(place, weights, table, o, u1, u2, d1, d2, blurred, upstream, image_ref, mapped_ref, out_ref, row_ref, *scratch):
    source, middle, back = scratch
    apply_stencils(place, weights, (o, u1, u2, d1, d2), source, middle, back)
    out_ref[...] = x_forward(back[8:40, :], table).reshape(32, 8, 128)
    mapped_ref[...] = middle[1, 1, 8:40, :]
    image_ref[...] = blurred[...] + back[...]
    b, ab, u = o[8:40, :], image_ref[8:40, :], upstream[...]
    row_ref[...] = row_of(((0, b * b), (1, b * ab), (2, ab * ab), (4, u * b), (5, u * ab)))


def loss_kernel(place, weights, o, u1, u2, d1, d2, back_ref, mapped_ref, source, middle):
    apply_stencils(place, weights, (o, u1, u2, d1, d2), source, middle, back_ref)
    mapped_ref[...] = middle[1, 1, 8:40, :]


def further_kernel(place, weights, o, u1, u2, d1, d2, back_ref, mapped_ref, row_ref, source, middle):
    apply_stencils(place, weights, (o, u1, u2, d1, d2), source, middle, back_ref)
    mapped = middle[1, 1, 8:40, :]
    mapped_ref[...] = mapped
    row_ref[...] = row_of(((3, mapped * mapped),))


def last_kernel(
    place, weights, factor, table, o, u1, u2, d1, d2, image_back, loss_back, upstream, mapped_ref, out_ref, source, middle, back
):
    apply_stencils(place, weights, (o, u1, u2, d1, d2), source, middle, back)
    mapped_ref[...] = middle[1, 1, 8:40, :]
    u, again = upstream[...], image_back[8:40, :]
    first = factor[0] * u + factor[1] * loss_back[8:40, :] + factor[4] * again + factor[5] * back[8:40, :]
    second = factor[1] * u + factor[5] * again
    out_ref[:, 0:8, :] = x_forward(first, table).reshape(32, 8, 128)
    out_ref[:, 8:16, :] = x_forward(second, table).reshape(32, 8, 128)


def correlate_kernel(factor_ref, *refs):
    out_ref, scaled, mapped = refs[-3:]
    right, image, further, upstream = refs[0:3], refs[3:6], refs[6:9], refs[9:12]
    right_map, image_map, further_map, upstream_map = refs[12:16]
    f = [factor_ref[k] for k in range(5)]
    for p in range(3):
        scaled[p] = f[0] * upstream[p][...] + f[1] * right[p][...] + f[2] * image[p][...] + f[3] * further[p][...]
    mapped[0] = (
        f[0] * upstream_map[...] + f[1] * right_map[...] + f[2] * image_map[...] + f[3] * further_map[...]
    )
    mapped[1] = right_map[...]
    mapped[2] = f[4] * image_map[...]
    lane = lanes((1, 128))
    out = jnp.zeros((1, 128), F32)
    column = lanes((ROWS, COLS))
    left_edge, right_edge = column < COLS - 1, column >= 1
    for c in range(3):
        parts = []
        for k in range(3):
            value = mapped[k]
            if c == 0:
                value = jnp.where(left_edge, pltpu.roll(value, COLS - 1, 1), 0.0)
            elif c == 2:
                value = jnp.where(right_edge, pltpu.roll(value, 1, 1), 0.0)
            parts.append(value)
        for a in range(3):
            for b in range(3):
                rows = slice(7 + b, 39 + b)
                total = parts[0] * right[a][rows, :] + parts[1] * scaled[a, rows, :] + parts[2] * image[a][rows, :]
                out = jnp.where(lane == 9 * a + 3 * b + c, jnp.sum(total), out)
    out_ref[...] = out


def shape(*dims):
    return jax.ShapeDtypeStruct(dims, F32)


STENCIL_SCRATCH = (pltpu.VMEM((3, 5, FRAME, COLS), F32), pltpu.VMEM((3, 3, FRAME, COLS), F32))
BACK_SCRATCH = (pltpu.VMEM((FRAME, COLS), F32),)


def call(body, out_shape, scalars, operands, scratch=(), flops=400_000_000):
    smem, vmem = pl.BlockSpec(memory_space=pltpu.SMEM), pl.BlockSpec(memory_space=pltpu.VMEM)
    return pl.pallas_call(
        body,
        out_shape=out_shape,
        in_specs=[smem] * len(scalars) + [vmem] * len(operands),
        out_specs=jax.tree.map(lambda _: vmem, out_shape),
        scratch_shapes=list(scratch),
        compiler_params=pltpu.CompilerParams(vmem_limit_bytes=VMEM),
        cost_estimate=pl.CostEstimate(flops=flops, bytes_accessed=4_000_000, transcendentals=0),
    )(*scalars, *operands)


def exchange(value):
    return lax.all_to_all(value, GY, 0, 0, tiled=True)


def neighbours(value):
    size = lax.axis_size(GZ)

    def moved(by):
        pairs = [(i, i + by) for i in range(size) if 0 <= i + by < size]
        return lax.ppermute(value, GZ, pairs)

    return value, moved(1), moved(2), moved(-1), moved(-2)


def with_rows(value):
    size = lax.axis_size(GY)
    below = lax.ppermute(value[24:32], GY, [(i, i + 1) for i in range(size - 1)])
    above = lax.ppermute(value[0:8], GY, [(i + 1, i) for i in range(size - 1)])
    return jnp.concatenate([below, value, above], 0)


def from_all(row, axis):
    size = lax.axis_size(axis)
    return lax.all_to_all(jnp.broadcast_to(row[None], (size, 1, 128)), axis, 0, 0, tiled=True)


def over_ring(row, axis):
    for bit in (1, 2, 4, 8):
        row = row + lax.ppermute(row, axis, [(i, i ^ bit) for i in range(16)])
    return row


def factors(m0, m1, m2, m3, u0, u1):
    def pair(m0, m1, m2, m3):
        step0 = m0 / m1
        norm1 = m0 - 2.0 * step0 * m1 + step0 * step0 * m2
        ratio = norm1 / m0
        keep = 1.0 + ratio
        curvature = keep * keep * m1 - 2.0 * keep * step0 * m2 + step0 * step0 * m3
        step1 = norm1 / curvature
        return step0 + step1 * keep, -step1 * step0

    (alpha, gamma), back = jax.vjp(pair, m0, m1, m2, m3)
    return (alpha, gamma, *back((u0, u1)))


def factors_kernel(rows, filter_ref, stencil_ref):
    total = jnp.sum(rows[...], 0)
    lane = lanes((1, 128))
    moments = [jnp.sum(jnp.where(lane == k, total, 0.0), axis=1, keepdims=True) for k in range(6)]
    alpha, gamma, g0, g1, g2, g3 = factors(*moments)
    for k, value in enumerate((alpha, gamma, 2.0 * g0, 2.0 * g1, 2.0 * g2, 2.0 * g3)):
        filter_ref[k] = value[0, 0]
    for k, value in enumerate((gamma, g1, 2.0 * g2, 2.0 * g3, 2.0 * g3)):
        stencil_ref[k] = value[0, 0]


def local(measured, point_spread, stencil_weights, upstream):
    cells = measured.size * lax.axis_size(GY) * lax.axis_size(GZ)
    device, plane = lax.axis_index(GY), lax.axis_index(GZ)
    is_first = jnp.where(device == 0, 1.0, 0.0).astype(F32).reshape(1)
    place = jnp.stack([device, plane, jnp.int32(lax.axis_size(GZ))]).astype(jnp.int32)
    weights = stencil_weights.reshape(27)
    table, along_y, turns = jnp.asarray(X_TABLE), jnp.asarray(Y_TABLE), jnp.asarray(Y_TURNS)
    measured, upstream = measured[0], upstream[0]
    tile, tiles, three = shape(32, 8, 128), shape(32, 16, 128), shape(32, 24, 128)
    spectral, frame, rows, row = shape(32 * BLOCKS, 128), shape(FRAME, COLS), shape(ROWS, COLS), shape(1, 128)

    first = exchange(call(spread_kernel, tiles, [], [table, measured, point_spread]))
    first, grown = lax.optimization_barrier((first, with_rows(upstream)))

    right_out, real, imaginary, power, spectrum = call(
        first_filter_kernel, (three,) + (spectral,) * 4, [is_first], [along_y, turns, first]
    )
    right_arrived = exchange(right_out)
    loss_parts = neighbours(grown)
    loss_back, loss_map = call(loss_kernel, (frame, rows), [place, weights], [*loss_parts], STENCIL_SCRATCH)
    right_arrived, loss_back = lax.optimization_barrier((right_arrived, loss_back))
    right, blurred = call(gather_two_kernel, (frame, frame), [], [table, right_arrived])

    right_parts = neighbours(right)
    image, right_map, image_send, row_b = call(
        image_kernel,
        (frame, rows, tile, row),
        [place, weights],
        [table, *right_parts, blurred, upstream],
        STENCIL_SCRATCH + BACK_SCRATCH,
    )
    image_arrived = exchange(image_send)
    image_parts = neighbours(image)
    image_back, image_map, row_ab = call(
        further_kernel, (frame, rows, row), [place, weights], [*image_parts], STENCIL_SCRATCH
    )
    image_arrived, image_back = lax.optimization_barrier((image_arrived, image_back))
    further_out, image_spectrum = call(
        second_filter_kernel,
        (tiles, spectral),
        [is_first],
        [along_y, turns, image_arrived, power, spectrum, row_b, row_ab],
    )
    further, row_sum = call(gather_sum_kernel, (frame, row), [], [table, exchange(further_out), image_back])
    smem = pl.BlockSpec(memory_space=pltpu.SMEM)
    filter_factors, stencil_factors = pl.pallas_call(
        factors_kernel,
        out_shape=(shape(6), shape(5)),
        in_specs=[pl.BlockSpec(memory_space=pltpu.VMEM)],
        out_specs=(smem, smem),
    )(from_all(row_sum, GZ))

    further_parts = neighbours(further)
    further_map, last_send = call(
        last_kernel,
        (rows, tiles),
        [place, weights, filter_factors],
        [table, *further_parts, image_back, loss_back, upstream],
        STENCIL_SCRATCH + BACK_SCRATCH,
    )
    last_arrived = exchange(last_send)

    operands = []
    for parts in (right_parts, image_parts, further_parts, loss_parts):
        operands += [parts[1], parts[0], parts[3]]
    operands += [right_map, image_map, further_map, loss_map]
    scratch = (pltpu.VMEM((3, FRAME, COLS), F32), pltpu.VMEM((3, ROWS, COLS), F32))
    terms = call(correlate_kernel, row, [stencil_factors], operands, scratch)
    terms = lax.psum(lax.psum(lax.psum(terms, "gz_1"), "gz_0"), "gy_1")
    last_arrived, terms = lax.optimization_barrier((last_arrived, terms))
    result_out = call(
        last_filter_kernel,
        tile,
        [is_first, filter_factors],
        [along_y, turns, last_arrived, real, imaginary, power, spectrum, image_spectrum],
    )
    result_out, terms = lax.optimization_barrier((result_out, terms))
    grad_measured = call(final_kernel, rows, [], [table, exchange(result_out)])
    terms = over_ring(terms, "gy_0")
    grad_stencil = terms[0, :27].reshape(3, 3, 3) / math.sqrt(cells)
    return grad_measured[None], grad_stencil


def solution(mesh):
    groups, planes = mesh.devices.shape
    finer = Mesh(mesh.devices.reshape(groups // 2, 2, 4, planes // 4), GY + GZ)
    return jax.shard_map(
        local,
        mesh=finer,
        in_specs=(P(GZ, GY, None), P(GY, None), P(), P(GZ, GY, None)),
        out_specs=(P(GZ, GY, None), P()),
        check_vma=False,
    )
```

time: 407 us -> 317 us (0.78)
  waiting for transfers between devices: 83.1 us -> 42 us
  between operations: 18.4 us -> 1.18 us
  local copies, waits for them, and re-layouts: 47.5 us -> 30.4 us
  blocking collectives: 88.7 us -> 72.5 us
  starting transfers between devices: 126 us -> 136 us
  Pallas kernels: 35.8 us -> 30.6 us
    all_to_all x9 -> x5, waiting for transfers between devices: 83.1 us -> 16.5 us  [exchange(): return lax.all_to_all(value, GY, 0, 0, tiled=True)]
    all_to_all x4 -> x2, blocking collectives: 88.7 us -> 52.2 us  [the longest x1 34.7 us: exchange(): return lax.all_to_all(value, GY, 0, 0, tiled=True)]
    ppermute x18 -> x22, starting transfers between devices: 52.9 us -> 87.5 us  [the longest x16 54.1 us: moved(): return lax.ppermute(value, GZ, pairs)]
    ppermute x18 -> x22, waiting for transfers between devices: 0.05 us -> 25.5 us  [the longest x16 13.4 us: moved(): return lax.ppermute(value, GZ, pairs)]
    all_to_all x9 -> x5, starting transfers between devices: 73 us -> 48.1 us  [exchange(): return lax.all_to_all(value, GY, 0, 0, tiled=True)]
    psum x0 -> x3, blocking collectives: none -> 20.2 us  [local(): terms = lax.psum(lax.psum(lax.psum(terms, 'gz_1'), 'gz_0'), 'gy_1')]
    unnamed x154 -> x96, local copies, waits for them, and re-layouts: 40.7 us -> 29.6 us
    pallas_call x14 -> x13, Pallas kernels: 35.8 us -> 30.6 us  [the longest x12 29.2 us: call(): pl.pallas_call(body, out_shape=out_shape, in_specs=[smem] * len(scalars)...]
  transfers between devices with their start and end apart: 27 -> 27, of which waited for: 6 -> 13; matrix products, arithmetic and copies ran while one was open for 2% -> 0% of each run, Pallas kernels for 6% -> 3%
where the time goes in v2:
time: 317 us; the launch traced here: 312 us
  starting transfers between devices  136 us (43%)
  blocking collectives  72.5 us (23%)
  waiting for transfers between devices  42 us (13%)
  Pallas kernels  30.6 us (10%)
  local copies, waits for them, and re-layouts  30.4 us (10%)
    ppermute x16, starting transfers between devices, moved(): return lax.ppermute(value, GZ, pairs)  54.1 us
    all_to_all x5, starting transfers between devices, exchange(): return lax.all_to_all(value, GY, 0, 0, tiled=True)  48.1 us
    all_to_all x1, blocking collectives, exchange(): return lax.all_to_all(value, GY, 0, 0, tiled=True)  34.7 us
    unnamed x96, local copies, waits for them, and re-layouts  29.6 us
    pallas_call x12, Pallas kernels, call(): pl.pallas_call(body, out_shape=out_shape, in_specs=[smem] * len(scalars)...  29.2 us
    ppermute x4, starting transfers between devices, over_ring(): row = row + lax.ppermute(row, axis, [(i, i ^ bit) for i in range(16)])  27.9 us
    psum x3, blocking collectives, local(): terms = lax.psum(lax.psum(lax.psum(terms, 'gz_1'), 'gz_0'), 'gy_1')  20.2 us
    all_to_all x1, blocking collectives, from_all(): lax.all_to_all(jnp.broadcast_to(row[None], (size, 1, 128)), axis, 0, 0, t...  17.6 us
  transfers between devices with their start and end apart: 27, of which 13 were waited for; matrix products, arithmetic and copies ran while one was open for 0% of the time, Pallas kernels for 3%

profile of v2, /device:TPU:1, one launch (start us, length us, event | category | flops | bytes accessed | tf_op | source)
XLA Modules:
  0.0 312.4 jit_solution(7940018511399834318)
XLA Ops:
  0.6 1.6 copy-done
  4.0 2.7 shard_map.86
  6.7 16.9 %all-to-all-start = ((f32[32,16,128]{2,1,0:T(8,128)}), f32[32,16,128]{2,1,0:T(8,128)S(1)}, u32[]{:S(2)}, u32[]{:S(2)}) async-start(f32[32,16,128]{2,1,0:T(8,128)} %shard_map.86), calls=%async_computation | async-start | bytes 524288 | tf_op jit(solution)/shard_map/all_to_all | solution.py:439
  23.7 3.5 %collective-permute-start = (f32[8,1024]{1,0:T(8,128)S(1)}, f32[8,1024]{1,0:T(8,128)S(1)}, u32[]{:S(2)}, u32[]{:S(2)}) collective-permute-start(f32[8,1024]{1,0:T(8,128)S(1)} %get-tuple-element.70), channel_id=1, source_target_pairs={{0,16},{16,32},{32,48},{48,64},{64,80},{80,96},{96,112},{112,128},... | collective-permute-start | bytes 98312 | tf_op jit(solution)/shard_map/ppermute | solution.py:454
  27.2 1.9 collective-permute-start.1
  29.2 1.5 collective-permute-done
  30.6 6.2 %collective-permute-done.1 = f32[8,1024]{1,0:T(8,128)S(1)} collective-permute-done((f32[8,1024]{1,0:T(8,128)S(1)}, f32[8,1024]{1,0:T(8,128)S(1)}, u32[]{:S(2)}, u32[]{:S(2)}) %collective-permute-start.1) | collective-permute-done | bytes 32800 | tf_op jit(solution)/shard_map/ppermute | solution.py:455
  36.8 8.6 %all-to-all-done.arrived = f32[32,16,128]{2,1,0:T(8,128)S(1)} async-done(((f32[32,16,128]{2,1,0:T(8,128)}), f32[32,16,128]{2,1,0:T(8,128)S(1)}, u32[]{:S(2)}, u32[]{:S(2)}) %all-to-all-start) | async-done | bytes 262176 | tf_op jit(solution)/shard_map/all_to_all | solution.py:439
  45.5 2.9 shard_map.87
  51.0 4.9 %all-to-all-start.1 = ((f32[32,24,128]{2,1,0:T(8,128)}), f32[32,24,128]{2,1,0:T(8,128)S(1)}, u32[]{:S(2)}, u32[]{:S(2)}) async-start(f32[32,24,128]{2,1,0:T(8,128)} %get-tuple-element.37), calls=%async_computation.1 | async-start | bytes 786432 | tf_op jit(solution)/shard_map/all_to_all | solution.py:439
  55.9 1.3 collective-permute-start.5
  57.2 1.3 collective-permute-start.4
  58.5 6.8 %collective-permute-start.3 = (f32[48,1024]{1,0:T(8,128)S(1)}, f32[48,1024]{1,0:T(8,128)}, u32[]{:S(2)}, u32[]{:S(2)}) collective-permute-start(f32[48,1024]{1,0:T(8,128)S(1)} %pad_maximum_fusion.o.refs_10_), channel_id=1, source_target_pairs={{0,2},{1,3},{2,4},{3,5},{4,6},{5,7},{6,8},{7,9},{8,10},{9,11},{10,... | collective-permute-start | bytes 589832 | tf_op jit(solution)/shard_map/ppermute | solution.py:447
  65.3 3.1 collective-permute-start.2
  68.7 3.9 %collective-permute-done.2.u1.refs_9_ = f32[48,1024]{1,0:T(8,128)S(1)} collective-permute-done((f32[48,1024]{1,0:T(8,128)S(1)}, f32[48,1024]{1,0:T(8,128)S(1)}, u32[]{:S(2)}, u32[]{:S(2)}) %collective-permute-start.2) | collective-permute-done | bytes 196640 | tf_op jit(solution)/shard_map/ppermute | solution.py:447
  72.6 2.8 shard_map.88
  76.1 7.8 %all-to-all-done.1.arrived = f32[32,24,128]{2,1,0:T(8,128)S(1)} async-done(((f32[32,24,128]{2,1,0:T(8,128)}), f32[32,24,128]{2,1,0:T(8,128)S(1)}, u32[]{:S(2)}, u32[]{:S(2)}) %all-to-all-start.1) | async-done | bytes 393248 | tf_op jit(solution)/shard_map/all_to_all | solution.py:439
  84.8 1.3 collective-permute-start.9
  86.1 1.3 collective-permute-start.8
  87.4 6.1 %collective-permute-start.7 = (f32[48,1024]{1,0:T(8,128)S(1)}, f32[48,1024]{1,0:T(8,128)S(1)}, u32[]{:S(2)}, u32[]{:S(2)}) collective-permute-start(f32[48,1024]{1,0:T(8,128)S(1)} %get-tuple-element.41.o.refs_1_), channel_id=1, source_target_pairs={{0,2},{1,3},{2,4},{3,5},{4,6},{5,7},{6,8},{7,9},{8,10},{9,11},{10,... | collective-permute-start | bytes 589832 | tf_op jit(solution)/shard_map/ppermute | solution.py:447
  93.6 3.1 %collective-permute-start.6 = (f32[48,1024]{1,0:T(8,128)S(1)}, f32[48,1024]{1,0:T(8,128)S(1)}, u32[]{:S(2)}, u32[]{:S(2)}) collective-permute-start(f32[48,1024]{1,0:T(8,128)S(1)} %get-tuple-element.41.o.refs_1_), channel_id=1, source_target_pairs={{0,1},{1,2},{2,3},{3,4},{4,5},{5,6},{6,7},{7,8},{8,9},{9,10},{10,1... | collective-permute-start | bytes 589832 | tf_op jit(solution)/shard_map/ppermute | solution.py:447
  96.9 4.6 %collective-permute-done.6.u1.refs_0_ = f32[48,1024]{1,0:T(8,128)S(1)} collective-permute-done((f32[48,1024]{1,0:T(8,128)S(1)}, f32[48,1024]{1,0:T(8,128)S(1)}, u32[]{:S(2)}, u32[]{:S(2)}) %collective-permute-start.6) | collective-permute-done | bytes 196640 | tf_op jit(solution)/shard_map/ppermute | solution.py:447
  101.5 4.1 %shard_map.90 = (f32[48,1024]{1,0:T(8,128)S(1)}, f32[32,1024]{1,0:T(8,128)S(1)}, f32[32,8,128]{2,1,0:T(8,128)}, f32[1,128]{1,0:T(1,128)S(1)}) custom-call(s32[3]{0:T(128)S(1)} %pad_add_fusion.place, f32[27]{0:T(128)S(1)} %reshape.18.weights, bf16[2048,512]{1,0:T(8,128)(2,1)S(1)} %copy-done.1, f32[48,1024]{1,0:T(8,128)S(1)} %get-tuple-element.41.o.refs_1_, ...), custom_call_target="tpu_custom_call" | custom-call | flops 400000000 | bytes 4000000 | tf_op jit(solution)/shard_map/pallas_call | solution.py:427
  106.2 7.0 %all-to-all-start.2 = ((f32[32,8,128]{2,1,0:T(8,128)}), f32[32,8,128]{2,1,0:T(8,128)S(1)}, u32[]{:S(2)}, u32[]{:S(2)}) async-start(f32[32,8,128]{2,1,0:T(8,128)} %get-tuple-element.43), calls=%async_computation.2 | async-start | bytes 262144 | tf_op jit(solution)/shard_map/all_to_all | solution.py:439
  113.2 1.3 collective-permute-start.13
  115.8 8.3 %collective-permute-start.11 = (f32[48,1024]{1,0:T(8,128)S(1)}, f32[48,1024]{1,0:T(8,128)S(1)}, u32[]{:S(2)}, u32[]{:S(2)}) collective-permute-start(f32[48,1024]{1,0:T(8,128)S(1)} %get-tuple-element.44.o.refs_4_), channel_id=1, source_target_pairs={{0,2},{1,3},{2,4},{3,5},{4,6},{5,7},{6,8},{7,9},{8,10},{9,11},{10,... | collective-permute-start | bytes 589832 | tf_op jit(solution)/shard_map/ppermute | solution.py:447
  124.1 3.5 %collective-permute-start.10 = (f32[48,1024]{1,0:T(8,128)S(1)}, f32[48,1024]{1,0:T(8,128)S(1)}, u32[]{:S(2)}, u32[]{:S(2)}) collective-permute-start(f32[48,1024]{1,0:T(8,128)S(1)} %get-tuple-element.44.o.refs_4_), channel_id=1, source_target_pairs={{0,1},{1,2},{2,3},{3,4},{4,5},{5,6},{6,7},{7,8},{8,9},{9,10},{10,1... | collective-permute-start | bytes 589832 | tf_op jit(solution)/shard_map/ppermute | solution.py:447
  128.1 4.2 %collective-permute-done.10.u1.refs_3_ = f32[48,1024]{1,0:T(8,128)S(1)} collective-permute-done((f32[48,1024]{1,0:T(8,128)S(1)}, f32[48,1024]{1,0:T(8,128)S(1)}, u32[]{:S(2)}, u32[]{:S(2)}) %collective-permute-start.10) | collective-permute-done | bytes 196640 | tf_op jit(solution)/shard_map/ppermute | solution.py:447
  132.3 2.5 shard_map.91
  140.3 1.4 shard_map.92
  141.8 34.7 %all_to_all.35.arrived = f32[32,16,128]{2,1,0:T(8,128)S(1)} all-to-all(f32[32,16,128]{2,1,0:T(8,128)S(1)} %get-tuple-element.51), channel_id=1, replica_groups=mesh['gy_0'=16,'gy_1'=2,'gz_0'=4,'gz_1'=4] {'gy_0','gy_1'}, dimensions={0} | all-to-all | bytes 524288 | tf_op jit(solution)/shard_map/all_to_all | solution.py:439
  179.7 8.7 %collective-permute-start.15 = (f32[48,1024]{1,0:T(8,128)S(1)}, f32[48,1024]{1,0:T(8,128)}, u32[]{:S(2)}, u32[]{:S(2)}) collective-permute-start(f32[48,1024]{1,0:T(8,128)S(1)} %get-tuple-element.55.o.refs_7_), channel_id=1, source_target_pairs={{0,2},{1,3},{2,4},{3,5},{4,6},{5,7},{6,8},{7,9},{8,10},{9,11},{10,... | collective-permute-start | bytes 589832 | tf_op jit(solution)/shard_map/ppermute | solution.py:447
  188.3 4.2 %collective-permute-start.14 = (f32[48,1024]{1,0:T(8,128)S(1)}, f32[48,1024]{1,0:T(8,128)}, u32[]{:S(2)}, u32[]{:S(2)}) collective-permute-start(f32[48,1024]{1,0:T(8,128)S(1)} %get-tuple-element.55.o.refs_7_), channel_id=1, source_target_pairs={{0,1},{1,2},{2,3},{3,4},{4,5},{5,6},{6,7},{7,8},{8,9},{9,10},{10,1... | collective-permute-start | bytes 589832 | tf_op jit(solution)/shard_map/ppermute | solution.py:447
  192.5 17.6 %all_to_all.36.rows = f32[16,1,128]{2,1,0:T(1,128)} all-to-all(f32[16,1,128]{2,1,0:T(1,128)S(1)} %broadcast_in_dim.12), channel_id=1, replica_groups=mesh['gy_0'=16,'gy_1'=2,'gz_0'=4,'gz_1'=4] {'gz_0','gz_1'}, dimensions={0} | all-to-all | bytes 16384 | tf_op jit(solution)/shard_map/all_to_all | solution.py:461
  210.1 1.4 shard_map.94
  213.1 4.8 %shard_map.95 = (f32[32,1024]{1,0:T(8,128)S(1)}, f32[32,16,128]{2,1,0:T(8,128)S(1)}) custom-call(s32[3]{0:T(128)S(1)} %pad_add_fusion.place, f32[27]{0:T(128)S(1)} %reshape.18.weights, f32[6]{0:T(128)S(1)} %copy-done.26, bf16[2048,512]{1,0:T(8,128)(2,1)S(1)} %copy-done.1, f32[48,1024]{1,0:T(8,128)S(1)} %get-tuple-element.55.o.refs_7_, ...), custom_call_target="tpu_custom_call" | custom-call | flops 400000000 | bytes 4000000 | tf_op jit(solution)/shard_map/pallas_call | solution.py:427
  219.3 7.1 %all-to-all-start.5 = ((f32[32,16,128]{2,1,0:T(8,128)}), f32[32,16,128]{2,1,0:T(8,128)S(1)}, u32[]{:S(2)}, u32[]{:S(2)}) async-start(f32[32,16,128]{2,1,0:T(8,128)} %copy-done.5), calls=%async_computation.5 | async-start | bytes 524288 | tf_op jit(solution)/shard_map/all_to_all | solution.py:439
  234.7 2.5 shard_map.96
  237.2 7.2 %psum.21 = f32[1,128]{1,0:T(1,128)S(1)} all-reduce(f32[1,128]{1,0:T(1,128)S(1)} %shard_map.96), channel_id=1, replica_groups=mesh['gy_0'=16,'gy_1'=2,'gz_0'=4,'gz_1'=4] {'gz_1'}, use_global_device_ids=true, to_apply=%region_0.1 | all-reduce | flops 128 | bytes 1024 | tf_op jit(solution)/shard_map/psum | solution.py:563
  244.4 6.9 %psum.22 = f32[1,128]{1,0:T(1,128)S(1)} all-reduce(f32[1,128]{1,0:T(1,128)S(1)} %psum.21), channel_id=1, replica_groups=mesh['gy_0'=16,'gy_1'=2,'gz_0'=4,'gz_1'=4] {'gz_0'}, use_global_device_ids=true, to_apply=%region_1.2 | all-reduce | flops 128 | bytes 1024 | tf_op jit(solution)/shard_map/psum | solution.py:563
  251.2 6.2 %psum.23 = f32[1,128]{1,0:T(1,128)S(1)} all-reduce(f32[1,128]{1,0:T(1,128)S(1)} %psum.22), channel_id=1, replica_groups=mesh['gy_0'=16,'gy_1'=2,'gz_0'=4,'gz_1'=4] {'gy_1'}, use_global_device_ids=true, to_apply=%region_2.3 | all-reduce | flops 128 | bytes 1024 | tf_op jit(solution)/shard_map/psum | solution.py:563
  262.9 2.9 shard_map.97
  265.8 12.3 %all-to-all-start.6 = ((f32[32,8,128]{2,1,0:T(8,128)}), f32[32,8,128]{2,1,0:T(8,128)S(1)}, u32[]{:S(2)}, u32[]{:S(2)}) async-start(f32[32,8,128]{2,1,0:T(8,128)} %shard_map.97), calls=%async_computation.6 | async-start | bytes 262144 | tf_op jit(solution)/shard_map/all_to_all | solution.py:439
  278.1 3.3 %collective-permute-start.18 = (f32[1,128]{1,0:T(1,128)S(1)}, f32[1,128]{1,0:T(1,128)S(1)}, u32[]{:S(2)}, u32[]{:S(2)}) collective-permute-start(f32[1,128]{1,0:T(1,128)S(1)} %psum.23), channel_id=1, source_target_pairs={{0,32},{32,0},{64,96},{96,64},{128,160},{160,128},{192,224},{224,1... | collective-permute-start | bytes 1544 | tf_op jit(solution)/shard_map/ppermute | solution.py:466
  281.4 1.5 collective-permute-done.18
  282.8 4.6 %collective-permute-start.19 = (f32[1,128]{1,0:T(1,128)S(1)}, f32[1,128]{1,0:T(1,128)S(1)}, u32[]{:S(2)}, u32[]{:S(2)}) collective-permute-start(f32[1,128]{1,0:T(1,128)S(1)} %add.26), channel_id=1, source_target_pairs={{0,64},{32,96},{64,0},{96,32},{128,192},{160,224},{192,128},{224,1... | collective-permute-start | bytes 1544 | tf_op jit(solution)/shard_map/ppermute | solution.py:466
  288.7 7.9 %collective-permute-start.20 = (f32[1,128]{1,0:T(1,128)S(1)}, f32[1,128]{1,0:T(1,128)S(1)}, u32[]{:S(2)}, u32[]{:S(2)}) collective-permute-start(f32[1,128]{1,0:T(1,128)S(1)} %add.27), channel_id=1, source_target_pairs={{0,128},{32,160},{64,192},{96,224},{128,0},{160,32},{192,64},{224,... | collective-permute-start | bytes 1544 | tf_op jit(solution)/shard_map/ppermute | solution.py:466
  297.5 12.1 %collective-permute-start.21 = (f32[1,128]{1,0:T(1,128)S(1)}, f32[1,128]{1,0:T(1,128)S(1)}, u32[]{:S(2)}, u32[]{:S(2)}) collective-permute-start(f32[1,128]{1,0:T(1,128)S(1)} %add.28), channel_id=1, source_target_pairs={{0,256},{32,288},{64,320},{96,352},{128,384},{160,416},{192,448},{... | collective-permute-start | bytes 1544 | tf_op jit(solution)/shard_map/ppermute | solution.py:466
  (131 shorter events, 39.2 us)
Async XLA Ops:
  0.6 1.6 copy-start
  4.0 19.6 %copy-start.2 = (f32[1,32,1024]{2,1,0:T(8,128)S(1)}, f32[1,32,1024]{2,1,0:T(8,128)}, u32[]{:S(2)}) copy-start(f32[1,32,1024]{2,1,0:T(8,128)} %param.10) | copy-start | bytes 393220
  4.0 41.4 %copy-start.29 = (bf16[640,128]{1,0:T(8,128)(2,1)S(1)}, bf16[640,128]{1,0:T(8,128)(2,1)}, u32[]{:S(2)}) copy-start(bf16[640,128]{1,0:T(8,128)(2,1)} %constant.40.clone.table) | copy-start | bytes 491524
  4.0 41.4 %copy-start.32 = (f32[64,128]{1,0:T(8,128)S(1)}, f32[64,128]{1,0:T(8,128)}, u32[]{:S(2)}) copy-start(f32[64,128]{1,0:T(8,128)} %constant.41.clone.turns) | copy-start | bytes 98308
  6.7 61.7 %copy-start.47 = (f32[3,3,3]{2,1,0:T(4,128)S(1)}, f32[3,3,3]{2,1,0:T(4,128)}, u32[]{:S(2)}) copy-start(f32[3,3,3]{2,1,0:T(4,128)} %param.9) | copy-start | bytes 328
  6.7 38.7 %all-to-all-start = ((f32[32,16,128]{2,1,0:T(8,128)}), f32[32,16,128]{2,1,0:T(8,128)S(1)}, u32[]{:S(2)}, u32[]{:S(2)}) async-start(f32[32,16,128]{2,1,0:T(8,128)} %shard_map.86), calls=%async_computation | async-start | bytes 524288 | tf_op jit(solution)/shard_map/all_to_all | solution.py:439
  23.7 7.0 %collective-permute-start = (f32[8,1024]{1,0:T(8,128)S(1)}, f32[8,1024]{1,0:T(8,128)S(1)}, u32[]{:S(2)}, u32[]{:S(2)}) collective-permute-start(f32[8,1024]{1,0:T(8,128)S(1)} %get-tuple-element.70), channel_id=1, source_target_pairs={{0,16},{16,32},{32,48},{48,64},{64,80},{80,96},{96,112},{112,128},... | collective-permute-start | bytes 98312 | tf_op jit(solution)/shard_map/ppermute | solution.py:454
  27.2 9.6 %collective-permute-start.1 = (f32[8,1024]{1,0:T(8,128)S(1)}, f32[8,1024]{1,0:T(8,128)S(1)}, u32[]{:S(2)}, u32[]{:S(2)}) collective-permute-start(f32[8,1024]{1,0:T(8,128)S(1)} %get-tuple-element.71), channel_id=1, source_target_pairs={{16,0},{32,16},{48,32},{64,48},{80,64},{96,80},{112,96},{128,112},... | collective-permute-start | bytes 98312 | tf_op jit(solution)/shard_map/ppermute | solution.py:455
  29.1 54.8 %copy-start.1 = (bf16[2048,512]{1,0:T(8,128)(2,1)S(1)}, bf16[2048,512]{1,0:T(8,128)(2,1)}, u32[]{:S(2)}) copy-start(bf16[2048,512]{1,0:T(8,128)(2,1)} %constant.39.clone.table_ref.table) | copy-start | bytes 6291460
  36.8 47.2 %copy-start.3 = (f32[48,1024]{1,0:T(8,128)}, f32[48,1024]{1,0:T(8,128)S(1)}, u32[]{:S(2)}) copy-start(f32[48,1024]{1,0:T(8,128)S(1)} %pad_maximum_fusion.o.refs_10_) | copy-start | bytes 589828
  51.0 32.9 %all-to-all-start.1 = ((f32[32,24,128]{2,1,0:T(8,128)}), f32[32,24,128]{2,1,0:T(8,128)S(1)}, u32[]{:S(2)}, u32[]{:S(2)}) async-start(f32[32,24,128]{2,1,0:T(8,128)} %get-tuple-element.37), calls=%async_computation.1 | async-start | bytes 786432 | tf_op jit(solution)/shard_map/all_to_all | solution.py:439
  55.9 12.7 %collective-permute-start.5 = (f32[48,1024]{1,0:T(8,128)S(1)}, f32[48,1024]{1,0:T(8,128)S(1)}, u32[]{:S(2)}, u32[]{:S(2)}) collective-permute-start(f32[48,1024]{1,0:T(8,128)S(1)} %pad_maximum_fusion.o.refs_10_), channel_id=1, source_target_pairs={{2,0},{3,1},{4,2},{5,3},{6,4},{7,5},{8,6},{9,7},{10,8},{11,9},{12,... | collective-permute-start | bytes 589832 | tf_op jit(solution)/shard_map/ppermute | solution.py:447
  57.2 11.4 %collective-permute-start.4 = (f32[48,1024]{1,0:T(8,128)S(1)}, f32[48,1024]{1,0:T(8,128)S(1)}, u32[]{:S(2)}, u32[]{:S(2)}) collective-permute-start(f32[48,1024]{1,0:T(8,128)S(1)} %pad_maximum_fusion.o.refs_10_), channel_id=1, source_target_pairs={{1,0},{2,1},{3,2},{4,3},{5,4},{6,5},{7,6},{8,7},{9,8},{10,9},{11,1... | collective-permute-start | bytes 589832 | tf_op jit(solution)/shard_map/ppermute | solution.py:447
  58.5 10.1 %collective-permute-start.3 = (f32[48,1024]{1,0:T(8,128)S(1)}, f32[48,1024]{1,0:T(8,128)}, u32[]{:S(2)}, u32[]{:S(2)}) collective-permute-start(f32[48,1024]{1,0:T(8,128)S(1)} %pad_maximum_fusion.o.refs_10_), channel_id=1, source_target_pairs={{0,2},{1,3},{2,4},{3,5},{4,6},{5,7},{6,8},{7,9},{8,10},{9,11},{10,... | collective-permute-start | bytes 589832 | tf_op jit(solution)/shard_map/ppermute | solution.py:447
  65.3 7.2 %collective-permute-start.2 = (f32[48,1024]{1,0:T(8,128)S(1)}, f32[48,1024]{1,0:T(8,128)S(1)}, u32[]{:S(2)}, u32[]{:S(2)}) collective-permute-start(f32[48,1024]{1,0:T(8,128)S(1)} %pad_maximum_fusion.o.refs_10_), channel_id=1, source_target_pairs={{0,1},{1,2},{2,3},{3,4},{4,5},{5,6},{6,7},{7,8},{8,9},{9,10},{10,1... | collective-permute-start | bytes 589832 | tf_op jit(solution)/shard_map/ppermute | solution.py:447
  68.6 18.8 %copy-start.8 = (f32[48,1024]{1,0:T(8,128)}, f32[48,1024]{1,0:T(8,128)S(1)}, u32[]{:S(2)}) copy-start(f32[48,1024]{1,0:T(8,128)S(1)} %collective-permute-done.4.d1.refs_11_) | copy-start | bytes 589828
  72.6 33.0 %copy-start.10 = (f32[48,1024]{1,0:T(8,128)}, f32[48,1024]{1,0:T(8,128)S(1)}, u32[]{:S(2)}) copy-start(f32[48,1024]{1,0:T(8,128)S(1)} %collective-permute-done.2.u1.refs_9_) | copy-start | bytes 589828
  84.8 11.9 %collective-permute-start.9 = (f32[48,1024]{1,0:T(8,128)S(1)}, f32[48,1024]{1,0:T(8,128)S(1)}, u32[]{:S(2)}, u32[]{:S(2)}) collective-permute-start(f32[48,1024]{1,0:T(8,128)S(1)} %get-tuple-element.41.o.refs_1_), channel_id=1, source_target_pairs={{2,0},{3,1},{4,2},{5,3},{6,4},{7,5},{8,6},{9,7},{10,8},{11,9},{12,... | collective-permute-start | bytes 589832 | tf_op jit(solution)/shard_map/ppermute | solution.py:447
  86.1 10.6 %collective-permute-start.8 = (f32[48,1024]{1,0:T(8,128)S(1)}, f32[48,1024]{1,0:T(8,128)S(1)}, u32[]{:S(2)}, u32[]{:S(2)}) collective-permute-start(f32[48,1024]{1,0:T(8,128)S(1)} %get-tuple-element.41.o.refs_1_), channel_id=1, source_target_pairs={{1,0},{2,1},{3,2},{4,3},{5,4},{6,5},{7,6},{8,7},{9,8},{10,9},{11,1... | collective-permute-start | bytes 589832 | tf_op jit(solution)/shard_map/ppermute | solution.py:447
  87.4 9.5 %collective-permute-start.7 = (f32[48,1024]{1,0:T(8,128)S(1)}, f32[48,1024]{1,0:T(8,128)S(1)}, u32[]{:S(2)}, u32[]{:S(2)}) collective-permute-start(f32[48,1024]{1,0:T(8,128)S(1)} %get-tuple-element.41.o.refs_1_), channel_id=1, source_target_pairs={{0,2},{1,3},{2,4},{3,5},{4,6},{5,7},{6,8},{7,9},{8,10},{9,11},{10,... | collective-permute-start | bytes 589832 | tf_op jit(solution)/shard_map/ppermute | solution.py:447
  93.6 7.9 %collective-permute-start.6 = (f32[48,1024]{1,0:T(8,128)S(1)}, f32[48,1024]{1,0:T(8,128)S(1)}, u32[]{:S(2)}, u32[]{:S(2)}) collective-permute-start(f32[48,1024]{1,0:T(8,128)S(1)} %get-tuple-element.41.o.refs_1_), channel_id=1, source_target_pairs={{0,1},{1,2},{2,3},{3,4},{4,5},{5,6},{6,7},{7,8},{8,9},{9,10},{10,1... | collective-permute-start | bytes 589832 | tf_op jit(solution)/shard_map/ppermute | solution.py:447
  106.2 70.9 %copy-start.12 = (f32[48,1024]{1,0:T(8,128)}, f32[48,1024]{1,0:T(8,128)S(1)}, u32[]{:S(2)}) copy-start(f32[48,1024]{1,0:T(8,128)S(1)} %get-tuple-element.44.o.refs_4_) | copy-start | bytes 589828
  106.2 30.6 %all-to-all-start.2 = ((f32[32,8,128]{2,1,0:T(8,128)}), f32[32,8,128]{2,1,0:T(8,128)S(1)}, u32[]{:S(2)}, u32[]{:S(2)}) async-start(f32[32,8,128]{2,1,0:T(8,128)} %get-tuple-element.43), calls=%async_computation.2 | async-start | bytes 262144 | tf_op jit(solution)/shard_map/all_to_all | solution.py:439
  113.2 14.4 %collective-permute-start.13 = (f32[48,1024]{1,0:T(8,128)S(1)}, f32[48,1024]{1,0:T(8,128)S(1)}, u32[]{:S(2)}, u32[]{:S(2)}) collective-permute-start(f32[48,1024]{1,0:T(8,128)S(1)} %get-tuple-element.44.o.refs_4_), channel_id=1, source_target_pairs={{2,0},{3,1},{4,2},{5,3},{6,4},{7,5},{8,6},{9,7},{10,8},{11,9},{12,... | collective-permute-start | bytes 589832 | tf_op jit(solution)/shard_map/ppermute | solution.py:447
  114.5 13.1 %collective-permute-start.12 = (f32[48,1024]{1,0:T(8,128)S(1)}, f32[48,1024]{1,0:T(8,128)S(1)}, u32[]{:S(2)}, u32[]{:S(2)}) collective-permute-start(f32[48,1024]{1,0:T(8,128)S(1)} %get-tuple-element.44.o.refs_4_), channel_id=1, source_target_pairs={{1,0},{2,1},{3,2},{4,3},{5,4},{6,5},{7,6},{8,7},{9,8},{10,9},{11,1... | collective-permute-start | bytes 589832 | tf_op jit(solution)/shard_map/ppermute | solution.py:447
  115.8 12.3 %collective-permute-start.11 = (f32[48,1024]{1,0:T(8,128)S(1)}, f32[48,1024]{1,0:T(8,128)S(1)}, u32[]{:S(2)}, u32[]{:S(2)}) collective-permute-start(f32[48,1024]{1,0:T(8,128)S(1)} %get-tuple-element.44.o.refs_4_), channel_id=1, source_target_pairs={{0,2},{1,3},{2,4},{3,5},{4,6},{5,7},{6,8},{7,9},{8,10},{9,11},{10,... | collective-permute-start | bytes 589832 | tf_op jit(solution)/shard_map/ppermute | solution.py:447
  124.1 8.3 %collective-permute-start.10 = (f32[48,1024]{1,0:T(8,128)S(1)}, f32[48,1024]{1,0:T(8,128)S(1)}, u32[]{:S(2)}, u32[]{:S(2)}) collective-permute-start(f32[48,1024]{1,0:T(8,128)S(1)} %get-tuple-element.44.o.refs_4_), channel_id=1, source_target_pairs={{0,1},{1,2},{2,3},{3,4},{4,5},{5,6},{6,7},{7,8},{8,9},{9,10},{10,1... | collective-permute-start | bytes 589832 | tf_op jit(solution)/shard_map/ppermute | solution.py:447
  141.8 50.7 %copy-start.45 = (f32[288,128]{1,0:T(8,128)}, f32[288,128]{1,0:T(8,128)S(1)}, u32[]{:S(2)}) copy-start(f32[288,128]{1,0:T(8,128)S(1)} %get-tuple-element.66.image_ref) | copy-start | bytes 442372
  177.1 34.4 %collective-permute-start.17 = (f32[48,1024]{1,0:T(8,128)S(1)}, f32[48,1024]{1,0:T(8,128)}, u32[]{:S(2)}, u32[]{:S(2)}) collective-permute-start(f32[48,1024]{1,0:T(8,128)S(1)} %get-tuple-element.55.o.refs_7_), channel_id=1, source_target_pairs={{2,0},{3,1},{4,2},{5,3},{6,4},{7,5},{8,6},{9,7},{10,8},{11,9},{12,... | collective-permute-start | bytes 589832 | tf_op jit(solution)/shard_map/ppermute | solution.py:447
  178.4 33.1 %collective-permute-start.16 = (f32[48,1024]{1,0:T(8,128)S(1)}, f32[48,1024]{1,0:T(8,128)S(1)}, u32[]{:S(2)}, u32[]{:S(2)}) collective-permute-start(f32[48,1024]{1,0:T(8,128)S(1)} %get-tuple-element.55.o.refs_7_), channel_id=1, source_target_pairs={{1,0},{2,1},{3,2},{4,3},{5,4},{6,5},{7,6},{8,7},{9,8},{10,9},{11,1... | collective-permute-start | bytes 589832 | tf_op jit(solution)/shard_map/ppermute | solution.py:447
  179.7 31.9 %collective-permute-start.15 = (f32[48,1024]{1,0:T(8,128)S(1)}, f32[48,1024]{1,0:T(8,128)}, u32[]{:S(2)}, u32[]{:S(2)}) collective-permute-start(f32[48,1024]{1,0:T(8,128)S(1)} %get-tuple-element.55.o.refs_7_), channel_id=1, source_target_pairs={{0,2},{1,3},{2,4},{3,5},{4,6},{5,7},{6,8},{7,9},{8,10},{9,11},{10,... | collective-permute-start | bytes 589832 | tf_op jit(solution)/shard_map/ppermute | solution.py:447
  188.3 23.2 %collective-permute-start.14 = (f32[48,1024]{1,0:T(8,128)S(1)}, f32[48,1024]{1,0:T(8,128)}, u32[]{:S(2)}, u32[]{:S(2)}) collective-permute-start(f32[48,1024]{1,0:T(8,128)S(1)} %get-tuple-element.55.o.refs_7_), channel_id=1, source_target_pairs={{0,1},{1,2},{2,3},{3,4},{4,5},{5,6},{6,7},{7,8},{8,9},{9,10},{10,1... | collective-permute-start | bytes 589832 | tf_op jit(solution)/shard_map/ppermute | solution.py:447
  211.5 14.9 %copy-start.28 = (f32[5]{0:T(128)S(1)}, f32[5]{0:T(128)}, u32[]{:S(2)}) copy-start(f32[5]{0:T(128)} %get-tuple-element.58.factor_ref) | copy-start | bytes 64
  211.6 0.9 copy-start.7
  219.3 38.1 %copy-start.27 = (f32[6]{0:T(128)S(1)}, f32[6]{0:T(128)}, u32[]{:S(2)}) copy-start(f32[6]{0:T(128)} %get-tuple-element.54.factor.factor_ref) | copy-start | bytes 76
  219.3 38.1 %copy-start.34 = (f32[64,128]{1,0:T(8,128)S(1)}, f32[64,128]{1,0:T(8,128)}, u32[]{:S(2)}) copy-start(f32[64,128]{1,0:T(8,128)} %constant.41.clone.turns) | copy-start | bytes 98308
  219.3 38.1 %all-to-all-start.5 = ((f32[32,16,128]{2,1,0:T(8,128)}), f32[32,16,128]{2,1,0:T(8,128)S(1)}, u32[]{:S(2)}, u32[]{:S(2)}) async-start(f32[32,16,128]{2,1,0:T(8,128)} %copy-done.5), calls=%async_computation.5 | async-start | bytes 524288 | tf_op jit(solution)/shard_map/all_to_all | solution.py:439
  226.4 0.9 copy-start.4
  227.3 0.9 copy-start.9
  228.2 0.9 copy-start.11
  229.2 0.9 copy-start.13
  230.1 0.9 copy-start.15
  231.0 0.9 copy-start.17
  265.8 45.5 %all-to-all-start.6 = ((f32[32,8,128]{2,1,0:T(8,128)}), f32[32,8,128]{2,1,0:T(8,128)S(1)}, u32[]{:S(2)}, u32[]{:S(2)}) async-start(f32[32,8,128]{2,1,0:T(8,128)} %shard_map.97), calls=%async_computation.6 | async-start | bytes 262144 | tf_op jit(solution)/shard_map/all_to_all | solution.py:439
  278.1 4.8 %collective-permute-start.18 = (f32[1,128]{1,0:T(1,128)S(1)}, f32[1,128]{1,0:T(1,128)S(1)}, u32[]{:S(2)}, u32[]{:S(2)}) collective-permute-start(f32[1,128]{1,0:T(1,128)S(1)} %psum.23), channel_id=1, source_target_pairs={{0,32},{32,0},{64,96},{96,64},{128,160},{160,128},{192,224},{224,1... | collective-permute-start | bytes 1544 | tf_op jit(solution)/shard_map/ppermute | solution.py:466
  282.8 5.9 %collective-permute-start.19 = (f32[1,128]{1,0:T(1,128)S(1)}, f32[1,128]{1,0:T(1,128)S(1)}, u32[]{:S(2)}, u32[]{:S(2)}) collective-permute-start(f32[1,128]{1,0:T(1,128)S(1)} %add.26), channel_id=1, source_target_pairs={{0,64},{32,96},{64,0},{96,32},{128,192},{160,224},{192,128},{224,1... | collective-permute-start | bytes 1544 | tf_op jit(solution)/shard_map/ppermute | solution.py:466
  288.7 8.8 %collective-permute-start.20 = (f32[1,128]{1,0:T(1,128)S(1)}, f32[1,128]{1,0:T(1,128)S(1)}, u32[]{:S(2)}, u32[]{:S(2)}) collective-permute-start(f32[1,128]{1,0:T(1,128)S(1)} %add.27), channel_id=1, source_target_pairs={{0,128},{32,160},{64,192},{96,224},{128,0},{160,32},{192,64},{224,... | collective-permute-start | bytes 1544 | tf_op jit(solution)/shard_map/ppermute | solution.py:466
  297.5 13.0 %collective-permute-start.21 = (f32[1,128]{1,0:T(1,128)S(1)}, f32[1,128]{1,0:T(1,128)S(1)}, u32[]{:S(2)}, u32[]{:S(2)}) collective-permute-start(f32[1,128]{1,0:T(1,128)S(1)} %add.28), channel_id=1, source_target_pairs={{0,256},{32,288},{64,320},{96,352},{128,384},{160,416},{192,448},{... | collective-permute-start | bytes 1544 | tf_op jit(solution)/shard_map/ppermute | solution.py:466
  (27 other events, 21.5 us)

commit v3 on v2

--- a/solution.py
+++ b/solution.py
@@ -62,12 +62,11 @@
     first, turn_cos, turn_sin, second = y_tables()
     first = np.pad(first, ((0, 0), (0, 96)))
     tables = [*split_table(second), *split_table(second.T), *split_table(first)]
-    turns = np.concatenate([turn_cos, turn_sin], 0).astype(np.float32)
-    return np.concatenate(tables, 0), turns
+    return np.concatenate([*tables, turn_cos, turn_sin], 0).astype(np.float32)
 
 
 X_TABLE = np.concatenate(split_table(x_table()), 0)
-Y_TABLE, Y_TURNS = packed_tables()
+Y_TABLE = packed_tables()
 SCALE = 2.0 / (COLS * 1024.0)
 
 
@@ -136,11 +135,14 @@
 
 
 class Lateral:
-    def __init__(self, table, turns, is_first):
-        self.second = (table[0:128, :], table[128:256, :])
-        self.back = (table[256:384, :], table[384:512, :])
-        self.first = (table[512:576, 0:32], table[576:640, 0:32])
-        self.cos, self.sin = turns[0:32, :], turns[32:64, :]
+    def __init__(self, table, is_first):
+        def piece(start, count, width):
+            return table[start : start + count, 0:width].astype(BF16)
+
+        self.second = (piece(0, 128, 128), piece(128, 128, 128))
+        self.back = (piece(256, 128, 128), piece(384, 128, 128))
+        self.first = (piece(512, 64, 32), piece(576, 64, 32))
+        self.cos, self.sin = table[640:672, :], table[672:704, :]
         self.is_first = is_first
         self.sign = jnp.where(lanes((32, 128)) < 64, 1.0, -1.0)
 
@@ -201,8 +203,8 @@
         out_ref[:, 8 * f : 8 * f + 8, :] = x_forward(ref[...], table_ref).reshape(32, 8, 128)
 
 
-def first_filter_kernel(is_first_ref, table, turns, arrived, out_ref, real_ref, imaginary_ref, power_ref, spectrum_ref):
-    lateral = Lateral(table, turns, is_first_ref[0])
+def first_filter_kernel(is_first_ref, table, arrived, out_ref, bank_ref):
+    lateral = Lateral(table, is_first_ref[0])
     transfer = lateral.forward(arrived, 8)
     observed = lateral.forward(arrived, 0)
     turned = swap(transfer)
@@ -220,16 +222,14 @@
         image_after, image_before = halo_rows(image[i])
         image_after, image_before = pltpu.roll(image_after, 8, 1), pltpu.roll(image_before, 120, 1)
         out_ref[:, 16 + i, :] = after + before + image_after + image_before
-    real_ref[...] = real
-    imaginary_ref[...] = imaginary
-    power_ref[...] = power
-    spectrum_ref[...] = spectrum
-
-
-def second_filter_kernel(is_first_ref, table, turns, arrived, power_ref, spectrum_ref, row_b, row_ab, out_ref, image_ref):
-    lateral = Lateral(table, turns, is_first_ref[0])
-    power = power_ref[...]
-    image = power * spectrum_ref[...] + lateral.forward(arrived, 0)
+    for k, value in enumerate((real, imaginary, power, spectrum)):
+        bank_ref[k] = value
+
+
+def second_filter_kernel(is_first_ref, table, arrived, bank_ref, row_b, row_ab, out_ref, image_ref):
+    lateral = Lateral(table, is_first_ref[0])
+    power = bank_ref[2]
+    image = power * bank_ref[3] + lateral.forward(arrived, 0)
     filtered = power * image
     blocks = lateral.inverse(filtered)
     for i in range(8):
@@ -243,17 +243,18 @@
 
 
 def last_filter_kernel(
-    is_first_ref, factor_ref, table, turns, arrived, real_ref, imaginary_ref, power_ref, spectrum_ref, image_ref, out_ref
+    is_first_ref, factor_ref, table, arrived, bank_ref, image_ref, terms, out_ref
 ):
-    lateral = Lateral(table, turns, is_first_ref[0])
-    power = power_ref[...]
+    lateral = Lateral(table, is_first_ref[0])
+    power = bank_ref[2]
     image = image_ref[...]
     total = factor_ref[4] * image + factor_ref[5] * (power * image) + lateral.forward(arrived, 8)
-    total = power * total + factor_ref[2] * spectrum_ref[...] + factor_ref[3] * image
+    total = power * total + factor_ref[2] * bank_ref[3] + factor_ref[3] * image
     total = total + lateral.forward(arrived, 0)
-    blocks = lateral.inverse(product(real_ref[...], -imaginary_ref[...], total))
+    blocks = lateral.inverse(product(bank_ref[0], -bank_ref[1], total))
     for i in range(8):
         out_ref[:, i, :] = blocks[i]
+        out_ref[:, 8 + i, :] = jnp.broadcast_to(terms[...], (32, 128))
 
 
 def gather_two_kernel(table_ref, arrived, right_ref, image_ref):
@@ -277,8 +278,9 @@
     out_ref[40:48, :] = base[40:48, :] + value[32:40]
 
 
-def final_kernel(table_ref, arrived, out_ref):
-    out_ref[...] = x_inverse([arrived[...].reshape(256, 128)], table_ref)
+def final_kernel(table_ref, arrived, out_ref, row_ref):
+    out_ref[...] = x_inverse([arrived[:, 0:8, :].reshape(256, 128)], table_ref)
+    row_ref[...] = jnp.sum(arrived[:, 8, :], 0, keepdims=True)
 
 
 def shifted_columns(value):
@@ -461,12 +463,6 @@
     return lax.all_to_all(jnp.broadcast_to(row[None], (size, 1, 128)), axis, 0, 0, tiled=True)
 
 
-def over_ring(row, axis):
-    for bit in (1, 2, 4, 8):
-        row = row + lax.ppermute(row, axis, [(i, i ^ bit) for i in range(16)])
-    return row
-
-
 def factors(m0, m1, m2, m3, u0, u1):
     def pair(m0, m1, m2, m3):
         step0 = m0 / m1
@@ -498,7 +494,7 @@
     is_first = jnp.where(device == 0, 1.0, 0.0).astype(F32).reshape(1)
     place = jnp.stack([device, plane, jnp.int32(lax.axis_size(GZ))]).astype(jnp.int32)
     weights = stencil_weights.reshape(27)
-    table, along_y, turns = jnp.asarray(X_TABLE), jnp.asarray(Y_TABLE), jnp.asarray(Y_TURNS)
+    table, along_y = jnp.asarray(X_TABLE), jnp.asarray(Y_TABLE)
     measured, upstream = measured[0], upstream[0]
     tile, tiles, three = shape(32, 8, 128), shape(32, 16, 128), shape(32, 24, 128)
     spectral, frame, rows, row = shape(32 * BLOCKS, 128), shape(FRAME, COLS), shape(ROWS, COLS), shape(1, 128)
@@ -506,8 +502,8 @@
     first = exchange(call(spread_kernel, tiles, [], [table, measured, point_spread]))
     first, grown = lax.optimization_barrier((first, with_rows(upstream)))
 
-    right_out, real, imaginary, power, spectrum = call(
-        first_filter_kernel, (three,) + (spectral,) * 4, [is_first], [along_y, turns, first]
+    right_out, bank = call(
+        first_filter_kernel, (three, shape(4, 32 * BLOCKS, 128)), [is_first], [along_y, first]
     )
     right_arrived = exchange(right_out)
     loss_parts = neighbours(grown)
@@ -533,16 +529,18 @@
         second_filter_kernel,
         (tiles, spectral),
         [is_first],
-        [along_y, turns, image_arrived, power, spectrum, row_b, row_ab],
+        [along_y, image_arrived, bank, row_b, row_ab],
     )
     further, row_sum = call(gather_sum_kernel, (frame, row), [], [table, exchange(further_out), image_back])
+    moments = from_all(row_sum, GZ)
+    further, moments = lax.optimization_barrier((further, moments))
     smem = pl.BlockSpec(memory_space=pltpu.SMEM)
     filter_factors, stencil_factors = pl.pallas_call(
         factors_kernel,
         out_shape=(shape(6), shape(5)),
         in_specs=[pl.BlockSpec(memory_space=pltpu.VMEM)],
         out_specs=(smem, smem),
-    )(from_all(row_sum, GZ))
+    )(moments)
 
     further_parts = neighbours(further)
     further_map, last_send = call(
@@ -560,17 +558,14 @@
     operands += [right_map, image_map, further_map, loss_map]
     scratch = (pltpu.VMEM((3, FRAME, COLS), F32), pltpu.VMEM((3, ROWS, COLS), F32))
     terms = call(correlate_kernel, row, [stencil_factors], operands, scratch)
-    terms = lax.psum(lax.psum(lax.psum(terms, "gz_1"), "gz_0"), "gy_1")
-    last_arrived, terms = lax.optimization_barrier((last_arrived, terms))
+    terms = lax.psum(lax.psum(terms, "gz_1"), "gz_0")
     result_out = call(
         last_filter_kernel,
-        tile,
+        tiles,
         [is_first, filter_factors],
-        [along_y, turns, last_arrived, real, imaginary, power, spectrum, image_spectrum],
-    )
-    result_out, terms = lax.optimization_barrier((result_out, terms))
-    grad_measured = call(final_kernel, rows, [], [table, exchange(result_out)])
-    terms = over_ring(terms, "gy_0")
+        [along_y, last_arrived, bank, image_spectrum, terms],
+    )
+    grad_measured, terms = call(final_kernel, (rows, row), [], [table, exchange(result_out)])
     grad_stencil = terms[0, :27].reshape(3, 3, 3) / math.sqrt(cells)
     return grad_measured[None], grad_stencil
 

time: 317 us -> 304 us (0.959)
  starting transfers between devices: 136 us -> 93.3 us
  blocking collectives: 72.5 us -> 108 us
    all_to_all x1 -> x2, blocking collectives: 34.7 us -> 72.2 us  [exchange(): return lax.all_to_all(value, GY, 0, 0, tiled=True)]
    ppermute x4 -> x0, starting transfers between devices: 27.9 us -> none  [over_ring(): row = row + lax.ppermute(row, axis, [(i, i ^ bit) for i in range(16)])]
    all_to_all x5 -> x4, starting transfers between devices: 48.1 us -> 35.5 us  [exchange(): return lax.all_to_all(value, GY, 0, 0, tiled=True)]
    ppermute x4 -> x0, waiting for transfers between devices: 4.49 us -> none  [over_ring(): row = row + lax.ppermute(row, axis, [(i, i ^ bit) for i in range(16)])]
    psum x3 -> x2, blocking collectives: 20.2 us -> 16.9 us  [local(): terms = lax.psum(lax.psum(terms, 'gz_1'), 'gz_0')]
    unnamed x96 -> x94, local copies, waits for them, and re-layouts: 29.6 us -> 30.5 us
    all_to_all x5 -> x4, waiting for transfers between devices: 16.5 us -> 15.7 us  [exchange(): return lax.all_to_all(value, GY, 0, 0, tiled=True)]
  transfers between devices with their start and end apart: 27 -> 22, of which waited for: 13 -> 10; matrix products, arithmetic and copies ran while one was open for 0% -> 0% of each run, Pallas kernels for 3% -> 3%
where the time goes in v3:
time: 304 us; the launch traced here: 302 us
  blocking collectives  108 us (36%)
  starting transfers between devices  93.3 us (31%)
  waiting for transfers between devices  39 us (13%)
  local copies, waits for them, and re-layouts  31.3 us (10%)
  Pallas kernels  29.6 us (10%)
    all_to_all x2, blocking collectives, exchange(): return lax.all_to_all(value, GY, 0, 0, tiled=True)  72.2 us
    ppermute x16, starting transfers between devices, moved(): return lax.ppermute(value, GZ, pairs)  52.3 us
    all_to_all x4, starting transfers between devices, exchange(): return lax.all_to_all(value, GY, 0, 0, tiled=True)  35.5 us
    unnamed x94, local copies, waits for them, and re-layouts  30.5 us
    pallas_call x12, Pallas kernels, call(): pl.pallas_call(body, out_shape=out_shape, in_specs=[smem] * len(scalars)...  28.2 us
    all_to_all x1, blocking collectives, from_all(): lax.all_to_all(jnp.broadcast_to(row[None], (size, 1, 128)), axis, 0, 0, t...  18.6 us
    psum x2, blocking collectives, local(): terms = lax.psum(lax.psum(terms, 'gz_1'), 'gz_0')  16.9 us
    all_to_all x4, waiting for transfers between devices, exchange(): return lax.all_to_all(value, GY, 0, 0, tiled=True)  15.7 us
  transfers between devices with their start and end apart: 22, of which 10 were waited for; matrix products, arithmetic and copies ran while one was open for 0% of the time, Pallas kernels for 3%

profile of v3, /device:TPU:1, one launch (start us, length us, event | category | flops | bytes accessed | tf_op | source)
XLA Modules:
  0.0 302.1 jit_solution(14704338404866427345)
XLA Ops:
  0.6 1.6 copy-done
  4.0 2.7 shard_map.77
  6.7 16.9 %all-to-all-start = ((f32[32,16,128]{2,1,0:T(8,128)}), f32[32,16,128]{2,1,0:T(8,128)S(1)}, u32[]{:S(2)}, u32[]{:S(2)}) async-start(f32[32,16,128]{2,1,0:T(8,128)} %shard_map.77), calls=%async_computation | async-start | bytes 524288 | tf_op jit(solution)/shard_map/all_to_all | solution.py:441
  23.6 3.5 %collective-permute-start = (f32[8,1024]{1,0:T(8,128)S(1)}, f32[8,1024]{1,0:T(8,128)S(1)}, u32[]{:S(2)}, u32[]{:S(2)}) collective-permute-start(f32[8,1024]{1,0:T(8,128)S(1)} %get-tuple-element.64), channel_id=1, source_target_pairs={{0,16},{16,32},{32,48},{48,64},{64,80},{80,96},{96,112},{112,128},... | collective-permute-start | bytes 98312 | tf_op jit(solution)/shard_map/ppermute | solution.py:456
  27.2 1.9 collective-permute-start.1
  29.1 1.5 collective-permute-done
  30.6 6.2 %collective-permute-done.1 = f32[8,1024]{1,0:T(8,128)S(1)} collective-permute-done((f32[8,1024]{1,0:T(8,128)S(1)}, f32[8,1024]{1,0:T(8,128)S(1)}, u32[]{:S(2)}, u32[]{:S(2)}) %collective-permute-start.1) | collective-permute-done | bytes 32800 | tf_op jit(solution)/shard_map/ppermute | solution.py:457
  36.8 8.6 %all-to-all-done.arrived = f32[32,16,128]{2,1,0:T(8,128)S(1)} async-done(((f32[32,16,128]{2,1,0:T(8,128)}), f32[32,16,128]{2,1,0:T(8,128)S(1)}, u32[]{:S(2)}, u32[]{:S(2)}) %all-to-all-start) | async-done | bytes 262176 | tf_op jit(solution)/shard_map/all_to_all | solution.py:441
  45.4 2.9 shard_map.78
  49.2 4.9 %all-to-all-start.1 = ((f32[32,24,128]{2,1,0:T(8,128)}), f32[32,24,128]{2,1,0:T(8,128)S(1)}, u32[]{:S(2)}, u32[]{:S(2)}) async-start(f32[32,24,128]{2,1,0:T(8,128)} %get-tuple-element.34), calls=%async_computation.1 | async-start | bytes 786432 | tf_op jit(solution)/shard_map/all_to_all | solution.py:441
  54.1 1.3 collective-permute-start.5
  55.4 1.3 collective-permute-start.4
  56.7 6.8 %collective-permute-start.3 = (f32[48,1024]{1,0:T(8,128)S(1)}, f32[48,1024]{1,0:T(8,128)}, u32[]{:S(2)}, u32[]{:S(2)}) collective-permute-start(f32[48,1024]{1,0:T(8,128)S(1)} %pad_maximum_fusion.o.refs_10_), channel_id=1, source_target_pairs={{0,2},{1,3},{2,4},{3,5},{4,6},{5,7},{6,8},{7,9},{8,10},{9,11},{10,... | collective-permute-start | bytes 589832 | tf_op jit(solution)/shard_map/ppermute | solution.py:449
  63.5 3.8 %collective-permute-start.2 = (f32[48,1024]{1,0:T(8,128)S(1)}, f32[48,1024]{1,0:T(8,128)}, u32[]{:S(2)}, u32[]{:S(2)}) collective-permute-start(f32[48,1024]{1,0:T(8,128)S(1)} %pad_maximum_fusion.o.refs_10_), channel_id=1, source_target_pairs={{0,1},{1,2},{2,3},{3,4},{4,5},{5,6},{6,7},{7,8},{8,9},{9,10},{10,1... | collective-permute-start | bytes 589832 | tf_op jit(solution)/shard_map/ppermute | solution.py:449
  67.5 3.3 %collective-permute-done.2.u1.refs_9_ = f32[48,1024]{1,0:T(8,128)} collective-permute-done((f32[48,1024]{1,0:T(8,128)S(1)}, f32[48,1024]{1,0:T(8,128)}, u32[]{:S(2)}, u32[]{:S(2)}) %collective-permute-start.2) | collective-permute-done | bytes 196640 | tf_op jit(solution)/shard_map/ppermute | solution.py:449
  70.8 3.0 shard_map.79
  75.1 7.1 %all-to-all-done.1.arrived = f32[32,24,128]{2,1,0:T(8,128)S(1)} async-done(((f32[32,24,128]{2,1,0:T(8,128)}), f32[32,24,128]{2,1,0:T(8,128)S(1)}, u32[]{:S(2)}, u32[]{:S(2)}) %all-to-all-start.1) | async-done | bytes 393248 | tf_op jit(solution)/shard_map/all_to_all | solution.py:441
  83.0 1.3 collective-permute-start.9
  84.3 1.3 collective-permute-start.8
  85.6 6.1 %collective-permute-start.7 = (f32[48,1024]{1,0:T(8,128)S(1)}, f32[48,1024]{1,0:T(8,128)S(1)}, u32[]{:S(2)}, u32[]{:S(2)}) collective-permute-start(f32[48,1024]{1,0:T(8,128)S(1)} %get-tuple-element.38.o.refs_1_), channel_id=1, source_target_pairs={{0,2},{1,3},{2,4},{3,5},{4,6},{5,7},{6,8},{7,9},{8,10},{9,11},{10,... | collective-permute-start | bytes 589832 | tf_op jit(solution)/shard_map/ppermute | solution.py:449
  91.7 3.1 %collective-permute-start.6 = (f32[48,1024]{1,0:T(8,128)S(1)}, f32[48,1024]{1,0:T(8,128)S(1)}, u32[]{:S(2)}, u32[]{:S(2)}) collective-permute-start(f32[48,1024]{1,0:T(8,128)S(1)} %get-tuple-element.38.o.refs_1_), channel_id=1, source_target_pairs={{0,1},{1,2},{2,3},{3,4},{4,5},{5,6},{6,7},{7,8},{8,9},{9,10},{10,1... | collective-permute-start | bytes 589832 | tf_op jit(solution)/shard_map/ppermute | solution.py:449
  95.1 4.6 %collective-permute-done.6.u1.refs_0_ = f32[48,1024]{1,0:T(8,128)S(1)} collective-permute-done((f32[48,1024]{1,0:T(8,128)S(1)}, f32[48,1024]{1,0:T(8,128)S(1)}, u32[]{:S(2)}, u32[]{:S(2)}) %collective-permute-start.6) | collective-permute-done | bytes 196640 | tf_op jit(solution)/shard_map/ppermute | solution.py:449
  99.6 3.4 %shard_map.81 = (f32[48,1024]{1,0:T(8,128)S(1)}, f32[32,1024]{1,0:T(8,128)S(1)}, f32[32,8,128]{2,1,0:T(8,128)S(1)}, f32[1,128]{1,0:T(1,128)S(1)}) custom-call(s32[3]{0:T(128)S(1)} %pad_add_fusion.place, f32[27]{0:T(128)S(1)} %reshape.18.weights, bf16[2048,512]{1,0:T(8,128)(2,1)S(1)} %copy-done.1, f32[48,1024]{1,0:T(8,128)S(1)} %get-tuple-element.38.o.refs_1_, ...), custom_call_target="tpu_custom_call" | custom-call | flops 400000000 | bytes 4000000 | tf_op jit(solution)/shard_map/pallas_call | solution.py:429
  105.5 7.7 %all-to-all-start.2 = ((f32[32,8,128]{2,1,0:T(8,128)}), f32[32,8,128]{2,1,0:T(8,128)S(1)}, u32[]{:S(2)}, u32[]{:S(2)}) async-start(f32[32,8,128]{2,1,0:T(8,128)} %copy-done.26), calls=%async_computation.2 | async-start | bytes 262144 | tf_op jit(solution)/shard_map/all_to_all | solution.py:441
  113.3 1.3 collective-permute-start.13
  114.6 1.3 collective-permute-start.12
  115.9 8.4 %collective-permute-start.11 = (f32[48,1024]{1,0:T(8,128)}, f32[48,1024]{1,0:T(8,128)S(1)}, u32[]{:S(2)}, u32[]{:S(2)}) collective-permute-start(f32[48,1024]{1,0:T(8,128)} %copy-done.15), channel_id=1, source_target_pairs={{0,2},{1,3},{2,4},{3,5},{4,6},{5,7},{6,8},{7,9},{8,10},{9,11},{10,... | collective-permute-start | bytes 589832 | tf_op jit(solution)/shard_map/ppermute | solution.py:449
  124.3 3.5 %collective-permute-start.10 = (f32[48,1024]{1,0:T(8,128)}, f32[48,1024]{1,0:T(8,128)S(1)}, u32[]{:S(2)}, u32[]{:S(2)}) collective-permute-start(f32[48,1024]{1,0:T(8,128)} %copy-done.15), channel_id=1, source_target_pairs={{0,1},{1,2},{2,3},{3,4},{4,5},{5,6},{6,7},{7,8},{8,9},{9,10},{10,1... | collective-permute-start | bytes 589832 | tf_op jit(solution)/shard_map/ppermute | solution.py:449
  128.6 4.2 %collective-permute-done.10.u1.refs_3_ = f32[48,1024]{1,0:T(8,128)S(1)} collective-permute-done((f32[48,1024]{1,0:T(8,128)}, f32[48,1024]{1,0:T(8,128)S(1)}, u32[]{:S(2)}, u32[]{:S(2)}) %collective-permute-start.10) | collective-permute-done | bytes 196640 | tf_op jit(solution)/shard_map/ppermute | solution.py:449
  133.8 2.5 shard_map.82
  139.5 1.1 copy-done.6
  142.7 1.4 shard_map.83
  144.1 34.7 %all_to_all.35.arrived = f32[32,16,128]{2,1,0:T(8,128)S(1)} all-to-all(f32[32,16,128]{2,1,0:T(8,128)S(1)} %get-tuple-element.47), channel_id=1, replica_groups=mesh['gy_0'=16,'gy_1'=2,'gz_0'=4,'gz_1'=4] {'gy_0','gy_1'}, dimensions={0} | all-to-all | bytes 524288 | tf_op jit(solution)/shard_map/all_to_all | solution.py:441
  179.4 18.6 %all_to_all.36.rows = f32[16,1,128]{2,1,0:T(1,128)} all-to-all(f32[16,1,128]{2,1,0:T(1,128)S(1)} %broadcast_in_dim.12), channel_id=1, replica_groups=mesh['gy_0'=16,'gy_1'=2,'gz_0'=4,'gz_1'=4] {'gz_0','gz_1'}, dimensions={0} | all-to-all | bytes 16384 | tf_op jit(solution)/shard_map/all_to_all | solution.py:463
  198.0 1.3 collective-permute-start.17
  199.3 1.3 collective-permute-start.16
  200.6 6.8 %collective-permute-start.15 = (f32[48,1024]{1,0:T(8,128)S(1)}, f32[48,1024]{1,0:T(8,128)}, u32[]{:S(2)}, u32[]{:S(2)}) collective-permute-start(f32[48,1024]{1,0:T(8,128)S(1)} %get-tuple-element.53.o.refs_7_), channel_id=1, source_target_pairs={{0,2},{1,3},{2,4},{3,5},{4,6},{5,7},{6,8},{7,9},{8,10},{9,11},{10,... | collective-permute-start | bytes 589832 | tf_op jit(solution)/shard_map/ppermute | solution.py:449
  207.4 3.4 %collective-permute-start.14 = (f32[48,1024]{1,0:T(8,128)S(1)}, f32[48,1024]{1,0:T(8,128)}, u32[]{:S(2)}, u32[]{:S(2)}) collective-permute-start(f32[48,1024]{1,0:T(8,128)S(1)} %get-tuple-element.53.o.refs_7_), channel_id=1, source_target_pairs={{0,1},{1,2},{2,3},{3,4},{4,5},{5,6},{6,7},{7,8},{8,9},{9,10},{10,1... | collective-permute-start | bytes 589832 | tf_op jit(solution)/shard_map/ppermute | solution.py:449
  210.9 1.4 shard_map.85
  212.3 2.6 collective-permute-done.14.u1.refs_6_
  217.7 4.8 %shard_map.86 = (f32[32,1024]{1,0:T(8,128)S(1)}, f32[32,16,128]{2,1,0:T(8,128)S(1)}) custom-call(s32[3]{0:T(128)S(1)} %copy-done.36, f32[27]{0:T(128)S(1)} %copy-done.38, f32[6]{0:T(128)S(1)} %copy-done.39, bf16[2048,512]{1,0:T(8,128)(2,1)S(1)} %copy-done.1, f32[48,1024]{1,0:T(8,128)S(1)} %get-tuple-element.53.o.refs_7_, ...), custom_call_target="tpu_custom_call" | custom-call | flops 400000000 | bytes 4000000 | tf_op jit(solution)/shard_map/pallas_call | solution.py:429
  223.9 6.0 %all-to-all-start.5 = ((f32[32,16,128]{2,1,0:T(8,128)}), f32[32,16,128]{2,1,0:T(8,128)S(1)}, u32[]{:S(2)}, u32[]{:S(2)}) async-start(f32[32,16,128]{2,1,0:T(8,128)} %copy-done.10), calls=%async_computation.5 | async-start | bytes 524288 | tf_op jit(solution)/shard_map/all_to_all | solution.py:441
  238.8 2.6 shard_map.87
  241.4 10.3 %psum.14 = f32[1,128]{1,0:T(1,128)S(1)} all-reduce(f32[1,128]{1,0:T(1,128)S(1)} %shard_map.87), channel_id=1, replica_groups=mesh['gy_0'=16,'gy_1'=2,'gz_0'=4,'gz_1'=4] {'gz_1'}, use_global_device_ids=true, to_apply=%region_0.1 | all-reduce | flops 128 | bytes 1024 | tf_op jit(solution)/shard_map/psum | solution.py:561
  251.7 6.6 %psum.15.terms = f32[1,128]{1,0:T(1,128)S(1)} all-reduce(f32[1,128]{1,0:T(1,128)S(1)} %psum.14), channel_id=1, replica_groups=mesh['gy_0'=16,'gy_1'=2,'gz_0'=4,'gz_1'=4] {'gz_0'}, use_global_device_ids=true, to_apply=%region_1.2 | all-reduce | flops 128 | bytes 1024 | tf_op jit(solution)/shard_map/psum | solution.py:561
  260.4 2.3 shard_map.88
  262.7 37.5 %all_to_all.37.arrived = f32[32,16,128]{2,1,0:T(8,128)S(1)} all-to-all(f32[32,16,128]{2,1,0:T(8,128)S(1)} %shard_map.88), channel_id=1, replica_groups=mesh['gy_0'=16,'gy_1'=2,'gz_0'=4,'gz_1'=4] {'gy_0','gy_1'}, dimensions={0} | all-to-all | bytes 524288 | tf_op jit(solution)/shard_map/all_to_all | solution.py:441
  300.2 1.2 shard_map.89
  (115 shorter events, 31.2 us)
Async XLA Ops:
  0.6 1.6 copy-start
  2.2 0.9 copy-start.22
  3.1 0.9 copy-start.23
  4.0 19.6 %copy-start.2 = (f32[1,32,1024]{2,1,0:T(8,128)S(1)}, f32[1,32,1024]{2,1,0:T(8,128)}, u32[]{:S(2)}) copy-start(f32[1,32,1024]{2,1,0:T(8,128)} %param.9) | copy-start | bytes 393220
  4.0 41.4 %copy-start.8 = (f32[704,128]{1,0:T(8,128)S(1)}, f32[704,128]{1,0:T(8,128)}, u32[]{:S(2)}) copy-start(f32[704,128]{1,0:T(8,128)} %constant.38.clone.table) | copy-start | bytes 1081348
  6.7 60.6 %copy-start.46 = (f32[3,3,3]{2,1,0:T(4,128)S(1)}, f32[3,3,3]{2,1,0:T(4,128)}, u32[]{:S(2)}) copy-start(f32[3,3,3]{2,1,0:T(4,128)} %param.8) | copy-start | bytes 328
  6.7 38.7 %all-to-all-start = ((f32[32,16,128]{2,1,0:T(8,128)}), f32[32,16,128]{2,1,0:T(8,128)S(1)}, u32[]{:S(2)}, u32[]{:S(2)}) async-start(f32[32,16,128]{2,1,0:T(8,128)} %shard_map.77), calls=%async_computation | async-start | bytes 524288 | tf_op jit(solution)/shard_map/all_to_all | solution.py:441
  23.6 7.0 %collective-permute-start = (f32[8,1024]{1,0:T(8,128)S(1)}, f32[8,1024]{1,0:T(8,128)S(1)}, u32[]{:S(2)}, u32[]{:S(2)}) collective-permute-start(f32[8,1024]{1,0:T(8,128)S(1)} %get-tuple-element.64), channel_id=1, source_target_pairs={{0,16},{16,32},{32,48},{48,64},{64,80},{80,96},{96,112},{112,128},... | collective-permute-start | bytes 98312 | tf_op jit(solution)/shard_map/ppermute | solution.py:456
  27.2 9.6 %collective-permute-start.1 = (f32[8,1024]{1,0:T(8,128)S(1)}, f32[8,1024]{1,0:T(8,128)S(1)}, u32[]{:S(2)}, u32[]{:S(2)}) collective-permute-start(f32[8,1024]{1,0:T(8,128)S(1)} %get-tuple-element.65), channel_id=1, source_target_pairs={{16,0},{32,16},{48,32},{64,48},{80,64},{96,80},{112,96},{128,112},... | collective-permute-start | bytes 98312 | tf_op jit(solution)/shard_map/ppermute | solution.py:457
  29.1 53.0 %copy-start.1 = (bf16[2048,512]{1,0:T(8,128)(2,1)S(1)}, bf16[2048,512]{1,0:T(8,128)(2,1)}, u32[]{:S(2)}) copy-start(bf16[2048,512]{1,0:T(8,128)(2,1)} %constant.37.clone.table_ref.table) | copy-start | bytes 6291460
  36.8 45.4 %copy-start.3 = (f32[48,1024]{1,0:T(8,128)}, f32[48,1024]{1,0:T(8,128)S(1)}, u32[]{:S(2)}) copy-start(f32[48,1024]{1,0:T(8,128)S(1)} %pad_maximum_fusion.o.refs_10_) | copy-start | bytes 589828
  49.2 32.9 %all-to-all-start.1 = ((f32[32,24,128]{2,1,0:T(8,128)}), f32[32,24,128]{2,1,0:T(8,128)S(1)}, u32[]{:S(2)}, u32[]{:S(2)}) async-start(f32[32,24,128]{2,1,0:T(8,128)} %get-tuple-element.34), calls=%async_computation.1 | async-start | bytes 786432 | tf_op jit(solution)/shard_map/all_to_all | solution.py:441
  54.1 13.4 %collective-permute-start.5 = (f32[48,1024]{1,0:T(8,128)S(1)}, f32[48,1024]{1,0:T(8,128)}, u32[]{:S(2)}, u32[]{:S(2)}) collective-permute-start(f32[48,1024]{1,0:T(8,128)S(1)} %pad_maximum_fusion.o.refs_10_), channel_id=1, source_target_pairs={{2,0},{3,1},{4,2},{5,3},{6,4},{7,5},{8,6},{9,7},{10,8},{11,9},{12,... | collective-permute-start | bytes 589832 | tf_op jit(solution)/shard_map/ppermute | solution.py:449
  55.4 12.1 %collective-permute-start.4 = (f32[48,1024]{1,0:T(8,128)S(1)}, f32[48,1024]{1,0:T(8,128)S(1)}, u32[]{:S(2)}, u32[]{:S(2)}) collective-permute-start(f32[48,1024]{1,0:T(8,128)S(1)} %pad_maximum_fusion.o.refs_10_), channel_id=1, source_target_pairs={{1,0},{2,1},{3,2},{4,3},{5,4},{6,5},{7,6},{8,7},{9,8},{10,9},{11,1... | collective-permute-start | bytes 589832 | tf_op jit(solution)/shard_map/ppermute | solution.py:449
  56.7 10.8 %collective-permute-start.3 = (f32[48,1024]{1,0:T(8,128)S(1)}, f32[48,1024]{1,0:T(8,128)}, u32[]{:S(2)}, u32[]{:S(2)}) collective-permute-start(f32[48,1024]{1,0:T(8,128)S(1)} %pad_maximum_fusion.o.refs_10_), channel_id=1, source_target_pairs={{0,2},{1,3},{2,4},{3,5},{4,6},{5,7},{6,8},{7,9},{8,10},{9,11},{10,... | collective-permute-start | bytes 589832 | tf_op jit(solution)/shard_map/ppermute | solution.py:449
  63.5 7.3 %collective-permute-start.2 = (f32[48,1024]{1,0:T(8,128)S(1)}, f32[48,1024]{1,0:T(8,128)}, u32[]{:S(2)}, u32[]{:S(2)}) collective-permute-start(f32[48,1024]{1,0:T(8,128)S(1)} %pad_maximum_fusion.o.refs_10_), channel_id=1, source_target_pairs={{0,1},{1,2},{2,3},{3,4},{4,5},{5,6},{6,7},{7,8},{8,9},{9,10},{10,1... | collective-permute-start | bytes 589832 | tf_op jit(solution)/shard_map/ppermute | solution.py:449
  67.4 65.5 %copy-start.37 = (f32[27]{0:T(128)}, f32[27]{0:T(128)S(1)}, u32[]{:S(2)}) copy-start(f32[27]{0:T(128)S(1)} %reshape.18.weights) | copy-start | bytes 328
  67.5 65.4 %copy-start.35 = (s32[3]{0:T(128)}, s32[3]{0:T(128)S(1)}, u32[]{:S(2)}) copy-start(s32[3]{0:T(128)S(1)} %pad_add_fusion.place) | copy-start | bytes 40
  67.5 18.1 %copy-start.13 = (f32[48,1024]{1,0:T(8,128)}, f32[48,1024]{1,0:T(8,128)S(1)}, u32[]{:S(2)}) copy-start(f32[48,1024]{1,0:T(8,128)S(1)} %collective-permute-done.4.d1.refs_11_) | copy-start | bytes 589828
  83.0 11.9 %collective-permute-start.9 = (f32[48,1024]{1,0:T(8,128)S(1)}, f32[48,1024]{1,0:T(8,128)S(1)}, u32[]{:S(2)}, u32[]{:S(2)}) collective-permute-start(f32[48,1024]{1,0:T(8,128)S(1)} %get-tuple-element.38.o.refs_1_), channel_id=1, source_target_pairs={{2,0},{3,1},{4,2},{5,3},{6,4},{7,5},{8,6},{9,7},{10,8},{11,9},{12,... | collective-permute-start | bytes 589832 | tf_op jit(solution)/shard_map/ppermute | solution.py:449
  84.3 10.6 %collective-permute-start.8 = (f32[48,1024]{1,0:T(8,128)S(1)}, f32[48,1024]{1,0:T(8,128)S(1)}, u32[]{:S(2)}, u32[]{:S(2)}) collective-permute-start(f32[48,1024]{1,0:T(8,128)S(1)} %get-tuple-element.38.o.refs_1_), channel_id=1, source_target_pairs={{1,0},{2,1},{3,2},{4,3},{5,4},{6,5},{7,6},{8,7},{9,8},{10,9},{11,1... | collective-permute-start | bytes 589832 | tf_op jit(solution)/shard_map/ppermute | solution.py:449
  85.6 9.5 %collective-permute-start.7 = (f32[48,1024]{1,0:T(8,128)S(1)}, f32[48,1024]{1,0:T(8,128)S(1)}, u32[]{:S(2)}, u32[]{:S(2)}) collective-permute-start(f32[48,1024]{1,0:T(8,128)S(1)} %get-tuple-element.38.o.refs_1_), channel_id=1, source_target_pairs={{0,2},{1,3},{2,4},{3,5},{4,6},{5,7},{6,8},{7,9},{8,10},{9,11},{10,... | collective-permute-start | bytes 589832 | tf_op jit(solution)/shard_map/ppermute | solution.py:449
  91.7 7.9 %collective-permute-start.6 = (f32[48,1024]{1,0:T(8,128)S(1)}, f32[48,1024]{1,0:T(8,128)S(1)}, u32[]{:S(2)}, u32[]{:S(2)}) collective-permute-start(f32[48,1024]{1,0:T(8,128)S(1)} %get-tuple-element.38.o.refs_1_), channel_id=1, source_target_pairs={{0,1},{1,2},{2,3},{3,4},{4,5},{5,6},{6,7},{7,8},{8,9},{9,10},{10,1... | collective-permute-start | bytes 589832 | tf_op jit(solution)/shard_map/ppermute | solution.py:449
  105.5 33.3 %all-to-all-start.2 = ((f32[32,8,128]{2,1,0:T(8,128)}), f32[32,8,128]{2,1,0:T(8,128)S(1)}, u32[]{:S(2)}, u32[]{:S(2)}) async-start(f32[32,8,128]{2,1,0:T(8,128)} %copy-done.26), calls=%async_computation.2 | async-start | bytes 262144 | tf_op jit(solution)/shard_map/all_to_all | solution.py:441
  113.3 14.5 %collective-permute-start.13 = (f32[48,1024]{1,0:T(8,128)}, f32[48,1024]{1,0:T(8,128)S(1)}, u32[]{:S(2)}, u32[]{:S(2)}) collective-permute-start(f32[48,1024]{1,0:T(8,128)} %copy-done.15), channel_id=1, source_target_pairs={{2,0},{3,1},{4,2},{5,3},{6,4},{7,5},{8,6},{9,7},{10,8},{11,9},{12,... | collective-permute-start | bytes 589832 | tf_op jit(solution)/shard_map/ppermute | solution.py:449
  114.6 13.2 %collective-permute-start.12 = (f32[48,1024]{1,0:T(8,128)}, f32[48,1024]{1,0:T(8,128)S(1)}, u32[]{:S(2)}, u32[]{:S(2)}) collective-permute-start(f32[48,1024]{1,0:T(8,128)} %copy-done.15), channel_id=1, source_target_pairs={{1,0},{2,1},{3,2},{4,3},{5,4},{6,5},{7,6},{8,7},{9,8},{10,9},{11,1... | collective-permute-start | bytes 589832 | tf_op jit(solution)/shard_map/ppermute | solution.py:449
  115.9 12.8 %collective-permute-start.11 = (f32[48,1024]{1,0:T(8,128)}, f32[48,1024]{1,0:T(8,128)S(1)}, u32[]{:S(2)}, u32[]{:S(2)}) collective-permute-start(f32[48,1024]{1,0:T(8,128)} %copy-done.15), channel_id=1, source_target_pairs={{0,2},{1,3},{2,4},{3,5},{4,6},{5,7},{6,8},{7,9},{8,10},{9,11},{10,... | collective-permute-start | bytes 589832 | tf_op jit(solution)/shard_map/ppermute | solution.py:449
  124.3 8.6 %collective-permute-start.10 = (f32[48,1024]{1,0:T(8,128)}, f32[48,1024]{1,0:T(8,128)S(1)}, u32[]{:S(2)}, u32[]{:S(2)}) collective-permute-start(f32[48,1024]{1,0:T(8,128)} %copy-done.15), channel_id=1, source_target_pairs={{0,1},{1,2},{2,3},{3,4},{4,5},{5,6},{6,7},{7,8},{8,9},{9,10},{10,1... | collective-permute-start | bytes 589832 | tf_op jit(solution)/shard_map/ppermute | solution.py:449
  132.9 0.9 copy-start.16
  139.5 1.1 copy-start.6
  140.5 0.9 copy-start.25
  198.0 14.2 %collective-permute-start.17 = (f32[48,1024]{1,0:T(8,128)S(1)}, f32[48,1024]{1,0:T(8,128)}, u32[]{:S(2)}, u32[]{:S(2)}) collective-permute-start(f32[48,1024]{1,0:T(8,128)S(1)} %get-tuple-element.53.o.refs_7_), channel_id=1, source_target_pairs={{2,0},{3,1},{4,2},{5,3},{6,4},{7,5},{8,6},{9,7},{10,8},{11,9},{12,... | collective-permute-start | bytes 589832 | tf_op jit(solution)/shard_map/ppermute | solution.py:449
  199.3 13.0 %collective-permute-start.16 = (f32[48,1024]{1,0:T(8,128)S(1)}, f32[48,1024]{1,0:T(8,128)S(1)}, u32[]{:S(2)}, u32[]{:S(2)}) collective-permute-start(f32[48,1024]{1,0:T(8,128)S(1)} %get-tuple-element.53.o.refs_7_), channel_id=1, source_target_pairs={{1,0},{2,1},{3,2},{4,3},{5,4},{6,5},{7,6},{8,7},{9,8},{10,9},{11,1... | collective-permute-start | bytes 589832 | tf_op jit(solution)/shard_map/ppermute | solution.py:449
  200.6 11.7 %collective-permute-start.15 = (f32[48,1024]{1,0:T(8,128)S(1)}, f32[48,1024]{1,0:T(8,128)}, u32[]{:S(2)}, u32[]{:S(2)}) collective-permute-start(f32[48,1024]{1,0:T(8,128)S(1)} %get-tuple-element.53.o.refs_7_), channel_id=1, source_target_pairs={{0,2},{1,3},{2,4},{3,5},{4,6},{5,7},{6,8},{7,9},{8,10},{9,11},{10,... | collective-permute-start | bytes 589832 | tf_op jit(solution)/shard_map/ppermute | solution.py:449
  207.4 7.5 %collective-permute-start.14 = (f32[48,1024]{1,0:T(8,128)S(1)}, f32[48,1024]{1,0:T(8,128)}, u32[]{:S(2)}, u32[]{:S(2)}) collective-permute-start(f32[48,1024]{1,0:T(8,128)S(1)} %get-tuple-element.53.o.refs_7_), channel_id=1, source_target_pairs={{0,1},{1,2},{2,3},{3,4},{4,5},{5,6},{6,7},{7,8},{8,9},{9,10},{10,1... | collective-permute-start | bytes 589832 | tf_op jit(solution)/shard_map/ppermute | solution.py:449
  214.9 0.9 copy-start.12
  223.9 34.4 %copy-start.40 = (f32[6]{0:T(128)S(1)}, f32[6]{0:T(128)}, u32[]{:S(2)}) copy-start(f32[6]{0:T(128)} %get-tuple-element.52.factor.factor_ref) | copy-start | bytes 76
  223.9 34.4 %all-to-all-start.5 = ((f32[32,16,128]{2,1,0:T(8,128)}), f32[32,16,128]{2,1,0:T(8,128)S(1)}, u32[]{:S(2)}, u32[]{:S(2)}) async-start(f32[32,16,128]{2,1,0:T(8,128)} %copy-done.10), calls=%async_computation.5 | async-start | bytes 524288 | tf_op jit(solution)/shard_map/all_to_all | solution.py:441
  229.9 0.9 copy-start.4
  230.8 0.9 copy-start.14
  231.8 0.9 copy-start.17
  232.7 0.9 copy-start.19
  233.6 0.9 copy-start.21
  234.6 0.9 copy-start.28
  235.5 0.9 copy-start.30
  236.4 0.9 copy-start.32
  258.3 1.1 copy-start.7
  259.4 1.0 copy-start.9
  (21 other events, 13.9 us)

commit v4 on v3

--- a/solution.py
+++ b/solution.py
@@ -8,18 +8,17 @@
 from jax import lax
 from jax.experimental import pallas as pl
 from jax.experimental.pallas import tpu as pltpu
-from jax.sharding import Mesh
 from jax.sharding import PartitionSpec as P
 
-GY = ("gy_0", "gy_1")
-GZ = ("gz_0", "gz_1")
+GY = "gy"
+GZ = "gz"
 ROWS = 32
 COLS = 1024
 FRAME = 48
 BLOCKS = 9
 F32 = jnp.float32
 BF16 = jnp.bfloat16
-VMEM = 14 * 1024 * 1024
+VMEM = 60 * 1024 * 1024
 
 
 def split_table(table):
@@ -306,39 +305,49 @@
     return total
 
 
-def apply_stencils(place_ref, weights_ref, parts, source, middle, back_ref):
+def load_planes(parts, source, sems):
+    copies = [pltpu.make_async_copy(ref, source.at[1, p], sems.at[p]) for p, ref in enumerate(parts)]
+    for copy in copies:
+        copy.start()
+    for copy in copies:
+        copy.wait()
+    for p in range(len(parts)):
+        source[0, p], source[2, p] = shifted_columns(source[1, p])
+
+
+def row_bounds(place_ref):
     device, plane, planes = place_ref[0], place_ref[1], place_ref[2]
-    own, up1, up2, down1, down2 = parts
-    for p, ref in enumerate((up2, up1, own, down1, down2)):
-        value = ref[...]
-        left, right = shifted_columns(value)
-        source[0, p], source[1, p], source[2, p] = left, value, right
-    row = sublanes((FRAME, 128))
     lowest = jnp.where(device > 0, 0, 8)
     highest = jnp.where(device < 31, FRAME, 40)
 
-    def weight(a, b, c):
-        return weights_ref[9 * a + 3 * b + c]
-
-    def flipped(a, b, c):
-        return weights_ref[26 - 9 * a - 3 * b - c]
-
+    def highest_at(here):
+        return jnp.where((here >= 0) & (here < planes), highest, 0)
+
+    return sublanes((FRAME, 128)), lowest, highest, lambda p: highest_at(plane + p)
+
+
+def weight_of(weights_ref):
+    return lambda a, b, c: weights_ref[9 * a + 3 * b + c]
+
+
+def flipped_of(weights_ref):
+    return lambda a, b, c: weights_ref[26 - 9 * a - 3 * b - c]
+
+
+def apply_stencils(place_ref, weights_ref, source, middle, back_ref):
+    row, lowest, highest, highest_at = row_bounds(place_ref)
     for p in range(3):
-        here = plane + (p - 1)
-        end = jnp.where((here >= 0) & (here < planes), highest, 0)
-        valid = (row >= lowest) & (row < end)
+        valid = (row >= lowest) & (row < highest_at(p - 1))
         for k in range(8):
             cols = slice(128 * k, 128 * k + 128)
-            value = stencil_sum(weight, source, p, cols)
+            value = stencil_sum(weight_of(weights_ref), source, p, cols)
             middle[1, p, :, cols] = jnp.where(valid, value, 0.0)
     for p in range(3):
-        value = middle[1, p]
-        left, right = shifted_columns(value)
-        middle[0, p], middle[2, p] = left, right
+        middle[0, p], middle[2, p] = shifted_columns(middle[1, p])
     inside = (row >= lowest) & (row < highest)
     for k in range(8):
         cols = slice(128 * k, 128 * k + 128)
-        back_ref[:, cols] = jnp.where(inside, stencil_sum(flipped, middle, 0, cols), 0.0)
+        back_ref[:, cols] = jnp.where(inside, stencil_sum(flipped_of(weights_ref), middle, 0, cols), 0.0)
 
 
 def row_of(values):
@@ -349,32 +358,43 @@
     return out
 
 
-def image_kernel(place, weights, table, o, u1, u2, d1, d2, blurred, upstream, image_ref, mapped_ref, out_ref, row_ref, *scratch):
-    source, middle, back = scratch
-    apply_stencils(place, weights, (o, u1, u2, d1, d2), source, middle, back)
+def image_kernel(place, weights, table, blurred, upstream, u2, u1, o, d1, d2, image_ref, mapped_ref, out_ref, row_ref, *scratch):
+    source, middle, sems, back = scratch
+    load_planes((u2, u1, o, d1, d2), source, sems)
+    apply_stencils(place, weights, source, middle, back)
     out_ref[...] = x_forward(back[8:40, :], table).reshape(32, 8, 128)
     mapped_ref[...] = middle[1, 1, 8:40, :]
     image_ref[...] = blurred[...] + back[...]
-    b, ab, u = o[8:40, :], image_ref[8:40, :], upstream[...]
+    b, ab, u = source[1, 2, 8:40, :], image_ref[8:40, :], upstream[...]
     row_ref[...] = row_of(((0, b * b), (1, b * ab), (2, ab * ab), (4, u * b), (5, u * ab)))
 
 
-def loss_kernel(place, weights, o, u1, u2, d1, d2, back_ref, mapped_ref, source, middle):
-    apply_stencils(place, weights, (o, u1, u2, d1, d2), source, middle, back_ref)
+def loss_kernel(place, weights, u2, u1, o, d1, d2, back_ref, mapped_ref, source, middle, sems):
+    load_planes((u2, u1, o, d1, d2), source, sems)
+    apply_stencils(place, weights, source, middle, back_ref)
     mapped_ref[...] = middle[1, 1, 8:40, :]
 
 
-def further_kernel(place, weights, o, u1, u2, d1, d2, back_ref, mapped_ref, row_ref, source, middle):
-    apply_stencils(place, weights, (o, u1, u2, d1, d2), source, middle, back_ref)
-    mapped = middle[1, 1, 8:40, :]
+def map_kernel(weights, u1, o, d1, mapped_ref, row_ref, source, whole, sems):
+    load_planes((u1, o, d1), source, sems)
+    for k in range(8):
+        cols = slice(128 * k, 128 * k + 128)
+        whole[:, cols] = stencil_sum(weight_of(weights), source, 0, cols)
+    mapped = whole[8:40, :]
     mapped_ref[...] = mapped
     row_ref[...] = row_of(((3, mapped * mapped),))
 
 
+def further_kernel(place, weights, u2, u1, o, d1, d2, back_ref, source, middle, sems):
+    load_planes((u2, u1, o, d1, d2), source, sems)
+    apply_stencils(place, weights, source, middle, back_ref)
+
+
 def last_kernel(
-    place, weights, factor, table, o, u1, u2, d1, d2, image_back, loss_back, upstream, mapped_ref, out_ref, source, middle, back
+    place, weights, factor, table, image_back, loss_back, upstream, u2, u1, o, d1, d2, mapped_ref, out_ref, source, middle, sems, back
 ):
-    apply_stencils(place, weights, (o, u1, u2, d1, d2), source, middle, back)
+    load_planes((u2, u1, o, d1, d2), source, sems)
+    apply_stencils(place, weights, source, middle, back)
     mapped_ref[...] = middle[1, 1, 8:40, :]
     u, again = upstream[...], image_back[8:40, :]
     first = factor[0] * u + factor[1] * loss_back[8:40, :] + factor[4] * again + factor[5] * back[8:40, :]
@@ -420,35 +440,68 @@
     return jax.ShapeDtypeStruct(dims, F32)
 
 
-STENCIL_SCRATCH = (pltpu.VMEM((3, 5, FRAME, COLS), F32), pltpu.VMEM((3, 3, FRAME, COLS), F32))
+STENCIL_SCRATCH = (
+    pltpu.VMEM((3, 5, FRAME, COLS), F32),
+    pltpu.VMEM((3, 3, FRAME, COLS), F32),
+    pltpu.SemaphoreType.DMA((5,)),
+)
 BACK_SCRATCH = (pltpu.VMEM((FRAME, COLS), F32),)
 
 
-def call(body, out_shape, scalars, operands, scratch=(), flops=400_000_000):
-    smem, vmem = pl.BlockSpec(memory_space=pltpu.SMEM), pl.BlockSpec(memory_space=pltpu.VMEM)
+def call(body, out_shape, scalars, operands, scratch=(), far=(), far_out=(), planes=(), flops=400_000_000):
+    smem, vmem, hbm = (pl.BlockSpec(memory_space=m) for m in (pltpu.SMEM, pltpu.VMEM, pltpu.HBM))
+    outs = out_shape if isinstance(out_shape, tuple) else (out_shape,)
+    first, count = len(scalars), len(scalars) + len(operands) + len(planes)
+    buffers = [pltpu.VMEM(operands[i].shape, operands[i].dtype) for i in far]
+    buffers += [pltpu.VMEM(outs[i].shape, outs[i].dtype) for i in far_out]
+    extra = [*buffers, pltpu.SemaphoreType.DMA((len(buffers),))] if buffers else []
+
+    def whole(*refs):
+        ins, results = list(refs[:count]), list(refs[count : count + len(outs)])
+        own = refs[count + len(outs) :]
+        held, sems, own = own[: len(buffers)], own[len(buffers)] if buffers else None, own[len(extra) :]
+        copies = []
+        for k, i in enumerate(far):
+            copies.append(pltpu.make_async_copy(ins[first + i], held[k], sems.at[k]))
+            ins[first + i] = held[k]
+        for copy in copies:
+            copy.start()
+        for copy in copies:
+            copy.wait()
+        copies = []
+        for k, i in enumerate(far_out, len(far)):
+            copies.append(pltpu.make_async_copy(held[k], results[i], sems.at[k]))
+            results[i] = held[k]
+        body(*ins, *results, *own)
+        for copy in copies:
+            copy.start()
+        for copy in copies:
+            copy.wait()
+
+    spec_in = [smem] * len(scalars) + [hbm if i in far else vmem for i in range(len(operands))] + [hbm] * len(planes)
+    spec_out = tuple(hbm if i in far_out else vmem for i in range(len(outs)))
     return pl.pallas_call(
-        body,
+        whole,
         out_shape=out_shape,
-        in_specs=[smem] * len(scalars) + [vmem] * len(operands),
-        out_specs=jax.tree.map(lambda _: vmem, out_shape),
-        scratch_shapes=list(scratch),
+        in_specs=spec_in,
+        out_specs=spec_out if isinstance(out_shape, tuple) else spec_out[0],
+        scratch_shapes=[*extra, *scratch],
         compiler_params=pltpu.CompilerParams(vmem_limit_bytes=VMEM),
         cost_estimate=pl.CostEstimate(flops=flops, bytes_accessed=4_000_000, transcendentals=0),
-    )(*scalars, *operands)
+    )(*scalars, *operands, *planes)
 
 
 def exchange(value):
     return lax.all_to_all(value, GY, 0, 0, tiled=True)
 
 
+def moved(value, by):
+    size = lax.axis_size(GZ)
+    return lax.ppermute(value, GZ, [(i, i + by) for i in range(size) if 0 <= i + by < size])
+
+
 def neighbours(value):
-    size = lax.axis_size(GZ)
-
-    def moved(by):
-        pairs = [(i, i + by) for i in range(size) if 0 <= i + by < size]
-        return lax.ppermute(value, GZ, pairs)
-
-    return value, moved(1), moved(2), moved(-1), moved(-2)
+    return moved(value, 2), moved(value, 1), value, moved(value, -1), moved(value, -2)
 
 
 def with_rows(value):
@@ -458,9 +511,18 @@
     return jnp.concatenate([below, value, above], 0)
 
 
-def from_all(row, axis):
-    size = lax.axis_size(axis)
-    return lax.all_to_all(jnp.broadcast_to(row[None], (size, 1, 128)), axis, 0, 0, tiled=True)
+def from_all(row):
+    size = lax.axis_size(GZ)
+    return lax.all_to_all(jnp.broadcast_to(row[None], (size, 8, 128)), GZ, 0, 0, tiled=True)
+
+
+def over_planes(row):
+    size = lax.axis_size(GZ)
+    bit = 1
+    while bit < size:
+        row = row + lax.ppermute(row, GZ, [(i, i ^ bit) for i in range(size)])
+        bit *= 2
+    return row
 
 
 def factors(m0, m1, m2, m3, u0, u1):
@@ -478,7 +540,7 @@
 
 
 def factors_kernel(rows, filter_ref, stencil_ref):
-    total = jnp.sum(rows[...], 0)
+    total = jnp.sum(rows[:, 0, :], 0, keepdims=True)
     lane = lanes((1, 128))
     moments = [jnp.sum(jnp.where(lane == k, total, 0.0), axis=1, keepdims=True) for k in range(6)]
     alpha, gamma, g0, g1, g2, g3 = factors(*moments)
@@ -499,71 +561,87 @@
     tile, tiles, three = shape(32, 8, 128), shape(32, 16, 128), shape(32, 24, 128)
     spectral, frame, rows, row = shape(32 * BLOCKS, 128), shape(FRAME, COLS), shape(ROWS, COLS), shape(1, 128)
 
-    first = exchange(call(spread_kernel, tiles, [], [table, measured, point_spread]))
+    first = exchange(call(spread_kernel, tiles, [], [table, measured, point_spread], far=(1, 2), far_out=(0,)))
     first, grown = lax.optimization_barrier((first, with_rows(upstream)))
 
     right_out, bank = call(
-        first_filter_kernel, (three, shape(4, 32 * BLOCKS, 128)), [is_first], [along_y, first]
+        first_filter_kernel, (three, shape(4, 32 * BLOCKS, 128)), [is_first], [along_y, first], far_out=(0, 1)
     )
     right_arrived = exchange(right_out)
     loss_parts = neighbours(grown)
-    loss_back, loss_map = call(loss_kernel, (frame, rows), [place, weights], [*loss_parts], STENCIL_SCRATCH)
+    loss_back, loss_map = call(
+        loss_kernel, (frame, rows), [place, weights], [], STENCIL_SCRATCH, far_out=(0, 1), planes=loss_parts
+    )
     right_arrived, loss_back = lax.optimization_barrier((right_arrived, loss_back))
-    right, blurred = call(gather_two_kernel, (frame, frame), [], [table, right_arrived])
+    right, blurred = call(gather_two_kernel, (frame, frame), [], [table, right_arrived], far_out=(0, 1))
 
     right_parts = neighbours(right)
     image, right_map, image_send, row_b = call(
         image_kernel,
         (frame, rows, tile, row),
         [place, weights],
-        [table, *right_parts, blurred, upstream],
+        [table, blurred, upstream],
         STENCIL_SCRATCH + BACK_SCRATCH,
+        far=(1, 2),
+        far_out=(0, 1, 2, 3),
+        planes=right_parts,
     )
     image_arrived = exchange(image_send)
-    image_parts = neighbours(image)
-    image_back, image_map, row_ab = call(
-        further_kernel, (frame, rows, row), [place, weights], [*image_parts], STENCIL_SCRATCH
-    )
-    image_arrived, image_back = lax.optimization_barrier((image_arrived, image_back))
+    image_near = (moved(image, 1), image, moved(image, -1))
+    map_scratch = (pltpu.VMEM((3, 3, FRAME, COLS), F32), pltpu.VMEM((FRAME, COLS), F32), pltpu.SemaphoreType.DMA((3,)))
+    image_map, row_ab = call(map_kernel, (rows, row), [weights], [], map_scratch, far_out=(0, 1), planes=image_near)
     further_out, image_spectrum = call(
         second_filter_kernel,
         (tiles, spectral),
         [is_first],
         [along_y, image_arrived, bank, row_b, row_ab],
-    )
-    further, row_sum = call(gather_sum_kernel, (frame, row), [], [table, exchange(further_out), image_back])
-    moments = from_all(row_sum, GZ)
-    further, moments = lax.optimization_barrier((further, moments))
+        far=(2, 3, 4),
+        far_out=(0, 1),
+    )
+    further_out, image_again = lax.optimization_barrier((further_out, image))
+    further_arrived = exchange(further_out)
+    image_parts = (moved(image_again, 2), *image_near, moved(image_again, -2))
+    image_back = call(further_kernel, frame, [place, weights], [], STENCIL_SCRATCH, far_out=(0,), planes=image_parts)
+    further_arrived, image_back = lax.optimization_barrier((further_arrived, image_back))
+
+    further, row_sum = call(
+        gather_sum_kernel, (frame, row), [], [table, further_arrived, image_back], far=(2,), far_out=(0,)
+    )
     smem = pl.BlockSpec(memory_space=pltpu.SMEM)
     filter_factors, stencil_factors = pl.pallas_call(
         factors_kernel,
         out_shape=(shape(6), shape(5)),
         in_specs=[pl.BlockSpec(memory_space=pltpu.VMEM)],
         out_specs=(smem, smem),
-    )(moments)
+    )(from_all(row_sum))
 
     further_parts = neighbours(further)
     further_map, last_send = call(
         last_kernel,
         (rows, tiles),
         [place, weights, filter_factors],
-        [table, *further_parts, image_back, loss_back, upstream],
+        [table, image_back, loss_back, upstream],
         STENCIL_SCRATCH + BACK_SCRATCH,
+        far=(1, 2, 3),
+        far_out=(0, 1),
+        planes=further_parts,
     )
     last_arrived = exchange(last_send)
 
     operands = []
     for parts in (right_parts, image_parts, further_parts, loss_parts):
-        operands += [parts[1], parts[0], parts[3]]
+        operands += parts[1:4]
     operands += [right_map, image_map, further_map, loss_map]
     scratch = (pltpu.VMEM((3, FRAME, COLS), F32), pltpu.VMEM((3, ROWS, COLS), F32))
-    terms = call(correlate_kernel, row, [stencil_factors], operands, scratch)
-    terms = lax.psum(lax.psum(terms, "gz_1"), "gz_0")
+    terms = call(correlate_kernel, row, [stencil_factors], operands, scratch, far=tuple(range(16)), far_out=(0,))
+    terms = over_planes(terms)
     result_out = call(
         last_filter_kernel,
         tiles,
         [is_first, filter_factors],
         [along_y, last_arrived, bank, image_spectrum, terms],
+        far=(2, 3, 4),
+        far_out=(0,),
     )
     grad_measured, terms = call(final_kernel, (rows, row), [], [table, exchange(result_out)])
     grad_stencil = terms[0, :27].reshape(3, 3, 3) / math.sqrt(cells)
@@ -571,11 +649,9 @@
 
 
 def solution(mesh):
-    groups, planes = mesh.devices.shape
-    finer = Mesh(mesh.devices.reshape(groups // 2, 2, 4, planes // 4), GY + GZ)
     return jax.shard_map(
         local,
-        mesh=finer,
+        mesh=mesh,
         in_specs=(P(GZ, GY, None), P(GY, None), P(), P(GZ, GY, None)),
         out_specs=(P(GZ, GY, None), P()),
         check_vma=False,

time: 304 us -> 314 us (1.033)
  blocking collectives: 108 us -> 54.7 us
  starting transfers between devices: 93.3 us -> 128 us
  Pallas kernels: 29.6 us -> 64.2 us
  local copies, waits for them, and re-layouts: 31.3 us -> 9.09 us
  waiting for transfers between devices: 39 us -> 52.5 us
    pallas_call x12 -> x13, Pallas kernels: 28.2 us -> 62.7 us  [call(): pl.pallas_call(whole, out_shape=out_shape, in_specs=spec_in, out_specs=sp...]
    all_to_all x2 -> x1, blocking collectives: 72.2 us -> 38.2 us  [exchange(): return lax.all_to_all(value, GY, 0, 0, tiled=True)]
    unnamed x94 -> x50, local copies, waits for them, and re-layouts: 30.5 us -> 7.07 us
    all_to_all x4 -> x5, starting transfers between devices: 35.5 us -> 57 us  [exchange(): return lax.all_to_all(value, GY, 0, 0, tiled=True)]
    psum x2 -> x0, blocking collectives: 16.9 us -> none  [local(): terms = lax.psum(lax.psum(terms, 'gz_1'), 'gz_0')]
    ppermute x16 -> x20, starting transfers between devices: 52.3 us -> 65.6 us  [the longest x16 55.6 us: moved(): lax.ppermute(value, GZ, [(i, i + by) for i in range(size) if 0 <= i + by...]
    ppermute x16 -> x20, waiting for transfers between devices: 15.6 us -> 24.5 us  [the longest x16 13.5 us: moved(): lax.ppermute(value, GZ, [(i, i + by) for i in range(size) if 0 <= i + by...]
    all_to_all x4 -> x5, waiting for transfers between devices: 15.7 us -> 20.4 us  [exchange(): return lax.all_to_all(value, GY, 0, 0, tiled=True)]
  transfers between devices with their start and end apart: 22 -> 27, of which waited for: 10 -> 16; matrix products, arithmetic and copies ran while one was open for 0% -> 1% of each run, Pallas kernels for 3% -> 6%
where the time goes in v4:
time: 314 us; the launch traced here: 312 us
  starting transfers between devices  128 us (41%)
  Pallas kernels  64.2 us (20%)
  blocking collectives  54.7 us (17%)
  waiting for transfers between devices  52.5 us (17%)
  local copies, waits for them, and re-layouts  9.09 us (3%)
    pallas_call x13, Pallas kernels, call(): pl.pallas_call(whole, out_shape=out_shape, in_specs=spec_in, out_specs=sp...  62.7 us
    all_to_all x5, starting transfers between devices, exchange(): return lax.all_to_all(value, GY, 0, 0, tiled=True)  57 us
    ppermute x16, starting transfers between devices, moved(): lax.ppermute(value, GZ, [(i, i + by) for i in range(size) if 0 <= i + by...  55.6 us
    all_to_all x1, blocking collectives, exchange(): return lax.all_to_all(value, GY, 0, 0, tiled=True)  38.2 us
    all_to_all x5, waiting for transfers between devices, exchange(): return lax.all_to_all(value, GY, 0, 0, tiled=True)  20.4 us
    all_to_all x1, blocking collectives, from_all(): lax.all_to_all(jnp.broadcast_to(row[None], (size, 8, 128)), GZ, 0, 0, til...  16.6 us
    ppermute x16, waiting for transfers between devices, moved(): lax.ppermute(value, GZ, [(i, i + by) for i in range(size) if 0 <= i + by...  13.5 us
    ppermute x4, waiting for transfers between devices, over_planes(): row = row + lax.ppermute(row, GZ, [(i, i ^ bit) for i in range(size)])  11 us
  transfers between devices with their start and end apart: 27, of which 16 were waited for; matrix products, arithmetic and copies ran while one was open for 1% of the time, Pallas kernels for 6%

profile of v4, /device:TPU:1, one launch (start us, length us, event | category | flops | bytes accessed | tf_op | source)
XLA Modules:
  0.0 312.3 jit_solution(11374239834808909807)
XLA Ops:
  0.6 5.3 %shard_map.77 = f32[32,16,128]{2,1,0:T(8,128)} custom-call(bf16[2048,512]{1,0:T(8,128)(2,1)} %constant.24.clone.refs_0_.refs_2_.refs_3_, f32[32,1024]{1,0:T(8,128)} %bitcast.14, f32[32,1024]{1,0:T(8,128)} %refs_2_.3), custom_call_target="tpu_custom_call" | custom-call | flops 400000000 | bytes 4000000 | tf_op jit(solution)/shard_map/pallas_call | solution.py:483
  6.0 16.8 %all-to-all-start = ((f32[32,16,128]{2,1,0:T(8,128)}), f32[32,16,128]{2,1,0:T(8,128)S(1)}, u32[]{:S(2)}, u32[]{:S(2)}) async-start(f32[32,16,128]{2,1,0:T(8,128)} %shard_map.77), calls=%async_computation | async-start | bytes 524288 | tf_op jit(solution)/shard_map/all_to_all | solution.py:495
  22.8 3.5 %collective-permute-start = (f32[8,1024]{1,0:T(8,128)S(1)}, f32[8,1024]{1,0:T(8,128)S(1)}, u32[]{:S(2)}, u32[]{:S(2)}) collective-permute-start(f32[8,1024]{1,0:T(8,128)S(1)} %get-tuple-element.62), channel_id=1, source_target_pairs={{0,16},{16,32},{32,48},{48,64},{64,80},{80,96},{96,112},{112,128},... | collective-permute-start | bytes 98312 | tf_op jit(solution)/shard_map/ppermute | solution.py:509
  26.3 1.9 collective-permute-start.1
  28.2 1.5 collective-permute-done
  29.7 6.2 %collective-permute-done.1 = f32[8,1024]{1,0:T(8,128)S(1)} collective-permute-done((f32[8,1024]{1,0:T(8,128)S(1)}, f32[8,1024]{1,0:T(8,128)S(1)}, u32[]{:S(2)}, u32[]{:S(2)}) %collective-permute-start.1) | collective-permute-done | bytes 32800 | tf_op jit(solution)/shard_map/ppermute | solution.py:510
  35.9 8.6 %all-to-all-done.refs_2_ = f32[32,16,128]{2,1,0:T(8,128)S(1)} async-done(((f32[32,16,128]{2,1,0:T(8,128)}), f32[32,16,128]{2,1,0:T(8,128)S(1)}, u32[]{:S(2)}, u32[]{:S(2)}) %all-to-all-start) | async-done | bytes 262176 | tf_op jit(solution)/shard_map/all_to_all | solution.py:495
  45.2 4.2 %shard_map.78 = (f32[32,24,128]{2,1,0:T(8,128)}, f32[4,288,128]{2,1,0:T(8,128)}) custom-call(f32[1]{0:T(128)} %bitcast.refs_0_, f32[704,128]{1,0:T(8,128)} %constant.25.clone.refs_1_.refs_2_, f32[32,16,128]{2,1,0:T(8,128)} %copy-done.9), custom_call_target="tpu_custom_call" | custom-call | flops 400000000 | bytes 4000000 | tf_op jit(solution)/shard_map/pallas_call | solution.py:483
  49.5 4.9 %all-to-all-start.1 = ((f32[32,24,128]{2,1,0:T(8,128)}), f32[32,24,128]{2,1,0:T(8,128)S(1)}, u32[]{:S(2)}, u32[]{:S(2)}) async-start(f32[32,24,128]{2,1,0:T(8,128)} %get-tuple-element.33), calls=%async_computation.1 | async-start | bytes 786432 | tf_op jit(solution)/shard_map/all_to_all | solution.py:495
  57.0 4.0 %collective-permute-start.3 = (f32[48,1024]{1,0:T(8,128)S(1)}, f32[48,1024]{1,0:T(8,128)S(1)}, u32[]{:S(2)}, u32[]{:S(2)}) collective-permute-start(f32[48,1024]{1,0:T(8,128)S(1)} %pad_maximum_fusion.refs_4_.refs_11_), channel_id=1, source_target_pairs={{0,1},{1,2},{2,3},{3,4},{4,5},{5,6},{6,7},{7,8},{8,9},{9,10},{10,1... | collective-permute-start | bytes 589832 | tf_op jit(solution)/shard_map/ppermute | solution.py:500
  61.0 5.9 %collective-permute-start.2 = (f32[48,1024]{1,0:T(8,128)S(1)}, f32[48,1024]{1,0:T(8,128)S(1)}, u32[]{:S(2)}, u32[]{:S(2)}) collective-permute-start(f32[48,1024]{1,0:T(8,128)S(1)} %pad_maximum_fusion.refs_4_.refs_11_), channel_id=1, source_target_pairs={{0,2},{1,3},{2,4},{3,5},{4,6},{5,7},{6,8},{7,9},{8,10},{9,11},{10,... | collective-permute-start | bytes 589832 | tf_op jit(solution)/shard_map/ppermute | solution.py:500
  68.2 2.0 collective-permute-done.2.refs_2_
  70.8 4.9 %shard_map.79 = (f32[48,1024]{1,0:T(8,128)}, f32[32,1024]{1,0:T(8,128)}) custom-call(s32[3]{0:T(128)} %pad_add_fusion.refs_0_, f32[27]{0:T(128)} %reshape.16.refs_1_.refs_0_, f32[48,1024]{1,0:T(8,128)} %copy-done.22, f32[48,1024]{1,0:T(8,128)} %copy-done.15, f32[48,1024]{1,0:T(8,128)} %copy-done.8, f32[48,1024]{1,0:T(8,128)} %copy-done.14, f32[48,1024]{1,0:T(8,128)} %copy-done.21), custom_call_target="tpu_custom_call" | custom-call | flops 400000000 | bytes 4000000 | tf_op jit(solution)/shard_map/pallas_call | solution.py:483
  75.7 6.7 %all-to-all-done.1.refs_1_ = f32[32,24,128]{2,1,0:T(8,128)S(1)} async-done(((f32[32,24,128]{2,1,0:T(8,128)}), f32[32,24,128]{2,1,0:T(8,128)S(1)}, u32[]{:S(2)}, u32[]{:S(2)}) %all-to-all-start.1) | async-done | bytes 393248 | tf_op jit(solution)/shard_map/all_to_all | solution.py:495
  83.2 3.2 %shard_map.80 = (f32[48,1024]{1,0:T(8,128)}, f32[48,1024]{1,0:T(8,128)}) custom-call(bf16[2048,512]{1,0:T(8,128)(2,1)} %constant.24.clone.refs_0_.refs_2_.refs_3_, f32[32,24,128]{2,1,0:T(8,128)} %copy-done.1), custom_call_target="tpu_custom_call" | custom-call | flops 400000000 | bytes 4000000 | tf_op jit(solution)/shard_map/pallas_call | solution.py:483
  89.0 4.0 %collective-permute-start.7 = (f32[48,1024]{1,0:T(8,128)}, f32[48,1024]{1,0:T(8,128)S(1)}, u32[]{:S(2)}, u32[]{:S(2)}) collective-permute-start(f32[48,1024]{1,0:T(8,128)} %get-tuple-element.38.refs_7_.refs_2_), channel_id=1, source_target_pairs={{0,1},{1,2},{2,3},{3,4},{4,5},{5,6},{6,7},{7,8},{8,9},{9,10},{10,1... | collective-permute-start | bytes 589832 | tf_op jit(solution)/shard_map/ppermute | solution.py:500
  93.0 5.9 %collective-permute-start.6 = (f32[48,1024]{1,0:T(8,128)}, f32[48,1024]{1,0:T(8,128)S(1)}, u32[]{:S(2)}, u32[]{:S(2)}) collective-permute-start(f32[48,1024]{1,0:T(8,128)} %get-tuple-element.38.refs_7_.refs_2_), channel_id=1, source_target_pairs={{0,2},{1,3},{2,4},{3,5},{4,6},{5,7},{6,8},{7,9},{8,10},{9,11},{10,... | collective-permute-start | bytes 589832 | tf_op jit(solution)/shard_map/ppermute | solution.py:500
  98.9 3.3 %collective-permute-done.6.refs_5_ = f32[48,1024]{1,0:T(8,128)S(1)} collective-permute-done((f32[48,1024]{1,0:T(8,128)}, f32[48,1024]{1,0:T(8,128)S(1)}, u32[]{:S(2)}, u32[]{:S(2)}) %collective-permute-start.6) | collective-permute-done | bytes 196640 | tf_op jit(solution)/shard_map/ppermute | solution.py:500
  102.9 7.7 %shard_map.81 = (f32[48,1024]{1,0:T(8,128)}, f32[32,1024]{1,0:T(8,128)}, f32[32,8,128]{2,1,0:T(8,128)}, f32[1,128]{1,0:T(1,128)}) custom-call(s32[3]{0:T(128)} %pad_add_fusion.refs_0_, f32[27]{0:T(128)} %reshape.16.refs_1_.refs_0_, bf16[2048,512]{1,0:T(8,128)(2,1)} %constant.24.clone.refs_0_.refs_2_.refs_3_, f32[48,1024]{1,0:T(8,128)} %get-tuple-element.37.refs_3_, ...), custom_call_target="tpu_custom_call" | custom-call | flops 400000000 | bytes 4000000 | tf_op jit(solution)/shard_map/pallas_call | solution.py:483
  110.6 10.4 %all-to-all-start.2 = ((f32[32,8,128]{2,1,0:T(8,128)}), f32[32,8,128]{2,1,0:T(8,128)S(1)}, u32[]{:S(2)}, u32[]{:S(2)}) async-start(f32[32,8,128]{2,1,0:T(8,128)} %get-tuple-element.39), calls=%async_computation.2 | async-start | bytes 262144 | tf_op jit(solution)/shard_map/all_to_all | solution.py:495
  122.4 6.0 %collective-permute-start.10 = (f32[48,1024]{1,0:T(8,128)}, f32[48,1024]{1,0:T(8,128)S(1)}, u32[]{:S(2)}, u32[]{:S(2)}) collective-permute-start(f32[48,1024]{1,0:T(8,128)} %get-tuple-element.46.refs_2_.refs_4_.refs_5_), channel_id=1, source_target_pairs={{0,1},{1,2},{2,3},{3,4},{4,5},{5,6},{6,7},{7,8},{8,9},{9,10},{10,1... | collective-permute-start | bytes 589832 | tf_op jit(solution)/shard_map/ppermute | solution.py:500
  128.3 3.2 %collective-permute-done.11.refs_3_.refs_5_.refs_6_ = f32[48,1024]{1,0:T(8,128)S(1)} collective-permute-done((f32[48,1024]{1,0:T(8,128)}, f32[48,1024]{1,0:T(8,128)S(1)}, u32[]{:S(2)}, u32[]{:S(2)}) %collective-permute-start.11) | collective-permute-done | bytes 196640 | tf_op jit(solution)/shard_map/ppermute | solution.py:500
  133.2 3.0 shard_map.82
  137.6 4.3 %shard_map.83 = (f32[32,16,128]{2,1,0:T(8,128)}, f32[288,128]{1,0:T(8,128)}) custom-call(f32[1]{0:T(128)} %bitcast.refs_0_, f32[704,128]{1,0:T(8,128)} %constant.25.clone.refs_1_.refs_2_, f32[32,8,128]{2,1,0:T(8,128)} %copy-done.19, f32[4,288,128]{2,1,0:T(8,128)} %get-tuple-element.40.refs_3_.refs_4_, f32[1,128]{1,0:T(1,128)} %get-tuple-element.41.refs_4_, ...), custom_call_target="tpu_custom_call" | custom-call | flops 400000000 | bytes 4000000 | tf_op jit(solution)/shard_map/pallas_call | solution.py:483
  141.9 12.2 %all-to-all-start.3 = ((f32[32,16,128]{2,1,0:T(8,128)}), f32[32,16,128]{2,1,0:T(8,128)S(1)}, u32[]{:S(2)}, u32[]{:S(2)}) async-start(f32[32,16,128]{2,1,0:T(8,128)} %get-tuple-element.45), calls=%async_computation.3 | async-start | bytes 524288 | tf_op jit(solution)/shard_map/all_to_all | solution.py:495
  155.3 6.8 %collective-permute-start.12 = (f32[48,1024]{1,0:T(8,128)S(1)}, f32[48,1024]{1,0:T(8,128)S(1)}, u32[]{:S(2)}, u32[]{:S(2)}) collective-permute-start(f32[48,1024]{1,0:T(8,128)S(1)} %copy-done.16), channel_id=1, source_target_pairs={{0,2},{1,3},{2,4},{3,5},{4,6},{5,7},{6,8},{7,9},{8,10},{9,11},{10,... | collective-permute-start | bytes 589832 | tf_op jit(solution)/shard_map/ppermute | solution.py:500
  162.1 3.2 %collective-permute-done.13.refs_6_ = f32[48,1024]{1,0:T(8,128)S(1)} collective-permute-done((f32[48,1024]{1,0:T(8,128)S(1)}, f32[48,1024]{1,0:T(8,128)S(1)}, u32[]{:S(2)}, u32[]{:S(2)}) %collective-permute-start.13) | collective-permute-done | bytes 196640 | tf_op jit(solution)/shard_map/ppermute | solution.py:500
  166.8 4.9 %shard_map.84.refs_2_.refs_4_ = f32[48,1024]{1,0:T(8,128)} custom-call(s32[3]{0:T(128)} %pad_add_fusion.refs_0_, f32[27]{0:T(128)} %reshape.16.refs_1_.refs_0_, f32[48,1024]{1,0:T(8,128)} %copy-done.24, f32[48,1024]{1,0:T(8,128)} %copy-done.18, f32[48,1024]{1,0:T(8,128)} %get-tuple-element.46.refs_2_.refs_4_.refs_5_, f32[48,1024]{1,0:T(8,128)} %copy-done.17, ...), custom_call_target="tpu_custom_call" | custom-call | flops 400000000 | bytes 4000000 | tf_op jit(solution)/shard_map/pallas_call | solution.py:483
  171.7 4.3 %all-to-all-done.3.refs_1_ = f32[32,16,128]{2,1,0:T(8,128)S(1)} async-done(((f32[32,16,128]{2,1,0:T(8,128)}), f32[32,16,128]{2,1,0:T(8,128)S(1)}, u32[]{:S(2)}, u32[]{:S(2)}) %all-to-all-start.3) | async-done | bytes 262176 | tf_op jit(solution)/shard_map/all_to_all | solution.py:495
  176.7 4.3 %shard_map.85 = (f32[48,1024]{1,0:T(8,128)}, f32[1,128]{1,0:T(1,128)}) custom-call(bf16[2048,512]{1,0:T(8,128)(2,1)} %constant.24.clone.refs_0_.refs_2_.refs_3_, f32[32,16,128]{2,1,0:T(8,128)} %copy-done.2, f32[48,1024]{1,0:T(8,128)} %shard_map.84.refs_2_.refs_4_), custom_call_target="tpu_custom_call" | custom-call | flops 400000000 | bytes 4000000 | tf_op jit(solution)/shard_map/pallas_call | solution.py:483
  183.7 4.6 %collective-permute-start.15 = (f32[48,1024]{1,0:T(8,128)}, f32[48,1024]{1,0:T(8,128)S(1)}, u32[]{:S(2)}, u32[]{:S(2)}) collective-permute-start(f32[48,1024]{1,0:T(8,128)} %get-tuple-element.52.refs_9_.refs_8_), channel_id=1, source_target_pairs={{0,1},{1,2},{2,3},{3,4},{4,5},{5,6},{6,7},{7,8},{8,9},{9,10},{10,1... | collective-permute-start | bytes 589832 | tf_op jit(solution)/shard_map/ppermute | solution.py:500
  188.3 8.2 %collective-permute-start.14 = (f32[48,1024]{1,0:T(8,128)}, f32[48,1024]{1,0:T(8,128)S(1)}, u32[]{:S(2)}, u32[]{:S(2)}) collective-permute-start(f32[48,1024]{1,0:T(8,128)} %get-tuple-element.52.refs_9_.refs_8_), channel_id=1, source_target_pairs={{0,2},{1,3},{2,4},{3,5},{4,6},{5,7},{6,8},{7,9},{8,10},{9,11},{10,... | collective-permute-start | bytes 589832 | tf_op jit(solution)/shard_map/ppermute | solution.py:500
  197.2 16.6 %all_to_all.35.rows = f32[16,8,128]{2,1,0:T(8,128)} all-to-all(f32[16,8,128]{2,1,0:T(8,128)S(1)} %broadcast_in_dim.12), channel_id=1, replica_groups=mesh['gy'=32,'gz'=16] {'gz'}, dimensions={0} | all-to-all | bytes 131072 | tf_op jit(solution)/shard_map/all_to_all | solution.py:516
  213.8 1.5 shard_map.86
  216.2 8.7 %shard_map.87 = (f32[32,1024]{1,0:T(8,128)}, f32[32,16,128]{2,1,0:T(8,128)}) custom-call(s32[3]{0:T(128)} %pad_add_fusion.refs_0_, f32[27]{0:T(128)} %reshape.16.refs_1_.refs_0_, f32[6]{0:T(128)} %get-tuple-element.50.refs_2_.refs_1_, bf16[2048,512]{1,0:T(8,128)(2,1)} %constant.24.clone.refs_0_.refs_2_.refs_3_, f32[48,1024]{1,0:T(8,128)} %shard_map.84.refs_2_.refs_4_, ...), custom_call_target="tpu_custom_call" | custom-call | flops 400000000 | bytes 4000000 | tf_op jit(solution)/shard_map/pallas_call | solution.py:483
  224.9 12.8 %all-to-all-start.5 = ((f32[32,16,128]{2,1,0:T(8,128)}), f32[32,16,128]{2,1,0:T(8,128)S(1)}, u32[]{:S(2)}, u32[]{:S(2)}) async-start(f32[32,16,128]{2,1,0:T(8,128)} %get-tuple-element.53), calls=%async_computation.5 | async-start | bytes 524288 | tf_op jit(solution)/shard_map/all_to_all | solution.py:495
  237.7 4.7 %shard_map.88 = f32[1,128]{1,0:T(1,128)} custom-call(f32[5]{0:T(128)} %get-tuple-element.55.refs_0_, f32[48,1024]{1,0:T(8,128)} %copy-done.5, f32[48,1024]{1,0:T(8,128)} %get-tuple-element.38.refs_7_.refs_2_, f32[48,1024]{1,0:T(8,128)} %copy-done.4, f32[48,1024]{1,0:T(8,128)} %copy-done.18, f32[48,1024]{1,0:T(8,128)} %get-tuple-element.46.refs_2_.refs_4_.refs_5_, ...), custom_call_target="tpu_custom_call" | custom-call | flops 400000000 | bytes 4000000 | tf_op jit(solution)/shard_map/pallas_call | solution.py:483
  242.5 2.2 collective-permute-start.18
  244.7 2.4 collective-permute-done.18
  247.7 2.9 collective-permute-start.19
  250.6 3.1 %collective-permute-done.19 = f32[1,128]{1,0:T(1,128)S(1)} collective-permute-done((f32[1,128]{1,0:T(1,128)S(1)}, f32[1,128]{1,0:T(1,128)S(1)}, u32[]{:S(2)}, u32[]{:S(2)}) %collective-permute-start.19) | collective-permute-done | bytes 544 | tf_op jit(solution)/shard_map/ppermute | solution.py:523
  253.8 2.1 collective-permute-start.20
  255.9 2.4 collective-permute-done.20
  258.4 2.8 collective-permute-start.21
  261.2 3.0 collective-permute-done.21
  265.4 4.6 %shard_map.89 = f32[32,16,128]{2,1,0:T(8,128)} custom-call(f32[1]{0:T(128)} %bitcast.refs_0_, f32[6]{0:T(128)} %get-tuple-element.50.refs_2_.refs_1_, f32[704,128]{1,0:T(8,128)} %constant.25.clone.refs_1_.refs_2_, f32[32,16,128]{2,1,0:T(8,128)} %copy-done.3, f32[4,288,128]{2,1,0:T(8,128)} %get-tuple-element.40.refs_3_.refs_4_, ...), custom_call_target="tpu_custom_call" | custom-call | flops 400000000 | bytes 4000000 | tf_op jit(solution)/shard_map/pallas_call | solution.py:483
  270.0 38.2 %all_to_all.36.refs_1_ = f32[32,16,128]{2,1,0:T(8,128)} all-to-all(f32[32,16,128]{2,1,0:T(8,128)} %shard_map.89), channel_id=1, replica_groups=mesh['gy'=32,'gz'=16] {'gy'}, dimensions={0} | all-to-all | bytes 524288 | tf_op jit(solution)/shard_map/all_to_all | solution.py:495
  308.1 2.8 shard_map.90
  (83 shorter events, 24.4 us)
Async XLA Ops:
  0.6 22.1 %copy-start = (f32[1,32,1024]{2,1,0:T(8,128)S(1)}, f32[1,32,1024]{2,1,0:T(8,128)}, u32[]{:S(2)}) copy-start(f32[1,32,1024]{2,1,0:T(8,128)} %param.9) | copy-start | bytes 393220
  5.9 60.9 %copy-start.20 = (f32[3,3,3]{2,1,0:T(4,128)S(1)}, f32[3,3,3]{2,1,0:T(4,128)}, u32[]{:S(2)}) copy-start(f32[3,3,3]{2,1,0:T(4,128)} %param.8) | copy-start | bytes 328
  6.0 38.6 %all-to-all-start = ((f32[32,16,128]{2,1,0:T(8,128)}), f32[32,16,128]{2,1,0:T(8,128)S(1)}, u32[]{:S(2)}, u32[]{:S(2)}) async-start(f32[32,16,128]{2,1,0:T(8,128)} %shard_map.77), calls=%async_computation | async-start | bytes 524288 | tf_op jit(solution)/shard_map/all_to_all | solution.py:495
  22.8 7.0 %collective-permute-start = (f32[8,1024]{1,0:T(8,128)S(1)}, f32[8,1024]{1,0:T(8,128)S(1)}, u32[]{:S(2)}, u32[]{:S(2)}) collective-permute-start(f32[8,1024]{1,0:T(8,128)S(1)} %get-tuple-element.62), channel_id=1, source_target_pairs={{0,16},{16,32},{32,48},{48,64},{64,80},{80,96},{96,112},{112,128},... | collective-permute-start | bytes 98312 | tf_op jit(solution)/shard_map/ppermute | solution.py:509
  26.3 9.6 %collective-permute-start.1 = (f32[8,1024]{1,0:T(8,128)S(1)}, f32[8,1024]{1,0:T(8,128)S(1)}, u32[]{:S(2)}, u32[]{:S(2)}) collective-permute-start(f32[8,1024]{1,0:T(8,128)S(1)} %get-tuple-element.63), channel_id=1, source_target_pairs={{16,0},{32,16},{48,32},{64,48},{80,64},{96,80},{112,96},{128,112},... | collective-permute-start | bytes 98312 | tf_op jit(solution)/shard_map/ppermute | solution.py:510
  35.9 34.2 %copy-start.8 = (f32[48,1024]{1,0:T(8,128)}, f32[48,1024]{1,0:T(8,128)S(1)}, u32[]{:S(2)}) copy-start(f32[48,1024]{1,0:T(8,128)S(1)} %pad_maximum_fusion.refs_4_.refs_11_) | copy-start | bytes 589828
  44.6 0.7 copy-start.9
  49.5 32.9 %all-to-all-start.1 = ((f32[32,24,128]{2,1,0:T(8,128)}), f32[32,24,128]{2,1,0:T(8,128)S(1)}, u32[]{:S(2)}, u32[]{:S(2)}) async-start(f32[32,24,128]{2,1,0:T(8,128)} %get-tuple-element.33), calls=%async_computation.1 | async-start | bytes 786432 | tf_op jit(solution)/shard_map/all_to_all | solution.py:495
  54.4 13.7 %collective-permute-start.5 = (f32[48,1024]{1,0:T(8,128)S(1)}, f32[48,1024]{1,0:T(8,128)S(1)}, u32[]{:S(2)}, u32[]{:S(2)}) collective-permute-start(f32[48,1024]{1,0:T(8,128)S(1)} %pad_maximum_fusion.refs_4_.refs_11_), channel_id=1, source_target_pairs={{2,0},{3,1},{4,2},{5,3},{6,4},{7,5},{8,6},{9,7},{10,8},{11,9},{12,... | collective-permute-start | bytes 589832 | tf_op jit(solution)/shard_map/ppermute | solution.py:500
  55.7 12.4 %collective-permute-start.4 = (f32[48,1024]{1,0:T(8,128)S(1)}, f32[48,1024]{1,0:T(8,128)S(1)}, u32[]{:S(2)}, u32[]{:S(2)}) collective-permute-start(f32[48,1024]{1,0:T(8,128)S(1)} %pad_maximum_fusion.refs_4_.refs_11_), channel_id=1, source_target_pairs={{1,0},{2,1},{3,2},{4,3},{5,4},{6,5},{7,6},{8,7},{9,8},{10,9},{11,1... | collective-permute-start | bytes 589832 | tf_op jit(solution)/shard_map/ppermute | solution.py:500
  57.0 11.2 %collective-permute-start.3 = (f32[48,1024]{1,0:T(8,128)S(1)}, f32[48,1024]{1,0:T(8,128)S(1)}, u32[]{:S(2)}, u32[]{:S(2)}) collective-permute-start(f32[48,1024]{1,0:T(8,128)S(1)} %pad_maximum_fusion.refs_4_.refs_11_), channel_id=1, source_target_pairs={{0,1},{1,2},{2,3},{3,4},{4,5},{5,6},{6,7},{7,8},{8,9},{9,10},{10,1... | collective-permute-start | bytes 589832 | tf_op jit(solution)/shard_map/ppermute | solution.py:500
  61.0 9.1 %collective-permute-start.2 = (f32[48,1024]{1,0:T(8,128)S(1)}, f32[48,1024]{1,0:T(8,128)S(1)}, u32[]{:S(2)}, u32[]{:S(2)}) collective-permute-start(f32[48,1024]{1,0:T(8,128)S(1)} %pad_maximum_fusion.refs_4_.refs_11_), channel_id=1, source_target_pairs={{0,2},{1,3},{2,4},{3,5},{4,6},{5,7},{6,8},{7,9},{8,10},{9,11},{10,... | collective-permute-start | bytes 589832 | tf_op jit(solution)/shard_map/ppermute | solution.py:500
  68.1 2.0 copy-start.21
  68.1 2.0 copy-start.14
  68.1 2.0 copy-start.15
  70.1 0.7 copy-start.22
  82.4 0.7 copy-start.1
  86.4 12.5 %collective-permute-start.9 = (f32[48,1024]{1,0:T(8,128)}, f32[48,1024]{1,0:T(8,128)S(1)}, u32[]{:S(2)}, u32[]{:S(2)}) collective-permute-start(f32[48,1024]{1,0:T(8,128)} %get-tuple-element.38.refs_7_.refs_2_), channel_id=1, source_target_pairs={{2,0},{3,1},{4,2},{5,3},{6,4},{7,5},{8,6},{9,7},{10,8},{11,9},{12,... | collective-permute-start | bytes 589832 | tf_op jit(solution)/shard_map/ppermute | solution.py:500
  87.7 11.2 %collective-permute-start.8 = (f32[48,1024]{1,0:T(8,128)}, f32[48,1024]{1,0:T(8,128)S(1)}, u32[]{:S(2)}, u32[]{:S(2)}) collective-permute-start(f32[48,1024]{1,0:T(8,128)} %get-tuple-element.38.refs_7_.refs_2_), channel_id=1, source_target_pairs={{1,0},{2,1},{3,2},{4,3},{5,4},{6,5},{7,6},{8,7},{9,8},{10,9},{11,1... | collective-permute-start | bytes 589832 | tf_op jit(solution)/shard_map/ppermute | solution.py:500
  89.0 9.9 %collective-permute-start.7 = (f32[48,1024]{1,0:T(8,128)}, f32[48,1024]{1,0:T(8,128)S(1)}, u32[]{:S(2)}, u32[]{:S(2)}) collective-permute-start(f32[48,1024]{1,0:T(8,128)} %get-tuple-element.38.refs_7_.refs_2_), channel_id=1, source_target_pairs={{0,1},{1,2},{2,3},{3,4},{4,5},{5,6},{6,7},{7,8},{8,9},{9,10},{10,1... | collective-permute-start | bytes 589832 | tf_op jit(solution)/shard_map/ppermute | solution.py:500
  93.0 9.2 %collective-permute-start.6 = (f32[48,1024]{1,0:T(8,128)}, f32[48,1024]{1,0:T(8,128)S(1)}, u32[]{:S(2)}, u32[]{:S(2)}) collective-permute-start(f32[48,1024]{1,0:T(8,128)} %get-tuple-element.38.refs_7_.refs_2_), channel_id=1, source_target_pairs={{0,2},{1,3},{2,4},{3,5},{4,6},{5,7},{6,8},{7,9},{8,10},{9,11},{10,... | collective-permute-start | bytes 589832 | tf_op jit(solution)/shard_map/ppermute | solution.py:500
  98.9 3.3 %copy-start.11 = (f32[48,1024]{1,0:T(8,128)}, f32[48,1024]{1,0:T(8,128)S(1)}, u32[]{:S(2)}) copy-start(f32[48,1024]{1,0:T(8,128)S(1)} %collective-permute-done.9.refs_9_) | copy-start | bytes 589828
  98.9 3.3 %copy-start.4 = (f32[48,1024]{1,0:T(8,128)}, f32[48,1024]{1,0:T(8,128)S(1)}, u32[]{:S(2)}) copy-start(f32[48,1024]{1,0:T(8,128)S(1)} %collective-permute-done.8.refs_8_.refs_3_) | copy-start | bytes 589828
  98.9 3.3 %copy-start.5 = (f32[48,1024]{1,0:T(8,128)}, f32[48,1024]{1,0:T(8,128)S(1)}, u32[]{:S(2)}) copy-start(f32[48,1024]{1,0:T(8,128)S(1)} %collective-permute-done.7.refs_6_.refs_1_) | copy-start | bytes 589828
  102.2 0.7 copy-start.13
  110.6 43.4 %copy-start.16 = (f32[48,1024]{1,0:T(8,128)S(1)}, f32[48,1024]{1,0:T(8,128)}, u32[]{:S(2)}) copy-start(f32[48,1024]{1,0:T(8,128)} %get-tuple-element.46.refs_2_.refs_4_.refs_5_) | copy-start | bytes 589828
  110.6 26.3 %all-to-all-start.2 = ((f32[32,8,128]{2,1,0:T(8,128)}), f32[32,8,128]{2,1,0:T(8,128)S(1)}, u32[]{:S(2)}, u32[]{:S(2)}) async-start(f32[32,8,128]{2,1,0:T(8,128)} %get-tuple-element.39), calls=%async_computation.2 | async-start | bytes 262144 | tf_op jit(solution)/shard_map/all_to_all | solution.py:495
  121.1 10.5 %collective-permute-start.11 = (f32[48,1024]{1,0:T(8,128)}, f32[48,1024]{1,0:T(8,128)S(1)}, u32[]{:S(2)}, u32[]{:S(2)}) collective-permute-start(f32[48,1024]{1,0:T(8,128)} %get-tuple-element.46.refs_2_.refs_4_.refs_5_), channel_id=1, source_target_pairs={{1,0},{2,1},{3,2},{4,3},{5,4},{6,5},{7,6},{8,7},{9,8},{10,9},{11,1... | collective-permute-start | bytes 589832 | tf_op jit(solution)/shard_map/ppermute | solution.py:500
  122.4 10.1 %collective-permute-start.10 = (f32[48,1024]{1,0:T(8,128)}, f32[48,1024]{1,0:T(8,128)S(1)}, u32[]{:S(2)}, u32[]{:S(2)}) collective-permute-start(f32[48,1024]{1,0:T(8,128)} %get-tuple-element.46.refs_2_.refs_4_.refs_5_), channel_id=1, source_target_pairs={{0,1},{1,2},{2,3},{3,4},{4,5},{5,6},{6,7},{7,8},{8,9},{9,10},{10,1... | collective-permute-start | bytes 589832 | tf_op jit(solution)/shard_map/ppermute | solution.py:500
  131.5 1.0 copy-start.17
  141.9 34.2 %all-to-all-start.3 = ((f32[32,16,128]{2,1,0:T(8,128)}), f32[32,16,128]{2,1,0:T(8,128)S(1)}, u32[]{:S(2)}, u32[]{:S(2)}) async-start(f32[32,16,128]{2,1,0:T(8,128)} %get-tuple-element.45), calls=%async_computation.3 | async-start | bytes 524288 | tf_op jit(solution)/shard_map/all_to_all | solution.py:495
  154.0 11.2 %collective-permute-start.13 = (f32[48,1024]{1,0:T(8,128)S(1)}, f32[48,1024]{1,0:T(8,128)S(1)}, u32[]{:S(2)}, u32[]{:S(2)}) collective-permute-start(f32[48,1024]{1,0:T(8,128)S(1)} %copy-done.16), channel_id=1, source_target_pairs={{2,0},{3,1},{4,2},{5,3},{6,4},{7,5},{8,6},{9,7},{10,8},{11,9},{12,... | collective-permute-start | bytes 589832 | tf_op jit(solution)/shard_map/ppermute | solution.py:500
  155.3 10.8 %collective-permute-start.12 = (f32[48,1024]{1,0:T(8,128)S(1)}, f32[48,1024]{1,0:T(8,128)S(1)}, u32[]{:S(2)}, u32[]{:S(2)}) collective-permute-start(f32[48,1024]{1,0:T(8,128)S(1)} %copy-done.16), channel_id=1, source_target_pairs={{0,2},{1,3},{2,4},{3,5},{4,6},{5,7},{6,8},{7,9},{8,10},{9,11},{10,... | collective-permute-start | bytes 589832 | tf_op jit(solution)/shard_map/ppermute | solution.py:500
  165.3 0.9 copy-start.23
  176.0 0.7 copy-start.2
  181.1 34.3 %collective-permute-start.17 = (f32[48,1024]{1,0:T(8,128)}, f32[48,1024]{1,0:T(8,128)S(1)}, u32[]{:S(2)}, u32[]{:S(2)}) collective-permute-start(f32[48,1024]{1,0:T(8,128)} %get-tuple-element.52.refs_9_.refs_8_), channel_id=1, source_target_pairs={{2,0},{3,1},{4,2},{5,3},{6,4},{7,5},{8,6},{9,7},{10,8},{11,9},{12,... | collective-permute-start | bytes 589832 | tf_op jit(solution)/shard_map/ppermute | solution.py:500
  182.4 33.0 %collective-permute-start.16 = (f32[48,1024]{1,0:T(8,128)}, f32[48,1024]{1,0:T(8,128)S(1)}, u32[]{:S(2)}, u32[]{:S(2)}) collective-permute-start(f32[48,1024]{1,0:T(8,128)} %get-tuple-element.52.refs_9_.refs_8_), channel_id=1, source_target_pairs={{1,0},{2,1},{3,2},{4,3},{5,4},{6,5},{7,6},{8,7},{9,8},{10,9},{11,1... | collective-permute-start | bytes 589832 | tf_op jit(solution)/shard_map/ppermute | solution.py:500
  183.7 31.7 %collective-permute-start.15 = (f32[48,1024]{1,0:T(8,128)}, f32[48,1024]{1,0:T(8,128)S(1)}, u32[]{:S(2)}, u32[]{:S(2)}) collective-permute-start(f32[48,1024]{1,0:T(8,128)} %get-tuple-element.52.refs_9_.refs_8_), channel_id=1, source_target_pairs={{0,1},{1,2},{2,3},{3,4},{4,5},{5,6},{6,7},{7,8},{8,9},{9,10},{10,1... | collective-permute-start | bytes 589832 | tf_op jit(solution)/shard_map/ppermute | solution.py:500
  188.3 27.1 %collective-permute-start.14 = (f32[48,1024]{1,0:T(8,128)}, f32[48,1024]{1,0:T(8,128)S(1)}, u32[]{:S(2)}, u32[]{:S(2)}) collective-permute-start(f32[48,1024]{1,0:T(8,128)} %get-tuple-element.52.refs_9_.refs_8_), channel_id=1, source_target_pairs={{0,2},{1,3},{2,4},{3,5},{4,6},{5,7},{6,8},{7,9},{8,10},{9,11},{10,... | collective-permute-start | bytes 589832 | tf_op jit(solution)/shard_map/ppermute | solution.py:500
  215.3 0.7 copy-start.6
  215.4 0.8 copy-start.7
  215.4 0.8 copy-start.12
  224.9 39.8 %all-to-all-start.5 = ((f32[32,16,128]{2,1,0:T(8,128)}), f32[32,16,128]{2,1,0:T(8,128)S(1)}, u32[]{:S(2)}, u32[]{:S(2)}) async-start(f32[32,16,128]{2,1,0:T(8,128)} %get-tuple-element.53), calls=%async_computation.5 | async-start | bytes 524288 | tf_op jit(solution)/shard_map/all_to_all | solution.py:495
  242.5 4.6 %collective-permute-start.18 = (f32[1,128]{1,0:T(1,128)}, f32[1,128]{1,0:T(1,128)S(1)}, u32[]{:S(2)}, u32[]{:S(2)}) collective-permute-start(f32[1,128]{1,0:T(1,128)} %shard_map.88), channel_id=1, source_target_pairs={{0,1},{1,0},{2,3},{3,2},{4,5},{5,4},{6,7},{7,6},{8,9},{9,8},{10,11... | collective-permute-start | bytes 1544 | tf_op jit(solution)/shard_map/ppermute | solution.py:523
  247.7 6.1 %collective-permute-start.19 = (f32[1,128]{1,0:T(1,128)S(1)}, f32[1,128]{1,0:T(1,128)S(1)}, u32[]{:S(2)}, u32[]{:S(2)}) collective-permute-start(f32[1,128]{1,0:T(1,128)S(1)} %add.12), channel_id=1, source_target_pairs={{0,2},{1,3},{2,0},{3,1},{4,6},{5,7},{6,4},{7,5},{8,10},{9,11},{10,... | collective-permute-start | bytes 1544 | tf_op jit(solution)/shard_map/ppermute | solution.py:523
  253.8 4.6 %collective-permute-start.20 = (f32[1,128]{1,0:T(1,128)S(1)}, f32[1,128]{1,0:T(1,128)S(1)}, u32[]{:S(2)}, u32[]{:S(2)}) collective-permute-start(f32[1,128]{1,0:T(1,128)S(1)} %add.13), channel_id=1, source_target_pairs={{0,4},{1,5},{2,6},{3,7},{4,0},{5,1},{6,2},{7,3},{8,12},{9,13},{10,... | collective-permute-start | bytes 1544 | tf_op jit(solution)/shard_map/ppermute | solution.py:523
  258.4 5.8 %collective-permute-start.21 = (f32[1,128]{1,0:T(1,128)S(1)}, f32[1,128]{1,0:T(1,128)S(1)}, u32[]{:S(2)}, u32[]{:S(2)}) collective-permute-start(f32[1,128]{1,0:T(1,128)S(1)} %add.14), channel_id=1, source_target_pairs={{0,8},{1,9},{2,10},{3,11},{4,12},{5,13},{6,14},{7,15},{8,0},{9,1},... | collective-permute-start | bytes 1544 | tf_op jit(solution)/shard_map/ppermute | solution.py:523
  264.7 0.7 copy-start.3
  (4 other events, 2.7 us)

commit v5 on v4

--- a/solution.py
+++ b/solution.py
@@ -18,7 +18,7 @@
 BLOCKS = 9
 F32 = jnp.float32
 BF16 = jnp.bfloat16
-VMEM = 60 * 1024 * 1024
+VMEM = 14 * 1024 * 1024
 
 
 def split_table(table):
@@ -134,7 +134,7 @@
 
 
 class Lateral:
-    def __init__(self, table, is_first):
+    def __init__(self, table):
         def piece(start, count, width):
             return table[start : start + count, 0:width].astype(BF16)
 
@@ -142,7 +142,7 @@
         self.back = (piece(256, 128, 128), piece(384, 128, 128))
         self.first = (piece(512, 64, 32), piece(576, 64, 32))
         self.cos, self.sin = table[640:672, :], table[672:704, :]
-        self.is_first = is_first
+        self.is_first = jnp.where(lax.axis_index(GY) == 0, 1.0, 0.0).astype(F32)
         self.sign = jnp.where(lanes((32, 128)) < 64, 1.0, -1.0)
 
     def over_s(self, blocks, direction):
@@ -197,19 +197,21 @@
     return real * value + imaginary * swap(value)
 
 
+def conjugate_factors(transfer):
+    turned, left = swap(transfer), lanes(transfer.shape) < 64
+    return jnp.where(left, transfer, turned), jnp.where(left, turned, -transfer)
+
+
 def spread_kernel(table_ref, measured, point_spread, out_ref):
     for f, ref in enumerate((measured, point_spread)):
         out_ref[:, 8 * f : 8 * f + 8, :] = x_forward(ref[...], table_ref).reshape(32, 8, 128)
 
 
-def first_filter_kernel(is_first_ref, table, arrived, out_ref, bank_ref):
-    lateral = Lateral(table, is_first_ref[0])
+def first_filter_kernel(table, arrived, out_ref, bank_ref):
+    lateral = Lateral(table)
     transfer = lateral.forward(arrived, 8)
     observed = lateral.forward(arrived, 0)
-    turned = swap(transfer)
-    left = lanes(transfer.shape) < 64
-    real = jnp.where(left, transfer, turned)
-    imaginary = jnp.where(left, turned, -transfer)
+    real, imaginary = conjugate_factors(transfer)
     power = real * real + imaginary * imaginary
     spectrum = product(real, imaginary, observed)
     right = lateral.inverse(spectrum)
@@ -221,14 +223,15 @@
         image_after, image_before = halo_rows(image[i])
         image_after, image_before = pltpu.roll(image_after, 8, 1), pltpu.roll(image_before, 120, 1)
         out_ref[:, 16 + i, :] = after + before + image_after + image_before
-    for k, value in enumerate((real, imaginary, power, spectrum)):
-        bank_ref[k] = value
-
-
-def second_filter_kernel(is_first_ref, table, arrived, bank_ref, row_b, row_ab, out_ref, image_ref):
-    lateral = Lateral(table, is_first_ref[0])
-    power = bank_ref[2]
-    image = power * bank_ref[3] + lateral.forward(arrived, 0)
+    bank_ref[0] = transfer
+    bank_ref[1] = spectrum
+
+
+def second_filter_kernel(table, arrived, bank_ref, sums, out_ref, image_ref):
+    lateral = Lateral(table)
+    real, imaginary = conjugate_factors(bank_ref[0])
+    power = real * real + imaginary * imaginary
+    image = power * bank_ref[1] + lateral.forward(arrived, 0)
     filtered = power * image
     blocks = lateral.inverse(filtered)
     for i in range(8):
@@ -236,21 +239,22 @@
         after, before = halo_rows(blocks[i])
         out_ref[:, 8 + i, :] = after + before
     image_ref[...] = image
-    row = row_b[...] + row_ab[...]
-    row = row + jnp.where(lanes((1, 128)) == 3, lateral.weighted_sum(image * filtered), 0.0)
+    row = sums[...] + jnp.where(lanes((1, 128)) == 3, lateral.weighted_sum(image * filtered), 0.0)
     out_ref[:, 8, :] = out_ref[:, 8, :] + pltpu.roll(jnp.broadcast_to(row, (32, 128)), 8, 1)
 
 
 def last_filter_kernel(
-    is_first_ref, factor_ref, table, arrived, bank_ref, image_ref, terms, out_ref
+    factors_ref, table, arrived, bank_ref, image_ref, terms, out_ref
 ):
-    lateral = Lateral(table, is_first_ref[0])
-    power = bank_ref[2]
+    lateral = Lateral(table)
+    factor_ref = [factors_ref[27 + k] for k in range(6)]
+    real, imaginary = conjugate_factors(bank_ref[0])
+    power = real * real + imaginary * imaginary
     image = image_ref[...]
     total = factor_ref[4] * image + factor_ref[5] * (power * image) + lateral.forward(arrived, 8)
-    total = power * total + factor_ref[2] * bank_ref[3] + factor_ref[3] * image
+    total = power * total + factor_ref[2] * bank_ref[1] + factor_ref[3] * image
     total = total + lateral.forward(arrived, 0)
-    blocks = lateral.inverse(product(bank_ref[0], -bank_ref[1], total))
+    blocks = lateral.inverse(product(real, -imaginary, total))
     for i in range(8):
         out_ref[:, i, :] = blocks[i]
         out_ref[:, 8 + i, :] = jnp.broadcast_to(terms[...], (32, 128))
@@ -305,18 +309,15 @@
     return total
 
 
-def load_planes(parts, source, sems):
-    copies = [pltpu.make_async_copy(ref, source.at[1, p], sems.at[p]) for p, ref in enumerate(parts)]
-    for copy in copies:
-        copy.start()
-    for copy in copies:
-        copy.wait()
-    for p in range(len(parts)):
-        source[0, p], source[2, p] = shifted_columns(source[1, p])
-
-
-def row_bounds(place_ref):
-    device, plane, planes = place_ref[0], place_ref[1], place_ref[2]
+def load_planes(parts, source):
+    for p, ref in enumerate(parts):
+        value = ref[...]
+        source[1, p] = value
+        source[0, p], source[2, p] = shifted_columns(value)
+
+
+def row_bounds():
+    device, plane, planes = lax.axis_index(GY), lax.axis_index(GZ), lax.axis_size(GZ)
     lowest = jnp.where(device > 0, 0, 8)
     highest = jnp.where(device < 31, FRAME, 40)
 
@@ -334,8 +335,8 @@
     return lambda a, b, c: weights_ref[26 - 9 * a - 3 * b - c]
 
 
-def apply_stencils(place_ref, weights_ref, source, middle, back_ref):
-    row, lowest, highest, highest_at = row_bounds(place_ref)
+def apply_stencils(weights_ref, source, middle, back_ref):
+    row, lowest, highest, highest_at = row_bounds()
     for p in range(3):
         valid = (row >= lowest) & (row < highest_at(p - 1))
         for k in range(8):
@@ -358,10 +359,10 @@
     return out
 
 
-def image_kernel(place, weights, table, blurred, upstream, u2, u1, o, d1, d2, image_ref, mapped_ref, out_ref, row_ref, *scratch):
-    source, middle, sems, back = scratch
-    load_planes((u2, u1, o, d1, d2), source, sems)
-    apply_stencils(place, weights, source, middle, back)
+def image_kernel(weights, table, blurred, upstream, u2, u1, o, d1, d2, image_ref, mapped_ref, out_ref, row_ref, *scratch):
+    source, middle, back = scratch
+    load_planes((u2, u1, o, d1, d2), source)
+    apply_stencils(weights, source, middle, back)
     out_ref[...] = x_forward(back[8:40, :], table).reshape(32, 8, 128)
     mapped_ref[...] = middle[1, 1, 8:40, :]
     image_ref[...] = blurred[...] + back[...]
@@ -369,33 +370,34 @@
     row_ref[...] = row_of(((0, b * b), (1, b * ab), (2, ab * ab), (4, u * b), (5, u * ab)))
 
 
-def loss_kernel(place, weights, u2, u1, o, d1, d2, back_ref, mapped_ref, source, middle, sems):
-    load_planes((u2, u1, o, d1, d2), source, sems)
-    apply_stencils(place, weights, source, middle, back_ref)
+def loss_kernel(weights, u2, u1, o, d1, d2, back_ref, mapped_ref, source, middle):
+    load_planes((u2, u1, o, d1, d2), source)
+    apply_stencils(weights, source, middle, back_ref)
     mapped_ref[...] = middle[1, 1, 8:40, :]
 
 
-def map_kernel(weights, u1, o, d1, mapped_ref, row_ref, source, whole, sems):
-    load_planes((u1, o, d1), source, sems)
+def map_kernel(weights, row_b, u1, o, d1, mapped_ref, row_ref, source, whole):
+    load_planes((u1, o, d1), source)
     for k in range(8):
         cols = slice(128 * k, 128 * k + 128)
         whole[:, cols] = stencil_sum(weight_of(weights), source, 0, cols)
     mapped = whole[8:40, :]
     mapped_ref[...] = mapped
-    row_ref[...] = row_of(((3, mapped * mapped),))
-
-
-def further_kernel(place, weights, u2, u1, o, d1, d2, back_ref, source, middle, sems):
-    load_planes((u2, u1, o, d1, d2), source, sems)
-    apply_stencils(place, weights, source, middle, back_ref)
+    row_ref[...] = row_b[...] + row_of(((3, mapped * mapped),))
+
+
+def further_kernel(weights, u2, u1, o, d1, d2, back_ref, source, middle):
+    load_planes((u2, u1, o, d1, d2), source)
+    apply_stencils(weights, source, middle, back_ref)
 
 
 def last_kernel(
-    place, weights, factor, table, image_back, loss_back, upstream, u2, u1, o, d1, d2, mapped_ref, out_ref, source, middle, sems, back
+    weights, table, image_back, loss_back, upstream, u2, u1, o, d1, d2, mapped_ref, out_ref, source, middle, back
 ):
-    load_planes((u2, u1, o, d1, d2), source, sems)
-    apply_stencils(place, weights, source, middle, back)
+    load_planes((u2, u1, o, d1, d2), source)
+    apply_stencils(weights, source, middle, back)
     mapped_ref[...] = middle[1, 1, 8:40, :]
+    factor = [weights[27 + k] for k in range(6)]
     u, again = upstream[...], image_back[8:40, :]
     first = factor[0] * u + factor[1] * loss_back[8:40, :] + factor[4] * again + factor[5] * back[8:40, :]
     second = factor[1] * u + factor[5] * again
@@ -407,7 +409,7 @@
     out_ref, scaled, mapped = refs[-3:]
     right, image, further, upstream = refs[0:3], refs[3:6], refs[6:9], refs[9:12]
     right_map, image_map, further_map, upstream_map = refs[12:16]
-    f = [factor_ref[k] for k in range(5)]
+    f = [factor_ref[33 + k] for k in range(5)]
     for p in range(3):
         scaled[p] = f[0] * upstream[p][...] + f[1] * right[p][...] + f[2] * image[p][...] + f[3] * further[p][...]
     mapped[0] = (
@@ -443,17 +445,16 @@
 STENCIL_SCRATCH = (
     pltpu.VMEM((3, 5, FRAME, COLS), F32),
     pltpu.VMEM((3, 3, FRAME, COLS), F32),
-    pltpu.SemaphoreType.DMA((5,)),
 )
 BACK_SCRATCH = (pltpu.VMEM((FRAME, COLS), F32),)
 
 
-def call(body, out_shape, scalars, operands, scratch=(), far=(), far_out=(), planes=(), flops=400_000_000):
+def call(body, out_shape, scalars, operands, scratch=(), far=(), planes=(), flops=400_000_000):
+    operands = [*operands, *planes]
     smem, vmem, hbm = (pl.BlockSpec(memory_space=m) for m in (pltpu.SMEM, pltpu.VMEM, pltpu.HBM))
     outs = out_shape if isinstance(out_shape, tuple) else (out_shape,)
-    first, count = len(scalars), len(scalars) + len(operands) + len(planes)
+    first, count = len(scalars), len(scalars) + len(operands)
     buffers = [pltpu.VMEM(operands[i].shape, operands[i].dtype) for i in far]
-    buffers += [pltpu.VMEM(outs[i].shape, outs[i].dtype) for i in far_out]
     extra = [*buffers, pltpu.SemaphoreType.DMA((len(buffers),))] if buffers else []
 
     def whole(*refs):
@@ -468,18 +469,10 @@
             copy.start()
         for copy in copies:
             copy.wait()
-        copies = []
-        for k, i in enumerate(far_out, len(far)):
-            copies.append(pltpu.make_async_copy(held[k], results[i], sems.at[k]))
-            results[i] = held[k]
         body(*ins, *results, *own)
-        for copy in copies:
-            copy.start()
-        for copy in copies:
-            copy.wait()
-
-    spec_in = [smem] * len(scalars) + [hbm if i in far else vmem for i in range(len(operands))] + [hbm] * len(planes)
-    spec_out = tuple(hbm if i in far_out else vmem for i in range(len(outs)))
+
+    spec_in = [smem] * len(scalars) + [hbm if i in far else vmem for i in range(len(operands))]
+    spec_out = (vmem,) * len(outs)
     return pl.pallas_call(
         whole,
         out_shape=out_shape,
@@ -488,7 +481,7 @@
         scratch_shapes=[*extra, *scratch],
         compiler_params=pltpu.CompilerParams(vmem_limit_bytes=VMEM),
         cost_estimate=pl.CostEstimate(flops=flops, bytes_accessed=4_000_000, transcendentals=0),
-    )(*scalars, *operands, *planes)
+    )(*scalars, *operands)
 
 
 def exchange(value):
@@ -516,16 +509,7 @@
     return lax.all_to_all(jnp.broadcast_to(row[None], (size, 8, 128)), GZ, 0, 0, tiled=True)
 
 
-def over_planes(row):
-    size = lax.axis_size(GZ)
-    bit = 1
-    while bit < size:
-        row = row + lax.ppermute(row, GZ, [(i, i ^ bit) for i in range(size)])
-        bit *= 2
-    return row
-
-
-def factors(m0, m1, m2, m3, u0, u1):
+def factors_of(m0, m1, m2, m3, u0, u1):
     def pair(m0, m1, m2, m3):
         step0 = m0 / m1
         norm1 = m0 - 2.0 * step0 * m1 + step0 * step0 * m2
@@ -539,91 +523,75 @@
     return (alpha, gamma, *back((u0, u1)))
 
 
-def factors_kernel(rows, filter_ref, stencil_ref):
+def factors_kernel(weights_ref, rows, out_ref):
     total = jnp.sum(rows[:, 0, :], 0, keepdims=True)
     lane = lanes((1, 128))
     moments = [jnp.sum(jnp.where(lane == k, total, 0.0), axis=1, keepdims=True) for k in range(6)]
-    alpha, gamma, g0, g1, g2, g3 = factors(*moments)
-    for k, value in enumerate((alpha, gamma, 2.0 * g0, 2.0 * g1, 2.0 * g2, 2.0 * g3)):
-        filter_ref[k] = value[0, 0]
-    for k, value in enumerate((gamma, g1, 2.0 * g2, 2.0 * g3, 2.0 * g3)):
-        stencil_ref[k] = value[0, 0]
+    alpha, gamma, g0, g1, g2, g3 = factors_of(*moments)
+    for k in range(27):
+        out_ref[k] = weights_ref[k]
+    values = (alpha, gamma, 2.0 * g0, 2.0 * g1, 2.0 * g2, 2.0 * g3, gamma, g1, 2.0 * g2, 2.0 * g3, 2.0 * g3)
+    for k, value in enumerate(values):
+        out_ref[27 + k] = value[0, 0]
 
 
 def local(measured, point_spread, stencil_weights, upstream):
     cells = measured.size * lax.axis_size(GY) * lax.axis_size(GZ)
-    device, plane = lax.axis_index(GY), lax.axis_index(GZ)
-    is_first = jnp.where(device == 0, 1.0, 0.0).astype(F32).reshape(1)
-    place = jnp.stack([device, plane, jnp.int32(lax.axis_size(GZ))]).astype(jnp.int32)
     weights = stencil_weights.reshape(27)
     table, along_y = jnp.asarray(X_TABLE), jnp.asarray(Y_TABLE)
     measured, upstream = measured[0], upstream[0]
     tile, tiles, three = shape(32, 8, 128), shape(32, 16, 128), shape(32, 24, 128)
     spectral, frame, rows, row = shape(32 * BLOCKS, 128), shape(FRAME, COLS), shape(ROWS, COLS), shape(1, 128)
 
-    first = exchange(call(spread_kernel, tiles, [], [table, measured, point_spread], far=(1, 2), far_out=(0,)))
+    first = exchange(call(spread_kernel, tiles, [], [table, measured, point_spread], far=(0, 1, 2)))
     first, grown = lax.optimization_barrier((first, with_rows(upstream)))
 
-    right_out, bank = call(
-        first_filter_kernel, (three, shape(4, 32 * BLOCKS, 128)), [is_first], [along_y, first], far_out=(0, 1)
-    )
+    right_out, bank = call(first_filter_kernel, (three, shape(2, 32 * BLOCKS, 128)), [], [along_y, first])
     right_arrived = exchange(right_out)
     loss_parts = neighbours(grown)
-    loss_back, loss_map = call(
-        loss_kernel, (frame, rows), [place, weights], [], STENCIL_SCRATCH, far_out=(0, 1), planes=loss_parts
-    )
-    right_arrived, loss_back = lax.optimization_barrier((right_arrived, loss_back))
-    right, blurred = call(gather_two_kernel, (frame, frame), [], [table, right_arrived], far_out=(0, 1))
+    right_arrived, loss_parts = lax.optimization_barrier((right_arrived, loss_parts))
+    right, blurred = call(gather_two_kernel, (frame, frame), [], [table, right_arrived])
 
     right_parts = neighbours(right)
     image, right_map, image_send, row_b = call(
         image_kernel,
         (frame, rows, tile, row),
-        [place, weights],
+        [weights],
         [table, blurred, upstream],
         STENCIL_SCRATCH + BACK_SCRATCH,
-        far=(1, 2),
-        far_out=(0, 1, 2, 3),
         planes=right_parts,
     )
     image_arrived = exchange(image_send)
     image_near = (moved(image, 1), image, moved(image, -1))
-    map_scratch = (pltpu.VMEM((3, 3, FRAME, COLS), F32), pltpu.VMEM((FRAME, COLS), F32), pltpu.SemaphoreType.DMA((3,)))
-    image_map, row_ab = call(map_kernel, (rows, row), [weights], [], map_scratch, far_out=(0, 1), planes=image_near)
+    map_scratch = (pltpu.VMEM((3, 3, FRAME, COLS), F32), pltpu.VMEM((FRAME, COLS), F32))
+    image_map, sums = call(map_kernel, (rows, row), [weights], [row_b], map_scratch, planes=image_near)
     further_out, image_spectrum = call(
-        second_filter_kernel,
-        (tiles, spectral),
-        [is_first],
-        [along_y, image_arrived, bank, row_b, row_ab],
-        far=(2, 3, 4),
-        far_out=(0, 1),
+        second_filter_kernel, (tiles, spectral), [], [along_y, image_arrived, bank, sums]
     )
-    further_out, image_again = lax.optimization_barrier((further_out, image))
+    further_out, image_again, loss_parts = lax.optimization_barrier((further_out, image, loss_parts))
     further_arrived = exchange(further_out)
     image_parts = (moved(image_again, 2), *image_near, moved(image_again, -2))
-    image_back = call(further_kernel, frame, [place, weights], [], STENCIL_SCRATCH, far_out=(0,), planes=image_parts)
-    further_arrived, image_back = lax.optimization_barrier((further_arrived, image_back))
-
-    further, row_sum = call(
-        gather_sum_kernel, (frame, row), [], [table, further_arrived, image_back], far=(2,), far_out=(0,)
-    )
-    smem = pl.BlockSpec(memory_space=pltpu.SMEM)
-    filter_factors, stencil_factors = pl.pallas_call(
+    loss_back, loss_map = call(loss_kernel, (frame, rows), [weights], [], STENCIL_SCRATCH, planes=loss_parts)
+    image_back = call(further_kernel, frame, [weights], [], STENCIL_SCRATCH, planes=image_parts)
+    further_arrived, image_back, loss_back = lax.optimization_barrier((further_arrived, image_back, loss_back))
+
+    further, row_sum = call(gather_sum_kernel, (frame, row), [], [table, further_arrived, image_back])
+    moments = from_all(row_sum)
+    further, moments = lax.optimization_barrier((further, moments))
+    factors = pl.pallas_call(
         factors_kernel,
-        out_shape=(shape(6), shape(5)),
-        in_specs=[pl.BlockSpec(memory_space=pltpu.VMEM)],
-        out_specs=(smem, smem),
-    )(from_all(row_sum))
+        out_shape=shape(38),
+        in_specs=[pl.BlockSpec(memory_space=pltpu.SMEM), pl.BlockSpec(memory_space=pltpu.VMEM)],
+        out_specs=pl.BlockSpec(memory_space=pltpu.SMEM),
+    )(weights, moments)
 
     further_parts = neighbours(further)
     further_map, last_send = call(
         last_kernel,
         (rows, tiles),
-        [place, weights, filter_factors],
+        [factors],
         [table, image_back, loss_back, upstream],
         STENCIL_SCRATCH + BACK_SCRATCH,
-        far=(1, 2, 3),
-        far_out=(0, 1),
         planes=further_parts,
     )
     last_arrived = exchange(last_send)
@@ -633,18 +601,11 @@
         operands += parts[1:4]
     operands += [right_map, image_map, further_map, loss_map]
     scratch = (pltpu.VMEM((3, FRAME, COLS), F32), pltpu.VMEM((3, ROWS, COLS), F32))
-    terms = call(correlate_kernel, row, [stencil_factors], operands, scratch, far=tuple(range(16)), far_out=(0,))
-    terms = over_planes(terms)
-    result_out = call(
-        last_filter_kernel,
-        tiles,
-        [is_first, filter_factors],
-        [along_y, last_arrived, bank, image_spectrum, terms],
-        far=(2, 3, 4),
-        far_out=(0,),
-    )
+    terms = call(correlate_kernel, row, [factors], operands, scratch)
+    result_out = call(last_filter_kernel, tiles, [factors], [along_y, last_arrived, bank, image_spectrum, terms])
     grad_measured, terms = call(final_kernel, (rows, row), [], [table, exchange(result_out)])
-    grad_stencil = terms[0, :27].reshape(3, 3, 3) / math.sqrt(cells)
+    terms = jnp.sum(from_all(terms)[:, 0, :], 0)
+    grad_stencil = terms[:27].reshape(3, 3, 3) / math.sqrt(cells)
     return grad_measured[None], grad_stencil
 
 

time: 314 us -> 293 us (0.933)
  Pallas kernels: 64.2 us -> 32.2 us
  local copies, waits for them, and re-layouts: 9.09 us -> 37.3 us
  starting transfers between devices: 128 us -> 111 us
  blocking collectives: 54.7 us -> 58.2 us
    pallas_call x13, Pallas kernels: 62.7 us -> 30.7 us  [call(): pl.pallas_call(whole, out_shape=out_shape, in_specs=spec_in, out_specs=sp...]
    unnamed x50 -> x106, local copies, waits for them, and re-layouts: 7.07 us -> 36.5 us
    all_to_all x1 -> x2, blocking collectives: 16.6 us -> 32.6 us  [from_all(): lax.all_to_all(jnp.broadcast_to(row[None], (size, 8, 128)), GZ, 0, 0, til...]
    all_to_all x5, waiting for transfers between devices: 20.4 us -> 34.6 us  [exchange(): return lax.all_to_all(value, GY, 0, 0, tiled=True)]
    all_to_all x1, blocking collectives: 38.2 us -> 25.6 us  [exchange(): return lax.all_to_all(value, GY, 0, 0, tiled=True)]
    ppermute x4 -> x0, waiting for transfers between devices: 11 us -> none  [over_planes(): row = row + lax.ppermute(row, GZ, [(i, i ^ bit) for i in range(size)])]
    ppermute x4 -> x0, starting transfers between devices: 10 us -> none  [over_planes(): row = row + lax.ppermute(row, GZ, [(i, i ^ bit) for i in range(size)])]
    all_to_all x5, starting transfers between devices: 57 us -> 52.4 us  [exchange(): return lax.all_to_all(value, GY, 0, 0, tiled=True)]
  transfers between devices with their start and end apart: 27 -> 23, of which waited for: 16 -> 12; matrix products, arithmetic and copies ran while one was open for 1% -> 0% of each run, Pallas kernels for 6% -> 3%
where the time goes in v5:
time: 293 us; the launch traced here: 291 us
  starting transfers between devices  111 us (38%)
  blocking collectives  58.2 us (20%)
  waiting for transfers between devices  51.3 us (18%)
  local copies, waits for them, and re-layouts  37.3 us (13%)
  Pallas kernels  32.2 us (11%)
    ppermute x16, starting transfers between devices, moved(): lax.ppermute(value, GZ, [(i, i + by) for i in range(size) if 0 <= i + by...  52.9 us
    all_to_all x5, starting transfers between devices, exchange(): return lax.all_to_all(value, GY, 0, 0, tiled=True)  52.4 us
    unnamed x106, local copies, waits for them, and re-layouts  36.5 us
    all_to_all x5, waiting for transfers between devices, exchange(): return lax.all_to_all(value, GY, 0, 0, tiled=True)  34.6 us
    all_to_all x2, blocking collectives, from_all(): lax.all_to_all(jnp.broadcast_to(row[None], (size, 8, 128)), GZ, 0, 0, til...  32.6 us
    pallas_call x13, Pallas kernels, call(): pl.pallas_call(whole, out_shape=out_shape, in_specs=spec_in, out_specs=sp...  30.7 us
    all_to_all x1, blocking collectives, exchange(): return lax.all_to_all(value, GY, 0, 0, tiled=True)  25.6 us
    ppermute x16, waiting for transfers between devices, moved(): lax.ppermute(value, GZ, [(i, i + by) for i in range(size) if 0 <= i + by...  9.08 us
  transfers between devices with their start and end apart: 23, of which 12 were waited for; matrix products, arithmetic and copies ran while one was open for 0% of the time, Pallas kernels for 3%

profile of v5, /device:TPU:1, one launch (start us, length us, event | category | flops | bytes accessed | tf_op | source)
XLA Modules:
  0.0 291.0 jit_solution(8893673465511942180)
XLA Ops:
  0.6 1.6 copy-done
  4.0 3.2 %shard_map.77 = f32[32,16,128]{2,1,0:T(8,128)} custom-call(bf16[2048,512]{1,0:T(8,128)(2,1)S(1)} %copy-done, f32[32,1024]{1,0:T(8,128)S(1)} %bitcast.13, f32[32,1024]{1,0:T(8,128)S(1)} %copy-done.28), custom_call_target="tpu_custom_call" | custom-call | flops 400000000 | bytes 4000000 | tf_op jit(solution)/shard_map/pallas_call | solution.py:476
  7.2 16.9 %all-to-all-start = ((f32[32,16,128]{2,1,0:T(8,128)}), f32[32,16,128]{2,1,0:T(8,128)S(1)}, u32[]{:S(2)}, u32[]{:S(2)}) async-start(f32[32,16,128]{2,1,0:T(8,128)} %shard_map.77), calls=%async_computation | async-start | bytes 524288 | tf_op jit(solution)/shard_map/all_to_all | solution.py:488
  24.2 3.5 %collective-permute-start = (f32[8,1024]{1,0:T(8,128)S(1)}, f32[8,1024]{1,0:T(8,128)S(1)}, u32[]{:S(2)}, u32[]{:S(2)}) collective-permute-start(f32[8,1024]{1,0:T(8,128)S(1)} %get-tuple-element.82), channel_id=1, source_target_pairs={{0,16},{16,32},{32,48},{48,64},{64,80},{80,96},{96,112},{112,128},... | collective-permute-start | bytes 98312 | tf_op jit(solution)/shard_map/ppermute | solution.py:502
  27.7 1.9 collective-permute-start.1
  29.6 1.5 collective-permute-done
  31.1 6.2 %collective-permute-done.1 = f32[8,1024]{1,0:T(8,128)S(1)} collective-permute-done((f32[8,1024]{1,0:T(8,128)S(1)}, f32[8,1024]{1,0:T(8,128)S(1)}, u32[]{:S(2)}, u32[]{:S(2)}) %collective-permute-start.1) | collective-permute-done | bytes 32800 | tf_op jit(solution)/shard_map/ppermute | solution.py:503
  37.3 8.6 %all-to-all-done.refs_1_ = f32[32,16,128]{2,1,0:T(8,128)S(1)} async-done(((f32[32,16,128]{2,1,0:T(8,128)}), f32[32,16,128]{2,1,0:T(8,128)S(1)}, u32[]{:S(2)}, u32[]{:S(2)}) %all-to-all-start) | async-done | bytes 262176 | tf_op jit(solution)/shard_map/all_to_all | solution.py:488
  46.0 3.0 %shard_map.78 = (f32[32,24,128]{2,1,0:T(8,128)}, f32[2,288,128]{2,1,0:T(8,128)S(1)}) custom-call(f32[704,128]{1,0:T(8,128)S(1)} %copy-done.44, f32[32,16,128]{2,1,0:T(8,128)S(1)} %all-to-all-done.refs_1_), custom_call_target="tpu_custom_call" | custom-call | flops 400000000 | bytes 4000000 | tf_op jit(solution)/shard_map/pallas_call | solution.py:476
  49.6 4.9 %all-to-all-start.1 = ((f32[32,24,128]{2,1,0:T(8,128)}), f32[32,24,128]{2,1,0:T(8,128)S(1)}, u32[]{:S(2)}, u32[]{:S(2)}) async-start(f32[32,24,128]{2,1,0:T(8,128)} %get-tuple-element.43), calls=%async_computation.1 | async-start | bytes 786432 | tf_op jit(solution)/shard_map/all_to_all | solution.py:488
  54.5 1.3 collective-permute-start.5
  55.8 1.3 collective-permute-start.4
  57.1 4.0 %collective-permute-start.3 = (f32[48,1024]{1,0:T(8,128)S(1)}, f32[48,1024]{1,0:T(8,128)S(1)}, u32[]{:S(2)}, u32[]{:S(2)}) collective-permute-start(f32[48,1024]{1,0:T(8,128)S(1)} %pad_maximum_fusion.refs_3_.refs_11_), channel_id=1, source_target_pairs={{0,1},{1,2},{2,3},{3,4},{4,5},{5,6},{6,7},{7,8},{8,9},{9,10},{10,1... | collective-permute-start | bytes 589832 | tf_op jit(solution)/shard_map/ppermute | solution.py:493
  61.1 5.9 %collective-permute-start.2 = (f32[48,1024]{1,0:T(8,128)S(1)}, f32[48,1024]{1,0:T(8,128)S(1)}, u32[]{:S(2)}, u32[]{:S(2)}) collective-permute-start(f32[48,1024]{1,0:T(8,128)S(1)} %pad_maximum_fusion.refs_3_.refs_11_), channel_id=1, source_target_pairs={{0,2},{1,3},{2,4},{3,5},{4,6},{5,7},{6,8},{7,9},{8,10},{9,11},{10,... | collective-permute-start | bytes 589832 | tf_op jit(solution)/shard_map/ppermute | solution.py:493
  69.0 1.2 collective-permute-done.2.refs_1_
  70.9 11.6 %all-to-all-done.1.refs_1_ = f32[32,24,128]{2,1,0:T(8,128)S(1)} async-done(((f32[32,24,128]{2,1,0:T(8,128)}), f32[32,24,128]{2,1,0:T(8,128)S(1)}, u32[]{:S(2)}, u32[]{:S(2)}) %all-to-all-start.1) | async-done | bytes 393248 | tf_op jit(solution)/shard_map/all_to_all | solution.py:488
  84.1 1.3 collective-permute-start.9
  85.4 1.3 collective-permute-start.8
  86.7 4.0 %collective-permute-start.7 = (f32[48,1024]{1,0:T(8,128)S(1)}, f32[48,1024]{1,0:T(8,128)S(1)}, u32[]{:S(2)}, u32[]{:S(2)}) collective-permute-start(f32[48,1024]{1,0:T(8,128)S(1)} %get-tuple-element.47.refs_6_.refs_2_), channel_id=1, source_target_pairs={{0,1},{1,2},{2,3},{3,4},{4,5},{5,6},{6,7},{7,8},{8,9},{9,10},{10,1... | collective-permute-start | bytes 589832 | tf_op jit(solution)/shard_map/ppermute | solution.py:493
  90.7 5.9 %collective-permute-start.6 = (f32[48,1024]{1,0:T(8,128)S(1)}, f32[48,1024]{1,0:T(8,128)S(1)}, u32[]{:S(2)}, u32[]{:S(2)}) collective-permute-start(f32[48,1024]{1,0:T(8,128)S(1)} %get-tuple-element.47.refs_6_.refs_2_), channel_id=1, source_target_pairs={{0,2},{1,3},{2,4},{3,5},{4,6},{5,7},{6,8},{7,9},{8,10},{9,11},{10,... | collective-permute-start | bytes 589832 | tf_op jit(solution)/shard_map/ppermute | solution.py:493
  96.7 2.9 collective-permute-done.6.refs_4_
  100.5 4.1 %shard_map.80 = (f32[48,1024]{1,0:T(8,128)S(1)}, f32[32,1024]{1,0:T(8,128)S(1)}, f32[32,8,128]{2,1,0:T(8,128)}, f32[1,128]{1,0:T(1,128)S(1)}) custom-call(f32[27]{0:T(128)S(1)} %reshape.14.refs_0_.weights_ref, bf16[2048,512]{1,0:T(8,128)(2,1)S(1)} %copy-done.1, f32[48,1024]{1,0:T(8,128)S(1)} %copy-done.8, f32[32,1024]{1,0:T(8,128)S(1)} %bitcast.11, ...), custom_call_target="tpu_custom_call" | custom-call | flops 400000000 | bytes 4000000 | tf_op jit(solution)/shard_map/pallas_call | solution.py:476
  105.9 5.6 %all-to-all-start.2 = ((f32[32,8,128]{2,1,0:T(8,128)}), f32[32,8,128]{2,1,0:T(8,128)S(1)}, u32[]{:S(2)}, u32[]{:S(2)}) async-start(f32[32,8,128]{2,1,0:T(8,128)} %get-tuple-element.48), calls=%async_computation.2 | async-start | bytes 262144 | tf_op jit(solution)/shard_map/all_to_all | solution.py:488
  111.5 1.3 collective-permute-start.11
  112.8 5.5 %collective-permute-start.10 = (f32[48,1024]{1,0:T(8,128)}, f32[48,1024]{1,0:T(8,128)S(1)}, u32[]{:S(2)}, u32[]{:S(2)}) collective-permute-start(f32[48,1024]{1,0:T(8,128)} %copy-done.15), channel_id=1, source_target_pairs={{0,1},{1,2},{2,3},{3,4},{4,5},{5,6},{6,7},{7,8},{8,9},{9,10},{10,1... | collective-permute-start | bytes 589832 | tf_op jit(solution)/shard_map/ppermute | solution.py:493
  118.3 3.3 %collective-permute-done.11.refs_4_.refs_6_ = f32[48,1024]{1,0:T(8,128)S(1)} collective-permute-done((f32[48,1024]{1,0:T(8,128)}, f32[48,1024]{1,0:T(8,128)S(1)}, u32[]{:S(2)}, u32[]{:S(2)}) %collective-permute-start.11) | collective-permute-done | bytes 196640 | tf_op jit(solution)/shard_map/ppermute | solution.py:493
  125.9 1.7 all-to-all-done.2.refs_1_
  129.6 1.4 shard_map.82
  132.4 11.3 %all-to-all-start.3 = ((f32[32,16,128]{2,1,0:T(8,128)}), f32[32,16,128]{2,1,0:T(8,128)S(1)}, u32[]{:S(2)}, u32[]{:S(2)}) async-start(f32[32,16,128]{2,1,0:T(8,128)} %copy-done.5), calls=%async_computation.3 | async-start | bytes 524288 | tf_op jit(solution)/shard_map/all_to_all | solution.py:488
  143.8 1.3 collective-permute-start.13
  145.1 7.0 %collective-permute-start.12 = (f32[48,1024]{1,0:T(8,128)}, f32[48,1024]{1,0:T(8,128)S(1)}, u32[]{:S(2)}, u32[]{:S(2)}) collective-permute-start(f32[48,1024]{1,0:T(8,128)} %copy-done.15), channel_id=1, source_target_pairs={{0,2},{1,3},{2,4},{3,5},{4,6},{5,7},{6,8},{7,9},{8,10},{9,11},{10,... | collective-permute-start | bytes 589832 | tf_op jit(solution)/shard_map/ppermute | solution.py:493
  155.8 2.4 shard_map.84
  161.8 2.5 shard_map.83.refs_2_
  164.3 1.5 all-to-all-done.3.refs_1_
  165.8 1.3 shard_map.85
  167.1 18.7 %all_to_all.40.rows = f32[16,8,128]{2,1,0:T(8,128)} all-to-all(f32[16,8,128]{2,1,0:T(8,128)S(1)} %broadcast_in_dim.20), channel_id=1, replica_groups=mesh['gy'=32,'gz'=16] {'gz'}, dimensions={0} | all-to-all | bytes 131072 | tf_op jit(solution)/shard_map/all_to_all | solution.py:509
  185.8 1.4 collective-permute-start.17
  187.2 1.3 collective-permute-start.16
  188.5 4.7 %collective-permute-start.15 = (f32[48,1024]{1,0:T(8,128)}, f32[48,1024]{1,0:T(8,128)}, u32[]{:S(2)}, u32[]{:S(2)}) collective-permute-start(f32[48,1024]{1,0:T(8,128)} %get-tuple-element.73.refs_7_.refs_8_), channel_id=1, source_target_pairs={{0,1},{1,2},{2,3},{3,4},{4,5},{5,6},{6,7},{7,8},{8,9},{9,10},{10,1... | collective-permute-start | bytes 589832 | tf_op jit(solution)/shard_map/ppermute | solution.py:493
  193.2 5.5 %collective-permute-start.14 = (f32[48,1024]{1,0:T(8,128)}, f32[48,1024]{1,0:T(8,128)}, u32[]{:S(2)}, u32[]{:S(2)}) collective-permute-start(f32[48,1024]{1,0:T(8,128)} %get-tuple-element.73.refs_7_.refs_8_), channel_id=1, source_target_pairs={{0,2},{1,3},{2,4},{3,5},{4,6},{5,7},{6,8},{7,9},{8,10},{9,11},{10,... | collective-permute-start | bytes 589832 | tf_op jit(solution)/shard_map/ppermute | solution.py:493
  198.7 1.5 shard_map.86.refs_0_
  202.5 4.9 %shard_map.87 = (f32[32,1024]{1,0:T(8,128)S(1)}, f32[32,16,128]{2,1,0:T(8,128)S(1)}) custom-call(f32[38]{0:T(128)S(1)} %copy-done.38, bf16[2048,512]{1,0:T(8,128)(2,1)S(1)} %copy-done.1, f32[48,1024]{1,0:T(8,128)S(1)} %shard_map.83.refs_2_, f32[48,1024]{1,0:T(8,128)S(1)} %copy-done.26, f32[32,1024]{1,0:T(8,128)S(1)} %bitcast.12, ...), custom_call_target="tpu_custom_call" | custom-call | flops 400000000 | bytes 4000000 | tf_op jit(solution)/shard_map/pallas_call | solution.py:476
  208.8 13.7 %all-to-all-start.5 = ((f32[32,16,128]{2,1,0:T(8,128)}), f32[32,16,128]{2,1,0:T(8,128)S(1)}, u32[]{:S(2)}, u32[]{:S(2)}) async-start(f32[32,16,128]{2,1,0:T(8,128)} %copy-done.6), calls=%async_computation.5 | async-start | bytes 524288 | tf_op jit(solution)/shard_map/all_to_all | solution.py:488
  230.8 2.5 shard_map.88.refs_5_
  233.3 11.2 %all-to-all-done.5.refs_2_ = f32[32,16,128]{2,1,0:T(8,128)S(1)} async-done(((f32[32,16,128]{2,1,0:T(8,128)}), f32[32,16,128]{2,1,0:T(8,128)S(1)}, u32[]{:S(2)}, u32[]{:S(2)}) %all-to-all-start.5) | async-done | bytes 262176 | tf_op jit(solution)/shard_map/all_to_all | solution.py:488
  247.3 2.3 shard_map.89
  249.6 25.6 %all_to_all.41.refs_1_ = f32[32,16,128]{2,1,0:T(8,128)S(1)} all-to-all(f32[32,16,128]{2,1,0:T(8,128)S(1)} %shard_map.89), channel_id=1, replica_groups=mesh['gy'=32,'gz'=16] {'gy'}, dimensions={0} | all-to-all | bytes 524288 | tf_op jit(solution)/shard_map/all_to_all | solution.py:488
  276.4 13.8 %all_to_all.42 = f32[16,8,128]{2,1,0:T(8,128)S(1)} all-to-all(f32[16,8,128]{2,1,0:T(8,128)S(1)} %broadcast_in_dim.23), channel_id=1, replica_groups=mesh['gy'=32,'gz'=16] {'gz'}, dimensions={0} | all-to-all | bytes 131072 | tf_op jit(solution)/shard_map/all_to_all | solution.py:509
  (130 shorter events, 40.6 us)
Async XLA Ops:
  0.6 1.6 copy-start
  4.0 20.1 %copy-start.2 = (f32[1,32,1024]{2,1,0:T(8,128)S(1)}, f32[1,32,1024]{2,1,0:T(8,128)}, u32[]{:S(2)}) copy-start(f32[1,32,1024]{2,1,0:T(8,128)} %param.9) | copy-start | bytes 393220
  4.0 41.9 %copy-start.44 = (f32[704,128]{1,0:T(8,128)S(1)}, f32[704,128]{1,0:T(8,128)}, u32[]{:S(2)}) copy-start(f32[704,128]{1,0:T(8,128)} %constant.10.clone.refs_0_.refs_1_) | copy-start | bytes 1081348
  7.2 75.3 %copy-start.1 = (bf16[2048,512]{1,0:T(8,128)(2,1)S(1)}, bf16[2048,512]{1,0:T(8,128)(2,1)}, u32[]{:S(2)}) copy-start(bf16[2048,512]{1,0:T(8,128)(2,1)} %constant.9.clone.refs_0_.refs_1_) | copy-start | bytes 6291460
  7.2 38.7 %all-to-all-start = ((f32[32,16,128]{2,1,0:T(8,128)}), f32[32,16,128]{2,1,0:T(8,128)S(1)}, u32[]{:S(2)}, u32[]{:S(2)}) async-start(f32[32,16,128]{2,1,0:T(8,128)} %shard_map.77), calls=%async_computation | async-start | bytes 524288 | tf_op jit(solution)/shard_map/all_to_all | solution.py:488
  24.2 7.0 %collective-permute-start = (f32[8,1024]{1,0:T(8,128)S(1)}, f32[8,1024]{1,0:T(8,128)S(1)}, u32[]{:S(2)}, u32[]{:S(2)}) collective-permute-start(f32[8,1024]{1,0:T(8,128)S(1)} %get-tuple-element.82), channel_id=1, source_target_pairs={{0,16},{16,32},{32,48},{48,64},{64,80},{80,96},{96,112},{112,128},... | collective-permute-start | bytes 98312 | tf_op jit(solution)/shard_map/ppermute | solution.py:502
  27.7 9.6 %collective-permute-start.1 = (f32[8,1024]{1,0:T(8,128)S(1)}, f32[8,1024]{1,0:T(8,128)S(1)}, u32[]{:S(2)}, u32[]{:S(2)}) collective-permute-start(f32[8,1024]{1,0:T(8,128)S(1)} %get-tuple-element.83), channel_id=1, source_target_pairs={{16,0},{32,16},{48,32},{64,48},{80,64},{96,80},{112,96},{128,112},... | collective-permute-start | bytes 98312 | tf_op jit(solution)/shard_map/ppermute | solution.py:503
  37.3 114.8 %copy-start.3 = (f32[48,1024]{1,0:T(8,128)}, f32[48,1024]{1,0:T(8,128)S(1)}, u32[]{:S(2)}) copy-start(f32[48,1024]{1,0:T(8,128)S(1)} %pad_maximum_fusion.refs_3_.refs_11_) | copy-start | bytes 589828
  37.3 59.2 %copy-start.52 = (f32[3,3,3]{2,1,0:T(4,128)S(1)}, f32[3,3,3]{2,1,0:T(4,128)}, u32[]{:S(2)}) copy-start(f32[3,3,3]{2,1,0:T(4,128)} %param.8) | copy-start | bytes 328
  49.6 32.9 %all-to-all-start.1 = ((f32[32,24,128]{2,1,0:T(8,128)}), f32[32,24,128]{2,1,0:T(8,128)S(1)}, u32[]{:S(2)}, u32[]{:S(2)}) async-start(f32[32,24,128]{2,1,0:T(8,128)} %get-tuple-element.43), calls=%async_computation.1 | async-start | bytes 786432 | tf_op jit(solution)/shard_map/all_to_all | solution.py:488
  54.5 12.5 %collective-permute-start.5 = (f32[48,1024]{1,0:T(8,128)S(1)}, f32[48,1024]{1,0:T(8,128)S(1)}, u32[]{:S(2)}, u32[]{:S(2)}) collective-permute-start(f32[48,1024]{1,0:T(8,128)S(1)} %pad_maximum_fusion.refs_3_.refs_11_), channel_id=1, source_target_pairs={{2,0},{3,1},{4,2},{5,3},{6,4},{7,5},{8,6},{9,7},{10,8},{11,9},{12,... | collective-permute-start | bytes 589832 | tf_op jit(solution)/shard_map/ppermute | solution.py:493
  55.8 11.9 %collective-permute-start.4 = (f32[48,1024]{1,0:T(8,128)S(1)}, f32[48,1024]{1,0:T(8,128)S(1)}, u32[]{:S(2)}, u32[]{:S(2)}) collective-permute-start(f32[48,1024]{1,0:T(8,128)S(1)} %pad_maximum_fusion.refs_3_.refs_11_), channel_id=1, source_target_pairs={{1,0},{2,1},{3,2},{4,3},{5,4},{6,5},{7,6},{8,7},{9,8},{10,9},{11,1... | collective-permute-start | bytes 589832 | tf_op jit(solution)/shard_map/ppermute | solution.py:493
  57.1 11.3 %collective-permute-start.3 = (f32[48,1024]{1,0:T(8,128)S(1)}, f32[48,1024]{1,0:T(8,128)S(1)}, u32[]{:S(2)}, u32[]{:S(2)}) collective-permute-start(f32[48,1024]{1,0:T(8,128)S(1)} %pad_maximum_fusion.refs_3_.refs_11_), channel_id=1, source_target_pairs={{0,1},{1,2},{2,3},{3,4},{4,5},{5,6},{6,7},{7,8},{8,9},{9,10},{10,1... | collective-permute-start | bytes 589832 | tf_op jit(solution)/shard_map/ppermute | solution.py:493
  61.1 9.1 %collective-permute-start.2 = (f32[48,1024]{1,0:T(8,128)S(1)}, f32[48,1024]{1,0:T(8,128)S(1)}, u32[]{:S(2)}, u32[]{:S(2)}) collective-permute-start(f32[48,1024]{1,0:T(8,128)S(1)} %pad_maximum_fusion.refs_3_.refs_11_), channel_id=1, source_target_pairs={{0,2},{1,3},{2,4},{3,5},{4,6},{5,7},{6,8},{7,9},{8,10},{9,11},{10,... | collective-permute-start | bytes 589832 | tf_op jit(solution)/shard_map/ppermute | solution.py:493
  84.1 12.6 %collective-permute-start.9 = (f32[48,1024]{1,0:T(8,128)S(1)}, f32[48,1024]{1,0:T(8,128)S(1)}, u32[]{:S(2)}, u32[]{:S(2)}) collective-permute-start(f32[48,1024]{1,0:T(8,128)S(1)} %get-tuple-element.47.refs_6_.refs_2_), channel_id=1, source_target_pairs={{2,0},{3,1},{4,2},{5,3},{6,4},{7,5},{8,6},{9,7},{10,8},{11,9},{12,... | collective-permute-start | bytes 589832 | tf_op jit(solution)/shard_map/ppermute | solution.py:493
  85.4 11.3 %collective-permute-start.8 = (f32[48,1024]{1,0:T(8,128)S(1)}, f32[48,1024]{1,0:T(8,128)S(1)}, u32[]{:S(2)}, u32[]{:S(2)}) collective-permute-start(f32[48,1024]{1,0:T(8,128)S(1)} %get-tuple-element.47.refs_6_.refs_2_), channel_id=1, source_target_pairs={{1,0},{2,1},{3,2},{4,3},{5,4},{6,5},{7,6},{8,7},{9,8},{10,9},{11,1... | collective-permute-start | bytes 589832 | tf_op jit(solution)/shard_map/ppermute | solution.py:493
  86.7 10.0 %collective-permute-start.7 = (f32[48,1024]{1,0:T(8,128)S(1)}, f32[48,1024]{1,0:T(8,128)S(1)}, u32[]{:S(2)}, u32[]{:S(2)}) collective-permute-start(f32[48,1024]{1,0:T(8,128)S(1)} %get-tuple-element.47.refs_6_.refs_2_), channel_id=1, source_target_pairs={{0,1},{1,2},{2,3},{3,4},{4,5},{5,6},{6,7},{7,8},{8,9},{9,10},{10,1... | collective-permute-start | bytes 589832 | tf_op jit(solution)/shard_map/ppermute | solution.py:493
  90.7 8.9 %collective-permute-start.6 = (f32[48,1024]{1,0:T(8,128)S(1)}, f32[48,1024]{1,0:T(8,128)S(1)}, u32[]{:S(2)}, u32[]{:S(2)}) collective-permute-start(f32[48,1024]{1,0:T(8,128)S(1)} %get-tuple-element.47.refs_6_.refs_2_), channel_id=1, source_target_pairs={{0,2},{1,3},{2,4},{3,5},{4,6},{5,7},{6,8},{7,9},{8,10},{9,11},{10,... | collective-permute-start | bytes 589832 | tf_op jit(solution)/shard_map/ppermute | solution.py:493
  96.6 62.3 %copy-start.37 = (f32[27]{0:T(128)}, f32[27]{0:T(128)S(1)}, u32[]{:S(2)}) copy-start(f32[27]{0:T(128)S(1)} %reshape.14.refs_0_.weights_ref) | copy-start | bytes 328
  99.6 0.9 copy-start.8
  105.9 21.8 %all-to-all-start.2 = ((f32[32,8,128]{2,1,0:T(8,128)}), f32[32,8,128]{2,1,0:T(8,128)S(1)}, u32[]{:S(2)}, u32[]{:S(2)}) async-start(f32[32,8,128]{2,1,0:T(8,128)} %get-tuple-element.48), calls=%async_computation.2 | async-start | bytes 262144 | tf_op jit(solution)/shard_map/all_to_all | solution.py:488
  111.5 10.1 %collective-permute-start.11 = (f32[48,1024]{1,0:T(8,128)}, f32[48,1024]{1,0:T(8,128)S(1)}, u32[]{:S(2)}, u32[]{:S(2)}) collective-permute-start(f32[48,1024]{1,0:T(8,128)} %copy-done.15), channel_id=1, source_target_pairs={{1,0},{2,1},{3,2},{4,3},{5,4},{6,5},{7,6},{8,7},{9,8},{10,9},{11,1... | collective-permute-start | bytes 589832 | tf_op jit(solution)/shard_map/ppermute | solution.py:493
  112.8 9.8 %collective-permute-start.10 = (f32[48,1024]{1,0:T(8,128)}, f32[48,1024]{1,0:T(8,128)S(1)}, u32[]{:S(2)}, u32[]{:S(2)}) collective-permute-start(f32[48,1024]{1,0:T(8,128)} %copy-done.15), channel_id=1, source_target_pairs={{0,1},{1,2},{2,3},{3,4},{4,5},{5,6},{6,7},{7,8},{8,9},{9,10},{10,1... | collective-permute-start | bytes 589832 | tf_op jit(solution)/shard_map/ppermute | solution.py:493
  121.6 10.8 %copy-start.19 = (f32[48,1024]{1,0:T(8,128)}, f32[48,1024]{1,0:T(8,128)S(1)}, u32[]{:S(2)}) copy-start(f32[48,1024]{1,0:T(8,128)S(1)} %collective-permute-done.11.refs_4_.refs_6_) | copy-start | bytes 589828
  122.6 0.9 copy-start.16
  127.7 1.0 copy-start.45
  128.6 1.0 copy-start.48
  132.4 33.3 %all-to-all-start.3 = ((f32[32,16,128]{2,1,0:T(8,128)}), f32[32,16,128]{2,1,0:T(8,128)S(1)}, u32[]{:S(2)}, u32[]{:S(2)}) async-start(f32[32,16,128]{2,1,0:T(8,128)} %copy-done.5), calls=%async_computation.3 | async-start | bytes 524288 | tf_op jit(solution)/shard_map/all_to_all | solution.py:488
  143.8 15.2 %collective-permute-start.13 = (f32[48,1024]{1,0:T(8,128)}, f32[48,1024]{1,0:T(8,128)S(1)}, u32[]{:S(2)}, u32[]{:S(2)}) collective-permute-start(f32[48,1024]{1,0:T(8,128)} %copy-done.15), channel_id=1, source_target_pairs={{2,0},{3,1},{4,2},{5,3},{6,4},{7,5},{8,6},{9,7},{10,8},{11,9},{12,... | collective-permute-start | bytes 589832 | tf_op jit(solution)/shard_map/ppermute | solution.py:493
  145.1 13.9 %collective-permute-start.12 = (f32[48,1024]{1,0:T(8,128)}, f32[48,1024]{1,0:T(8,128)S(1)}, u32[]{:S(2)}, u32[]{:S(2)}) collective-permute-start(f32[48,1024]{1,0:T(8,128)} %copy-done.15), channel_id=1, source_target_pairs={{0,2},{1,3},{2,4},{3,5},{4,6},{5,7},{6,8},{7,9},{8,10},{9,11},{10,... | collective-permute-start | bytes 589832 | tf_op jit(solution)/shard_map/ppermute | solution.py:493
  152.1 0.9 copy-start.10
  153.0 0.9 copy-start.13
  154.0 0.9 copy-start.41
  154.9 0.9 copy-start.43
  158.9 26.9 %copy-start.33 = (f32[32,1024]{1,0:T(8,128)}, f32[32,1024]{1,0:T(8,128)S(1)}, u32[]{:S(2)}) copy-start(f32[32,1024]{1,0:T(8,128)S(1)} %get-tuple-element.79.refs_16_) | copy-start | bytes 393220
  159.0 1.0 copy-start.17
  159.9 0.9 copy-start.20
  185.8 36.7 %copy-start.4 = (f32[48,1024]{1,0:T(8,128)S(1)}, f32[48,1024]{1,0:T(8,128)}, u32[]{:S(2)}) copy-start(f32[48,1024]{1,0:T(8,128)} %copy-done.3) | copy-start | bytes 589828
  185.8 14.5 %collective-permute-start.17 = (f32[48,1024]{1,0:T(8,128)}, f32[48,1024]{1,0:T(8,128)}, u32[]{:S(2)}, u32[]{:S(2)}) collective-permute-start(f32[48,1024]{1,0:T(8,128)} %get-tuple-element.73.refs_7_.refs_8_), channel_id=1, source_target_pairs={{2,0},{3,1},{4,2},{5,3},{6,4},{7,5},{8,6},{9,7},{10,8},{11,9},{12,... | collective-permute-start | bytes 589832 | tf_op jit(solution)/shard_map/ppermute | solution.py:493
  187.2 13.0 %collective-permute-start.16 = (f32[48,1024]{1,0:T(8,128)}, f32[48,1024]{1,0:T(8,128)S(1)}, u32[]{:S(2)}, u32[]{:S(2)}) collective-permute-start(f32[48,1024]{1,0:T(8,128)} %get-tuple-element.73.refs_7_.refs_8_), channel_id=1, source_target_pairs={{1,0},{2,1},{3,2},{4,3},{5,4},{6,5},{7,6},{8,7},{9,8},{10,9},{11,1... | collective-permute-start | bytes 589832 | tf_op jit(solution)/shard_map/ppermute | solution.py:493
  188.5 11.8 %collective-permute-start.15 = (f32[48,1024]{1,0:T(8,128)}, f32[48,1024]{1,0:T(8,128)}, u32[]{:S(2)}, u32[]{:S(2)}) collective-permute-start(f32[48,1024]{1,0:T(8,128)} %get-tuple-element.73.refs_7_.refs_8_), channel_id=1, source_target_pairs={{0,1},{1,2},{2,3},{3,4},{4,5},{5,6},{6,7},{7,8},{8,9},{9,10},{10,1... | collective-permute-start | bytes 589832 | tf_op jit(solution)/shard_map/ppermute | solution.py:493
  193.2 7.8 %collective-permute-start.14 = (f32[48,1024]{1,0:T(8,128)}, f32[48,1024]{1,0:T(8,128)}, u32[]{:S(2)}, u32[]{:S(2)}) collective-permute-start(f32[48,1024]{1,0:T(8,128)} %get-tuple-element.73.refs_7_.refs_8_), channel_id=1, source_target_pairs={{0,2},{1,3},{2,4},{3,5},{4,6},{5,7},{6,8},{7,9},{8,10},{9,11},{10,... | collective-permute-start | bytes 589832 | tf_op jit(solution)/shard_map/ppermute | solution.py:493
  202.5 20.0 %copy-start.39 = (f32[38]{0:T(128)S(1)}, f32[38]{0:T(128)}, u32[]{:S(2)}) copy-start(f32[38]{0:T(128)} %shard_map.86.refs_0_) | copy-start | bytes 460
  208.8 35.7 %all-to-all-start.5 = ((f32[32,16,128]{2,1,0:T(8,128)}), f32[32,16,128]{2,1,0:T(8,128)S(1)}, u32[]{:S(2)}, u32[]{:S(2)}) async-start(f32[32,16,128]{2,1,0:T(8,128)} %copy-done.6), calls=%async_computation.5 | async-start | bytes 524288 | tf_op jit(solution)/shard_map/all_to_all | solution.py:488
  222.5 0.9 copy-start.11
  224.4 0.9 copy-start.18
  244.5 1.0 copy-start.46
  245.5 1.0 copy-start.49
  (28 other events, 21.8 us)

commit v6 on v5

--- a/solution.py
+++ b/solution.py
@@ -8,10 +8,11 @@
 from jax import lax
 from jax.experimental import pallas as pl
 from jax.experimental.pallas import tpu as pltpu
+from jax.sharding import Mesh
 from jax.sharding import PartitionSpec as P
 
 GY = "gy"
-GZ = "gz"
+GZ = ("gz_0", "gz_1")
 ROWS = 32
 COLS = 1024
 FRAME = 48
@@ -19,6 +20,7 @@
 F32 = jnp.float32
 BF16 = jnp.bfloat16
 VMEM = 14 * 1024 * 1024
+ALL_VMEM = 60 * 1024 * 1024
 
 
 def split_table(table):
@@ -370,12 +372,6 @@
     row_ref[...] = row_of(((0, b * b), (1, b * ab), (2, ab * ab), (4, u * b), (5, u * ab)))
 
 
-def loss_kernel(weights, u2, u1, o, d1, d2, back_ref, mapped_ref, source, middle):
-    load_planes((u2, u1, o, d1, d2), source)
-    apply_stencils(weights, source, middle, back_ref)
-    mapped_ref[...] = middle[1, 1, 8:40, :]
-
-
 def map_kernel(weights, row_b, u1, o, d1, mapped_ref, row_ref, source, whole):
     load_planes((u1, o, d1), source)
     for k in range(8):
@@ -392,31 +388,29 @@
 
 
 def last_kernel(
-    weights, table, image_back, loss_back, upstream, u2, u1, o, d1, d2, mapped_ref, out_ref, source, middle, back
+    weights, table, image_back, upstream, u2, u1, o, d1, d2, mapped_ref, out_ref, source, middle, back
 ):
     load_planes((u2, u1, o, d1, d2), source)
     apply_stencils(weights, source, middle, back)
     mapped_ref[...] = middle[1, 1, 8:40, :]
-    factor = [weights[27 + k] for k in range(6)]
+    alpha, gamma, twice_g2, twice_g3 = weights[27], weights[28], weights[31], weights[32]
     u, again = upstream[...], image_back[8:40, :]
-    first = factor[0] * u + factor[1] * loss_back[8:40, :] + factor[4] * again + factor[5] * back[8:40, :]
-    second = factor[1] * u + factor[5] * again
+    first = alpha * u + twice_g2 * again + back[8:40, :]
+    second = gamma * u + twice_g3 * again
     out_ref[:, 0:8, :] = x_forward(first, table).reshape(32, 8, 128)
     out_ref[:, 8:16, :] = x_forward(second, table).reshape(32, 8, 128)
 
 
 def correlate_kernel(factor_ref, *refs):
     out_ref, scaled, mapped = refs[-3:]
-    right, image, further, upstream = refs[0:3], refs[3:6], refs[6:9], refs[9:12]
-    right_map, image_map, further_map, upstream_map = refs[12:16]
-    f = [factor_ref[33 + k] for k in range(5)]
+    right, image, mixed = refs[0:3], refs[3:6], refs[6:9]
+    right_map, image_map, mixed_map = refs[9:12]
+    g1, twice_g2, twice_g3 = (factor_ref[k] for k in (33, 31, 32))
     for p in range(3):
-        scaled[p] = f[0] * upstream[p][...] + f[1] * right[p][...] + f[2] * image[p][...] + f[3] * further[p][...]
-    mapped[0] = (
-        f[0] * upstream_map[...] + f[1] * right_map[...] + f[2] * image_map[...] + f[3] * further_map[...]
-    )
+        scaled[p] = mixed[p][...] + g1 * right[p][...] + twice_g2 * image[p][...]
+    mapped[0] = mixed_map[...] + g1 * right_map[...] + twice_g2 * image_map[...]
     mapped[1] = right_map[...]
-    mapped[2] = f[4] * image_map[...]
+    mapped[2] = twice_g3 * image_map[...]
     lane = lanes((1, 128))
     out = jnp.zeros((1, 128), F32)
     column = lanes((ROWS, COLS))
@@ -449,7 +443,7 @@
 BACK_SCRATCH = (pltpu.VMEM((FRAME, COLS), F32),)
 
 
-def call(body, out_shape, scalars, operands, scratch=(), far=(), planes=(), flops=400_000_000):
+def call(body, out_shape, scalars, operands, scratch=(), far=(), planes=(), limit=VMEM, flops=400_000_000):
     operands = [*operands, *planes]
     smem, vmem, hbm = (pl.BlockSpec(memory_space=m) for m in (pltpu.SMEM, pltpu.VMEM, pltpu.HBM))
     outs = out_shape if isinstance(out_shape, tuple) else (out_shape,)
@@ -479,7 +473,7 @@
         in_specs=spec_in,
         out_specs=spec_out if isinstance(out_shape, tuple) else spec_out[0],
         scratch_shapes=[*extra, *scratch],
-        compiler_params=pltpu.CompilerParams(vmem_limit_bytes=VMEM),
+        compiler_params=pltpu.CompilerParams(vmem_limit_bytes=limit),
         cost_estimate=pl.CostEstimate(flops=flops, bytes_accessed=4_000_000, transcendentals=0),
     )(*scalars, *operands)
 
@@ -523,16 +517,16 @@
     return (alpha, gamma, *back((u0, u1)))
 
 
-def factors_kernel(weights_ref, rows, out_ref):
+def factors_kernel(weights_ref, rows, further, grown, out_ref, mixed_ref):
     total = jnp.sum(rows[:, 0, :], 0, keepdims=True)
     lane = lanes((1, 128))
     moments = [jnp.sum(jnp.where(lane == k, total, 0.0), axis=1, keepdims=True) for k in range(6)]
     alpha, gamma, g0, g1, g2, g3 = factors_of(*moments)
     for k in range(27):
         out_ref[k] = weights_ref[k]
-    values = (alpha, gamma, 2.0 * g0, 2.0 * g1, 2.0 * g2, 2.0 * g3, gamma, g1, 2.0 * g2, 2.0 * g3, 2.0 * g3)
-    for k, value in enumerate(values):
+    for k, value in enumerate((alpha, gamma, 2.0 * g0, 2.0 * g1, 2.0 * g2, 2.0 * g3, g1)):
         out_ref[27 + k] = value[0, 0]
+    mixed_ref[...] = gamma * grown[...] + (2.0 * g3) * further[...]
 
 
 def local(measured, point_spread, stencil_weights, upstream):
@@ -543,14 +537,13 @@
     tile, tiles, three = shape(32, 8, 128), shape(32, 16, 128), shape(32, 24, 128)
     spectral, frame, rows, row = shape(32 * BLOCKS, 128), shape(FRAME, COLS), shape(ROWS, COLS), shape(1, 128)
 
-    first = exchange(call(spread_kernel, tiles, [], [table, measured, point_spread], far=(0, 1, 2)))
+    first = exchange(
+        call(spread_kernel, tiles, [], [table, measured, point_spread], far=(0, 1, 2), limit=ALL_VMEM)
+    )
     first, grown = lax.optimization_barrier((first, with_rows(upstream)))
 
     right_out, bank = call(first_filter_kernel, (three, shape(2, 32 * BLOCKS, 128)), [], [along_y, first])
-    right_arrived = exchange(right_out)
-    loss_parts = neighbours(grown)
-    right_arrived, loss_parts = lax.optimization_barrier((right_arrived, loss_parts))
-    right, blurred = call(gather_two_kernel, (frame, frame), [], [table, right_arrived])
+    right, blurred = call(gather_two_kernel, (frame, frame), [], [table, exchange(right_out)])
 
     right_parts = neighbours(right)
     image, right_map, image_send, row_b = call(
@@ -568,51 +561,51 @@
     further_out, image_spectrum = call(
         second_filter_kernel, (tiles, spectral), [], [along_y, image_arrived, bank, sums]
     )
-    further_out, image_again, loss_parts = lax.optimization_barrier((further_out, image, loss_parts))
+    further_out, image_again = lax.optimization_barrier((further_out, image))
     further_arrived = exchange(further_out)
     image_parts = (moved(image_again, 2), *image_near, moved(image_again, -2))
-    loss_back, loss_map = call(loss_kernel, (frame, rows), [weights], [], STENCIL_SCRATCH, planes=loss_parts)
     image_back = call(further_kernel, frame, [weights], [], STENCIL_SCRATCH, planes=image_parts)
-    further_arrived, image_back, loss_back = lax.optimization_barrier((further_arrived, image_back, loss_back))
+    further_arrived, image_back = lax.optimization_barrier((further_arrived, image_back))
 
     further, row_sum = call(gather_sum_kernel, (frame, row), [], [table, further_arrived, image_back])
-    moments = from_all(row_sum)
-    further, moments = lax.optimization_barrier((further, moments))
-    factors = pl.pallas_call(
+    smem, vmem = (pl.BlockSpec(memory_space=m) for m in (pltpu.SMEM, pltpu.VMEM))
+    factors, mixed = pl.pallas_call(
         factors_kernel,
-        out_shape=shape(38),
-        in_specs=[pl.BlockSpec(memory_space=pltpu.SMEM), pl.BlockSpec(memory_space=pltpu.VMEM)],
-        out_specs=pl.BlockSpec(memory_space=pltpu.SMEM),
-    )(weights, moments)
-
-    further_parts = neighbours(further)
-    further_map, last_send = call(
+        out_shape=(shape(34), frame),
+        in_specs=[smem, vmem, vmem, vmem],
+        out_specs=(smem, vmem),
+        compiler_params=pltpu.CompilerParams(vmem_limit_bytes=VMEM),
+    )(weights, from_all(row_sum), further, grown)
+
+    mixed_parts = neighbours(mixed)
+    mixed_map, last_send = call(
         last_kernel,
         (rows, tiles),
         [factors],
-        [table, image_back, loss_back, upstream],
+        [table, image_back, upstream],
         STENCIL_SCRATCH + BACK_SCRATCH,
-        planes=further_parts,
+        planes=mixed_parts,
     )
+    operands = []
+    for parts in (right_parts, image_parts, mixed_parts):
+        operands += parts[1:4]
+    operands += [right_map, image_map, mixed_map]
+    scratch = (pltpu.VMEM((3, FRAME, COLS), F32), pltpu.VMEM((3, ROWS, COLS), F32))
+    terms = call(correlate_kernel, row, [factors], operands, scratch, far=tuple(range(12)), limit=ALL_VMEM)
+    terms = lax.psum(terms, "gz_1")
     last_arrived = exchange(last_send)
-
-    operands = []
-    for parts in (right_parts, image_parts, further_parts, loss_parts):
-        operands += parts[1:4]
-    operands += [right_map, image_map, further_map, loss_map]
-    scratch = (pltpu.VMEM((3, FRAME, COLS), F32), pltpu.VMEM((3, ROWS, COLS), F32))
-    terms = call(correlate_kernel, row, [factors], operands, scratch)
     result_out = call(last_filter_kernel, tiles, [factors], [along_y, last_arrived, bank, image_spectrum, terms])
     grad_measured, terms = call(final_kernel, (rows, row), [], [table, exchange(result_out)])
-    terms = jnp.sum(from_all(terms)[:, 0, :], 0)
-    grad_stencil = terms[:27].reshape(3, 3, 3) / math.sqrt(cells)
+    grad_stencil = lax.psum(terms, "gz_0")[0, :27].reshape(3, 3, 3) / math.sqrt(cells)
     return grad_measured[None], grad_stencil
 
 
 def solution(mesh):
+    groups, planes = mesh.devices.shape
+    finer = Mesh(mesh.devices.reshape(groups, 4, planes // 4), (GY, *GZ))
     return jax.shard_map(
         local,
-        mesh=mesh,
+        mesh=finer,
         in_specs=(P(GZ, GY, None), P(GY, None), P(), P(GZ, GY, None)),
         out_specs=(P(GZ, GY, None), P()),
         check_vma=False,

time: 293 us -> 284 us (0.969)
  blocking collectives: 58.2 us -> 98.9 us
  local copies, waits for them, and re-layouts: 37.3 us -> 13.1 us
  starting transfers between devices: 111 us -> 94.1 us
  waiting for transfers between devices: 51.3 us -> 40.8 us
    all_to_all x1 -> x2, blocking collectives: 25.6 us -> 62 us  [exchange(): return lax.all_to_all(value, GY, 0, 0, tiled=True)]
    unnamed x106 -> x60, local copies, waits for them, and re-layouts: 36.5 us -> 12.3 us
    psum x0 -> x2, blocking collectives: none -> 18.8 us  [the longest x1 12.1 us: local(): terms = lax.psum(terms, 'gz_1')]
    all_to_all x2 -> x1, blocking collectives: 32.6 us -> 18 us  [from_all(): lax.all_to_all(jnp.broadcast_to(row[None], (size, 8, 128)), GZ, 0, 0, til...]
    all_to_all x5 -> x4, waiting for transfers between devices: 34.6 us -> 20.3 us  [exchange(): return lax.all_to_all(value, GY, 0, 0, tiled=True)]
    ppermute x16 -> x12, starting transfers between devices: 52.9 us -> 40.4 us  [moved(): lax.ppermute(value, GZ, [(i, i + by) for i in range(size) if 0 <= i + by...]
    all_to_all x5 -> x4, starting transfers between devices: 52.4 us -> 48.2 us  [exchange(): return lax.all_to_all(value, GY, 0, 0, tiled=True)]
    ppermute x16 -> x12, waiting for transfers between devices: 9.08 us -> 12.8 us  [moved(): lax.ppermute(value, GZ, [(i, i + by) for i in range(size) if 0 <= i + by...]
  transfers between devices with their start and end apart: 23 -> 18, of which waited for: 12 -> 12; matrix products, arithmetic and copies ran while one was open for 0% -> 0% of each run, Pallas kernels for 3% -> 3%
where the time goes in v6:
time: 284 us; the launch traced here: 281 us
  blocking collectives  98.9 us (35%)
  starting transfers between devices  94.1 us (33%)
  waiting for transfers between devices  40.8 us (14%)
  Pallas kernels  33.5 us (12%)
  local copies, waits for them, and re-layouts  13.1 us (5%)
    all_to_all x2, blocking collectives, exchange(): return lax.all_to_all(value, GY, 0, 0, tiled=True)  62 us
    all_to_all x4, starting transfers between devices, exchange(): return lax.all_to_all(value, GY, 0, 0, tiled=True)  48.2 us
    ppermute x12, starting transfers between devices, moved(): lax.ppermute(value, GZ, [(i, i + by) for i in range(size) if 0 <= i + by...  40.4 us
    pallas_call x12, Pallas kernels, call(): pl.pallas_call(whole, out_shape=out_shape, in_specs=spec_in, out_specs=sp...  32.1 us
    all_to_all x4, waiting for transfers between devices, exchange(): return lax.all_to_all(value, GY, 0, 0, tiled=True)  20.3 us
    all_to_all x1, blocking collectives, from_all(): lax.all_to_all(jnp.broadcast_to(row[None], (size, 8, 128)), GZ, 0, 0, til...  18 us
    ppermute x12, waiting for transfers between devices, moved(): lax.ppermute(value, GZ, [(i, i + by) for i in range(size) if 0 <= i + by...  12.8 us
    unnamed x60, local copies, waits for them, and re-layouts  12.3 us
  transfers between devices with their start and end apart: 18, of which 12 were waited for; matrix products, arithmetic and copies ran while one was open for 0% of the time, Pallas kernels for 3%

profile of v6, /device:TPU:1, one launch (start us, length us, event | category | flops | bytes accessed | tf_op | source)
XLA Modules:
  0.0 281.4 jit_solution(12068289978439495005)
XLA Ops:
  0.7 4.4 %shard_map.77 = f32[32,16,128]{2,1,0:T(8,128)} custom-call(bf16[2048,512]{1,0:T(8,128)(2,1)} %constant.7.clone.refs_0_.refs_1_, f32[32,1024]{1,0:T(8,128)} %bitcast.12, f32[32,1024]{1,0:T(8,128)} %refs_2_.1), custom_call_target="tpu_custom_call" | custom-call | flops 400000000 | bytes 4000000 | tf_op jit(solution)/shard_map/pallas_call | solution.py:470
  5.0 16.9 %all-to-all-start = ((f32[32,16,128]{2,1,0:T(8,128)}), f32[32,16,128]{2,1,0:T(8,128)S(1)}, u32[]{:S(2)}, u32[]{:S(2)}) async-start(f32[32,16,128]{2,1,0:T(8,128)} %shard_map.77), calls=%async_computation | async-start | bytes 524288 | tf_op jit(solution)/shard_map/all_to_all | solution.py:482
  22.0 3.5 %collective-permute-start = (f32[8,1024]{1,0:T(8,128)S(1)}, f32[8,1024]{1,0:T(8,128)S(1)}, u32[]{:S(2)}, u32[]{:S(2)}) collective-permute-start(f32[8,1024]{1,0:T(8,128)S(1)} %get-tuple-element.54), channel_id=1, source_target_pairs={{0,16},{16,32},{32,48},{48,64},{64,80},{80,96},{96,112},{112,128},... | collective-permute-start | bytes 98312 | tf_op jit(solution)/shard_map/ppermute | solution.py:496
  25.5 1.9 collective-permute-start.1
  27.4 1.5 collective-permute-done
  28.9 6.2 %collective-permute-done.1 = f32[8,1024]{1,0:T(8,128)S(1)} collective-permute-done((f32[8,1024]{1,0:T(8,128)S(1)}, f32[8,1024]{1,0:T(8,128)S(1)}, u32[]{:S(2)}, u32[]{:S(2)}) %collective-permute-start.1) | collective-permute-done | bytes 32800 | tf_op jit(solution)/shard_map/ppermute | solution.py:497
  35.1 8.6 %all-to-all-done.refs_1_ = f32[32,16,128]{2,1,0:T(8,128)S(1)} async-done(((f32[32,16,128]{2,1,0:T(8,128)}), f32[32,16,128]{2,1,0:T(8,128)S(1)}, u32[]{:S(2)}, u32[]{:S(2)}) %all-to-all-start) | async-done | bytes 262176 | tf_op jit(solution)/shard_map/all_to_all | solution.py:482
  43.8 2.2 shard_map.78
  46.7 32.0 %all_to_all.35.refs_1_ = f32[32,24,128]{2,1,0:T(8,128)S(1)} all-to-all(f32[32,24,128]{2,1,0:T(8,128)S(1)} %get-tuple-element.29), channel_id=1, replica_groups=mesh['gy'=32,'gz_0'=4,'gz_1'=4] {'gy'}, dimensions={0} | all-to-all | bytes 786432 | tf_op jit(solution)/shard_map/all_to_all | solution.py:482
  79.5 1.3 collective-permute-start.5
  80.8 1.3 collective-permute-start.4
  82.1 4.0 %collective-permute-start.3 = (f32[48,1024]{1,0:T(8,128)S(1)}, f32[48,1024]{1,0:T(8,128)S(1)}, u32[]{:S(2)}, u32[]{:S(2)}) collective-permute-start(f32[48,1024]{1,0:T(8,128)S(1)} %get-tuple-element.31.refs_6_.refs_2_), channel_id=1, source_target_pairs={{0,1},{1,2},{2,3},{3,4},{4,5},{5,6},{6,7},{7,8},{8,9},{9,10},{10,1... | collective-permute-start | bytes 589832 | tf_op jit(solution)/shard_map/ppermute | solution.py:487
  86.1 6.5 %collective-permute-start.2 = (f32[48,1024]{1,0:T(8,128)S(1)}, f32[48,1024]{1,0:T(8,128)}, u32[]{:S(2)}, u32[]{:S(2)}) collective-permute-start(f32[48,1024]{1,0:T(8,128)S(1)} %get-tuple-element.31.refs_6_.refs_2_), channel_id=1, source_target_pairs={{0,2},{1,3},{2,4},{3,5},{4,6},{5,7},{6,8},{7,9},{8,10},{9,11},{10,... | collective-permute-start | bytes 589832 | tf_op jit(solution)/shard_map/ppermute | solution.py:487
  92.8 2.2 collective-permute-done.2.refs_4_
  95.0 4.6 %shard_map.80 = (f32[48,1024]{1,0:T(8,128)S(1)}, f32[32,1024]{1,0:T(8,128)S(1)}, f32[32,8,128]{2,1,0:T(8,128)}, f32[1,128]{1,0:T(1,128)S(1)}) custom-call(f32[27]{0:T(128)S(1)} %reshape.12.refs_0_.weights_ref, bf16[2048,512]{1,0:T(8,128)(2,1)S(1)} %copy-done, f32[48,1024]{1,0:T(8,128)S(1)} %get-tuple-element.30.refs_2_, f32[32,1024]{1,0:T(8,128)S(1)} %bitcast.9, ...), custom_call_target="tpu_custom_call" | custom-call | flops 400000000 | bytes 4000000 | tf_op jit(solution)/shard_map/pallas_call | solution.py:470
  100.9 6.3 %all-to-all-start.2 = ((f32[32,8,128]{2,1,0:T(8,128)}), f32[32,8,128]{2,1,0:T(8,128)}, u32[]{:S(2)}, u32[]{:S(2)}) async-start(f32[32,8,128]{2,1,0:T(8,128)} %get-tuple-element.32), calls=%async_computation.2 | async-start | bytes 262144 | tf_op jit(solution)/shard_map/all_to_all | solution.py:482
  107.3 1.3 collective-permute-start.7
  108.6 5.5 %collective-permute-start.6 = (f32[48,1024]{1,0:T(8,128)}, f32[48,1024]{1,0:T(8,128)S(1)}, u32[]{:S(2)}, u32[]{:S(2)}) collective-permute-start(f32[48,1024]{1,0:T(8,128)} %copy-done.8), channel_id=1, source_target_pairs={{0,1},{1,2},{2,3},{3,4},{4,5},{5,6},{6,7},{7,8},{8,9},{9,10},{10,1... | collective-permute-start | bytes 589832 | tf_op jit(solution)/shard_map/ppermute | solution.py:487
  114.1 3.3 %collective-permute-done.7.refs_4_.refs_6_ = f32[48,1024]{1,0:T(8,128)S(1)} collective-permute-done((f32[48,1024]{1,0:T(8,128)}, f32[48,1024]{1,0:T(8,128)S(1)}, u32[]{:S(2)}, u32[]{:S(2)}) %collective-permute-start.7) | collective-permute-done | bytes 196640 | tf_op jit(solution)/shard_map/ppermute | solution.py:487
  119.2 1.1 shard_map.81
  121.7 1.8 all-to-all-done.2.refs_1_
  123.5 1.0 copy-done.22
  124.5 1.0 copy-done.25
  125.5 3.0 %shard_map.82 = (f32[32,16,128]{2,1,0:T(8,128)}, f32[288,128]{1,0:T(8,128)S(1)}) custom-call(f32[704,128]{1,0:T(8,128)S(1)} %copy-done.22, f32[32,8,128]{2,1,0:T(8,128)} %all-to-all-done.2.refs_1_, f32[2,288,128]{2,1,0:T(8,128)S(1)} %copy-done.25, f32[1,128]{1,0:T(1,128)S(1)} %get-tuple-element.36.refs_3_), custom_call_target="tpu_custom_call" | custom-call | flops 400000000 | bytes 4000000 | tf_op jit(solution)/shard_map/pallas_call | solution.py:470
  128.5 11.3 %all-to-all-start.3 = ((f32[32,16,128]{2,1,0:T(8,128)}), f32[32,16,128]{2,1,0:T(8,128)S(1)}, u32[]{:S(2)}, u32[]{:S(2)}) async-start(f32[32,16,128]{2,1,0:T(8,128)} %get-tuple-element.38), calls=%async_computation.3 | async-start | bytes 524288 | tf_op jit(solution)/shard_map/all_to_all | solution.py:482
  139.9 1.3 collective-permute-start.9
  141.2 7.1 %collective-permute-start.8 = (f32[48,1024]{1,0:T(8,128)S(1)}, f32[48,1024]{1,0:T(8,128)S(1)}, u32[]{:S(2)}, u32[]{:S(2)}) collective-permute-start(f32[48,1024]{1,0:T(8,128)S(1)} %copy-done.10), channel_id=1, source_target_pairs={{0,2},{1,3},{2,4},{3,5},{4,6},{5,7},{6,8},{7,9},{8,10},{9,11},{10,... | collective-permute-start | bytes 589832 | tf_op jit(solution)/shard_map/ppermute | solution.py:487
  148.3 3.0 %collective-permute-done.9.refs_5_ = f32[48,1024]{1,0:T(8,128)S(1)} collective-permute-done((f32[48,1024]{1,0:T(8,128)S(1)}, f32[48,1024]{1,0:T(8,128)S(1)}, u32[]{:S(2)}, u32[]{:S(2)}) %collective-permute-start.9) | collective-permute-done | bytes 196640 | tf_op jit(solution)/shard_map/ppermute | solution.py:487
  154.9 2.5 shard_map.83.refs_2_
  157.4 4.4 %all-to-all-done.3.refs_1_ = f32[32,16,128]{2,1,0:T(8,128)S(1)} async-done(((f32[32,16,128]{2,1,0:T(8,128)}), f32[32,16,128]{2,1,0:T(8,128)S(1)}, u32[]{:S(2)}, u32[]{:S(2)}) %all-to-all-start.3) | async-done | bytes 262176 | tf_op jit(solution)/shard_map/all_to_all | solution.py:482
  162.5 18.0 %all_to_all.36.rows = f32[16,8,128]{2,1,0:T(8,128)S(1)} all-to-all(f32[16,8,128]{2,1,0:T(8,128)S(1)} %broadcast_in_dim.12), channel_id=1, replica_groups=mesh['gy'=32,'gz_0'=4,'gz_1'=4] {'gz_0','gz_1'}, dimensions={0} | all-to-all | bytes 131072 | tf_op jit(solution)/shard_map/all_to_all | solution.py:503
  180.5 1.3 shard_map.85
  181.9 1.3 collective-permute-start.13
  183.2 1.3 collective-permute-start.12
  184.5 4.0 %collective-permute-start.11 = (f32[48,1024]{1,0:T(8,128)S(1)}, f32[48,1024]{1,0:T(8,128)S(1)}, u32[]{:S(2)}, u32[]{:S(2)}) collective-permute-start(f32[48,1024]{1,0:T(8,128)S(1)} %get-tuple-element.46.refs_6_.refs_8_), channel_id=1, source_target_pairs={{0,1},{1,2},{2,3},{3,4},{4,5},{5,6},{6,7},{7,8},{8,9},{9,10},{10,1... | collective-permute-start | bytes 589832 | tf_op jit(solution)/shard_map/ppermute | solution.py:487
  188.5 5.5 %collective-permute-start.10 = (f32[48,1024]{1,0:T(8,128)S(1)}, f32[48,1024]{1,0:T(8,128)S(1)}, u32[]{:S(2)}, u32[]{:S(2)}) collective-permute-start(f32[48,1024]{1,0:T(8,128)S(1)} %get-tuple-element.46.refs_6_.refs_8_), channel_id=1, source_target_pairs={{0,2},{1,3},{2,4},{3,5},{4,6},{5,7},{6,8},{7,9},{8,10},{9,11},{10,... | collective-permute-start | bytes 589832 | tf_op jit(solution)/shard_map/ppermute | solution.py:487
  194.1 2.6 collective-permute-done.10.refs_4_
  196.6 5.0 %shard_map.86 = (f32[32,1024]{1,0:T(8,128)S(1)}, f32[32,16,128]{2,1,0:T(8,128)}) custom-call(f32[34]{0:T(128)S(1)} %get-tuple-element.45.refs_0_, bf16[2048,512]{1,0:T(8,128)(2,1)S(1)} %copy-done, f32[48,1024]{1,0:T(8,128)S(1)} %shard_map.83.refs_2_, f32[32,1024]{1,0:T(8,128)S(1)} %bitcast.10, f32[48,1024]{1,0:T(8,128)S(1)} %collective-permute-done.10.refs_4_, ...), custom_call_target="tpu_custom_call" | custom-call | flops 400000000 | bytes 4000000 | tf_op jit(solution)/shard_map/pallas_call | solution.py:470
  202.3 13.6 %all-to-all-start.5 = ((f32[32,16,128]{2,1,0:T(8,128)}), f32[32,16,128]{2,1,0:T(8,128)S(1)}, u32[]{:S(2)}, u32[]{:S(2)}) async-start(f32[32,16,128]{2,1,0:T(8,128)} %get-tuple-element.47), calls=%async_computation.5 | async-start | bytes 524288 | tf_op jit(solution)/shard_map/all_to_all | solution.py:482
  215.9 4.5 %shard_map.87 = f32[1,128]{1,0:T(1,128)} custom-call(f32[34]{0:T(128)} %copy-done.19, f32[48,1024]{1,0:T(8,128)} %copy-done.4, f32[48,1024]{1,0:T(8,128)} %copy-done.2, f32[48,1024]{1,0:T(8,128)} %copy-done.3, f32[48,1024]{1,0:T(8,128)} %copy-done.14, f32[48,1024]{1,0:T(8,128)} %copy-done.8, f32[48,1024]{1,0:T(8,128)} %copy-done.12, f32[48,1024]{1,0:T(8,128)} %copy-done.7, ...), custom_call_target="tpu_custom_call" | custom-call | flops 400000000 | bytes 4000000 | tf_op jit(solution)/shard_map/pallas_call | solution.py:470
  220.4 12.1 %psum.14.refs_5_ = f32[1,128]{1,0:T(1,128)S(1)} all-reduce(f32[1,128]{1,0:T(1,128)} %shard_map.87), channel_id=1, replica_groups=mesh['gy'=32,'gz_0'=4,'gz_1'=4] {'gz_1'}, use_global_device_ids=true, to_apply=%region_0.0 | all-reduce | flops 128 | bytes 1024 | tf_op jit(solution)/shard_map/psum | solution.py:595
  232.5 5.4 %all-to-all-done.5.refs_2_ = f32[32,16,128]{2,1,0:T(8,128)S(1)} async-done(((f32[32,16,128]{2,1,0:T(8,128)}), f32[32,16,128]{2,1,0:T(8,128)S(1)}, u32[]{:S(2)}, u32[]{:S(2)}) %all-to-all-start.5) | async-done | bytes 262176 | tf_op jit(solution)/shard_map/all_to_all | solution.py:482
  238.5 1.0 copy-done.23
  239.5 1.0 copy-done.26
  240.5 2.3 shard_map.88
  242.8 30.0 %all_to_all.37.refs_1_ = f32[32,16,128]{2,1,0:T(8,128)S(1)} all-to-all(f32[32,16,128]{2,1,0:T(8,128)S(1)} %shard_map.88), channel_id=1, replica_groups=mesh['gy'=32,'gz_0'=4,'gz_1'=4] {'gy'}, dimensions={0} | all-to-all | bytes 524288 | tf_op jit(solution)/shard_map/all_to_all | solution.py:482
  272.8 1.2 shard_map.89
  274.0 6.7 %psum.15 = f32[1,128]{1,0:T(1,128)S(1)} all-reduce(f32[1,128]{1,0:T(1,128)S(1)} %get-tuple-element.53), channel_id=1, replica_groups=mesh['gy'=32,'gz_0'=4,'gz_1'=4] {'gz_0'}, use_global_device_ids=true, to_apply=%region_1.0 | all-reduce | flops 128 | bytes 1024 | tf_op jit(solution)/shard_map/psum | solution.py:599
  (72 shorter events, 12.5 us)
Async XLA Ops:
  0.6 43.1 %copy-start.21 = (f32[704,128]{1,0:T(8,128)S(1)}, f32[704,128]{1,0:T(8,128)}, u32[]{:S(2)}) copy-start(f32[704,128]{1,0:T(8,128)} %constant.8.clone.refs_0_.refs_1_) | copy-start | bytes 1081348
  0.6 21.3 %copy-start.1 = (f32[1,32,1024]{2,1,0:T(8,128)S(1)}, f32[1,32,1024]{2,1,0:T(8,128)}, u32[]{:S(2)}) copy-start(f32[1,32,1024]{2,1,0:T(8,128)} %param.9) | copy-start | bytes 393220
  5.0 73.6 %copy-start = (bf16[2048,512]{1,0:T(8,128)(2,1)S(1)}, bf16[2048,512]{1,0:T(8,128)(2,1)}, u32[]{:S(2)}) copy-start(bf16[2048,512]{1,0:T(8,128)(2,1)} %constant.7.clone.refs_0_.refs_1_) | copy-start | bytes 6291460
  5.0 38.7 %all-to-all-start = ((f32[32,16,128]{2,1,0:T(8,128)}), f32[32,16,128]{2,1,0:T(8,128)S(1)}, u32[]{:S(2)}, u32[]{:S(2)}) async-start(f32[32,16,128]{2,1,0:T(8,128)} %shard_map.77), calls=%async_computation | async-start | bytes 524288 | tf_op jit(solution)/shard_map/all_to_all | solution.py:482
  22.0 7.0 %collective-permute-start = (f32[8,1024]{1,0:T(8,128)S(1)}, f32[8,1024]{1,0:T(8,128)S(1)}, u32[]{:S(2)}, u32[]{:S(2)}) collective-permute-start(f32[8,1024]{1,0:T(8,128)S(1)} %get-tuple-element.54), channel_id=1, source_target_pairs={{0,16},{16,32},{32,48},{48,64},{64,80},{80,96},{96,112},{112,128},... | collective-permute-start | bytes 98312 | tf_op jit(solution)/shard_map/ppermute | solution.py:496
  25.5 9.6 %collective-permute-start.1 = (f32[8,1024]{1,0:T(8,128)S(1)}, f32[8,1024]{1,0:T(8,128)S(1)}, u32[]{:S(2)}, u32[]{:S(2)}) collective-permute-start(f32[8,1024]{1,0:T(8,128)S(1)} %get-tuple-element.55), channel_id=1, source_target_pairs={{16,0},{32,16},{48,32},{64,48},{80,64},{96,80},{112,96},{128,112},... | collective-permute-start | bytes 98312 | tf_op jit(solution)/shard_map/ppermute | solution.py:497
  35.1 57.6 %copy-start.29 = (f32[3,3,3]{2,1,0:T(4,128)S(1)}, f32[3,3,3]{2,1,0:T(4,128)}, u32[]{:S(2)}) copy-start(f32[3,3,3]{2,1,0:T(4,128)} %param.8) | copy-start | bytes 328
  46.0 0.7 copy-start.24
  79.5 40.8 %copy-start.2 = (f32[48,1024]{1,0:T(8,128)}, f32[48,1024]{1,0:T(8,128)S(1)}, u32[]{:S(2)}) copy-start(f32[48,1024]{1,0:T(8,128)S(1)} %get-tuple-element.31.refs_6_.refs_2_) | copy-start | bytes 589828
  79.5 13.2 %collective-permute-start.5 = (f32[48,1024]{1,0:T(8,128)S(1)}, f32[48,1024]{1,0:T(8,128)S(1)}, u32[]{:S(2)}, u32[]{:S(2)}) collective-permute-start(f32[48,1024]{1,0:T(8,128)S(1)} %get-tuple-element.31.refs_6_.refs_2_), channel_id=1, source_target_pairs={{2,0},{3,1},{4,2},{5,3},{6,4},{7,5},{8,6},{9,7},{10,8},{11,9},{12,... | collective-permute-start | bytes 589832 | tf_op jit(solution)/shard_map/ppermute | solution.py:487
  80.8 11.9 %collective-permute-start.4 = (f32[48,1024]{1,0:T(8,128)S(1)}, f32[48,1024]{1,0:T(8,128)S(1)}, u32[]{:S(2)}, u32[]{:S(2)}) collective-permute-start(f32[48,1024]{1,0:T(8,128)S(1)} %get-tuple-element.31.refs_6_.refs_2_), channel_id=1, source_target_pairs={{1,0},{2,1},{3,2},{4,3},{5,4},{6,5},{7,6},{8,7},{9,8},{10,9},{11,1... | collective-permute-start | bytes 589832 | tf_op jit(solution)/shard_map/ppermute | solution.py:487
  82.1 10.6 %collective-permute-start.3 = (f32[48,1024]{1,0:T(8,128)S(1)}, f32[48,1024]{1,0:T(8,128)S(1)}, u32[]{:S(2)}, u32[]{:S(2)}) collective-permute-start(f32[48,1024]{1,0:T(8,128)S(1)} %get-tuple-element.31.refs_6_.refs_2_), channel_id=1, source_target_pairs={{0,1},{1,2},{2,3},{3,4},{4,5},{5,6},{6,7},{7,8},{8,9},{9,10},{10,1... | collective-permute-start | bytes 589832 | tf_op jit(solution)/shard_map/ppermute | solution.py:487
  86.1 8.9 %collective-permute-start.2 = (f32[48,1024]{1,0:T(8,128)S(1)}, f32[48,1024]{1,0:T(8,128)}, u32[]{:S(2)}, u32[]{:S(2)}) collective-permute-start(f32[48,1024]{1,0:T(8,128)S(1)} %get-tuple-element.31.refs_6_.refs_2_), channel_id=1, source_target_pairs={{0,2},{1,3},{2,4},{3,5},{4,6},{5,7},{6,8},{7,9},{8,10},{9,11},{10,... | collective-permute-start | bytes 589832 | tf_op jit(solution)/shard_map/ppermute | solution.py:487
  92.8 27.5 %copy-start.3 = (f32[48,1024]{1,0:T(8,128)}, f32[48,1024]{1,0:T(8,128)S(1)}, u32[]{:S(2)}) copy-start(f32[48,1024]{1,0:T(8,128)S(1)} %collective-permute-done.4.refs_7_.refs_3_) | copy-start | bytes 589828
  92.8 27.5 %copy-start.4 = (f32[48,1024]{1,0:T(8,128)}, f32[48,1024]{1,0:T(8,128)S(1)}, u32[]{:S(2)}) copy-start(f32[48,1024]{1,0:T(8,128)S(1)} %collective-permute-done.3.refs_5_.refs_1_) | copy-start | bytes 589828
  99.6 0.7 copy-start.8
  100.3 0.7 copy-start.16
  100.9 38.9 %copy-start.10 = (f32[48,1024]{1,0:T(8,128)S(1)}, f32[48,1024]{1,0:T(8,128)}, u32[]{:S(2)}) copy-start(f32[48,1024]{1,0:T(8,128)} %copy-done.8) | copy-start | bytes 589828
  100.9 22.6 %all-to-all-start.2 = ((f32[32,8,128]{2,1,0:T(8,128)}), f32[32,8,128]{2,1,0:T(8,128)}, u32[]{:S(2)}, u32[]{:S(2)}) async-start(f32[32,8,128]{2,1,0:T(8,128)} %get-tuple-element.32), calls=%async_computation.2 | async-start | bytes 262144 | tf_op jit(solution)/shard_map/all_to_all | solution.py:482
  107.3 10.1 %collective-permute-start.7 = (f32[48,1024]{1,0:T(8,128)}, f32[48,1024]{1,0:T(8,128)S(1)}, u32[]{:S(2)}, u32[]{:S(2)}) collective-permute-start(f32[48,1024]{1,0:T(8,128)} %copy-done.8), channel_id=1, source_target_pairs={{1,0},{2,1},{3,2},{4,3},{5,4},{6,5},{7,6},{8,7},{9,8},{10,9},{11,1... | collective-permute-start | bytes 589832 | tf_op jit(solution)/shard_map/ppermute | solution.py:487
  108.6 9.7 %collective-permute-start.6 = (f32[48,1024]{1,0:T(8,128)}, f32[48,1024]{1,0:T(8,128)S(1)}, u32[]{:S(2)}, u32[]{:S(2)}) collective-permute-start(f32[48,1024]{1,0:T(8,128)} %copy-done.8), channel_id=1, source_target_pairs={{0,1},{1,2},{2,3},{3,4},{4,5},{5,6},{6,7},{7,8},{8,9},{9,10},{10,1... | collective-permute-start | bytes 589832 | tf_op jit(solution)/shard_map/ppermute | solution.py:487
  117.4 11.1 %copy-start.12 = (f32[48,1024]{1,0:T(8,128)}, f32[48,1024]{1,0:T(8,128)S(1)}, u32[]{:S(2)}) copy-start(f32[48,1024]{1,0:T(8,128)S(1)} %collective-permute-done.7.refs_4_.refs_6_) | copy-start | bytes 589828
  118.2 0.9 copy-start.9
  120.3 0.7 copy-start.14
  121.0 0.6 copy-start.17
  123.5 1.0 copy-start.22
  124.5 1.0 copy-start.25
  128.5 22.8 %copy-start.27 = (f32[288,128]{1,0:T(8,128)}, f32[288,128]{1,0:T(8,128)S(1)}, u32[]{:S(2)}) copy-start(f32[288,128]{1,0:T(8,128)S(1)} %get-tuple-element.48.refs_4_) | copy-start | bytes 442372
  128.5 33.3 %all-to-all-start.3 = ((f32[32,16,128]{2,1,0:T(8,128)}), f32[32,16,128]{2,1,0:T(8,128)S(1)}, u32[]{:S(2)}, u32[]{:S(2)}) async-start(f32[32,16,128]{2,1,0:T(8,128)} %get-tuple-element.38), calls=%async_computation.3 | async-start | bytes 524288 | tf_op jit(solution)/shard_map/all_to_all | solution.py:482
  139.9 11.4 %collective-permute-start.9 = (f32[48,1024]{1,0:T(8,128)S(1)}, f32[48,1024]{1,0:T(8,128)S(1)}, u32[]{:S(2)}, u32[]{:S(2)}) collective-permute-start(f32[48,1024]{1,0:T(8,128)S(1)} %copy-done.10), channel_id=1, source_target_pairs={{2,0},{3,1},{4,2},{5,3},{6,4},{7,5},{8,6},{9,7},{10,8},{11,9},{12,... | collective-permute-start | bytes 589832 | tf_op jit(solution)/shard_map/ppermute | solution.py:487
  141.2 11.0 %collective-permute-start.8 = (f32[48,1024]{1,0:T(8,128)S(1)}, f32[48,1024]{1,0:T(8,128)S(1)}, u32[]{:S(2)}, u32[]{:S(2)}) collective-permute-start(f32[48,1024]{1,0:T(8,128)S(1)} %copy-done.10), channel_id=1, source_target_pairs={{0,2},{1,3},{2,4},{3,5},{4,6},{5,7},{6,8},{7,9},{8,10},{9,11},{10,... | collective-permute-start | bytes 589832 | tf_op jit(solution)/shard_map/ppermute | solution.py:487
  152.2 0.9 copy-start.11
  153.1 0.9 copy-start.13
  154.0 0.9 copy-start.15
  181.9 34.0 %copy-start.5 = (f32[48,1024]{1,0:T(8,128)}, f32[48,1024]{1,0:T(8,128)S(1)}, u32[]{:S(2)}) copy-start(f32[48,1024]{1,0:T(8,128)S(1)} %get-tuple-element.46.refs_6_.refs_8_) | copy-start | bytes 589828
  181.9 34.0 %copy-start.19 = (f32[34]{0:T(128)}, f32[34]{0:T(128)S(1)}, u32[]{:S(2)}) copy-start(f32[34]{0:T(128)S(1)} %get-tuple-element.45.refs_0_) | copy-start | bytes 412
  181.9 12.1 %collective-permute-start.13 = (f32[48,1024]{1,0:T(8,128)S(1)}, f32[48,1024]{1,0:T(8,128)S(1)}, u32[]{:S(2)}, u32[]{:S(2)}) collective-permute-start(f32[48,1024]{1,0:T(8,128)S(1)} %get-tuple-element.46.refs_6_.refs_8_), channel_id=1, source_target_pairs={{2,0},{3,1},{4,2},{5,3},{6,4},{7,5},{8,6},{9,7},{10,8},{11,9},{12,... | collective-permute-start | bytes 589832 | tf_op jit(solution)/shard_map/ppermute | solution.py:487
  183.2 10.8 %collective-permute-start.12 = (f32[48,1024]{1,0:T(8,128)S(1)}, f32[48,1024]{1,0:T(8,128)S(1)}, u32[]{:S(2)}, u32[]{:S(2)}) collective-permute-start(f32[48,1024]{1,0:T(8,128)S(1)} %get-tuple-element.46.refs_6_.refs_8_), channel_id=1, source_target_pairs={{1,0},{2,1},{3,2},{4,3},{5,4},{6,5},{7,6},{8,7},{9,8},{10,9},{11,1... | collective-permute-start | bytes 589832 | tf_op jit(solution)/shard_map/ppermute | solution.py:487
  184.5 9.5 %collective-permute-start.11 = (f32[48,1024]{1,0:T(8,128)S(1)}, f32[48,1024]{1,0:T(8,128)S(1)}, u32[]{:S(2)}, u32[]{:S(2)}) collective-permute-start(f32[48,1024]{1,0:T(8,128)S(1)} %get-tuple-element.46.refs_6_.refs_8_), channel_id=1, source_target_pairs={{0,1},{1,2},{2,3},{3,4},{4,5},{5,6},{6,7},{7,8},{8,9},{9,10},{10,1... | collective-permute-start | bytes 589832 | tf_op jit(solution)/shard_map/ppermute | solution.py:487
  188.5 8.1 %collective-permute-start.10 = (f32[48,1024]{1,0:T(8,128)S(1)}, f32[48,1024]{1,0:T(8,128)S(1)}, u32[]{:S(2)}, u32[]{:S(2)}) collective-permute-start(f32[48,1024]{1,0:T(8,128)S(1)} %get-tuple-element.46.refs_6_.refs_8_), channel_id=1, source_target_pairs={{0,2},{1,3},{2,4},{3,5},{4,6},{5,7},{6,8},{7,9},{8,10},{9,11},{10,... | collective-permute-start | bytes 589832 | tf_op jit(solution)/shard_map/ppermute | solution.py:487
  194.0 21.9 %copy-start.6 = (f32[48,1024]{1,0:T(8,128)}, f32[48,1024]{1,0:T(8,128)S(1)}, u32[]{:S(2)}) copy-start(f32[48,1024]{1,0:T(8,128)S(1)} %collective-permute-done.12.refs_7_.refs_9_) | copy-start | bytes 589828
  194.1 21.9 %copy-start.7 = (f32[48,1024]{1,0:T(8,128)}, f32[48,1024]{1,0:T(8,128)S(1)}, u32[]{:S(2)}) copy-start(f32[48,1024]{1,0:T(8,128)S(1)} %collective-permute-done.11.refs_5_.refs_7_) | copy-start | bytes 589828
  201.6 0.7 copy-start.18
  202.2 35.6 %copy-start.28 = (f32[288,128]{1,0:T(8,128)S(1)}, f32[288,128]{1,0:T(8,128)}, u32[]{:S(2)}) copy-start(f32[288,128]{1,0:T(8,128)} %copy-done.27) | copy-start | bytes 442372
  202.3 35.6 %all-to-all-start.5 = ((f32[32,16,128]{2,1,0:T(8,128)}), f32[32,16,128]{2,1,0:T(8,128)S(1)}, u32[]{:S(2)}, u32[]{:S(2)}) async-start(f32[32,16,128]{2,1,0:T(8,128)} %get-tuple-element.47), calls=%async_computation.5 | async-start | bytes 524288 | tf_op jit(solution)/shard_map/all_to_all | solution.py:482
  237.9 0.7 copy-start.20
  238.5 1.0 copy-start.23
  239.5 1.0 copy-start.26

commit v7 on v6

--- a/solution.py
+++ b/solution.py
@@ -62,8 +62,7 @@
 def packed_tables():
     first, turn_cos, turn_sin, second = y_tables()
     first = np.pad(first, ((0, 0), (0, 96)))
-    tables = [*split_table(second), *split_table(second.T), *split_table(first)]
-    return np.concatenate([*tables, turn_cos, turn_sin], 0).astype(np.float32)
+    return np.concatenate([second, first, turn_cos, turn_sin], 0).astype(np.float32)
 
 
 X_TABLE = np.concatenate(split_table(x_table()), 0)
@@ -137,13 +136,11 @@
 
 class Lateral:
     def __init__(self, table):
-        def piece(start, count, width):
-            return table[start : start + count, 0:width].astype(BF16)
-
-        self.second = (piece(0, 128, 128), piece(128, 128, 128))
-        self.back = (piece(256, 128, 128), piece(384, 128, 128))
-        self.first = (piece(512, 64, 32), piece(576, 64, 32))
-        self.cos, self.sin = table[640:672, :], table[672:704, :]
+        second = table[0:128, :]
+        self.second = halves(second)
+        self.back = halves(second.T)
+        self.first = halves(table[128:192, :][:, 0:32])
+        self.cos, self.sin = table[192:224, :], table[224:256, :]
         self.is_first = jnp.where(lax.axis_index(GY) == 0, 1.0, 0.0).astype(F32)
         self.sign = jnp.where(lanes((32, 128)) < 64, 1.0, -1.0)
 
@@ -372,19 +369,24 @@
     row_ref[...] = row_of(((0, b * b), (1, b * ab), (2, ab * ab), (4, u * b), (5, u * ab)))
 
 
-def map_kernel(weights, row_b, u1, o, d1, mapped_ref, row_ref, source, whole):
+def map_kernel(weights, row_b, u1, o, d1, mapped_ref, row_ref, source):
     load_planes((u1, o, d1), source)
+    row, lowest, highest, _ = row_bounds()
+    inside = (row >= lowest) & (row < highest)
     for k in range(8):
         cols = slice(128 * k, 128 * k + 128)
-        whole[:, cols] = stencil_sum(weight_of(weights), source, 0, cols)
-    mapped = whole[8:40, :]
-    mapped_ref[...] = mapped
+        mapped_ref[:, cols] = jnp.where(inside, stencil_sum(weight_of(weights), source, 0, cols), 0.0)
+    mapped = mapped_ref[8:40, :]
     row_ref[...] = row_b[...] + row_of(((3, mapped * mapped),))
 
 
-def further_kernel(weights, u2, u1, o, d1, d2, back_ref, source, middle):
-    load_planes((u2, u1, o, d1, d2), source)
-    apply_stencils(weights, source, middle, back_ref)
+def further_kernel(weights, u1, o, d1, back_ref, middle):
+    load_planes((u1, o, d1), middle)
+    row, lowest, highest, _ = row_bounds()
+    inside = (row >= lowest) & (row < highest)
+    for k in range(8):
+        cols = slice(128 * k, 128 * k + 128)
+        back_ref[:, cols] = jnp.where(inside, stencil_sum(flipped_of(weights), middle, 0, cols), 0.0)
 
 
 def last_kernel(
@@ -408,9 +410,9 @@
     g1, twice_g2, twice_g3 = (factor_ref[k] for k in (33, 31, 32))
     for p in range(3):
         scaled[p] = mixed[p][...] + g1 * right[p][...] + twice_g2 * image[p][...]
-    mapped[0] = mixed_map[...] + g1 * right_map[...] + twice_g2 * image_map[...]
+    mapped[0] = mixed_map[...] + g1 * right_map[...] + twice_g2 * image_map[8:40, :]
     mapped[1] = right_map[...]
-    mapped[2] = twice_g3 * image_map[...]
+    mapped[2] = twice_g3 * image_map[8:40, :]
     lane = lanes((1, 128))
     out = jnp.zeros((1, 128), F32)
     column = lanes((ROWS, COLS))
@@ -500,7 +502,7 @@
 
 def from_all(row):
     size = lax.axis_size(GZ)
-    return lax.all_to_all(jnp.broadcast_to(row[None], (size, 8, 128)), GZ, 0, 0, tiled=True)
+    return lax.all_to_all(jnp.broadcast_to(row[None], (size, 1, 128)), GZ, 0, 0, tiled=True)
 
 
 def factors_of(m0, m1, m2, m3, u0, u1):
@@ -518,7 +520,7 @@
 
 
 def factors_kernel(weights_ref, rows, further, grown, out_ref, mixed_ref):
-    total = jnp.sum(rows[:, 0, :], 0, keepdims=True)
+    total = jnp.sum(rows[...], 0)
     lane = lanes((1, 128))
     moments = [jnp.sum(jnp.where(lane == k, total, 0.0), axis=1, keepdims=True) for k in range(6)]
     alpha, gamma, g0, g1, g2, g3 = factors_of(*moments)
@@ -555,16 +557,16 @@
         planes=right_parts,
     )
     image_arrived = exchange(image_send)
-    image_near = (moved(image, 1), image, moved(image, -1))
-    map_scratch = (pltpu.VMEM((3, 3, FRAME, COLS), F32), pltpu.VMEM((FRAME, COLS), F32))
-    image_map, sums = call(map_kernel, (rows, row), [weights], [row_b], map_scratch, planes=image_near)
+    image_parts = (moved(image, 1), image, moved(image, -1))
+    plane_scratch = (pltpu.VMEM((3, 3, FRAME, COLS), F32),)
+    image_map, sums = call(map_kernel, (frame, row), [weights], [row_b], plane_scratch, planes=image_parts)
     further_out, image_spectrum = call(
         second_filter_kernel, (tiles, spectral), [], [along_y, image_arrived, bank, sums]
     )
-    further_out, image_again = lax.optimization_barrier((further_out, image))
+    further_out, image_map = lax.optimization_barrier((further_out, image_map))
     further_arrived = exchange(further_out)
-    image_parts = (moved(image_again, 2), *image_near, moved(image_again, -2))
-    image_back = call(further_kernel, frame, [weights], [], STENCIL_SCRATCH, planes=image_parts)
+    map_parts = (moved(image_map, 1), image_map, moved(image_map, -1))
+    image_back = call(further_kernel, frame, [weights], [], plane_scratch, planes=map_parts)
     further_arrived, image_back = lax.optimization_barrier((further_arrived, image_back))
 
     further, row_sum = call(gather_sum_kernel, (frame, row), [], [table, further_arrived, image_back])
@@ -586,10 +588,7 @@
         STENCIL_SCRATCH + BACK_SCRATCH,
         planes=mixed_parts,
     )
-    operands = []
-    for parts in (right_parts, image_parts, mixed_parts):
-        operands += parts[1:4]
-    operands += [right_map, image_map, mixed_map]
+    operands = [*right_parts[1:4], *image_parts, *mixed_parts[1:4], right_map, image_map, mixed_map]
     scratch = (pltpu.VMEM((3, FRAME, COLS), F32), pltpu.VMEM((3, ROWS, COLS), F32))
     terms = call(correlate_kernel, row, [factors], operands, scratch, far=tuple(range(12)), limit=ALL_VMEM)
     terms = lax.psum(terms, "gz_1")

time: 284 us -> 276 us (0.972)
  starting transfers between devices: 94.1 us -> 85.5 us
  waiting for transfers between devices: 40.8 us -> 47.1 us
  local copies, waits for them, and re-layouts: 13.1 us -> 9.53 us
    all_to_all x4, waiting for transfers between devices: 20.3 us -> 26.4 us  [exchange(): return lax.all_to_all(value, GY, 0, 0, tiled=True)]
    all_to_all x4, starting transfers between devices: 48.2 us -> 42.1 us  [exchange(): return lax.all_to_all(value, GY, 0, 0, tiled=True)]
    unnamed x60 -> x50, local copies, waits for them, and re-layouts: 12.3 us -> 8.75 us
  transfers between devices with their start and end apart: 18 -> 18, of which waited for: 12 -> 12; matrix products, arithmetic and copies ran while one was open for 0% -> 0% of each run, Pallas kernels for 3% -> 2%
where the time goes in v7:
time: 276 us; the launch traced here: 274 us
  blocking collectives  98.8 us (36%)
  starting transfers between devices  85.5 us (31%)
  waiting for transfers between devices  47.1 us (17%)
  Pallas kernels  32.2 us (12%)
  local copies, waits for them, and re-layouts  9.53 us (3%)
    all_to_all x2, blocking collectives, exchange(): return lax.all_to_all(value, GY, 0, 0, tiled=True)  62 us
    all_to_all x4, starting transfers between devices, exchange(): return lax.all_to_all(value, GY, 0, 0, tiled=True)  42.1 us
    ppermute x12, starting transfers between devices, moved(): lax.ppermute(value, GZ, [(i, i + by) for i in range(size) if 0 <= i + by...  37.9 us
    pallas_call x12, Pallas kernels, call(): pl.pallas_call(whole, out_shape=out_shape, in_specs=spec_in, out_specs=sp...  30.9 us
    all_to_all x4, waiting for transfers between devices, exchange(): return lax.all_to_all(value, GY, 0, 0, tiled=True)  26.4 us
    all_to_all x1, blocking collectives, from_all(): lax.all_to_all(jnp.broadcast_to(row[None], (size, 1, 128)), GZ, 0, 0, til...  17.9 us
    ppermute x12, waiting for transfers between devices, moved(): lax.ppermute(value, GZ, [(i, i + by) for i in range(size) if 0 <= i + by...  13 us
    psum x1, blocking collectives, local(): terms = lax.psum(terms, 'gz_1')  12.1 us
  transfers between devices with their start and end apart: 18, of which 12 were waited for; matrix products, arithmetic and copies ran while one was open for 0% of the time, Pallas kernels for 2%

profile of v7, /device:TPU:1, one launch (start us, length us, event | category | flops | bytes accessed | tf_op | source)
XLA Modules:
  0.0 274.2 jit_solution(13473128606567378935)
XLA Ops:
  0.7 4.4 %shard_map.77 = f32[32,16,128]{2,1,0:T(8,128)} custom-call(bf16[2048,512]{1,0:T(8,128)(2,1)} %constant.7.clone.refs_0_.refs_1_, f32[32,1024]{1,0:T(8,128)} %bitcast.12, f32[32,1024]{1,0:T(8,128)} %refs_2_.1), custom_call_target="tpu_custom_call" | custom-call | flops 400000000 | bytes 4000000 | tf_op jit(solution)/shard_map/pallas_call | solution.py:472
  5.0 16.9 %all-to-all-start = ((f32[32,16,128]{2,1,0:T(8,128)}), f32[32,16,128]{2,1,0:T(8,128)S(1)}, u32[]{:S(2)}, u32[]{:S(2)}) async-start(f32[32,16,128]{2,1,0:T(8,128)} %shard_map.77), calls=%async_computation | async-start | bytes 524288 | tf_op jit(solution)/shard_map/all_to_all | solution.py:484
  22.0 3.5 %collective-permute-start = (f32[8,1024]{1,0:T(8,128)S(1)}, f32[8,1024]{1,0:T(8,128)S(1)}, u32[]{:S(2)}, u32[]{:S(2)}) collective-permute-start(f32[8,1024]{1,0:T(8,128)S(1)} %get-tuple-element.54), channel_id=1, source_target_pairs={{0,16},{16,32},{32,48},{48,64},{64,80},{80,96},{96,112},{112,128},... | collective-permute-start | bytes 98312 | tf_op jit(solution)/shard_map/ppermute | solution.py:498
  25.5 1.9 collective-permute-start.1
  27.4 1.5 collective-permute-done
  28.9 6.2 %collective-permute-done.1 = f32[8,1024]{1,0:T(8,128)S(1)} collective-permute-done((f32[8,1024]{1,0:T(8,128)S(1)}, f32[8,1024]{1,0:T(8,128)S(1)}, u32[]{:S(2)}, u32[]{:S(2)}) %collective-permute-start.1) | collective-permute-done | bytes 32800 | tf_op jit(solution)/shard_map/ppermute | solution.py:499
  35.1 8.6 %all-to-all-done.refs_1_ = f32[32,16,128]{2,1,0:T(8,128)S(1)} async-done(((f32[32,16,128]{2,1,0:T(8,128)}), f32[32,16,128]{2,1,0:T(8,128)S(1)}, u32[]{:S(2)}, u32[]{:S(2)}) %all-to-all-start) | async-done | bytes 262176 | tf_op jit(solution)/shard_map/all_to_all | solution.py:484
  43.8 2.2 shard_map.78
  46.7 32.0 %all_to_all.35.refs_1_ = f32[32,24,128]{2,1,0:T(8,128)S(1)} all-to-all(f32[32,24,128]{2,1,0:T(8,128)S(1)} %get-tuple-element.29), channel_id=1, replica_groups=mesh['gy'=32,'gz_0'=4,'gz_1'=4] {'gy'}, dimensions={0} | all-to-all | bytes 786432 | tf_op jit(solution)/shard_map/all_to_all | solution.py:484
  79.6 1.3 collective-permute-start.5
  80.9 1.3 collective-permute-start.4
  82.2 4.0 %collective-permute-start.3 = (f32[48,1024]{1,0:T(8,128)S(1)}, f32[48,1024]{1,0:T(8,128)S(1)}, u32[]{:S(2)}, u32[]{:S(2)}) collective-permute-start(f32[48,1024]{1,0:T(8,128)S(1)} %get-tuple-element.31.refs_6_.refs_2_), channel_id=1, source_target_pairs={{0,1},{1,2},{2,3},{3,4},{4,5},{5,6},{6,7},{7,8},{8,9},{9,10},{10,1... | collective-permute-start | bytes 589832 | tf_op jit(solution)/shard_map/ppermute | solution.py:489
  86.2 6.5 %collective-permute-start.2 = (f32[48,1024]{1,0:T(8,128)S(1)}, f32[48,1024]{1,0:T(8,128)}, u32[]{:S(2)}, u32[]{:S(2)}) collective-permute-start(f32[48,1024]{1,0:T(8,128)S(1)} %get-tuple-element.31.refs_6_.refs_2_), channel_id=1, source_target_pairs={{0,2},{1,3},{2,4},{3,5},{4,6},{5,7},{6,8},{7,9},{8,10},{9,11},{10,... | collective-permute-start | bytes 589832 | tf_op jit(solution)/shard_map/ppermute | solution.py:489
  92.9 2.2 collective-permute-done.2.refs_4_
  95.1 4.6 %shard_map.80 = (f32[48,1024]{1,0:T(8,128)S(1)}, f32[32,1024]{1,0:T(8,128)S(1)}, f32[32,8,128]{2,1,0:T(8,128)}, f32[1,128]{1,0:T(1,128)S(1)}) custom-call(f32[27]{0:T(128)S(1)} %reshape.14.refs_0_.weights_ref, bf16[2048,512]{1,0:T(8,128)(2,1)S(1)} %copy-done, f32[48,1024]{1,0:T(8,128)S(1)} %get-tuple-element.30.refs_2_, f32[32,1024]{1,0:T(8,128)S(1)} %bitcast.9, ...), custom_call_target="tpu_custom_call" | custom-call | flops 400000000 | bytes 4000000 | tf_op jit(solution)/shard_map/pallas_call | solution.py:472
  101.0 6.2 %all-to-all-start.2 = ((f32[32,8,128]{2,1,0:T(8,128)}), f32[32,8,128]{2,1,0:T(8,128)}, u32[]{:S(2)}, u32[]{:S(2)}) async-start(f32[32,8,128]{2,1,0:T(8,128)} %get-tuple-element.32), calls=%async_computation.2 | async-start | bytes 262144 | tf_op jit(solution)/shard_map/all_to_all | solution.py:484
  107.2 1.3 collective-permute-start.7
  108.5 5.5 %collective-permute-start.6 = (f32[48,1024]{1,0:T(8,128)}, f32[48,1024]{1,0:T(8,128)S(1)}, u32[]{:S(2)}, u32[]{:S(2)}) collective-permute-start(f32[48,1024]{1,0:T(8,128)} %copy-done.8), channel_id=1, source_target_pairs={{0,1},{1,2},{2,3},{3,4},{4,5},{5,6},{6,7},{7,8},{8,9},{9,10},{10,1... | collective-permute-start | bytes 589832 | tf_op jit(solution)/shard_map/ppermute | solution.py:489
  114.0 3.3 %collective-permute-done.7.refs_4_.refs_6_ = f32[48,1024]{1,0:T(8,128)S(1)} collective-permute-done((f32[48,1024]{1,0:T(8,128)}, f32[48,1024]{1,0:T(8,128)S(1)}, u32[]{:S(2)}, u32[]{:S(2)}) %collective-permute-start.7) | collective-permute-done | bytes 196640 | tf_op jit(solution)/shard_map/ppermute | solution.py:489
  118.1 0.9 copy-done.9
  119.1 1.2 shard_map.81
  121.0 2.4 all-to-all-done.2.refs_1_
  123.4 1.0 copy-done.20
  124.4 3.1 %shard_map.82 = (f32[32,16,128]{2,1,0:T(8,128)}, f32[288,128]{1,0:T(8,128)S(1)}) custom-call(f32[256,128]{1,0:T(8,128)S(1)} %copy-done.18, f32[32,8,128]{2,1,0:T(8,128)} %all-to-all-done.2.refs_1_, f32[2,288,128]{2,1,0:T(8,128)S(1)} %copy-done.20, f32[1,128]{1,0:T(1,128)S(1)} %get-tuple-element.36.refs_3_), custom_call_target="tpu_custom_call" | custom-call | flops 400000000 | bytes 4000000 | tf_op jit(solution)/shard_map/pallas_call | solution.py:472
  127.4 10.8 %all-to-all-start.3 = ((f32[32,16,128]{2,1,0:T(8,128)}), f32[32,16,128]{2,1,0:T(8,128)S(1)}, u32[]{:S(2)}, u32[]{:S(2)}) async-start(f32[32,16,128]{2,1,0:T(8,128)} %get-tuple-element.39), calls=%async_computation.3 | async-start | bytes 524288 | tf_op jit(solution)/shard_map/all_to_all | solution.py:484
  138.3 1.3 collective-permute-start.9
  139.6 4.6 %collective-permute-start.8 = (f32[48,1024]{1,0:T(8,128)S(1)}, f32[48,1024]{1,0:T(8,128)S(1)}, u32[]{:S(2)}, u32[]{:S(2)}) collective-permute-start(f32[48,1024]{1,0:T(8,128)S(1)} %get-tuple-element.40.refs_2_.refs_11_), channel_id=1, source_target_pairs={{0,1},{1,2},{2,3},{3,4},{4,5},{5,6},{6,7},{7,8},{8,9},{9,10},{10,1... | collective-permute-start | bytes 589832 | tf_op jit(solution)/shard_map/ppermute | solution.py:489
  144.2 3.2 %collective-permute-done.9.refs_3_ = f32[48,1024]{1,0:T(8,128)S(1)} collective-permute-done((f32[48,1024]{1,0:T(8,128)S(1)}, f32[48,1024]{1,0:T(8,128)S(1)}, u32[]{:S(2)}, u32[]{:S(2)}) %collective-permute-start.9) | collective-permute-done | bytes 196640 | tf_op jit(solution)/shard_map/ppermute | solution.py:489
  148.3 0.9 copy-done.13
  149.2 1.1 shard_map.83.refs_2_
  150.3 10.0 %all-to-all-done.3.refs_1_ = f32[32,16,128]{2,1,0:T(8,128)S(1)} async-done(((f32[32,16,128]{2,1,0:T(8,128)}), f32[32,16,128]{2,1,0:T(8,128)S(1)}, u32[]{:S(2)}, u32[]{:S(2)}) %all-to-all-start.3) | async-done | bytes 262176 | tf_op jit(solution)/shard_map/all_to_all | solution.py:484
  160.9 17.9 %all_to_all.36.rows = f32[16,1,128]{2,1,0:T(1,128)S(1)} all-to-all(f32[16,1,128]{2,1,0:T(1,128)S(1)} %broadcast_in_dim.12), channel_id=1, replica_groups=mesh['gy'=32,'gz_0'=4,'gz_1'=4] {'gz_0','gz_1'}, dimensions={0} | all-to-all | bytes 16384 | tf_op jit(solution)/shard_map/all_to_all | solution.py:505
  178.9 1.3 shard_map.85
  180.2 1.3 collective-permute-start.13
  181.5 1.3 collective-permute-start.12
  182.8 4.0 %collective-permute-start.11 = (f32[48,1024]{1,0:T(8,128)S(1)}, f32[48,1024]{1,0:T(8,128)S(1)}, u32[]{:S(2)}, u32[]{:S(2)}) collective-permute-start(f32[48,1024]{1,0:T(8,128)S(1)} %get-tuple-element.47.refs_6_.refs_8_), channel_id=1, source_target_pairs={{0,1},{1,2},{2,3},{3,4},{4,5},{5,6},{6,7},{7,8},{8,9},{9,10},{10,1... | collective-permute-start | bytes 589832 | tf_op jit(solution)/shard_map/ppermute | solution.py:489
  186.8 5.5 %collective-permute-start.10 = (f32[48,1024]{1,0:T(8,128)S(1)}, f32[48,1024]{1,0:T(8,128)S(1)}, u32[]{:S(2)}, u32[]{:S(2)}) collective-permute-start(f32[48,1024]{1,0:T(8,128)S(1)} %get-tuple-element.47.refs_6_.refs_8_), channel_id=1, source_target_pairs={{0,2},{1,3},{2,4},{3,5},{4,6},{5,7},{6,8},{7,9},{8,10},{9,11},{10,... | collective-permute-start | bytes 589832 | tf_op jit(solution)/shard_map/ppermute | solution.py:489
  192.4 2.6 collective-permute-done.10.refs_4_
  195.0 5.0 %shard_map.86 = (f32[32,1024]{1,0:T(8,128)S(1)}, f32[32,16,128]{2,1,0:T(8,128)}) custom-call(f32[34]{0:T(128)S(1)} %get-tuple-element.46.refs_0_, bf16[2048,512]{1,0:T(8,128)(2,1)S(1)} %copy-done, f32[48,1024]{1,0:T(8,128)S(1)} %shard_map.83.refs_2_, f32[32,1024]{1,0:T(8,128)S(1)} %bitcast.10, f32[48,1024]{1,0:T(8,128)S(1)} %collective-permute-done.10.refs_4_, ...), custom_call_target="tpu_custom_call" | custom-call | flops 400000000 | bytes 4000000 | tf_op jit(solution)/shard_map/pallas_call | solution.py:472
  200.6 8.2 %all-to-all-start.5 = ((f32[32,16,128]{2,1,0:T(8,128)}), f32[32,16,128]{2,1,0:T(8,128)S(1)}, u32[]{:S(2)}, u32[]{:S(2)}) async-start(f32[32,16,128]{2,1,0:T(8,128)} %get-tuple-element.48), calls=%async_computation.5 | async-start | bytes 524288 | tf_op jit(solution)/shard_map/all_to_all | solution.py:484
  208.8 4.4 %shard_map.87 = f32[1,128]{1,0:T(1,128)} custom-call(f32[34]{0:T(128)} %copy-done.16, f32[48,1024]{1,0:T(8,128)} %copy-done.4, f32[48,1024]{1,0:T(8,128)} %copy-done.2, f32[48,1024]{1,0:T(8,128)} %copy-done.3, f32[48,1024]{1,0:T(8,128)} %copy-done.11, f32[48,1024]{1,0:T(8,128)} %copy-done.8, f32[48,1024]{1,0:T(8,128)} %copy-done.10, f32[48,1024]{1,0:T(8,128)} %copy-done.7, ...), custom_call_target="tpu_custom_call" | custom-call | flops 400000000 | bytes 4000000 | tf_op jit(solution)/shard_map/pallas_call | solution.py:472
  213.2 12.1 %psum.14.refs_5_ = f32[1,128]{1,0:T(1,128)S(1)} all-reduce(f32[1,128]{1,0:T(1,128)} %shard_map.87), channel_id=1, replica_groups=mesh['gy'=32,'gz_0'=4,'gz_1'=4] {'gz_1'}, use_global_device_ids=true, to_apply=%region_0.0 | all-reduce | flops 128 | bytes 1024 | tf_op jit(solution)/shard_map/psum | solution.py:594
  225.4 5.4 %all-to-all-done.5.refs_2_ = f32[32,16,128]{2,1,0:T(8,128)S(1)} async-done(((f32[32,16,128]{2,1,0:T(8,128)}), f32[32,16,128]{2,1,0:T(8,128)S(1)}, u32[]{:S(2)}, u32[]{:S(2)}) %all-to-all-start.5) | async-done | bytes 262176 | tf_op jit(solution)/shard_map/all_to_all | solution.py:484
  231.4 1.0 copy-done.21
  233.3 2.3 shard_map.88
  235.6 30.0 %all_to_all.37.refs_1_ = f32[32,16,128]{2,1,0:T(8,128)S(1)} all-to-all(f32[32,16,128]{2,1,0:T(8,128)S(1)} %shard_map.88), channel_id=1, replica_groups=mesh['gy'=32,'gz_0'=4,'gz_1'=4] {'gy'}, dimensions={0} | all-to-all | bytes 524288 | tf_op jit(solution)/shard_map/all_to_all | solution.py:484
  265.6 1.2 shard_map.89
  266.8 6.7 %psum.15 = f32[1,128]{1,0:T(1,128)S(1)} all-reduce(f32[1,128]{1,0:T(1,128)S(1)} %get-tuple-element.53), channel_id=1, replica_groups=mesh['gy'=32,'gz_0'=4,'gz_1'=4] {'gz_0'}, use_global_device_ids=true, to_apply=%region_1.0 | all-reduce | flops 128 | bytes 1024 | tf_op jit(solution)/shard_map/psum | solution.py:598
  (62 shorter events, 9.0 us)
Async XLA Ops:
  0.6 43.1 %copy-start.18 = (f32[256,128]{1,0:T(8,128)S(1)}, f32[256,128]{1,0:T(8,128)}, u32[]{:S(2)}) copy-start(f32[256,128]{1,0:T(8,128)} %constant.8.clone.refs_0_.refs_1_) | copy-start | bytes 393220
  0.6 21.3 %copy-start.1 = (f32[1,32,1024]{2,1,0:T(8,128)S(1)}, f32[1,32,1024]{2,1,0:T(8,128)}, u32[]{:S(2)}) copy-start(f32[1,32,1024]{2,1,0:T(8,128)} %param.9) | copy-start | bytes 393220
  5.0 73.7 %copy-start = (bf16[2048,512]{1,0:T(8,128)(2,1)S(1)}, bf16[2048,512]{1,0:T(8,128)(2,1)}, u32[]{:S(2)}) copy-start(bf16[2048,512]{1,0:T(8,128)(2,1)} %constant.7.clone.refs_0_.refs_1_) | copy-start | bytes 6291460
  5.0 38.7 %all-to-all-start = ((f32[32,16,128]{2,1,0:T(8,128)}), f32[32,16,128]{2,1,0:T(8,128)S(1)}, u32[]{:S(2)}, u32[]{:S(2)}) async-start(f32[32,16,128]{2,1,0:T(8,128)} %shard_map.77), calls=%async_computation | async-start | bytes 524288 | tf_op jit(solution)/shard_map/all_to_all | solution.py:484
  22.0 7.0 %collective-permute-start = (f32[8,1024]{1,0:T(8,128)S(1)}, f32[8,1024]{1,0:T(8,128)S(1)}, u32[]{:S(2)}, u32[]{:S(2)}) collective-permute-start(f32[8,1024]{1,0:T(8,128)S(1)} %get-tuple-element.54), channel_id=1, source_target_pairs={{0,16},{16,32},{32,48},{48,64},{64,80},{80,96},{96,112},{112,128},... | collective-permute-start | bytes 98312 | tf_op jit(solution)/shard_map/ppermute | solution.py:498
  25.5 9.6 %collective-permute-start.1 = (f32[8,1024]{1,0:T(8,128)S(1)}, f32[8,1024]{1,0:T(8,128)S(1)}, u32[]{:S(2)}, u32[]{:S(2)}) collective-permute-start(f32[8,1024]{1,0:T(8,128)S(1)} %get-tuple-element.55), channel_id=1, source_target_pairs={{16,0},{32,16},{48,32},{64,48},{80,64},{96,80},{112,96},{128,112},... | collective-permute-start | bytes 98312 | tf_op jit(solution)/shard_map/ppermute | solution.py:499
  35.1 57.6 %copy-start.24 = (f32[3,3,3]{2,1,0:T(4,128)S(1)}, f32[3,3,3]{2,1,0:T(4,128)}, u32[]{:S(2)}) copy-start(f32[3,3,3]{2,1,0:T(4,128)} %param.8) | copy-start | bytes 328
  46.0 0.7 copy-start.19
  79.6 40.7 %copy-start.2 = (f32[48,1024]{1,0:T(8,128)}, f32[48,1024]{1,0:T(8,128)S(1)}, u32[]{:S(2)}) copy-start(f32[48,1024]{1,0:T(8,128)S(1)} %get-tuple-element.31.refs_6_.refs_2_) | copy-start | bytes 589828
  79.6 13.2 %collective-permute-start.5 = (f32[48,1024]{1,0:T(8,128)S(1)}, f32[48,1024]{1,0:T(8,128)S(1)}, u32[]{:S(2)}, u32[]{:S(2)}) collective-permute-start(f32[48,1024]{1,0:T(8,128)S(1)} %get-tuple-element.31.refs_6_.refs_2_), channel_id=1, source_target_pairs={{2,0},{3,1},{4,2},{5,3},{6,4},{7,5},{8,6},{9,7},{10,8},{11,9},{12,... | collective-permute-start | bytes 589832 | tf_op jit(solution)/shard_map/ppermute | solution.py:489
  80.9 11.9 %collective-permute-start.4 = (f32[48,1024]{1,0:T(8,128)S(1)}, f32[48,1024]{1,0:T(8,128)S(1)}, u32[]{:S(2)}, u32[]{:S(2)}) collective-permute-start(f32[48,1024]{1,0:T(8,128)S(1)} %get-tuple-element.31.refs_6_.refs_2_), channel_id=1, source_target_pairs={{1,0},{2,1},{3,2},{4,3},{5,4},{6,5},{7,6},{8,7},{9,8},{10,9},{11,1... | collective-permute-start | bytes 589832 | tf_op jit(solution)/shard_map/ppermute | solution.py:489
  82.2 10.7 %collective-permute-start.3 = (f32[48,1024]{1,0:T(8,128)S(1)}, f32[48,1024]{1,0:T(8,128)S(1)}, u32[]{:S(2)}, u32[]{:S(2)}) collective-permute-start(f32[48,1024]{1,0:T(8,128)S(1)} %get-tuple-element.31.refs_6_.refs_2_), channel_id=1, source_target_pairs={{0,1},{1,2},{2,3},{3,4},{4,5},{5,6},{6,7},{7,8},{8,9},{9,10},{10,1... | collective-permute-start | bytes 589832 | tf_op jit(solution)/shard_map/ppermute | solution.py:489
  86.2 8.9 %collective-permute-start.2 = (f32[48,1024]{1,0:T(8,128)S(1)}, f32[48,1024]{1,0:T(8,128)}, u32[]{:S(2)}, u32[]{:S(2)}) collective-permute-start(f32[48,1024]{1,0:T(8,128)S(1)} %get-tuple-element.31.refs_6_.refs_2_), channel_id=1, source_target_pairs={{0,2},{1,3},{2,4},{3,5},{4,6},{5,7},{6,8},{7,9},{8,10},{9,11},{10,... | collective-permute-start | bytes 589832 | tf_op jit(solution)/shard_map/ppermute | solution.py:489
  92.8 27.5 %copy-start.3 = (f32[48,1024]{1,0:T(8,128)}, f32[48,1024]{1,0:T(8,128)S(1)}, u32[]{:S(2)}) copy-start(f32[48,1024]{1,0:T(8,128)S(1)} %collective-permute-done.4.refs_7_.refs_3_) | copy-start | bytes 589828
  92.9 27.5 %copy-start.4 = (f32[48,1024]{1,0:T(8,128)}, f32[48,1024]{1,0:T(8,128)S(1)}, u32[]{:S(2)}) copy-start(f32[48,1024]{1,0:T(8,128)S(1)} %collective-permute-done.3.refs_5_.refs_1_) | copy-start | bytes 589828
  99.6 0.7 copy-start.8
  100.3 0.7 copy-start.14
  101.0 22.5 %all-to-all-start.2 = ((f32[32,8,128]{2,1,0:T(8,128)}), f32[32,8,128]{2,1,0:T(8,128)}, u32[]{:S(2)}, u32[]{:S(2)}) async-start(f32[32,8,128]{2,1,0:T(8,128)} %get-tuple-element.32), calls=%async_computation.2 | async-start | bytes 262144 | tf_op jit(solution)/shard_map/all_to_all | solution.py:484
  107.2 10.1 %collective-permute-start.7 = (f32[48,1024]{1,0:T(8,128)}, f32[48,1024]{1,0:T(8,128)S(1)}, u32[]{:S(2)}, u32[]{:S(2)}) collective-permute-start(f32[48,1024]{1,0:T(8,128)} %copy-done.8), channel_id=1, source_target_pairs={{1,0},{2,1},{3,2},{4,3},{5,4},{6,5},{7,6},{8,7},{9,8},{10,9},{11,1... | collective-permute-start | bytes 589832 | tf_op jit(solution)/shard_map/ppermute | solution.py:489
  108.5 9.6 %collective-permute-start.6 = (f32[48,1024]{1,0:T(8,128)}, f32[48,1024]{1,0:T(8,128)S(1)}, u32[]{:S(2)}, u32[]{:S(2)}) collective-permute-start(f32[48,1024]{1,0:T(8,128)} %copy-done.8), channel_id=1, source_target_pairs={{0,1},{1,2},{2,3},{3,4},{4,5},{5,6},{6,7},{7,8},{8,9},{9,10},{10,1... | collective-permute-start | bytes 589832 | tf_op jit(solution)/shard_map/ppermute | solution.py:489
  117.3 10.2 %copy-start.10 = (f32[48,1024]{1,0:T(8,128)}, f32[48,1024]{1,0:T(8,128)S(1)}, u32[]{:S(2)}) copy-start(f32[48,1024]{1,0:T(8,128)S(1)} %collective-permute-done.7.refs_4_.refs_6_) | copy-start | bytes 589828
  118.1 0.9 copy-start.9
  120.3 0.7 copy-start.11
  121.0 26.4 %copy-start.12 = (f32[48,1024]{1,0:T(8,128)}, f32[48,1024]{1,0:T(8,128)S(1)}, u32[]{:S(2)}) copy-start(f32[48,1024]{1,0:T(8,128)S(1)} %get-tuple-element.40.refs_2_.refs_11_) | copy-start | bytes 589828
  123.4 1.0 copy-start.20
  127.4 20.0 %copy-start.22 = (f32[288,128]{1,0:T(8,128)}, f32[288,128]{1,0:T(8,128)S(1)}, u32[]{:S(2)}) copy-start(f32[288,128]{1,0:T(8,128)S(1)} %get-tuple-element.49.refs_4_) | copy-start | bytes 442372
  127.4 32.8 %all-to-all-start.3 = ((f32[32,16,128]{2,1,0:T(8,128)}), f32[32,16,128]{2,1,0:T(8,128)S(1)}, u32[]{:S(2)}, u32[]{:S(2)}) async-start(f32[32,16,128]{2,1,0:T(8,128)} %get-tuple-element.39), calls=%async_computation.3 | async-start | bytes 524288 | tf_op jit(solution)/shard_map/all_to_all | solution.py:484
  138.3 9.1 %collective-permute-start.9 = (f32[48,1024]{1,0:T(8,128)S(1)}, f32[48,1024]{1,0:T(8,128)S(1)}, u32[]{:S(2)}, u32[]{:S(2)}) collective-permute-start(f32[48,1024]{1,0:T(8,128)S(1)} %get-tuple-element.40.refs_2_.refs_11_), channel_id=1, source_target_pairs={{1,0},{2,1},{3,2},{4,3},{5,4},{6,5},{7,6},{8,7},{9,8},{10,9},{11,1... | collective-permute-start | bytes 589832 | tf_op jit(solution)/shard_map/ppermute | solution.py:489
  139.6 8.7 %collective-permute-start.8 = (f32[48,1024]{1,0:T(8,128)S(1)}, f32[48,1024]{1,0:T(8,128)S(1)}, u32[]{:S(2)}, u32[]{:S(2)}) collective-permute-start(f32[48,1024]{1,0:T(8,128)S(1)} %get-tuple-element.40.refs_2_.refs_11_), channel_id=1, source_target_pairs={{0,1},{1,2},{2,3},{3,4},{4,5},{5,6},{6,7},{7,8},{8,9},{9,10},{10,1... | collective-permute-start | bytes 589832 | tf_op jit(solution)/shard_map/ppermute | solution.py:489
  148.3 0.9 copy-start.13
  180.2 28.6 %copy-start.5 = (f32[48,1024]{1,0:T(8,128)}, f32[48,1024]{1,0:T(8,128)S(1)}, u32[]{:S(2)}) copy-start(f32[48,1024]{1,0:T(8,128)S(1)} %get-tuple-element.47.refs_6_.refs_8_) | copy-start | bytes 589828
  180.2 28.6 %copy-start.16 = (f32[34]{0:T(128)}, f32[34]{0:T(128)S(1)}, u32[]{:S(2)}) copy-start(f32[34]{0:T(128)S(1)} %get-tuple-element.46.refs_0_) | copy-start | bytes 412
  180.2 12.1 %collective-permute-start.13 = (f32[48,1024]{1,0:T(8,128)S(1)}, f32[48,1024]{1,0:T(8,128)S(1)}, u32[]{:S(2)}, u32[]{:S(2)}) collective-permute-start(f32[48,1024]{1,0:T(8,128)S(1)} %get-tuple-element.47.refs_6_.refs_8_), channel_id=1, source_target_pairs={{2,0},{3,1},{4,2},{5,3},{6,4},{7,5},{8,6},{9,7},{10,8},{11,9},{12,... | collective-permute-start | bytes 589832 | tf_op jit(solution)/shard_map/ppermute | solution.py:489
  181.5 10.8 %collective-permute-start.12 = (f32[48,1024]{1,0:T(8,128)S(1)}, f32[48,1024]{1,0:T(8,128)S(1)}, u32[]{:S(2)}, u32[]{:S(2)}) collective-permute-start(f32[48,1024]{1,0:T(8,128)S(1)} %get-tuple-element.47.refs_6_.refs_8_), channel_id=1, source_target_pairs={{1,0},{2,1},{3,2},{4,3},{5,4},{6,5},{7,6},{8,7},{9,8},{10,9},{11,1... | collective-permute-start | bytes 589832 | tf_op jit(solution)/shard_map/ppermute | solution.py:489
  182.8 9.5 %collective-permute-start.11 = (f32[48,1024]{1,0:T(8,128)S(1)}, f32[48,1024]{1,0:T(8,128)S(1)}, u32[]{:S(2)}, u32[]{:S(2)}) collective-permute-start(f32[48,1024]{1,0:T(8,128)S(1)} %get-tuple-element.47.refs_6_.refs_8_), channel_id=1, source_target_pairs={{0,1},{1,2},{2,3},{3,4},{4,5},{5,6},{6,7},{7,8},{8,9},{9,10},{10,1... | collective-permute-start | bytes 589832 | tf_op jit(solution)/shard_map/ppermute | solution.py:489
  186.8 8.1 %collective-permute-start.10 = (f32[48,1024]{1,0:T(8,128)S(1)}, f32[48,1024]{1,0:T(8,128)S(1)}, u32[]{:S(2)}, u32[]{:S(2)}) collective-permute-start(f32[48,1024]{1,0:T(8,128)S(1)} %get-tuple-element.47.refs_6_.refs_8_), channel_id=1, source_target_pairs={{0,2},{1,3},{2,4},{3,5},{4,6},{5,7},{6,8},{7,9},{8,10},{9,11},{10,... | collective-permute-start | bytes 589832 | tf_op jit(solution)/shard_map/ppermute | solution.py:489
  192.3 16.4 %copy-start.6 = (f32[48,1024]{1,0:T(8,128)}, f32[48,1024]{1,0:T(8,128)S(1)}, u32[]{:S(2)}) copy-start(f32[48,1024]{1,0:T(8,128)S(1)} %collective-permute-done.12.refs_7_.refs_9_) | copy-start | bytes 589828
  192.4 16.4 %copy-start.7 = (f32[48,1024]{1,0:T(8,128)}, f32[48,1024]{1,0:T(8,128)S(1)}, u32[]{:S(2)}) copy-start(f32[48,1024]{1,0:T(8,128)S(1)} %collective-permute-done.11.refs_5_.refs_7_) | copy-start | bytes 589828
  199.9 0.7 copy-start.15
  200.6 30.2 %all-to-all-start.5 = ((f32[32,16,128]{2,1,0:T(8,128)}), f32[32,16,128]{2,1,0:T(8,128)S(1)}, u32[]{:S(2)}, u32[]{:S(2)}) async-start(f32[32,16,128]{2,1,0:T(8,128)} %get-tuple-element.48), calls=%async_computation.5 | async-start | bytes 524288 | tf_op jit(solution)/shard_map/all_to_all | solution.py:484
  230.8 0.7 copy-start.17
  231.4 1.0 copy-start.21
  232.4 0.9 copy-start.23

commit v8 on v7

--- a/solution.py
+++ b/solution.py
@@ -95,7 +95,7 @@
     return lax.broadcasted_iota(jnp.int32, shape, 0)
 
 
-def x_forward(value, table_ref):
+def x_forward(value, table_ref, ready=None):
     left, right = value[:, : COLS // 2], value[:, COLS // 2 :]
     group = lanes((128, 128)) // 32
     outs = []
@@ -105,6 +105,8 @@
         out = None
         for h in range(4):
             start = 256 * h + 128 * parity
+            if ready:
+                ready(start)
             first = dot_nt(table_ref[start : start + 128, :], both)
             piece = first[:, :128] + first[:, 128:]
             piece = piece + dot_nt(table_ref[1024 + start : 1152 + start, :], both[:128])
@@ -201,9 +203,31 @@
     return jnp.where(left, transfer, turned), jnp.where(left, turned, -transfer)
 
 
-def spread_kernel(table_ref, measured, point_spread, out_ref):
-    for f, ref in enumerate((measured, point_spread)):
-        out_ref[:, 8 * f : 8 * f + 8, :] = x_forward(ref[...], table_ref).reshape(32, 8, 128)
+def spread_kernel(table_far, measured_far, spread_far, out_ref, table_ref, rows_ref, sems):
+    copies = [pltpu.make_async_copy(ref, rows_ref.at[f], sems.at[16 + f]) for f, ref in enumerate((measured_far, spread_far))]
+    pieces = {}
+    for parity in range(2):
+        for h in range(4):
+            start = 256 * h + 128 * parity
+            pieces[start] = []
+            for low in range(2):
+                part = pl.ds(1024 * low + start, 128)
+                sem = sems.at[8 * low + 4 * parity + h]
+                pieces[start].append(pltpu.make_async_copy(table_far.at[part, :], table_ref.at[part, :], sem))
+    for copy in copies:
+        copy.start()
+    for pair in pieces.values():
+        for copy in pair:
+            copy.start()
+
+    def ready(start):
+        for copy in pieces[start]:
+            copy.wait()
+
+    copies[0].wait()
+    out_ref[:, 0:8, :] = x_forward(rows_ref[0], table_ref, ready).reshape(32, 8, 128)
+    copies[1].wait()
+    out_ref[:, 8:16, :] = x_forward(rows_ref[1], table_ref).reshape(32, 8, 128)
 
 
 def first_filter_kernel(table, arrived, out_ref, bank_ref):
@@ -226,7 +250,7 @@
     bank_ref[1] = spectrum
 
 
-def second_filter_kernel(table, arrived, bank_ref, sums, out_ref, image_ref):
+def second_filter_kernel(table, arrived, bank_ref, out_ref, image_ref, row_ref):
     lateral = Lateral(table)
     real, imaginary = conjugate_factors(bank_ref[0])
     power = real * real + imaginary * imaginary
@@ -238,8 +262,7 @@
         after, before = halo_rows(blocks[i])
         out_ref[:, 8 + i, :] = after + before
     image_ref[...] = image
-    row = sums[...] + jnp.where(lanes((1, 128)) == 3, lateral.weighted_sum(image * filtered), 0.0)
-    out_ref[:, 8, :] = out_ref[:, 8, :] + pltpu.roll(jnp.broadcast_to(row, (32, 128)), 8, 1)
+    row_ref[...] = jnp.where(lanes((1, 128)) == 3, lateral.weighted_sum(image * filtered), 0.0)
 
 
 def last_filter_kernel(
@@ -369,7 +392,7 @@
     row_ref[...] = row_of(((0, b * b), (1, b * ab), (2, ab * ab), (4, u * b), (5, u * ab)))
 
 
-def map_kernel(weights, row_b, u1, o, d1, mapped_ref, row_ref, source):
+def map_kernel(weights, row_b, row_f, further, u1, o, d1, mapped_ref, out_ref, source):
     load_planes((u1, o, d1), source)
     row, lowest, highest, _ = row_bounds()
     inside = (row >= lowest) & (row < highest)
@@ -377,7 +400,9 @@
         cols = slice(128 * k, 128 * k + 128)
         mapped_ref[:, cols] = jnp.where(inside, stencil_sum(weight_of(weights), source, 0, cols), 0.0)
     mapped = mapped_ref[8:40, :]
-    row_ref[...] = row_b[...] + row_of(((3, mapped * mapped),))
+    sums = row_b[...] + row_f[...] + row_of(((3, mapped * mapped),))
+    out_ref[...] = further[...]
+    out_ref[:, 8, :] = further[:, 8, :] + pltpu.roll(jnp.broadcast_to(sums, (32, 128)), 8, 1)
 
 
 def further_kernel(weights, u1, o, d1, back_ref, middle):
@@ -539,9 +564,20 @@
     tile, tiles, three = shape(32, 8, 128), shape(32, 16, 128), shape(32, 24, 128)
     spectral, frame, rows, row = shape(32 * BLOCKS, 128), shape(FRAME, COLS), shape(ROWS, COLS), shape(1, 128)
 
-    first = exchange(
-        call(spread_kernel, tiles, [], [table, measured, point_spread], far=(0, 1, 2), limit=ALL_VMEM)
-    )
+    smem, vmem, hbm = (pl.BlockSpec(memory_space=m) for m in (pltpu.SMEM, pltpu.VMEM, pltpu.HBM))
+    sent = pl.pallas_call(
+        spread_kernel,
+        out_shape=tiles,
+        in_specs=[hbm] * 3,
+        out_specs=vmem,
+        scratch_shapes=[
+            pltpu.VMEM(table.shape, BF16),
+            pltpu.VMEM((2, ROWS, COLS), F32),
+            pltpu.SemaphoreType.DMA((18,)),
+        ],
+        compiler_params=pltpu.CompilerParams(vmem_limit_bytes=ALL_VMEM),
+    )(table, measured, point_spread)
+    first = exchange(sent)
     first, grown = lax.optimization_barrier((first, with_rows(upstream)))
 
     right_out, bank = call(first_filter_kernel, (three, shape(2, 32 * BLOCKS, 128)), [], [along_y, first])
@@ -559,18 +595,18 @@
     image_arrived = exchange(image_send)
     image_parts = (moved(image, 1), image, moved(image, -1))
     plane_scratch = (pltpu.VMEM((3, 3, FRAME, COLS), F32),)
-    image_map, sums = call(map_kernel, (frame, row), [weights], [row_b], plane_scratch, planes=image_parts)
-    further_out, image_spectrum = call(
-        second_filter_kernel, (tiles, spectral), [], [along_y, image_arrived, bank, sums]
+    further_out, image_spectrum, row_f = call(
+        second_filter_kernel, (tiles, spectral, row), [], [along_y, image_arrived, bank]
     )
-    further_out, image_map = lax.optimization_barrier((further_out, image_map))
+    image_map, further_out = call(
+        map_kernel, (frame, tiles), [weights], [row_b, row_f, further_out], plane_scratch, planes=image_parts
+    )
     further_arrived = exchange(further_out)
     map_parts = (moved(image_map, 1), image_map, moved(image_map, -1))
     image_back = call(further_kernel, frame, [weights], [], plane_scratch, planes=map_parts)
     further_arrived, image_back = lax.optimization_barrier((further_arrived, image_back))
 
     further, row_sum = call(gather_sum_kernel, (frame, row), [], [table, further_arrived, image_back])
-    smem, vmem = (pl.BlockSpec(memory_space=m) for m in (pltpu.SMEM, pltpu.VMEM))
     factors, mixed = pl.pallas_call(
         factors_kernel,
         out_shape=(shape(34), frame),

time: 276 us -> 273 us (0.989)
  starting transfers between devices: 85.5 us -> 80 us
  waiting for transfers between devices: 47.1 us -> 49.9 us
    all_to_all x4, waiting for transfers between devices: 26.4 us -> 33.7 us  [exchange(): return lax.all_to_all(value, GY, 0, 0, tiled=True)]
    all_to_all x4, starting transfers between devices: 42.1 us -> 35.6 us  [exchange(): return lax.all_to_all(value, GY, 0, 0, tiled=True)]
    pallas_call x0 -> x1, Pallas kernels: none -> 5.45 us  [local(): pl.pallas_call(spread_kernel, out_shape=tiles, in_specs=[hbm] * 3, out_sp...]
    ppermute x12, waiting for transfers between devices: 13 us -> 8.54 us  [moved(): lax.ppermute(value, GZ, [(i, i + by) for i in range(size) if 0 <= i + by...]
    pallas_call x12 -> x11, Pallas kernels: 30.9 us -> 26.6 us  [call(): pl.pallas_call(whole, out_shape=out_shape, in_specs=spec_in, out_specs=sp...]
    unnamed x50 -> x48, local copies, waits for them, and re-layouts: 8.75 us -> 7.33 us
  transfers between devices with their start and end apart: 18 -> 18, of which waited for: 12 -> 10; matrix products, arithmetic and copies ran while one was open for 0% -> 0% of each run, Pallas kernels for 2% -> 3%
where the time goes in v8:
time: 273 us; the launch traced here: 271 us
  blocking collectives  98.4 us (36%)
  starting transfers between devices  80 us (29%)
  waiting for transfers between devices  49.9 us (18%)
  Pallas kernels  33.4 us (12%)
  local copies, waits for them, and re-layouts  8.11 us (3%)
    all_to_all x2, blocking collectives, exchange(): return lax.all_to_all(value, GY, 0, 0, tiled=True)  62.1 us
    ppermute x12, starting transfers between devices, moved(): lax.ppermute(value, GZ, [(i, i + by) for i in range(size) if 0 <= i + by...  39 us
    all_to_all x4, starting transfers between devices, exchange(): return lax.all_to_all(value, GY, 0, 0, tiled=True)  35.6 us
    all_to_all x4, waiting for transfers between devices, exchange(): return lax.all_to_all(value, GY, 0, 0, tiled=True)  33.7 us
    pallas_call x11, Pallas kernels, call(): pl.pallas_call(whole, out_shape=out_shape, in_specs=spec_in, out_specs=sp...  26.6 us
    all_to_all x1, blocking collectives, from_all(): lax.all_to_all(jnp.broadcast_to(row[None], (size, 1, 128)), GZ, 0, 0, til...  17.5 us
    psum x1, blocking collectives, local(): terms = lax.psum(terms, 'gz_1')  12.1 us
    ppermute x12, waiting for transfers between devices, moved(): lax.ppermute(value, GZ, [(i, i + by) for i in range(size) if 0 <= i + by...  8.54 us
  transfers between devices with their start and end apart: 18, of which 10 were waited for; matrix products, arithmetic and copies ran while one was open for 0% of the time, Pallas kernels for 3%

profile of v8, /device:TPU:1, one launch (start us, length us, event | category | flops | bytes accessed | tf_op | source)
XLA Modules:
  0.0 271.0 jit_solution(13918792150312262721)
XLA Ops:
  0.7 5.5 %shard_map.77 = f32[32,16,128]{2,1,0:T(8,128)} custom-call(bf16[2048,512]{1,0:T(8,128)(2,1)} %constant.7.clone.table_far.refs_0_.refs_1_, f32[32,1024]{1,0:T(8,128)} %bitcast.12, f32[32,1024]{1,0:T(8,128)} %spread_far.1), custom_call_target="tpu_custom_call" | custom-call | tf_op jit(solution)/shard_map/pallas_call | solution.py:568
  6.1 16.9 %all-to-all-start = ((f32[32,16,128]{2,1,0:T(8,128)}), f32[32,16,128]{2,1,0:T(8,128)S(1)}, u32[]{:S(2)}, u32[]{:S(2)}) async-start(f32[32,16,128]{2,1,0:T(8,128)} %shard_map.77), calls=%async_computation | async-start | bytes 524288 | tf_op jit(solution)/shard_map/all_to_all | solution.py:509
  23.0 3.5 %collective-permute-start = (f32[8,1024]{1,0:T(8,128)S(1)}, f32[8,1024]{1,0:T(8,128)S(1)}, u32[]{:S(2)}, u32[]{:S(2)}) collective-permute-start(f32[8,1024]{1,0:T(8,128)S(1)} %get-tuple-element.52), channel_id=1, source_target_pairs={{0,16},{16,32},{32,48},{48,64},{64,80},{80,96},{96,112},{112,128},... | collective-permute-start | bytes 98312 | tf_op jit(solution)/shard_map/ppermute | solution.py:523
  26.6 1.9 collective-permute-start.1
  28.5 1.5 collective-permute-done
  30.0 6.2 %collective-permute-done.1 = f32[8,1024]{1,0:T(8,128)S(1)} collective-permute-done((f32[8,1024]{1,0:T(8,128)S(1)}, f32[8,1024]{1,0:T(8,128)S(1)}, u32[]{:S(2)}, u32[]{:S(2)}) %collective-permute-start.1) | collective-permute-done | bytes 32800 | tf_op jit(solution)/shard_map/ppermute | solution.py:524
  36.2 8.6 %all-to-all-done.refs_1_ = f32[32,16,128]{2,1,0:T(8,128)S(1)} async-done(((f32[32,16,128]{2,1,0:T(8,128)}), f32[32,16,128]{2,1,0:T(8,128)S(1)}, u32[]{:S(2)}, u32[]{:S(2)}) %all-to-all-start) | async-done | bytes 262176 | tf_op jit(solution)/shard_map/all_to_all | solution.py:509
  44.8 2.2 shard_map.78
  47.8 32.0 %all_to_all.35.refs_1_ = f32[32,24,128]{2,1,0:T(8,128)S(1)} all-to-all(f32[32,24,128]{2,1,0:T(8,128)S(1)} %get-tuple-element.28), channel_id=1, replica_groups=mesh['gy'=32,'gz_0'=4,'gz_1'=4] {'gy'}, dimensions={0} | all-to-all | bytes 786432 | tf_op jit(solution)/shard_map/all_to_all | solution.py:509
  80.7 1.3 collective-permute-start.5
  82.0 1.3 collective-permute-start.4
  83.3 4.0 %collective-permute-start.3 = (f32[48,1024]{1,0:T(8,128)S(1)}, f32[48,1024]{1,0:T(8,128)S(1)}, u32[]{:S(2)}, u32[]{:S(2)}) collective-permute-start(f32[48,1024]{1,0:T(8,128)S(1)} %get-tuple-element.30.refs_6_.refs_2_), channel_id=1, source_target_pairs={{0,1},{1,2},{2,3},{3,4},{4,5},{5,6},{6,7},{7,8},{8,9},{9,10},{10,1... | collective-permute-start | bytes 589832 | tf_op jit(solution)/shard_map/ppermute | solution.py:514
  87.3 6.5 %collective-permute-start.2 = (f32[48,1024]{1,0:T(8,128)S(1)}, f32[48,1024]{1,0:T(8,128)}, u32[]{:S(2)}, u32[]{:S(2)}) collective-permute-start(f32[48,1024]{1,0:T(8,128)S(1)} %get-tuple-element.30.refs_6_.refs_2_), channel_id=1, source_target_pairs={{0,2},{1,3},{2,4},{3,5},{4,6},{5,7},{6,8},{7,9},{8,10},{9,11},{10,... | collective-permute-start | bytes 589832 | tf_op jit(solution)/shard_map/ppermute | solution.py:514
  94.0 2.2 collective-permute-done.2.refs_4_
  96.2 4.6 %shard_map.80 = (f32[48,1024]{1,0:T(8,128)S(1)}, f32[32,1024]{1,0:T(8,128)S(1)}, f32[32,8,128]{2,1,0:T(8,128)}, f32[1,128]{1,0:T(1,128)S(1)}) custom-call(f32[27]{0:T(128)S(1)} %reshape.14.refs_0_.weights_ref, bf16[2048,512]{1,0:T(8,128)(2,1)S(1)} %copy-done, f32[48,1024]{1,0:T(8,128)S(1)} %get-tuple-element.29.refs_2_, f32[32,1024]{1,0:T(8,128)S(1)} %bitcast.9, ...), custom_call_target="tpu_custom_call" | custom-call | flops 400000000 | bytes 4000000 | tf_op jit(solution)/shard_map/pallas_call | solution.py:497
  102.1 6.2 %all-to-all-start.2 = ((f32[32,8,128]{2,1,0:T(8,128)}), f32[32,8,128]{2,1,0:T(8,128)}, u32[]{:S(2)}, u32[]{:S(2)}) async-start(f32[32,8,128]{2,1,0:T(8,128)} %get-tuple-element.32), calls=%async_computation.2 | async-start | bytes 262144 | tf_op jit(solution)/shard_map/all_to_all | solution.py:509
  108.3 1.3 collective-permute-start.7
  109.6 5.5 %collective-permute-start.6 = (f32[48,1024]{1,0:T(8,128)}, f32[48,1024]{1,0:T(8,128)S(1)}, u32[]{:S(2)}, u32[]{:S(2)}) collective-permute-start(f32[48,1024]{1,0:T(8,128)} %copy-done.8), channel_id=1, source_target_pairs={{0,1},{1,2},{2,3},{3,4},{4,5},{5,6},{6,7},{7,8},{8,9},{9,10},{10,1... | collective-permute-start | bytes 589832 | tf_op jit(solution)/shard_map/ppermute | solution.py:514
  115.1 9.4 %all-to-all-done.2.refs_1_ = f32[32,8,128]{2,1,0:T(8,128)} async-done(((f32[32,8,128]{2,1,0:T(8,128)}), f32[32,8,128]{2,1,0:T(8,128)}, u32[]{:S(2)}, u32[]{:S(2)}) %all-to-all-start.2) | async-done | bytes 131104 | tf_op jit(solution)/shard_map/all_to_all | solution.py:509
  124.5 1.0 copy-done.19
  125.5 2.3 shard_map.81
  127.9 1.1 copy-done.9
  129.0 2.0 shard_map.82
  131.1 4.9 %all-to-all-start.3 = ((f32[32,16,128]{2,1,0:T(8,128)}), f32[32,16,128]{2,1,0:T(8,128)S(1)}, u32[]{:S(2)}, u32[]{:S(2)}) async-start(f32[32,16,128]{2,1,0:T(8,128)} %get-tuple-element.37), calls=%async_computation.3 | async-start | bytes 524288 | tf_op jit(solution)/shard_map/all_to_all | solution.py:509
  135.9 1.3 collective-permute-start.9
  137.2 5.7 %collective-permute-start.8 = (f32[48,1024]{1,0:T(8,128)S(1)}, f32[48,1024]{1,0:T(8,128)S(1)}, u32[]{:S(2)}, u32[]{:S(2)}) collective-permute-start(f32[48,1024]{1,0:T(8,128)S(1)} %get-tuple-element.38.refs_2_.refs_11_), channel_id=1, source_target_pairs={{0,1},{1,2},{2,3},{3,4},{4,5},{5,6},{6,7},{7,8},{8,9},{9,10},{10,1... | collective-permute-start | bytes 589832 | tf_op jit(solution)/shard_map/ppermute | solution.py:514
  142.9 2.9 %collective-permute-done.9.refs_3_ = f32[48,1024]{1,0:T(8,128)S(1)} collective-permute-done((f32[48,1024]{1,0:T(8,128)S(1)}, f32[48,1024]{1,0:T(8,128)S(1)}, u32[]{:S(2)}, u32[]{:S(2)}) %collective-permute-start.9) | collective-permute-done | bytes 196640 | tf_op jit(solution)/shard_map/ppermute | solution.py:514
  145.8 0.9 collective-permute-done.8.refs_1_
  146.7 1.1 shard_map.83.refs_2_
  147.8 10.2 %all-to-all-done.3.refs_1_ = f32[32,16,128]{2,1,0:T(8,128)S(1)} async-done(((f32[32,16,128]{2,1,0:T(8,128)}), f32[32,16,128]{2,1,0:T(8,128)S(1)}, u32[]{:S(2)}, u32[]{:S(2)}) %all-to-all-start.3) | async-done | bytes 262176 | tf_op jit(solution)/shard_map/all_to_all | solution.py:509
  158.6 17.5 %all_to_all.36.rows = f32[16,1,128]{2,1,0:T(1,128)S(1)} all-to-all(f32[16,1,128]{2,1,0:T(1,128)S(1)} %broadcast_in_dim.12), channel_id=1, replica_groups=mesh['gy'=32,'gz_0'=4,'gz_1'=4] {'gz_0','gz_1'}, dimensions={0} | all-to-all | bytes 16384 | tf_op jit(solution)/shard_map/all_to_all | solution.py:530
  176.0 1.3 shard_map.85
  177.4 1.3 collective-permute-start.13
  178.7 1.3 collective-permute-start.12
  180.0 4.0 %collective-permute-start.11 = (f32[48,1024]{1,0:T(8,128)S(1)}, f32[48,1024]{1,0:T(8,128)S(1)}, u32[]{:S(2)}, u32[]{:S(2)}) collective-permute-start(f32[48,1024]{1,0:T(8,128)S(1)} %get-tuple-element.45.refs_6_.refs_8_), channel_id=1, source_target_pairs={{0,1},{1,2},{2,3},{3,4},{4,5},{5,6},{6,7},{7,8},{8,9},{9,10},{10,1... | collective-permute-start | bytes 589832 | tf_op jit(solution)/shard_map/ppermute | solution.py:514
  184.0 5.5 %collective-permute-start.10 = (f32[48,1024]{1,0:T(8,128)S(1)}, f32[48,1024]{1,0:T(8,128)S(1)}, u32[]{:S(2)}, u32[]{:S(2)}) collective-permute-start(f32[48,1024]{1,0:T(8,128)S(1)} %get-tuple-element.45.refs_6_.refs_8_), channel_id=1, source_target_pairs={{0,2},{1,3},{2,4},{3,5},{4,6},{5,7},{6,8},{7,9},{8,10},{9,11},{10,... | collective-permute-start | bytes 589832 | tf_op jit(solution)/shard_map/ppermute | solution.py:514
  189.6 2.6 collective-permute-done.10.refs_4_
  192.1 5.0 %shard_map.86 = (f32[32,1024]{1,0:T(8,128)S(1)}, f32[32,16,128]{2,1,0:T(8,128)}) custom-call(f32[34]{0:T(128)S(1)} %get-tuple-element.44.refs_0_, bf16[2048,512]{1,0:T(8,128)(2,1)S(1)} %copy-done, f32[48,1024]{1,0:T(8,128)S(1)} %shard_map.83.refs_2_, f32[32,1024]{1,0:T(8,128)S(1)} %bitcast.10, f32[48,1024]{1,0:T(8,128)S(1)} %collective-permute-done.10.refs_4_, ...), custom_call_target="tpu_custom_call" | custom-call | flops 400000000 | bytes 4000000 | tf_op jit(solution)/shard_map/pallas_call | solution.py:497
  197.8 7.6 %all-to-all-start.5 = ((f32[32,16,128]{2,1,0:T(8,128)}), f32[32,16,128]{2,1,0:T(8,128)S(1)}, u32[]{:S(2)}, u32[]{:S(2)}) async-start(f32[32,16,128]{2,1,0:T(8,128)} %get-tuple-element.46), calls=%async_computation.5 | async-start | bytes 524288 | tf_op jit(solution)/shard_map/all_to_all | solution.py:509
  205.4 4.4 %shard_map.87 = f32[1,128]{1,0:T(1,128)} custom-call(f32[34]{0:T(128)} %copy-done.15, f32[48,1024]{1,0:T(8,128)} %copy-done.4, f32[48,1024]{1,0:T(8,128)} %copy-done.2, f32[48,1024]{1,0:T(8,128)} %copy-done.3, f32[48,1024]{1,0:T(8,128)} %copy-done.11, f32[48,1024]{1,0:T(8,128)} %copy-done.8, f32[48,1024]{1,0:T(8,128)} %copy-done.10, f32[48,1024]{1,0:T(8,128)} %copy-done.7, ...), custom_call_target="tpu_custom_call" | custom-call | flops 400000000 | bytes 4000000 | tf_op jit(solution)/shard_map/pallas_call | solution.py:497
  209.9 12.1 %psum.14.refs_5_ = f32[1,128]{1,0:T(1,128)S(1)} all-reduce(f32[1,128]{1,0:T(1,128)} %shard_map.87), channel_id=1, replica_groups=mesh['gy'=32,'gz_0'=4,'gz_1'=4] {'gz_1'}, use_global_device_ids=true, to_apply=%region_0.0 | all-reduce | flops 128 | bytes 1024 | tf_op jit(solution)/shard_map/psum | solution.py:630
  222.0 5.4 %all-to-all-done.5.refs_2_ = f32[32,16,128]{2,1,0:T(8,128)S(1)} async-done(((f32[32,16,128]{2,1,0:T(8,128)}), f32[32,16,128]{2,1,0:T(8,128)S(1)}, u32[]{:S(2)}, u32[]{:S(2)}) %all-to-all-start.5) | async-done | bytes 262176 | tf_op jit(solution)/shard_map/all_to_all | solution.py:509
  228.0 1.0 copy-done.20
  229.0 0.9 copy-done.22
  229.9 2.3 shard_map.88
  232.3 30.1 %all_to_all.37.refs_1_ = f32[32,16,128]{2,1,0:T(8,128)S(1)} all-to-all(f32[32,16,128]{2,1,0:T(8,128)S(1)} %shard_map.88), channel_id=1, replica_groups=mesh['gy'=32,'gz_0'=4,'gz_1'=4] {'gy'}, dimensions={0} | all-to-all | bytes 524288 | tf_op jit(solution)/shard_map/all_to_all | solution.py:509
  262.3 1.2 shard_map.89
  263.5 6.8 %psum.15 = f32[1,128]{1,0:T(1,128)S(1)} all-reduce(f32[1,128]{1,0:T(1,128)S(1)} %get-tuple-element.51), channel_id=1, replica_groups=mesh['gy'=32,'gz_0'=4,'gz_1'=4] {'gz_0'}, use_global_device_ids=true, to_apply=%region_1.0 | all-reduce | flops 128 | bytes 1024 | tf_op jit(solution)/shard_map/psum | solution.py:634
  (60 shorter events, 5.7 us)
Async XLA Ops:
  0.6 44.2 %copy-start.17 = (f32[256,128]{1,0:T(8,128)S(1)}, f32[256,128]{1,0:T(8,128)}, u32[]{:S(2)}) copy-start(f32[256,128]{1,0:T(8,128)} %constant.8.clone.refs_0_.refs_1_) | copy-start | bytes 393220
  0.6 22.4 %copy-start.1 = (f32[1,32,1024]{2,1,0:T(8,128)S(1)}, f32[1,32,1024]{2,1,0:T(8,128)}, u32[]{:S(2)}) copy-start(f32[1,32,1024]{2,1,0:T(8,128)} %param.9) | copy-start | bytes 393220
  6.1 73.7 %copy-start = (bf16[2048,512]{1,0:T(8,128)(2,1)S(1)}, bf16[2048,512]{1,0:T(8,128)(2,1)}, u32[]{:S(2)}) copy-start(bf16[2048,512]{1,0:T(8,128)(2,1)} %constant.7.clone.table_far.refs_0_.refs_1_) | copy-start | bytes 6291460
  6.1 38.7 %all-to-all-start = ((f32[32,16,128]{2,1,0:T(8,128)}), f32[32,16,128]{2,1,0:T(8,128)S(1)}, u32[]{:S(2)}, u32[]{:S(2)}) async-start(f32[32,16,128]{2,1,0:T(8,128)} %shard_map.77), calls=%async_computation | async-start | bytes 524288 | tf_op jit(solution)/shard_map/all_to_all | solution.py:509
  23.0 7.0 %collective-permute-start = (f32[8,1024]{1,0:T(8,128)S(1)}, f32[8,1024]{1,0:T(8,128)S(1)}, u32[]{:S(2)}, u32[]{:S(2)}) collective-permute-start(f32[8,1024]{1,0:T(8,128)S(1)} %get-tuple-element.52), channel_id=1, source_target_pairs={{0,16},{16,32},{32,48},{48,64},{64,80},{80,96},{96,112},{112,128},... | collective-permute-start | bytes 98312 | tf_op jit(solution)/shard_map/ppermute | solution.py:523
  26.6 9.6 %collective-permute-start.1 = (f32[8,1024]{1,0:T(8,128)S(1)}, f32[8,1024]{1,0:T(8,128)S(1)}, u32[]{:S(2)}, u32[]{:S(2)}) collective-permute-start(f32[8,1024]{1,0:T(8,128)S(1)} %get-tuple-element.53), channel_id=1, source_target_pairs={{16,0},{32,16},{48,32},{64,48},{80,64},{96,80},{112,96},{128,112},... | collective-permute-start | bytes 98312 | tf_op jit(solution)/shard_map/ppermute | solution.py:524
  36.2 57.6 %copy-start.23 = (f32[3,3,3]{2,1,0:T(4,128)S(1)}, f32[3,3,3]{2,1,0:T(4,128)}, u32[]{:S(2)}) copy-start(f32[3,3,3]{2,1,0:T(4,128)} %param.8) | copy-start | bytes 328
  47.1 0.7 copy-start.18
  80.7 47.2 %copy-start.2 = (f32[48,1024]{1,0:T(8,128)}, f32[48,1024]{1,0:T(8,128)S(1)}, u32[]{:S(2)}) copy-start(f32[48,1024]{1,0:T(8,128)S(1)} %get-tuple-element.30.refs_6_.refs_2_) | copy-start | bytes 589828
  80.7 13.2 %collective-permute-start.5 = (f32[48,1024]{1,0:T(8,128)S(1)}, f32[48,1024]{1,0:T(8,128)S(1)}, u32[]{:S(2)}, u32[]{:S(2)}) collective-permute-start(f32[48,1024]{1,0:T(8,128)S(1)} %get-tuple-element.30.refs_6_.refs_2_), channel_id=1, source_target_pairs={{2,0},{3,1},{4,2},{5,3},{6,4},{7,5},{8,6},{9,7},{10,8},{11,9},{12,... | collective-permute-start | bytes 589832 | tf_op jit(solution)/shard_map/ppermute | solution.py:514
  82.0 11.9 %collective-permute-start.4 = (f32[48,1024]{1,0:T(8,128)S(1)}, f32[48,1024]{1,0:T(8,128)S(1)}, u32[]{:S(2)}, u32[]{:S(2)}) collective-permute-start(f32[48,1024]{1,0:T(8,128)S(1)} %get-tuple-element.30.refs_6_.refs_2_), channel_id=1, source_target_pairs={{1,0},{2,1},{3,2},{4,3},{5,4},{6,5},{7,6},{8,7},{9,8},{10,9},{11,1... | collective-permute-start | bytes 589832 | tf_op jit(solution)/shard_map/ppermute | solution.py:514
  83.3 10.7 %collective-permute-start.3 = (f32[48,1024]{1,0:T(8,128)S(1)}, f32[48,1024]{1,0:T(8,128)S(1)}, u32[]{:S(2)}, u32[]{:S(2)}) collective-permute-start(f32[48,1024]{1,0:T(8,128)S(1)} %get-tuple-element.30.refs_6_.refs_2_), channel_id=1, source_target_pairs={{0,1},{1,2},{2,3},{3,4},{4,5},{5,6},{6,7},{7,8},{8,9},{9,10},{10,1... | collective-permute-start | bytes 589832 | tf_op jit(solution)/shard_map/ppermute | solution.py:514
  87.3 8.9 %collective-permute-start.2 = (f32[48,1024]{1,0:T(8,128)S(1)}, f32[48,1024]{1,0:T(8,128)}, u32[]{:S(2)}, u32[]{:S(2)}) collective-permute-start(f32[48,1024]{1,0:T(8,128)S(1)} %get-tuple-element.30.refs_6_.refs_2_), channel_id=1, source_target_pairs={{0,2},{1,3},{2,4},{3,5},{4,6},{5,7},{6,8},{7,9},{8,10},{9,11},{10,... | collective-permute-start | bytes 589832 | tf_op jit(solution)/shard_map/ppermute | solution.py:514
  93.9 33.9 %copy-start.3 = (f32[48,1024]{1,0:T(8,128)}, f32[48,1024]{1,0:T(8,128)S(1)}, u32[]{:S(2)}) copy-start(f32[48,1024]{1,0:T(8,128)S(1)} %collective-permute-done.4.refs_7_.refs_3_) | copy-start | bytes 589828
  93.9 33.9 %copy-start.4 = (f32[48,1024]{1,0:T(8,128)}, f32[48,1024]{1,0:T(8,128)S(1)}, u32[]{:S(2)}) copy-start(f32[48,1024]{1,0:T(8,128)S(1)} %collective-permute-done.3.refs_5_.refs_1_) | copy-start | bytes 589828
  100.7 0.7 copy-start.8
  101.4 0.7 copy-start.13
  102.1 22.5 %all-to-all-start.2 = ((f32[32,8,128]{2,1,0:T(8,128)}), f32[32,8,128]{2,1,0:T(8,128)}, u32[]{:S(2)}, u32[]{:S(2)}) async-start(f32[32,8,128]{2,1,0:T(8,128)} %get-tuple-element.32), calls=%async_computation.2 | async-start | bytes 262144 | tf_op jit(solution)/shard_map/all_to_all | solution.py:509
  108.3 19.6 %collective-permute-start.7 = (f32[48,1024]{1,0:T(8,128)}, f32[48,1024]{1,0:T(8,128)S(1)}, u32[]{:S(2)}, u32[]{:S(2)}) collective-permute-start(f32[48,1024]{1,0:T(8,128)} %copy-done.8), channel_id=1, source_target_pairs={{1,0},{2,1},{3,2},{4,3},{5,4},{6,5},{7,6},{8,7},{9,8},{10,9},{11,1... | collective-permute-start | bytes 589832 | tf_op jit(solution)/shard_map/ppermute | solution.py:514
  109.6 18.3 %collective-permute-start.6 = (f32[48,1024]{1,0:T(8,128)}, f32[48,1024]{1,0:T(8,128)S(1)}, u32[]{:S(2)}, u32[]{:S(2)}) collective-permute-start(f32[48,1024]{1,0:T(8,128)} %copy-done.8), channel_id=1, source_target_pairs={{0,1},{1,2},{2,3},{3,4},{4,5},{5,6},{6,7},{7,8},{8,9},{9,10},{10,1... | collective-permute-start | bytes 589832 | tf_op jit(solution)/shard_map/ppermute | solution.py:514
  124.5 1.0 copy-start.19
  127.9 3.2 %copy-start.21 = (f32[288,128]{1,0:T(8,128)}, f32[288,128]{1,0:T(8,128)S(1)}, u32[]{:S(2)}) copy-start(f32[288,128]{1,0:T(8,128)S(1)} %get-tuple-element.47.refs_4_) | copy-start | bytes 442372
  127.9 3.2 %copy-start.10 = (f32[48,1024]{1,0:T(8,128)}, f32[48,1024]{1,0:T(8,128)S(1)}, u32[]{:S(2)}) copy-start(f32[48,1024]{1,0:T(8,128)S(1)} %collective-permute-done.7.refs_6_) | copy-start | bytes 589828
  127.9 3.1 %copy-start.11 = (f32[48,1024]{1,0:T(8,128)}, f32[48,1024]{1,0:T(8,128)S(1)}, u32[]{:S(2)}) copy-start(f32[48,1024]{1,0:T(8,128)S(1)} %collective-permute-done.6.refs_4_) | copy-start | bytes 589828
  127.9 1.1 copy-start.9
  131.0 27.5 %copy-start.12 = (f32[48,1024]{1,0:T(8,128)}, f32[48,1024]{1,0:T(8,128)S(1)}, u32[]{:S(2)}) copy-start(f32[48,1024]{1,0:T(8,128)S(1)} %get-tuple-element.38.refs_2_.refs_11_) | copy-start | bytes 589828
  131.1 26.9 %all-to-all-start.3 = ((f32[32,16,128]{2,1,0:T(8,128)}), f32[32,16,128]{2,1,0:T(8,128)S(1)}, u32[]{:S(2)}, u32[]{:S(2)}) async-start(f32[32,16,128]{2,1,0:T(8,128)} %get-tuple-element.37), calls=%async_computation.3 | async-start | bytes 524288 | tf_op jit(solution)/shard_map/all_to_all | solution.py:509
  135.9 9.9 %collective-permute-start.9 = (f32[48,1024]{1,0:T(8,128)S(1)}, f32[48,1024]{1,0:T(8,128)S(1)}, u32[]{:S(2)}, u32[]{:S(2)}) collective-permute-start(f32[48,1024]{1,0:T(8,128)S(1)} %get-tuple-element.38.refs_2_.refs_11_), channel_id=1, source_target_pairs={{1,0},{2,1},{3,2},{4,3},{5,4},{6,5},{7,6},{8,7},{9,8},{10,9},{11,1... | collective-permute-start | bytes 589832 | tf_op jit(solution)/shard_map/ppermute | solution.py:514
  137.2 9.4 %collective-permute-start.8 = (f32[48,1024]{1,0:T(8,128)S(1)}, f32[48,1024]{1,0:T(8,128)S(1)}, u32[]{:S(2)}, u32[]{:S(2)}) collective-permute-start(f32[48,1024]{1,0:T(8,128)S(1)} %get-tuple-element.38.refs_2_.refs_11_), channel_id=1, source_target_pairs={{0,1},{1,2},{2,3},{3,4},{4,5},{5,6},{6,7},{7,8},{8,9},{9,10},{10,1... | collective-permute-start | bytes 589832 | tf_op jit(solution)/shard_map/ppermute | solution.py:514
  177.4 28.0 %copy-start.5 = (f32[48,1024]{1,0:T(8,128)}, f32[48,1024]{1,0:T(8,128)S(1)}, u32[]{:S(2)}) copy-start(f32[48,1024]{1,0:T(8,128)S(1)} %get-tuple-element.45.refs_6_.refs_8_) | copy-start | bytes 589828
  177.4 28.0 %copy-start.15 = (f32[34]{0:T(128)}, f32[34]{0:T(128)S(1)}, u32[]{:S(2)}) copy-start(f32[34]{0:T(128)S(1)} %get-tuple-element.44.refs_0_) | copy-start | bytes 412
  177.4 12.1 %collective-permute-start.13 = (f32[48,1024]{1,0:T(8,128)S(1)}, f32[48,1024]{1,0:T(8,128)S(1)}, u32[]{:S(2)}, u32[]{:S(2)}) collective-permute-start(f32[48,1024]{1,0:T(8,128)S(1)} %get-tuple-element.45.refs_6_.refs_8_), channel_id=1, source_target_pairs={{2,0},{3,1},{4,2},{5,3},{6,4},{7,5},{8,6},{9,7},{10,8},{11,9},{12,... | collective-permute-start | bytes 589832 | tf_op jit(solution)/shard_map/ppermute | solution.py:514
  178.7 10.8 %collective-permute-start.12 = (f32[48,1024]{1,0:T(8,128)S(1)}, f32[48,1024]{1,0:T(8,128)S(1)}, u32[]{:S(2)}, u32[]{:S(2)}) collective-permute-start(f32[48,1024]{1,0:T(8,128)S(1)} %get-tuple-element.45.refs_6_.refs_8_), channel_id=1, source_target_pairs={{1,0},{2,1},{3,2},{4,3},{5,4},{6,5},{7,6},{8,7},{9,8},{10,9},{11,1... | collective-permute-start | bytes 589832 | tf_op jit(solution)/shard_map/ppermute | solution.py:514
  180.0 9.5 %collective-permute-start.11 = (f32[48,1024]{1,0:T(8,128)S(1)}, f32[48,1024]{1,0:T(8,128)S(1)}, u32[]{:S(2)}, u32[]{:S(2)}) collective-permute-start(f32[48,1024]{1,0:T(8,128)S(1)} %get-tuple-element.45.refs_6_.refs_8_), channel_id=1, source_target_pairs={{0,1},{1,2},{2,3},{3,4},{4,5},{5,6},{6,7},{7,8},{8,9},{9,10},{10,1... | collective-permute-start | bytes 589832 | tf_op jit(solution)/shard_map/ppermute | solution.py:514
  184.0 8.1 %collective-permute-start.10 = (f32[48,1024]{1,0:T(8,128)S(1)}, f32[48,1024]{1,0:T(8,128)S(1)}, u32[]{:S(2)}, u32[]{:S(2)}) collective-permute-start(f32[48,1024]{1,0:T(8,128)S(1)} %get-tuple-element.45.refs_6_.refs_8_), channel_id=1, source_target_pairs={{0,2},{1,3},{2,4},{3,5},{4,6},{5,7},{6,8},{7,9},{8,10},{9,11},{10,... | collective-permute-start | bytes 589832 | tf_op jit(solution)/shard_map/ppermute | solution.py:514
  189.5 15.9 %copy-start.6 = (f32[48,1024]{1,0:T(8,128)}, f32[48,1024]{1,0:T(8,128)S(1)}, u32[]{:S(2)}) copy-start(f32[48,1024]{1,0:T(8,128)S(1)} %collective-permute-done.12.refs_7_.refs_9_) | copy-start | bytes 589828
  189.5 15.9 %copy-start.7 = (f32[48,1024]{1,0:T(8,128)}, f32[48,1024]{1,0:T(8,128)S(1)}, u32[]{:S(2)}) copy-start(f32[48,1024]{1,0:T(8,128)S(1)} %collective-permute-done.11.refs_5_.refs_7_) | copy-start | bytes 589828
  197.1 0.7 copy-start.14
  197.8 29.6 %all-to-all-start.5 = ((f32[32,16,128]{2,1,0:T(8,128)}), f32[32,16,128]{2,1,0:T(8,128)S(1)}, u32[]{:S(2)}, u32[]{:S(2)}) async-start(f32[32,16,128]{2,1,0:T(8,128)} %get-tuple-element.46), calls=%async_computation.5 | async-start | bytes 524288 | tf_op jit(solution)/shard_map/all_to_all | solution.py:509
  227.4 0.7 copy-start.16
  228.0 1.0 copy-start.20
  229.0 0.9 copy-start.22

commit v9 on v7

--- a/solution.py
+++ b/solution.py
@@ -226,7 +226,7 @@
     bank_ref[1] = spectrum
 
 
-def second_filter_kernel(table, arrived, bank_ref, sums, out_ref, image_ref):
+def second_filter_kernel(table, arrived, bank_ref, out_ref, image_ref, row_ref):
     lateral = Lateral(table)
     real, imaginary = conjugate_factors(bank_ref[0])
     power = real * real + imaginary * imaginary
@@ -238,8 +238,7 @@
         after, before = halo_rows(blocks[i])
         out_ref[:, 8 + i, :] = after + before
     image_ref[...] = image
-    row = sums[...] + jnp.where(lanes((1, 128)) == 3, lateral.weighted_sum(image * filtered), 0.0)
-    out_ref[:, 8, :] = out_ref[:, 8, :] + pltpu.roll(jnp.broadcast_to(row, (32, 128)), 8, 1)
+    row_ref[...] = jnp.where(lanes((1, 128)) == 3, lateral.weighted_sum(image * filtered), 0.0)
 
 
 def last_filter_kernel(
@@ -369,7 +368,7 @@
     row_ref[...] = row_of(((0, b * b), (1, b * ab), (2, ab * ab), (4, u * b), (5, u * ab)))
 
 
-def map_kernel(weights, row_b, u1, o, d1, mapped_ref, row_ref, source):
+def map_kernel(weights, row_b, row_f, further, u1, o, d1, mapped_ref, out_ref, source):
     load_planes((u1, o, d1), source)
     row, lowest, highest, _ = row_bounds()
     inside = (row >= lowest) & (row < highest)
@@ -377,7 +376,9 @@
         cols = slice(128 * k, 128 * k + 128)
         mapped_ref[:, cols] = jnp.where(inside, stencil_sum(weight_of(weights), source, 0, cols), 0.0)
     mapped = mapped_ref[8:40, :]
-    row_ref[...] = row_b[...] + row_of(((3, mapped * mapped),))
+    sums = row_b[...] + row_f[...] + row_of(((3, mapped * mapped),))
+    out_ref[...] = further[...]
+    out_ref[:, 8, :] = further[:, 8, :] + pltpu.roll(jnp.broadcast_to(sums, (32, 128)), 8, 1)
 
 
 def further_kernel(weights, u1, o, d1, back_ref, middle):
@@ -559,11 +560,12 @@
     image_arrived = exchange(image_send)
     image_parts = (moved(image, 1), image, moved(image, -1))
     plane_scratch = (pltpu.VMEM((3, 3, FRAME, COLS), F32),)
-    image_map, sums = call(map_kernel, (frame, row), [weights], [row_b], plane_scratch, planes=image_parts)
-    further_out, image_spectrum = call(
-        second_filter_kernel, (tiles, spectral), [], [along_y, image_arrived, bank, sums]
+    further_out, image_spectrum, row_f = call(
+        second_filter_kernel, (tiles, spectral, row), [], [along_y, image_arrived, bank]
     )
-    further_out, image_map = lax.optimization_barrier((further_out, image_map))
+    image_map, further_out = call(
+        map_kernel, (frame, tiles), [weights], [row_b, row_f, further_out], plane_scratch, planes=image_parts
+    )
     further_arrived = exchange(further_out)
     map_parts = (moved(image_map, 1), image_map, moved(image_map, -1))
     image_back = call(further_kernel, frame, [weights], [], plane_scratch, planes=map_parts)

time: 276 us -> 272 us (0.986)
  starting transfers between devices: 85.5 us -> 79.8 us
  waiting for transfers between devices: 47.1 us -> 50.1 us
    all_to_all x4, waiting for transfers between devices: 26.4 us -> 33.7 us  [exchange(): return lax.all_to_all(value, GY, 0, 0, tiled=True)]
    all_to_all x4, starting transfers between devices: 42.1 us -> 35.6 us  [exchange(): return lax.all_to_all(value, GY, 0, 0, tiled=True)]
    ppermute x12, waiting for transfers between devices: 13 us -> 8.72 us  [moved(): lax.ppermute(value, GZ, [(i, i + by) for i in range(size) if 0 <= i + by...]
    unnamed x50 -> x48, local copies, waits for them, and re-layouts: 8.75 us -> 7.33 us
  transfers between devices with their start and end apart: 18 -> 18, of which waited for: 12 -> 10; matrix products, arithmetic and copies ran while one was open for 0% -> 0% of each run, Pallas kernels for 2% -> 3%
where the time goes in v9:
time: 272 us; the launch traced here: 270 us
  blocking collectives  98.4 us (36%)
  starting transfers between devices  79.8 us (29%)
  waiting for transfers between devices  50.1 us (18%)
  Pallas kernels  32.3 us (12%)
  local copies, waits for them, and re-layouts  8.11 us (3%)
    all_to_all x2, blocking collectives, exchange(): return lax.all_to_all(value, GY, 0, 0, tiled=True)  62.1 us
    ppermute x12, starting transfers between devices, moved(): lax.ppermute(value, GZ, [(i, i + by) for i in range(size) if 0 <= i + by...  38.8 us
    all_to_all x4, starting transfers between devices, exchange(): return lax.all_to_all(value, GY, 0, 0, tiled=True)  35.6 us
    all_to_all x4, waiting for transfers between devices, exchange(): return lax.all_to_all(value, GY, 0, 0, tiled=True)  33.7 us
    pallas_call x12, Pallas kernels, call(): pl.pallas_call(whole, out_shape=out_shape, in_specs=spec_in, out_specs=sp...  31 us
    all_to_all x1, blocking collectives, from_all(): lax.all_to_all(jnp.broadcast_to(row[None], (size, 1, 128)), GZ, 0, 0, til...  17.5 us
    psum x1, blocking collectives, local(): terms = lax.psum(terms, 'gz_1')  12.1 us
    ppermute x12, waiting for transfers between devices, moved(): lax.ppermute(value, GZ, [(i, i + by) for i in range(size) if 0 <= i + by...  8.72 us
  transfers between devices with their start and end apart: 18, of which 10 were waited for; matrix products, arithmetic and copies ran while one was open for 0% of the time, Pallas kernels for 3%

profile of v9, /device:TPU:1, one launch (start us, length us, event | category | flops | bytes accessed | tf_op | source)
XLA Modules:
  0.0 269.9 jit_solution(2901481985227646425)
XLA Ops:
  0.7 4.4 %shard_map.77 = f32[32,16,128]{2,1,0:T(8,128)} custom-call(bf16[2048,512]{1,0:T(8,128)(2,1)} %constant.7.clone.refs_0_.refs_1_, f32[32,1024]{1,0:T(8,128)} %bitcast.12, f32[32,1024]{1,0:T(8,128)} %refs_2_.1), custom_call_target="tpu_custom_call" | custom-call | flops 400000000 | bytes 4000000 | tf_op jit(solution)/shard_map/pallas_call | solution.py:473
  5.0 16.9 %all-to-all-start = ((f32[32,16,128]{2,1,0:T(8,128)}), f32[32,16,128]{2,1,0:T(8,128)S(1)}, u32[]{:S(2)}, u32[]{:S(2)}) async-start(f32[32,16,128]{2,1,0:T(8,128)} %shard_map.77), calls=%async_computation | async-start | bytes 524288 | tf_op jit(solution)/shard_map/all_to_all | solution.py:485
  22.0 3.5 %collective-permute-start = (f32[8,1024]{1,0:T(8,128)S(1)}, f32[8,1024]{1,0:T(8,128)S(1)}, u32[]{:S(2)}, u32[]{:S(2)}) collective-permute-start(f32[8,1024]{1,0:T(8,128)S(1)} %get-tuple-element.52), channel_id=1, source_target_pairs={{0,16},{16,32},{32,48},{48,64},{64,80},{80,96},{96,112},{112,128},... | collective-permute-start | bytes 98312 | tf_op jit(solution)/shard_map/ppermute | solution.py:499
  25.5 1.9 collective-permute-start.1
  27.4 1.5 collective-permute-done
  28.9 6.2 %collective-permute-done.1 = f32[8,1024]{1,0:T(8,128)S(1)} collective-permute-done((f32[8,1024]{1,0:T(8,128)S(1)}, f32[8,1024]{1,0:T(8,128)S(1)}, u32[]{:S(2)}, u32[]{:S(2)}) %collective-permute-start.1) | collective-permute-done | bytes 32800 | tf_op jit(solution)/shard_map/ppermute | solution.py:500
  35.1 8.6 %all-to-all-done.refs_1_ = f32[32,16,128]{2,1,0:T(8,128)S(1)} async-done(((f32[32,16,128]{2,1,0:T(8,128)}), f32[32,16,128]{2,1,0:T(8,128)S(1)}, u32[]{:S(2)}, u32[]{:S(2)}) %all-to-all-start) | async-done | bytes 262176 | tf_op jit(solution)/shard_map/all_to_all | solution.py:485
  43.8 2.2 shard_map.78
  46.7 32.0 %all_to_all.35.refs_1_ = f32[32,24,128]{2,1,0:T(8,128)S(1)} all-to-all(f32[32,24,128]{2,1,0:T(8,128)S(1)} %get-tuple-element.28), channel_id=1, replica_groups=mesh['gy'=32,'gz_0'=4,'gz_1'=4] {'gy'}, dimensions={0} | all-to-all | bytes 786432 | tf_op jit(solution)/shard_map/all_to_all | solution.py:485
  79.6 1.3 collective-permute-start.5
  80.9 1.3 collective-permute-start.4
  82.2 4.0 %collective-permute-start.3 = (f32[48,1024]{1,0:T(8,128)S(1)}, f32[48,1024]{1,0:T(8,128)S(1)}, u32[]{:S(2)}, u32[]{:S(2)}) collective-permute-start(f32[48,1024]{1,0:T(8,128)S(1)} %get-tuple-element.30.refs_6_.refs_2_), channel_id=1, source_target_pairs={{0,1},{1,2},{2,3},{3,4},{4,5},{5,6},{6,7},{7,8},{8,9},{9,10},{10,1... | collective-permute-start | bytes 589832 | tf_op jit(solution)/shard_map/ppermute | solution.py:490
  86.2 6.5 %collective-permute-start.2 = (f32[48,1024]{1,0:T(8,128)S(1)}, f32[48,1024]{1,0:T(8,128)}, u32[]{:S(2)}, u32[]{:S(2)}) collective-permute-start(f32[48,1024]{1,0:T(8,128)S(1)} %get-tuple-element.30.refs_6_.refs_2_), channel_id=1, source_target_pairs={{0,2},{1,3},{2,4},{3,5},{4,6},{5,7},{6,8},{7,9},{8,10},{9,11},{10,... | collective-permute-start | bytes 589832 | tf_op jit(solution)/shard_map/ppermute | solution.py:490
  92.9 2.2 collective-permute-done.2.refs_4_
  95.1 4.6 %shard_map.80 = (f32[48,1024]{1,0:T(8,128)S(1)}, f32[32,1024]{1,0:T(8,128)S(1)}, f32[32,8,128]{2,1,0:T(8,128)}, f32[1,128]{1,0:T(1,128)S(1)}) custom-call(f32[27]{0:T(128)S(1)} %reshape.14.refs_0_.weights_ref, bf16[2048,512]{1,0:T(8,128)(2,1)S(1)} %copy-done, f32[48,1024]{1,0:T(8,128)S(1)} %get-tuple-element.29.refs_2_, f32[32,1024]{1,0:T(8,128)S(1)} %bitcast.9, ...), custom_call_target="tpu_custom_call" | custom-call | flops 400000000 | bytes 4000000 | tf_op jit(solution)/shard_map/pallas_call | solution.py:473
  101.0 6.2 %all-to-all-start.2 = ((f32[32,8,128]{2,1,0:T(8,128)}), f32[32,8,128]{2,1,0:T(8,128)}, u32[]{:S(2)}, u32[]{:S(2)}) async-start(f32[32,8,128]{2,1,0:T(8,128)} %get-tuple-element.32), calls=%async_computation.2 | async-start | bytes 262144 | tf_op jit(solution)/shard_map/all_to_all | solution.py:485
  107.2 1.3 collective-permute-start.7
  108.5 5.5 %collective-permute-start.6 = (f32[48,1024]{1,0:T(8,128)}, f32[48,1024]{1,0:T(8,128)S(1)}, u32[]{:S(2)}, u32[]{:S(2)}) collective-permute-start(f32[48,1024]{1,0:T(8,128)} %copy-done.8), channel_id=1, source_target_pairs={{0,1},{1,2},{2,3},{3,4},{4,5},{5,6},{6,7},{7,8},{8,9},{9,10},{10,1... | collective-permute-start | bytes 589832 | tf_op jit(solution)/shard_map/ppermute | solution.py:490
  114.0 9.4 %all-to-all-done.2.refs_1_ = f32[32,8,128]{2,1,0:T(8,128)} async-done(((f32[32,8,128]{2,1,0:T(8,128)}), f32[32,8,128]{2,1,0:T(8,128)}, u32[]{:S(2)}, u32[]{:S(2)}) %all-to-all-start.2) | async-done | bytes 131104 | tf_op jit(solution)/shard_map/all_to_all | solution.py:485
  123.4 1.0 copy-done.19
  124.4 2.3 shard_map.81
  126.8 1.1 copy-done.9
  127.9 2.0 shard_map.82
  130.0 4.9 %all-to-all-start.3 = ((f32[32,16,128]{2,1,0:T(8,128)}), f32[32,16,128]{2,1,0:T(8,128)S(1)}, u32[]{:S(2)}, u32[]{:S(2)}) async-start(f32[32,16,128]{2,1,0:T(8,128)} %get-tuple-element.37), calls=%async_computation.3 | async-start | bytes 524288 | tf_op jit(solution)/shard_map/all_to_all | solution.py:485
  134.9 1.3 collective-permute-start.9
  136.2 5.5 %collective-permute-start.8 = (f32[48,1024]{1,0:T(8,128)S(1)}, f32[48,1024]{1,0:T(8,128)S(1)}, u32[]{:S(2)}, u32[]{:S(2)}) collective-permute-start(f32[48,1024]{1,0:T(8,128)S(1)} %get-tuple-element.38.refs_2_.refs_11_), channel_id=1, source_target_pairs={{0,1},{1,2},{2,3},{3,4},{4,5},{5,6},{6,7},{7,8},{8,9},{9,10},{10,1... | collective-permute-start | bytes 589832 | tf_op jit(solution)/shard_map/ppermute | solution.py:490
  141.7 3.0 %collective-permute-done.9.refs_3_ = f32[48,1024]{1,0:T(8,128)S(1)} collective-permute-done((f32[48,1024]{1,0:T(8,128)S(1)}, f32[48,1024]{1,0:T(8,128)S(1)}, u32[]{:S(2)}, u32[]{:S(2)}) %collective-permute-start.9) | collective-permute-done | bytes 196640 | tf_op jit(solution)/shard_map/ppermute | solution.py:490
  144.7 0.9 collective-permute-done.8.refs_1_
  145.6 1.1 shard_map.83.refs_2_
  146.7 10.2 %all-to-all-done.3.refs_1_ = f32[32,16,128]{2,1,0:T(8,128)S(1)} async-done(((f32[32,16,128]{2,1,0:T(8,128)}), f32[32,16,128]{2,1,0:T(8,128)S(1)}, u32[]{:S(2)}, u32[]{:S(2)}) %all-to-all-start.3) | async-done | bytes 262176 | tf_op jit(solution)/shard_map/all_to_all | solution.py:485
  157.5 17.5 %all_to_all.36.rows = f32[16,1,128]{2,1,0:T(1,128)S(1)} all-to-all(f32[16,1,128]{2,1,0:T(1,128)S(1)} %broadcast_in_dim.12), channel_id=1, replica_groups=mesh['gy'=32,'gz_0'=4,'gz_1'=4] {'gz_0','gz_1'}, dimensions={0} | all-to-all | bytes 16384 | tf_op jit(solution)/shard_map/all_to_all | solution.py:506
  175.0 1.3 shard_map.85
  176.3 1.3 collective-permute-start.13
  177.6 1.3 collective-permute-start.12
  178.9 4.0 %collective-permute-start.11 = (f32[48,1024]{1,0:T(8,128)S(1)}, f32[48,1024]{1,0:T(8,128)S(1)}, u32[]{:S(2)}, u32[]{:S(2)}) collective-permute-start(f32[48,1024]{1,0:T(8,128)S(1)} %get-tuple-element.45.refs_6_.refs_8_), channel_id=1, source_target_pairs={{0,1},{1,2},{2,3},{3,4},{4,5},{5,6},{6,7},{7,8},{8,9},{9,10},{10,1... | collective-permute-start | bytes 589832 | tf_op jit(solution)/shard_map/ppermute | solution.py:490
  182.9 5.5 %collective-permute-start.10 = (f32[48,1024]{1,0:T(8,128)S(1)}, f32[48,1024]{1,0:T(8,128)S(1)}, u32[]{:S(2)}, u32[]{:S(2)}) collective-permute-start(f32[48,1024]{1,0:T(8,128)S(1)} %get-tuple-element.45.refs_6_.refs_8_), channel_id=1, source_target_pairs={{0,2},{1,3},{2,4},{3,5},{4,6},{5,7},{6,8},{7,9},{8,10},{9,11},{10,... | collective-permute-start | bytes 589832 | tf_op jit(solution)/shard_map/ppermute | solution.py:490
  188.5 2.6 collective-permute-done.10.refs_4_
  191.1 5.0 %shard_map.86 = (f32[32,1024]{1,0:T(8,128)S(1)}, f32[32,16,128]{2,1,0:T(8,128)}) custom-call(f32[34]{0:T(128)S(1)} %get-tuple-element.44.refs_0_, bf16[2048,512]{1,0:T(8,128)(2,1)S(1)} %copy-done, f32[48,1024]{1,0:T(8,128)S(1)} %shard_map.83.refs_2_, f32[32,1024]{1,0:T(8,128)S(1)} %bitcast.10, f32[48,1024]{1,0:T(8,128)S(1)} %collective-permute-done.10.refs_4_, ...), custom_call_target="tpu_custom_call" | custom-call | flops 400000000 | bytes 4000000 | tf_op jit(solution)/shard_map/pallas_call | solution.py:473
  196.7 7.6 %all-to-all-start.5 = ((f32[32,16,128]{2,1,0:T(8,128)}), f32[32,16,128]{2,1,0:T(8,128)S(1)}, u32[]{:S(2)}, u32[]{:S(2)}) async-start(f32[32,16,128]{2,1,0:T(8,128)} %get-tuple-element.46), calls=%async_computation.5 | async-start | bytes 524288 | tf_op jit(solution)/shard_map/all_to_all | solution.py:485
  204.3 4.4 %shard_map.87 = f32[1,128]{1,0:T(1,128)} custom-call(f32[34]{0:T(128)} %copy-done.15, f32[48,1024]{1,0:T(8,128)} %copy-done.4, f32[48,1024]{1,0:T(8,128)} %copy-done.2, f32[48,1024]{1,0:T(8,128)} %copy-done.3, f32[48,1024]{1,0:T(8,128)} %copy-done.11, f32[48,1024]{1,0:T(8,128)} %copy-done.8, f32[48,1024]{1,0:T(8,128)} %copy-done.10, f32[48,1024]{1,0:T(8,128)} %copy-done.7, ...), custom_call_target="tpu_custom_call" | custom-call | flops 400000000 | bytes 4000000 | tf_op jit(solution)/shard_map/pallas_call | solution.py:473
  208.8 12.1 %psum.14.refs_5_ = f32[1,128]{1,0:T(1,128)S(1)} all-reduce(f32[1,128]{1,0:T(1,128)} %shard_map.87), channel_id=1, replica_groups=mesh['gy'=32,'gz_0'=4,'gz_1'=4] {'gz_1'}, use_global_device_ids=true, to_apply=%region_0.0 | all-reduce | flops 128 | bytes 1024 | tf_op jit(solution)/shard_map/psum | solution.py:596
  220.9 5.4 %all-to-all-done.5.refs_2_ = f32[32,16,128]{2,1,0:T(8,128)S(1)} async-done(((f32[32,16,128]{2,1,0:T(8,128)}), f32[32,16,128]{2,1,0:T(8,128)S(1)}, u32[]{:S(2)}, u32[]{:S(2)}) %all-to-all-start.5) | async-done | bytes 262176 | tf_op jit(solution)/shard_map/all_to_all | solution.py:485
  227.0 1.0 copy-done.20
  227.9 0.9 copy-done.22
  228.8 2.3 shard_map.88
  231.2 30.1 %all_to_all.37.refs_1_ = f32[32,16,128]{2,1,0:T(8,128)S(1)} all-to-all(f32[32,16,128]{2,1,0:T(8,128)S(1)} %shard_map.88), channel_id=1, replica_groups=mesh['gy'=32,'gz_0'=4,'gz_1'=4] {'gy'}, dimensions={0} | all-to-all | bytes 524288 | tf_op jit(solution)/shard_map/all_to_all | solution.py:485
  261.3 1.2 shard_map.89
  262.4 6.8 %psum.15 = f32[1,128]{1,0:T(1,128)S(1)} all-reduce(f32[1,128]{1,0:T(1,128)S(1)} %get-tuple-element.51), channel_id=1, replica_groups=mesh['gy'=32,'gz_0'=4,'gz_1'=4] {'gz_0'}, use_global_device_ids=true, to_apply=%region_1.0 | all-reduce | flops 128 | bytes 1024 | tf_op jit(solution)/shard_map/psum | solution.py:600
  (60 shorter events, 5.7 us)
Async XLA Ops:
  0.6 43.1 %copy-start.17 = (f32[256,128]{1,0:T(8,128)S(1)}, f32[256,128]{1,0:T(8,128)}, u32[]{:S(2)}) copy-start(f32[256,128]{1,0:T(8,128)} %constant.8.clone.refs_0_.refs_1_) | copy-start | bytes 393220
  0.6 21.3 %copy-start.1 = (f32[1,32,1024]{2,1,0:T(8,128)S(1)}, f32[1,32,1024]{2,1,0:T(8,128)}, u32[]{:S(2)}) copy-start(f32[1,32,1024]{2,1,0:T(8,128)} %param.9) | copy-start | bytes 393220
  5.0 73.7 %copy-start = (bf16[2048,512]{1,0:T(8,128)(2,1)S(1)}, bf16[2048,512]{1,0:T(8,128)(2,1)}, u32[]{:S(2)}) copy-start(bf16[2048,512]{1,0:T(8,128)(2,1)} %constant.7.clone.refs_0_.refs_1_) | copy-start | bytes 6291460
  5.0 38.7 %all-to-all-start = ((f32[32,16,128]{2,1,0:T(8,128)}), f32[32,16,128]{2,1,0:T(8,128)S(1)}, u32[]{:S(2)}, u32[]{:S(2)}) async-start(f32[32,16,128]{2,1,0:T(8,128)} %shard_map.77), calls=%async_computation | async-start | bytes 524288 | tf_op jit(solution)/shard_map/all_to_all | solution.py:485
  22.0 7.0 %collective-permute-start = (f32[8,1024]{1,0:T(8,128)S(1)}, f32[8,1024]{1,0:T(8,128)S(1)}, u32[]{:S(2)}, u32[]{:S(2)}) collective-permute-start(f32[8,1024]{1,0:T(8,128)S(1)} %get-tuple-element.52), channel_id=1, source_target_pairs={{0,16},{16,32},{32,48},{48,64},{64,80},{80,96},{96,112},{112,128},... | collective-permute-start | bytes 98312 | tf_op jit(solution)/shard_map/ppermute | solution.py:499
  25.5 9.6 %collective-permute-start.1 = (f32[8,1024]{1,0:T(8,128)S(1)}, f32[8,1024]{1,0:T(8,128)S(1)}, u32[]{:S(2)}, u32[]{:S(2)}) collective-permute-start(f32[8,1024]{1,0:T(8,128)S(1)} %get-tuple-element.53), channel_id=1, source_target_pairs={{16,0},{32,16},{48,32},{64,48},{80,64},{96,80},{112,96},{128,112},... | collective-permute-start | bytes 98312 | tf_op jit(solution)/shard_map/ppermute | solution.py:500
  35.1 57.6 %copy-start.23 = (f32[3,3,3]{2,1,0:T(4,128)S(1)}, f32[3,3,3]{2,1,0:T(4,128)}, u32[]{:S(2)}) copy-start(f32[3,3,3]{2,1,0:T(4,128)} %param.8) | copy-start | bytes 328
  46.0 0.7 copy-start.18
  79.6 47.2 %copy-start.2 = (f32[48,1024]{1,0:T(8,128)}, f32[48,1024]{1,0:T(8,128)S(1)}, u32[]{:S(2)}) copy-start(f32[48,1024]{1,0:T(8,128)S(1)} %get-tuple-element.30.refs_6_.refs_2_) | copy-start | bytes 589828
  79.6 13.2 %collective-permute-start.5 = (f32[48,1024]{1,0:T(8,128)S(1)}, f32[48,1024]{1,0:T(8,128)S(1)}, u32[]{:S(2)}, u32[]{:S(2)}) collective-permute-start(f32[48,1024]{1,0:T(8,128)S(1)} %get-tuple-element.30.refs_6_.refs_2_), channel_id=1, source_target_pairs={{2,0},{3,1},{4,2},{5,3},{6,4},{7,5},{8,6},{9,7},{10,8},{11,9},{12,... | collective-permute-start | bytes 589832 | tf_op jit(solution)/shard_map/ppermute | solution.py:490
  80.9 11.9 %collective-permute-start.4 = (f32[48,1024]{1,0:T(8,128)S(1)}, f32[48,1024]{1,0:T(8,128)S(1)}, u32[]{:S(2)}, u32[]{:S(2)}) collective-permute-start(f32[48,1024]{1,0:T(8,128)S(1)} %get-tuple-element.30.refs_6_.refs_2_), channel_id=1, source_target_pairs={{1,0},{2,1},{3,2},{4,3},{5,4},{6,5},{7,6},{8,7},{9,8},{10,9},{11,1... | collective-permute-start | bytes 589832 | tf_op jit(solution)/shard_map/ppermute | solution.py:490
  82.2 10.7 %collective-permute-start.3 = (f32[48,1024]{1,0:T(8,128)S(1)}, f32[48,1024]{1,0:T(8,128)S(1)}, u32[]{:S(2)}, u32[]{:S(2)}) collective-permute-start(f32[48,1024]{1,0:T(8,128)S(1)} %get-tuple-element.30.refs_6_.refs_2_), channel_id=1, source_target_pairs={{0,1},{1,2},{2,3},{3,4},{4,5},{5,6},{6,7},{7,8},{8,9},{9,10},{10,1... | collective-permute-start | bytes 589832 | tf_op jit(solution)/shard_map/ppermute | solution.py:490
  86.2 8.9 %collective-permute-start.2 = (f32[48,1024]{1,0:T(8,128)S(1)}, f32[48,1024]{1,0:T(8,128)}, u32[]{:S(2)}, u32[]{:S(2)}) collective-permute-start(f32[48,1024]{1,0:T(8,128)S(1)} %get-tuple-element.30.refs_6_.refs_2_), channel_id=1, source_target_pairs={{0,2},{1,3},{2,4},{3,5},{4,6},{5,7},{6,8},{7,9},{8,10},{9,11},{10,... | collective-permute-start | bytes 589832 | tf_op jit(solution)/shard_map/ppermute | solution.py:490
  92.8 33.9 %copy-start.3 = (f32[48,1024]{1,0:T(8,128)}, f32[48,1024]{1,0:T(8,128)S(1)}, u32[]{:S(2)}) copy-start(f32[48,1024]{1,0:T(8,128)S(1)} %collective-permute-done.4.refs_7_.refs_3_) | copy-start | bytes 589828
  92.9 33.9 %copy-start.4 = (f32[48,1024]{1,0:T(8,128)}, f32[48,1024]{1,0:T(8,128)S(1)}, u32[]{:S(2)}) copy-start(f32[48,1024]{1,0:T(8,128)S(1)} %collective-permute-done.3.refs_5_.refs_1_) | copy-start | bytes 589828
  99.6 0.7 copy-start.8
  100.3 0.7 copy-start.13
  101.0 22.5 %all-to-all-start.2 = ((f32[32,8,128]{2,1,0:T(8,128)}), f32[32,8,128]{2,1,0:T(8,128)}, u32[]{:S(2)}, u32[]{:S(2)}) async-start(f32[32,8,128]{2,1,0:T(8,128)} %get-tuple-element.32), calls=%async_computation.2 | async-start | bytes 262144 | tf_op jit(solution)/shard_map/all_to_all | solution.py:485
  107.2 19.6 %collective-permute-start.7 = (f32[48,1024]{1,0:T(8,128)}, f32[48,1024]{1,0:T(8,128)S(1)}, u32[]{:S(2)}, u32[]{:S(2)}) collective-permute-start(f32[48,1024]{1,0:T(8,128)} %copy-done.8), channel_id=1, source_target_pairs={{1,0},{2,1},{3,2},{4,3},{5,4},{6,5},{7,6},{8,7},{9,8},{10,9},{11,1... | collective-permute-start | bytes 589832 | tf_op jit(solution)/shard_map/ppermute | solution.py:490
  108.5 18.3 %collective-permute-start.6 = (f32[48,1024]{1,0:T(8,128)}, f32[48,1024]{1,0:T(8,128)S(1)}, u32[]{:S(2)}, u32[]{:S(2)}) collective-permute-start(f32[48,1024]{1,0:T(8,128)} %copy-done.8), channel_id=1, source_target_pairs={{0,1},{1,2},{2,3},{3,4},{4,5},{5,6},{6,7},{7,8},{8,9},{9,10},{10,1... | collective-permute-start | bytes 589832 | tf_op jit(solution)/shard_map/ppermute | solution.py:490
  123.4 1.0 copy-start.19
  126.8 3.2 %copy-start.21 = (f32[288,128]{1,0:T(8,128)}, f32[288,128]{1,0:T(8,128)S(1)}, u32[]{:S(2)}) copy-start(f32[288,128]{1,0:T(8,128)S(1)} %get-tuple-element.47.refs_4_) | copy-start | bytes 442372
  126.8 3.2 %copy-start.10 = (f32[48,1024]{1,0:T(8,128)}, f32[48,1024]{1,0:T(8,128)S(1)}, u32[]{:S(2)}) copy-start(f32[48,1024]{1,0:T(8,128)S(1)} %collective-permute-done.7.refs_6_) | copy-start | bytes 589828
  126.8 3.1 %copy-start.11 = (f32[48,1024]{1,0:T(8,128)}, f32[48,1024]{1,0:T(8,128)S(1)}, u32[]{:S(2)}) copy-start(f32[48,1024]{1,0:T(8,128)S(1)} %collective-permute-done.6.refs_4_) | copy-start | bytes 589828
  126.8 1.1 copy-start.9
  129.9 27.5 %copy-start.12 = (f32[48,1024]{1,0:T(8,128)}, f32[48,1024]{1,0:T(8,128)S(1)}, u32[]{:S(2)}) copy-start(f32[48,1024]{1,0:T(8,128)S(1)} %get-tuple-element.38.refs_2_.refs_11_) | copy-start | bytes 589828
  130.0 26.9 %all-to-all-start.3 = ((f32[32,16,128]{2,1,0:T(8,128)}), f32[32,16,128]{2,1,0:T(8,128)S(1)}, u32[]{:S(2)}, u32[]{:S(2)}) async-start(f32[32,16,128]{2,1,0:T(8,128)} %get-tuple-element.37), calls=%async_computation.3 | async-start | bytes 524288 | tf_op jit(solution)/shard_map/all_to_all | solution.py:485
  134.9 9.8 %collective-permute-start.9 = (f32[48,1024]{1,0:T(8,128)S(1)}, f32[48,1024]{1,0:T(8,128)S(1)}, u32[]{:S(2)}, u32[]{:S(2)}) collective-permute-start(f32[48,1024]{1,0:T(8,128)S(1)} %get-tuple-element.38.refs_2_.refs_11_), channel_id=1, source_target_pairs={{1,0},{2,1},{3,2},{4,3},{5,4},{6,5},{7,6},{8,7},{9,8},{10,9},{11,1... | collective-permute-start | bytes 589832 | tf_op jit(solution)/shard_map/ppermute | solution.py:490
  136.2 9.4 %collective-permute-start.8 = (f32[48,1024]{1,0:T(8,128)S(1)}, f32[48,1024]{1,0:T(8,128)S(1)}, u32[]{:S(2)}, u32[]{:S(2)}) collective-permute-start(f32[48,1024]{1,0:T(8,128)S(1)} %get-tuple-element.38.refs_2_.refs_11_), channel_id=1, source_target_pairs={{0,1},{1,2},{2,3},{3,4},{4,5},{5,6},{6,7},{7,8},{8,9},{9,10},{10,1... | collective-permute-start | bytes 589832 | tf_op jit(solution)/shard_map/ppermute | solution.py:490
  176.3 28.0 %copy-start.5 = (f32[48,1024]{1,0:T(8,128)}, f32[48,1024]{1,0:T(8,128)S(1)}, u32[]{:S(2)}) copy-start(f32[48,1024]{1,0:T(8,128)S(1)} %get-tuple-element.45.refs_6_.refs_8_) | copy-start | bytes 589828
  176.3 28.0 %copy-start.15 = (f32[34]{0:T(128)}, f32[34]{0:T(128)S(1)}, u32[]{:S(2)}) copy-start(f32[34]{0:T(128)S(1)} %get-tuple-element.44.refs_0_) | copy-start | bytes 412
  176.3 12.1 %collective-permute-start.13 = (f32[48,1024]{1,0:T(8,128)S(1)}, f32[48,1024]{1,0:T(8,128)S(1)}, u32[]{:S(2)}, u32[]{:S(2)}) collective-permute-start(f32[48,1024]{1,0:T(8,128)S(1)} %get-tuple-element.45.refs_6_.refs_8_), channel_id=1, source_target_pairs={{2,0},{3,1},{4,2},{5,3},{6,4},{7,5},{8,6},{9,7},{10,8},{11,9},{12,... | collective-permute-start | bytes 589832 | tf_op jit(solution)/shard_map/ppermute | solution.py:490
  177.6 10.8 %collective-permute-start.12 = (f32[48,1024]{1,0:T(8,128)S(1)}, f32[48,1024]{1,0:T(8,128)S(1)}, u32[]{:S(2)}, u32[]{:S(2)}) collective-permute-start(f32[48,1024]{1,0:T(8,128)S(1)} %get-tuple-element.45.refs_6_.refs_8_), channel_id=1, source_target_pairs={{1,0},{2,1},{3,2},{4,3},{5,4},{6,5},{7,6},{8,7},{9,8},{10,9},{11,1... | collective-permute-start | bytes 589832 | tf_op jit(solution)/shard_map/ppermute | solution.py:490
  178.9 9.5 %collective-permute-start.11 = (f32[48,1024]{1,0:T(8,128)S(1)}, f32[48,1024]{1,0:T(8,128)S(1)}, u32[]{:S(2)}, u32[]{:S(2)}) collective-permute-start(f32[48,1024]{1,0:T(8,128)S(1)} %get-tuple-element.45.refs_6_.refs_8_), channel_id=1, source_target_pairs={{0,1},{1,2},{2,3},{3,4},{4,5},{5,6},{6,7},{7,8},{8,9},{9,10},{10,1... | collective-permute-start | bytes 589832 | tf_op jit(solution)/shard_map/ppermute | solution.py:490
  182.9 8.1 %collective-permute-start.10 = (f32[48,1024]{1,0:T(8,128)S(1)}, f32[48,1024]{1,0:T(8,128)S(1)}, u32[]{:S(2)}, u32[]{:S(2)}) collective-permute-start(f32[48,1024]{1,0:T(8,128)S(1)} %get-tuple-element.45.refs_6_.refs_8_), channel_id=1, source_target_pairs={{0,2},{1,3},{2,4},{3,5},{4,6},{5,7},{6,8},{7,9},{8,10},{9,11},{10,... | collective-permute-start | bytes 589832 | tf_op jit(solution)/shard_map/ppermute | solution.py:490
  188.5 15.9 %copy-start.6 = (f32[48,1024]{1,0:T(8,128)}, f32[48,1024]{1,0:T(8,128)S(1)}, u32[]{:S(2)}) copy-start(f32[48,1024]{1,0:T(8,128)S(1)} %collective-permute-done.12.refs_7_.refs_9_) | copy-start | bytes 589828
  188.5 15.9 %copy-start.7 = (f32[48,1024]{1,0:T(8,128)}, f32[48,1024]{1,0:T(8,128)S(1)}, u32[]{:S(2)}) copy-start(f32[48,1024]{1,0:T(8,128)S(1)} %collective-permute-done.11.refs_5_.refs_7_) | copy-start | bytes 589828
  196.0 0.7 copy-start.14
  196.7 29.6 %all-to-all-start.5 = ((f32[32,16,128]{2,1,0:T(8,128)}), f32[32,16,128]{2,1,0:T(8,128)S(1)}, u32[]{:S(2)}, u32[]{:S(2)}) async-start(f32[32,16,128]{2,1,0:T(8,128)} %get-tuple-element.46), calls=%async_computation.5 | async-start | bytes 524288 | tf_op jit(solution)/shard_map/all_to_all | solution.py:485
  226.3 0.7 copy-start.16
  227.0 1.0 copy-start.20
  227.9 0.9 copy-start.22

commit v10 on v9

--- a/solution.py
+++ b/solution.py
@@ -593,11 +593,11 @@
     operands = [*right_parts[1:4], *image_parts, *mixed_parts[1:4], right_map, image_map, mixed_map]
     scratch = (pltpu.VMEM((3, FRAME, COLS), F32), pltpu.VMEM((3, ROWS, COLS), F32))
     terms = call(correlate_kernel, row, [factors], operands, scratch, far=tuple(range(12)), limit=ALL_VMEM)
-    terms = lax.psum(terms, "gz_1")
+    terms = lax.psum(lax.psum(terms, "gz_1"), "gz_0")
     last_arrived = exchange(last_send)
     result_out = call(last_filter_kernel, tiles, [factors], [along_y, last_arrived, bank, image_spectrum, terms])
     grad_measured, terms = call(final_kernel, (rows, row), [], [table, exchange(result_out)])
-    grad_stencil = lax.psum(terms, "gz_0")[0, :27].reshape(3, 3, 3) / math.sqrt(cells)
+    grad_stencil = terms[0, :27].reshape(3, 3, 3) / math.sqrt(cells)
     return grad_measured[None], grad_stencil
 
 

time: 272 us -> 273 us (level)
  blocking collectives: 98.4 us -> 105 us
  waiting for transfers between devices: 50.1 us -> 44.6 us
    all_to_all x2, blocking collectives: 62.1 us -> 69.2 us  [exchange(): return lax.all_to_all(value, GY, 0, 0, tiled=True)]
    all_to_all x4, waiting for transfers between devices: 33.7 us -> 28.3 us  [exchange(): return lax.all_to_all(value, GY, 0, 0, tiled=True)]
  transfers between devices with their start and end apart: 18 -> 18, of which waited for: 10 -> 9; matrix products, arithmetic and copies ran while one was open for 0% -> 0% of each run, Pallas kernels for 3% -> 3%
where the time goes in v10:
time: 273 us; the launch traced here: 271 us
  blocking collectives  105 us (38%)
  starting transfers between devices  79.8 us (29%)
  waiting for transfers between devices  44.6 us (16%)
  Pallas kernels  32.3 us (12%)
  local copies, waits for them, and re-layouts  8.11 us (3%)
    all_to_all x2, blocking collectives, exchange(): return lax.all_to_all(value, GY, 0, 0, tiled=True)  69.2 us
    ppermute x12, starting transfers between devices, moved(): lax.ppermute(value, GZ, [(i, i + by) for i in range(size) if 0 <= i + by...  38.8 us
    all_to_all x4, starting transfers between devices, exchange(): return lax.all_to_all(value, GY, 0, 0, tiled=True)  35.6 us
    pallas_call x12, Pallas kernels, call(): pl.pallas_call(whole, out_shape=out_shape, in_specs=spec_in, out_specs=sp...  31 us
    all_to_all x4, waiting for transfers between devices, exchange(): return lax.all_to_all(value, GY, 0, 0, tiled=True)  28.3 us
    psum x2, blocking collectives, local(): terms = lax.psum(lax.psum(terms, 'gz_1'), 'gz_0')  18.7 us
    all_to_all x1, blocking collectives, from_all(): lax.all_to_all(jnp.broadcast_to(row[None], (size, 1, 128)), GZ, 0, 0, til...  17.5 us
    ppermute x12, waiting for transfers between devices, moved(): lax.ppermute(value, GZ, [(i, i + by) for i in range(size) if 0 <= i + by...  8.72 us
  transfers between devices with their start and end apart: 18, of which 9 were waited for; matrix products, arithmetic and copies ran while one was open for 0% of the time, Pallas kernels for 3%

profile of v10, /device:TPU:1, one launch (start us, length us, event | category | flops | bytes accessed | tf_op | source)
XLA Modules:
  0.0 271.4 jit_solution(11094412916838468559)
XLA Ops:
  0.7 4.4 %shard_map.77 = f32[32,16,128]{2,1,0:T(8,128)} custom-call(bf16[2048,512]{1,0:T(8,128)(2,1)} %constant.7.clone.refs_0_.refs_1_, f32[32,1024]{1,0:T(8,128)} %bitcast.12, f32[32,1024]{1,0:T(8,128)} %refs_2_.1), custom_call_target="tpu_custom_call" | custom-call | flops 400000000 | bytes 4000000 | tf_op jit(solution)/shard_map/pallas_call | solution.py:473
  5.0 16.9 %all-to-all-start = ((f32[32,16,128]{2,1,0:T(8,128)}), f32[32,16,128]{2,1,0:T(8,128)S(1)}, u32[]{:S(2)}, u32[]{:S(2)}) async-start(f32[32,16,128]{2,1,0:T(8,128)} %shard_map.77), calls=%async_computation | async-start | bytes 524288 | tf_op jit(solution)/shard_map/all_to_all | solution.py:485
  22.0 3.5 %collective-permute-start = (f32[8,1024]{1,0:T(8,128)S(1)}, f32[8,1024]{1,0:T(8,128)S(1)}, u32[]{:S(2)}, u32[]{:S(2)}) collective-permute-start(f32[8,1024]{1,0:T(8,128)S(1)} %get-tuple-element.52), channel_id=1, source_target_pairs={{0,16},{16,32},{32,48},{48,64},{64,80},{80,96},{96,112},{112,128},... | collective-permute-start | bytes 98312 | tf_op jit(solution)/shard_map/ppermute | solution.py:499
  25.5 1.9 collective-permute-start.1
  27.4 1.5 collective-permute-done
  28.9 6.2 %collective-permute-done.1 = f32[8,1024]{1,0:T(8,128)S(1)} collective-permute-done((f32[8,1024]{1,0:T(8,128)S(1)}, f32[8,1024]{1,0:T(8,128)S(1)}, u32[]{:S(2)}, u32[]{:S(2)}) %collective-permute-start.1) | collective-permute-done | bytes 32800 | tf_op jit(solution)/shard_map/ppermute | solution.py:500
  35.1 8.6 %all-to-all-done.refs_1_ = f32[32,16,128]{2,1,0:T(8,128)S(1)} async-done(((f32[32,16,128]{2,1,0:T(8,128)}), f32[32,16,128]{2,1,0:T(8,128)S(1)}, u32[]{:S(2)}, u32[]{:S(2)}) %all-to-all-start) | async-done | bytes 262176 | tf_op jit(solution)/shard_map/all_to_all | solution.py:485
  43.8 2.2 shard_map.78
  46.7 32.0 %all_to_all.35.refs_1_ = f32[32,24,128]{2,1,0:T(8,128)S(1)} all-to-all(f32[32,24,128]{2,1,0:T(8,128)S(1)} %get-tuple-element.28), channel_id=1, replica_groups=mesh['gy'=32,'gz_0'=4,'gz_1'=4] {'gy'}, dimensions={0} | all-to-all | bytes 786432 | tf_op jit(solution)/shard_map/all_to_all | solution.py:485
  78.7 0.9 shard_map.79
  79.6 1.3 collective-permute-start.5
  80.9 1.3 collective-permute-start.4
  82.2 4.0 %collective-permute-start.3 = (f32[48,1024]{1,0:T(8,128)S(1)}, f32[48,1024]{1,0:T(8,128)S(1)}, u32[]{:S(2)}, u32[]{:S(2)}) collective-permute-start(f32[48,1024]{1,0:T(8,128)S(1)} %get-tuple-element.30.refs_6_.refs_2_), channel_id=1, source_target_pairs={{0,1},{1,2},{2,3},{3,4},{4,5},{5,6},{6,7},{7,8},{8,9},{9,10},{10,1... | collective-permute-start | bytes 589832 | tf_op jit(solution)/shard_map/ppermute | solution.py:490
  86.2 6.5 %collective-permute-start.2 = (f32[48,1024]{1,0:T(8,128)S(1)}, f32[48,1024]{1,0:T(8,128)}, u32[]{:S(2)}, u32[]{:S(2)}) collective-permute-start(f32[48,1024]{1,0:T(8,128)S(1)} %get-tuple-element.30.refs_6_.refs_2_), channel_id=1, source_target_pairs={{0,2},{1,3},{2,4},{3,5},{4,6},{5,7},{6,8},{7,9},{8,10},{9,11},{10,... | collective-permute-start | bytes 589832 | tf_op jit(solution)/shard_map/ppermute | solution.py:490
  92.9 2.2 collective-permute-done.2.refs_4_
  95.1 4.6 %shard_map.80 = (f32[48,1024]{1,0:T(8,128)S(1)}, f32[32,1024]{1,0:T(8,128)S(1)}, f32[32,8,128]{2,1,0:T(8,128)}, f32[1,128]{1,0:T(1,128)S(1)}) custom-call(f32[27]{0:T(128)S(1)} %reshape.14.refs_0_.weights_ref, bf16[2048,512]{1,0:T(8,128)(2,1)S(1)} %copy-done, f32[48,1024]{1,0:T(8,128)S(1)} %get-tuple-element.29.refs_2_, f32[32,1024]{1,0:T(8,128)S(1)} %bitcast.9, ...), custom_call_target="tpu_custom_call" | custom-call | flops 400000000 | bytes 4000000 | tf_op jit(solution)/shard_map/pallas_call | solution.py:473
  101.0 6.2 %all-to-all-start.2 = ((f32[32,8,128]{2,1,0:T(8,128)}), f32[32,8,128]{2,1,0:T(8,128)}, u32[]{:S(2)}, u32[]{:S(2)}) async-start(f32[32,8,128]{2,1,0:T(8,128)} %get-tuple-element.32), calls=%async_computation.2 | async-start | bytes 262144 | tf_op jit(solution)/shard_map/all_to_all | solution.py:485
  107.2 1.3 collective-permute-start.7
  108.5 5.5 %collective-permute-start.6 = (f32[48,1024]{1,0:T(8,128)}, f32[48,1024]{1,0:T(8,128)S(1)}, u32[]{:S(2)}, u32[]{:S(2)}) collective-permute-start(f32[48,1024]{1,0:T(8,128)} %copy-done.8), channel_id=1, source_target_pairs={{0,1},{1,2},{2,3},{3,4},{4,5},{5,6},{6,7},{7,8},{8,9},{9,10},{10,1... | collective-permute-start | bytes 589832 | tf_op jit(solution)/shard_map/ppermute | solution.py:490
  114.0 9.4 %all-to-all-done.2.refs_1_ = f32[32,8,128]{2,1,0:T(8,128)} async-done(((f32[32,8,128]{2,1,0:T(8,128)}), f32[32,8,128]{2,1,0:T(8,128)}, u32[]{:S(2)}, u32[]{:S(2)}) %all-to-all-start.2) | async-done | bytes 131104 | tf_op jit(solution)/shard_map/all_to_all | solution.py:485
  123.4 1.0 copy-done.19
  124.4 2.3 shard_map.81
  126.8 1.1 copy-done.9
  127.9 2.0 shard_map.82
  130.0 4.9 %all-to-all-start.3 = ((f32[32,16,128]{2,1,0:T(8,128)}), f32[32,16,128]{2,1,0:T(8,128)S(1)}, u32[]{:S(2)}, u32[]{:S(2)}) async-start(f32[32,16,128]{2,1,0:T(8,128)} %get-tuple-element.37), calls=%async_computation.3 | async-start | bytes 524288 | tf_op jit(solution)/shard_map/all_to_all | solution.py:485
  134.9 1.3 collective-permute-start.9
  136.2 5.5 %collective-permute-start.8 = (f32[48,1024]{1,0:T(8,128)S(1)}, f32[48,1024]{1,0:T(8,128)S(1)}, u32[]{:S(2)}, u32[]{:S(2)}) collective-permute-start(f32[48,1024]{1,0:T(8,128)S(1)} %get-tuple-element.38.refs_2_.refs_11_), channel_id=1, source_target_pairs={{0,1},{1,2},{2,3},{3,4},{4,5},{5,6},{6,7},{7,8},{8,9},{9,10},{10,1... | collective-permute-start | bytes 589832 | tf_op jit(solution)/shard_map/ppermute | solution.py:490
  141.7 3.0 %collective-permute-done.9.refs_3_ = f32[48,1024]{1,0:T(8,128)S(1)} collective-permute-done((f32[48,1024]{1,0:T(8,128)S(1)}, f32[48,1024]{1,0:T(8,128)S(1)}, u32[]{:S(2)}, u32[]{:S(2)}) %collective-permute-start.9) | collective-permute-done | bytes 196640 | tf_op jit(solution)/shard_map/ppermute | solution.py:490
  144.7 0.9 collective-permute-done.8.refs_1_
  145.6 1.1 shard_map.83.refs_2_
  146.7 10.2 %all-to-all-done.3.refs_1_ = f32[32,16,128]{2,1,0:T(8,128)S(1)} async-done(((f32[32,16,128]{2,1,0:T(8,128)}), f32[32,16,128]{2,1,0:T(8,128)S(1)}, u32[]{:S(2)}, u32[]{:S(2)}) %all-to-all-start.3) | async-done | bytes 262176 | tf_op jit(solution)/shard_map/all_to_all | solution.py:485
  157.5 17.5 %all_to_all.36.rows = f32[16,1,128]{2,1,0:T(1,128)S(1)} all-to-all(f32[16,1,128]{2,1,0:T(1,128)S(1)} %broadcast_in_dim.12), channel_id=1, replica_groups=mesh['gy'=32,'gz_0'=4,'gz_1'=4] {'gz_0','gz_1'}, dimensions={0} | all-to-all | bytes 16384 | tf_op jit(solution)/shard_map/all_to_all | solution.py:506
  175.0 1.3 shard_map.85
  176.3 1.3 collective-permute-start.13
  177.6 1.3 collective-permute-start.12
  178.9 4.0 %collective-permute-start.11 = (f32[48,1024]{1,0:T(8,128)S(1)}, f32[48,1024]{1,0:T(8,128)S(1)}, u32[]{:S(2)}, u32[]{:S(2)}) collective-permute-start(f32[48,1024]{1,0:T(8,128)S(1)} %get-tuple-element.45.refs_6_.refs_8_), channel_id=1, source_target_pairs={{0,1},{1,2},{2,3},{3,4},{4,5},{5,6},{6,7},{7,8},{8,9},{9,10},{10,1... | collective-permute-start | bytes 589832 | tf_op jit(solution)/shard_map/ppermute | solution.py:490
  182.9 5.5 %collective-permute-start.10 = (f32[48,1024]{1,0:T(8,128)S(1)}, f32[48,1024]{1,0:T(8,128)S(1)}, u32[]{:S(2)}, u32[]{:S(2)}) collective-permute-start(f32[48,1024]{1,0:T(8,128)S(1)} %get-tuple-element.45.refs_6_.refs_8_), channel_id=1, source_target_pairs={{0,2},{1,3},{2,4},{3,5},{4,6},{5,7},{6,8},{7,9},{8,10},{9,11},{10,... | collective-permute-start | bytes 589832 | tf_op jit(solution)/shard_map/ppermute | solution.py:490
  188.5 2.6 collective-permute-done.10.refs_4_
  191.1 5.0 %shard_map.86 = (f32[32,1024]{1,0:T(8,128)S(1)}, f32[32,16,128]{2,1,0:T(8,128)}) custom-call(f32[34]{0:T(128)S(1)} %get-tuple-element.44.refs_0_, bf16[2048,512]{1,0:T(8,128)(2,1)S(1)} %copy-done, f32[48,1024]{1,0:T(8,128)S(1)} %shard_map.83.refs_2_, f32[32,1024]{1,0:T(8,128)S(1)} %bitcast.10, f32[48,1024]{1,0:T(8,128)S(1)} %collective-permute-done.10.refs_4_, ...), custom_call_target="tpu_custom_call" | custom-call | flops 400000000 | bytes 4000000 | tf_op jit(solution)/shard_map/pallas_call | solution.py:473
  196.7 7.6 %all-to-all-start.5 = ((f32[32,16,128]{2,1,0:T(8,128)}), f32[32,16,128]{2,1,0:T(8,128)S(1)}, u32[]{:S(2)}, u32[]{:S(2)}) async-start(f32[32,16,128]{2,1,0:T(8,128)} %get-tuple-element.46), calls=%async_computation.5 | async-start | bytes 524288 | tf_op jit(solution)/shard_map/all_to_all | solution.py:485
  204.3 4.4 %shard_map.87 = f32[1,128]{1,0:T(1,128)} custom-call(f32[34]{0:T(128)} %copy-done.15, f32[48,1024]{1,0:T(8,128)} %copy-done.4, f32[48,1024]{1,0:T(8,128)} %copy-done.2, f32[48,1024]{1,0:T(8,128)} %copy-done.3, f32[48,1024]{1,0:T(8,128)} %copy-done.11, f32[48,1024]{1,0:T(8,128)} %copy-done.8, f32[48,1024]{1,0:T(8,128)} %copy-done.10, f32[48,1024]{1,0:T(8,128)} %copy-done.7, ...), custom_call_target="tpu_custom_call" | custom-call | flops 400000000 | bytes 4000000 | tf_op jit(solution)/shard_map/pallas_call | solution.py:473
  208.8 12.1 %psum.14 = f32[1,128]{1,0:T(1,128)S(1)} all-reduce(f32[1,128]{1,0:T(1,128)} %shard_map.87), channel_id=1, replica_groups=mesh['gy'=32,'gz_0'=4,'gz_1'=4] {'gz_1'}, use_global_device_ids=true, to_apply=%region_0.0 | all-reduce | flops 128 | bytes 1024 | tf_op jit(solution)/shard_map/psum | solution.py:596
  220.9 6.6 %psum.15.refs_5_ = f32[1,128]{1,0:T(1,128)S(1)} all-reduce(f32[1,128]{1,0:T(1,128)S(1)} %psum.14), channel_id=1, replica_groups=mesh['gy'=32,'gz_0'=4,'gz_1'=4] {'gz_0'}, use_global_device_ids=true, to_apply=%region_1.0 | all-reduce | flops 128 | bytes 1024 | tf_op jit(solution)/shard_map/psum | solution.py:596
  228.1 1.0 copy-done.20
  229.1 0.9 copy-done.22
  230.0 2.3 shard_map.88
  232.3 37.2 %all_to_all.37.refs_1_ = f32[32,16,128]{2,1,0:T(8,128)S(1)} all-to-all(f32[32,16,128]{2,1,0:T(8,128)S(1)} %shard_map.88), channel_id=1, replica_groups=mesh['gy'=32,'gz_0'=4,'gz_1'=4] {'gy'}, dimensions={0} | all-to-all | bytes 524288 | tf_op jit(solution)/shard_map/all_to_all | solution.py:485
  269.5 1.2 shard_map.89
  (60 shorter events, 4.9 us)
Async XLA Ops:
  0.6 43.1 %copy-start.17 = (f32[256,128]{1,0:T(8,128)S(1)}, f32[256,128]{1,0:T(8,128)}, u32[]{:S(2)}) copy-start(f32[256,128]{1,0:T(8,128)} %constant.8.clone.refs_0_.refs_1_) | copy-start | bytes 393220
  0.6 21.3 %copy-start.1 = (f32[1,32,1024]{2,1,0:T(8,128)S(1)}, f32[1,32,1024]{2,1,0:T(8,128)}, u32[]{:S(2)}) copy-start(f32[1,32,1024]{2,1,0:T(8,128)} %param.9) | copy-start | bytes 393220
  5.0 73.7 %copy-start = (bf16[2048,512]{1,0:T(8,128)(2,1)S(1)}, bf16[2048,512]{1,0:T(8,128)(2,1)}, u32[]{:S(2)}) copy-start(bf16[2048,512]{1,0:T(8,128)(2,1)} %constant.7.clone.refs_0_.refs_1_) | copy-start | bytes 6291460
  5.0 38.7 %all-to-all-start = ((f32[32,16,128]{2,1,0:T(8,128)}), f32[32,16,128]{2,1,0:T(8,128)S(1)}, u32[]{:S(2)}, u32[]{:S(2)}) async-start(f32[32,16,128]{2,1,0:T(8,128)} %shard_map.77), calls=%async_computation | async-start | bytes 524288 | tf_op jit(solution)/shard_map/all_to_all | solution.py:485
  22.0 7.0 %collective-permute-start = (f32[8,1024]{1,0:T(8,128)S(1)}, f32[8,1024]{1,0:T(8,128)S(1)}, u32[]{:S(2)}, u32[]{:S(2)}) collective-permute-start(f32[8,1024]{1,0:T(8,128)S(1)} %get-tuple-element.52), channel_id=1, source_target_pairs={{0,16},{16,32},{32,48},{48,64},{64,80},{80,96},{96,112},{112,128},... | collective-permute-start | bytes 98312 | tf_op jit(solution)/shard_map/ppermute | solution.py:499
  25.5 9.6 %collective-permute-start.1 = (f32[8,1024]{1,0:T(8,128)S(1)}, f32[8,1024]{1,0:T(8,128)S(1)}, u32[]{:S(2)}, u32[]{:S(2)}) collective-permute-start(f32[8,1024]{1,0:T(8,128)S(1)} %get-tuple-element.53), channel_id=1, source_target_pairs={{16,0},{32,16},{48,32},{64,48},{80,64},{96,80},{112,96},{128,112},... | collective-permute-start | bytes 98312 | tf_op jit(solution)/shard_map/ppermute | solution.py:500
  35.1 57.6 %copy-start.23 = (f32[3,3,3]{2,1,0:T(4,128)S(1)}, f32[3,3,3]{2,1,0:T(4,128)}, u32[]{:S(2)}) copy-start(f32[3,3,3]{2,1,0:T(4,128)} %param.8) | copy-start | bytes 328
  46.0 0.7 copy-start.18
  79.6 47.2 %copy-start.2 = (f32[48,1024]{1,0:T(8,128)}, f32[48,1024]{1,0:T(8,128)S(1)}, u32[]{:S(2)}) copy-start(f32[48,1024]{1,0:T(8,128)S(1)} %get-tuple-element.30.refs_6_.refs_2_) | copy-start | bytes 589828
  79.6 13.2 %collective-permute-start.5 = (f32[48,1024]{1,0:T(8,128)S(1)}, f32[48,1024]{1,0:T(8,128)S(1)}, u32[]{:S(2)}, u32[]{:S(2)}) collective-permute-start(f32[48,1024]{1,0:T(8,128)S(1)} %get-tuple-element.30.refs_6_.refs_2_), channel_id=1, source_target_pairs={{2,0},{3,1},{4,2},{5,3},{6,4},{7,5},{8,6},{9,7},{10,8},{11,9},{12,... | collective-permute-start | bytes 589832 | tf_op jit(solution)/shard_map/ppermute | solution.py:490
  80.9 11.9 %collective-permute-start.4 = (f32[48,1024]{1,0:T(8,128)S(1)}, f32[48,1024]{1,0:T(8,128)S(1)}, u32[]{:S(2)}, u32[]{:S(2)}) collective-permute-start(f32[48,1024]{1,0:T(8,128)S(1)} %get-tuple-element.30.refs_6_.refs_2_), channel_id=1, source_target_pairs={{1,0},{2,1},{3,2},{4,3},{5,4},{6,5},{7,6},{8,7},{9,8},{10,9},{11,1... | collective-permute-start | bytes 589832 | tf_op jit(solution)/shard_map/ppermute | solution.py:490
  82.2 10.7 %collective-permute-start.3 = (f32[48,1024]{1,0:T(8,128)S(1)}, f32[48,1024]{1,0:T(8,128)S(1)}, u32[]{:S(2)}, u32[]{:S(2)}) collective-permute-start(f32[48,1024]{1,0:T(8,128)S(1)} %get-tuple-element.30.refs_6_.refs_2_), channel_id=1, source_target_pairs={{0,1},{1,2},{2,3},{3,4},{4,5},{5,6},{6,7},{7,8},{8,9},{9,10},{10,1... | collective-permute-start | bytes 589832 | tf_op jit(solution)/shard_map/ppermute | solution.py:490
  86.2 8.9 %collective-permute-start.2 = (f32[48,1024]{1,0:T(8,128)S(1)}, f32[48,1024]{1,0:T(8,128)}, u32[]{:S(2)}, u32[]{:S(2)}) collective-permute-start(f32[48,1024]{1,0:T(8,128)S(1)} %get-tuple-element.30.refs_6_.refs_2_), channel_id=1, source_target_pairs={{0,2},{1,3},{2,4},{3,5},{4,6},{5,7},{6,8},{7,9},{8,10},{9,11},{10,... | collective-permute-start | bytes 589832 | tf_op jit(solution)/shard_map/ppermute | solution.py:490
  92.8 33.9 %copy-start.3 = (f32[48,1024]{1,0:T(8,128)}, f32[48,1024]{1,0:T(8,128)S(1)}, u32[]{:S(2)}) copy-start(f32[48,1024]{1,0:T(8,128)S(1)} %collective-permute-done.4.refs_7_.refs_3_) | copy-start | bytes 589828
  92.9 33.9 %copy-start.4 = (f32[48,1024]{1,0:T(8,128)}, f32[48,1024]{1,0:T(8,128)S(1)}, u32[]{:S(2)}) copy-start(f32[48,1024]{1,0:T(8,128)S(1)} %collective-permute-done.3.refs_5_.refs_1_) | copy-start | bytes 589828
  99.6 0.7 copy-start.8
  100.3 0.7 copy-start.13
  101.0 22.5 %all-to-all-start.2 = ((f32[32,8,128]{2,1,0:T(8,128)}), f32[32,8,128]{2,1,0:T(8,128)}, u32[]{:S(2)}, u32[]{:S(2)}) async-start(f32[32,8,128]{2,1,0:T(8,128)} %get-tuple-element.32), calls=%async_computation.2 | async-start | bytes 262144 | tf_op jit(solution)/shard_map/all_to_all | solution.py:485
  107.2 19.6 %collective-permute-start.7 = (f32[48,1024]{1,0:T(8,128)}, f32[48,1024]{1,0:T(8,128)S(1)}, u32[]{:S(2)}, u32[]{:S(2)}) collective-permute-start(f32[48,1024]{1,0:T(8,128)} %copy-done.8), channel_id=1, source_target_pairs={{1,0},{2,1},{3,2},{4,3},{5,4},{6,5},{7,6},{8,7},{9,8},{10,9},{11,1... | collective-permute-start | bytes 589832 | tf_op jit(solution)/shard_map/ppermute | solution.py:490
  108.5 18.3 %collective-permute-start.6 = (f32[48,1024]{1,0:T(8,128)}, f32[48,1024]{1,0:T(8,128)S(1)}, u32[]{:S(2)}, u32[]{:S(2)}) collective-permute-start(f32[48,1024]{1,0:T(8,128)} %copy-done.8), channel_id=1, source_target_pairs={{0,1},{1,2},{2,3},{3,4},{4,5},{5,6},{6,7},{7,8},{8,9},{9,10},{10,1... | collective-permute-start | bytes 589832 | tf_op jit(solution)/shard_map/ppermute | solution.py:490
  123.4 1.0 copy-start.19
  126.8 3.2 %copy-start.21 = (f32[288,128]{1,0:T(8,128)}, f32[288,128]{1,0:T(8,128)S(1)}, u32[]{:S(2)}) copy-start(f32[288,128]{1,0:T(8,128)S(1)} %get-tuple-element.47.refs_4_) | copy-start | bytes 442372
  126.8 3.2 %copy-start.10 = (f32[48,1024]{1,0:T(8,128)}, f32[48,1024]{1,0:T(8,128)S(1)}, u32[]{:S(2)}) copy-start(f32[48,1024]{1,0:T(8,128)S(1)} %collective-permute-done.7.refs_6_) | copy-start | bytes 589828
  126.8 3.1 %copy-start.11 = (f32[48,1024]{1,0:T(8,128)}, f32[48,1024]{1,0:T(8,128)S(1)}, u32[]{:S(2)}) copy-start(f32[48,1024]{1,0:T(8,128)S(1)} %collective-permute-done.6.refs_4_) | copy-start | bytes 589828
  126.8 1.1 copy-start.9
  129.9 27.5 %copy-start.12 = (f32[48,1024]{1,0:T(8,128)}, f32[48,1024]{1,0:T(8,128)S(1)}, u32[]{:S(2)}) copy-start(f32[48,1024]{1,0:T(8,128)S(1)} %get-tuple-element.38.refs_2_.refs_11_) | copy-start | bytes 589828
  130.0 26.9 %all-to-all-start.3 = ((f32[32,16,128]{2,1,0:T(8,128)}), f32[32,16,128]{2,1,0:T(8,128)S(1)}, u32[]{:S(2)}, u32[]{:S(2)}) async-start(f32[32,16,128]{2,1,0:T(8,128)} %get-tuple-element.37), calls=%async_computation.3 | async-start | bytes 524288 | tf_op jit(solution)/shard_map/all_to_all | solution.py:485
  134.9 9.8 %collective-permute-start.9 = (f32[48,1024]{1,0:T(8,128)S(1)}, f32[48,1024]{1,0:T(8,128)S(1)}, u32[]{:S(2)}, u32[]{:S(2)}) collective-permute-start(f32[48,1024]{1,0:T(8,128)S(1)} %get-tuple-element.38.refs_2_.refs_11_), channel_id=1, source_target_pairs={{1,0},{2,1},{3,2},{4,3},{5,4},{6,5},{7,6},{8,7},{9,8},{10,9},{11,1... | collective-permute-start | bytes 589832 | tf_op jit(solution)/shard_map/ppermute | solution.py:490
  136.2 9.4 %collective-permute-start.8 = (f32[48,1024]{1,0:T(8,128)S(1)}, f32[48,1024]{1,0:T(8,128)S(1)}, u32[]{:S(2)}, u32[]{:S(2)}) collective-permute-start(f32[48,1024]{1,0:T(8,128)S(1)} %get-tuple-element.38.refs_2_.refs_11_), channel_id=1, source_target_pairs={{0,1},{1,2},{2,3},{3,4},{4,5},{5,6},{6,7},{7,8},{8,9},{9,10},{10,1... | collective-permute-start | bytes 589832 | tf_op jit(solution)/shard_map/ppermute | solution.py:490
  176.3 28.0 %copy-start.5 = (f32[48,1024]{1,0:T(8,128)}, f32[48,1024]{1,0:T(8,128)S(1)}, u32[]{:S(2)}) copy-start(f32[48,1024]{1,0:T(8,128)S(1)} %get-tuple-element.45.refs_6_.refs_8_) | copy-start | bytes 589828
  176.3 28.0 %copy-start.15 = (f32[34]{0:T(128)}, f32[34]{0:T(128)S(1)}, u32[]{:S(2)}) copy-start(f32[34]{0:T(128)S(1)} %get-tuple-element.44.refs_0_) | copy-start | bytes 412
  176.3 12.1 %collective-permute-start.13 = (f32[48,1024]{1,0:T(8,128)S(1)}, f32[48,1024]{1,0:T(8,128)S(1)}, u32[]{:S(2)}, u32[]{:S(2)}) collective-permute-start(f32[48,1024]{1,0:T(8,128)S(1)} %get-tuple-element.45.refs_6_.refs_8_), channel_id=1, source_target_pairs={{2,0},{3,1},{4,2},{5,3},{6,4},{7,5},{8,6},{9,7},{10,8},{11,9},{12,... | collective-permute-start | bytes 589832 | tf_op jit(solution)/shard_map/ppermute | solution.py:490
  177.6 10.8 %collective-permute-start.12 = (f32[48,1024]{1,0:T(8,128)S(1)}, f32[48,1024]{1,0:T(8,128)S(1)}, u32[]{:S(2)}, u32[]{:S(2)}) collective-permute-start(f32[48,1024]{1,0:T(8,128)S(1)} %get-tuple-element.45.refs_6_.refs_8_), channel_id=1, source_target_pairs={{1,0},{2,1},{3,2},{4,3},{5,4},{6,5},{7,6},{8,7},{9,8},{10,9},{11,1... | collective-permute-start | bytes 589832 | tf_op jit(solution)/shard_map/ppermute | solution.py:490
  178.9 9.5 %collective-permute-start.11 = (f32[48,1024]{1,0:T(8,128)S(1)}, f32[48,1024]{1,0:T(8,128)S(1)}, u32[]{:S(2)}, u32[]{:S(2)}) collective-permute-start(f32[48,1024]{1,0:T(8,128)S(1)} %get-tuple-element.45.refs_6_.refs_8_), channel_id=1, source_target_pairs={{0,1},{1,2},{2,3},{3,4},{4,5},{5,6},{6,7},{7,8},{8,9},{9,10},{10,1... | collective-permute-start | bytes 589832 | tf_op jit(solution)/shard_map/ppermute | solution.py:490
  182.9 8.1 %collective-permute-start.10 = (f32[48,1024]{1,0:T(8,128)S(1)}, f32[48,1024]{1,0:T(8,128)S(1)}, u32[]{:S(2)}, u32[]{:S(2)}) collective-permute-start(f32[48,1024]{1,0:T(8,128)S(1)} %get-tuple-element.45.refs_6_.refs_8_), channel_id=1, source_target_pairs={{0,2},{1,3},{2,4},{3,5},{4,6},{5,7},{6,8},{7,9},{8,10},{9,11},{10,... | collective-permute-start | bytes 589832 | tf_op jit(solution)/shard_map/ppermute | solution.py:490
  188.5 15.9 %copy-start.6 = (f32[48,1024]{1,0:T(8,128)}, f32[48,1024]{1,0:T(8,128)S(1)}, u32[]{:S(2)}) copy-start(f32[48,1024]{1,0:T(8,128)S(1)} %collective-permute-done.12.refs_7_.refs_9_) | copy-start | bytes 589828
  188.5 15.9 %copy-start.7 = (f32[48,1024]{1,0:T(8,128)}, f32[48,1024]{1,0:T(8,128)S(1)}, u32[]{:S(2)}) copy-start(f32[48,1024]{1,0:T(8,128)S(1)} %collective-permute-done.11.refs_5_.refs_7_) | copy-start | bytes 589828
  196.0 0.7 copy-start.14
  196.7 30.8 %all-to-all-start.5 = ((f32[32,16,128]{2,1,0:T(8,128)}), f32[32,16,128]{2,1,0:T(8,128)S(1)}, u32[]{:S(2)}, u32[]{:S(2)}) async-start(f32[32,16,128]{2,1,0:T(8,128)} %get-tuple-element.46), calls=%async_computation.5 | async-start | bytes 524288 | tf_op jit(solution)/shard_map/all_to_all | solution.py:485
  227.5 0.7 copy-start.16
  228.1 1.0 copy-start.20
  229.1 0.9 copy-start.22

commit v11 on v9

--- a/solution.py
+++ b/solution.py
@@ -595,7 +595,14 @@
     terms = call(correlate_kernel, row, [factors], operands, scratch, far=tuple(range(12)), limit=ALL_VMEM)
     terms = lax.psum(terms, "gz_1")
     last_arrived = exchange(last_send)
-    result_out = call(last_filter_kernel, tiles, [factors], [along_y, last_arrived, bank, image_spectrum, terms])
+    result_out = call(
+        last_filter_kernel,
+        tiles,
+        [factors],
+        [along_y, last_arrived, bank, image_spectrum, terms],
+        far=(0, 2, 3, 4),
+        limit=ALL_VMEM,
+    )
     grad_measured, terms = call(final_kernel, (rows, row), [], [table, exchange(result_out)])
     grad_stencil = lax.psum(terms, "gz_0")[0, :27].reshape(3, 3, 3) / math.sqrt(cells)
     return grad_measured[None], grad_stencil

time: 272 us -> 273 us (level)
    unnamed x48 -> x44, local copies, waits for them, and re-layouts: 7.33 us -> 5.56 us
where the time goes in v11:
time: 273 us; the launch traced here: 271 us
  blocking collectives  99.8 us (37%)
  starting transfers between devices  79.8 us (29%)
  waiting for transfers between devices  49.6 us (18%)
  Pallas kernels  34.5 us (13%)
  local copies, waits for them, and re-layouts  6.34 us (2%)
    all_to_all x2, blocking collectives, exchange(): return lax.all_to_all(value, GY, 0, 0, tiled=True)  62.8 us
    ppermute x12, starting transfers between devices, moved(): lax.ppermute(value, GZ, [(i, i + by) for i in range(size) if 0 <= i + by...  38.8 us
    all_to_all x4, starting transfers between devices, exchange(): return lax.all_to_all(value, GY, 0, 0, tiled=True)  35.6 us
    all_to_all x4, waiting for transfers between devices, exchange(): return lax.all_to_all(value, GY, 0, 0, tiled=True)  33.2 us
    pallas_call x12, Pallas kernels, call(): pl.pallas_call(whole, out_shape=out_shape, in_specs=spec_in, out_specs=sp...  33.2 us
    all_to_all x1, blocking collectives, from_all(): lax.all_to_all(jnp.broadcast_to(row[None], (size, 1, 128)), GZ, 0, 0, til...  17.5 us
    psum x1, blocking collectives, local(): terms = lax.psum(terms, 'gz_1')  12.6 us
    ppermute x12, waiting for transfers between devices, moved(): lax.ppermute(value, GZ, [(i, i + by) for i in range(size) if 0 <= i + by...  8.73 us
  transfers between devices with their start and end apart: 18, of which 10 were waited for; matrix products, arithmetic and copies ran while one was open for 0% of the time, Pallas kernels for 3%

profile of v11, /device:TPU:1, one launch (start us, length us, event | category | flops | bytes accessed | tf_op | source)
XLA Modules:
  0.0 271.3 jit_solution(18217430971988852708)
XLA Ops:
  0.7 4.4 %shard_map.77 = f32[32,16,128]{2,1,0:T(8,128)} custom-call(bf16[2048,512]{1,0:T(8,128)(2,1)} %constant.7.clone.refs_0_.refs_1_, f32[32,1024]{1,0:T(8,128)} %bitcast.12, f32[32,1024]{1,0:T(8,128)} %refs_2_.1), custom_call_target="tpu_custom_call" | custom-call | flops 400000000 | bytes 4000000 | tf_op jit(solution)/shard_map/pallas_call | solution.py:473
  5.0 16.9 %all-to-all-start = ((f32[32,16,128]{2,1,0:T(8,128)}), f32[32,16,128]{2,1,0:T(8,128)S(1)}, u32[]{:S(2)}, u32[]{:S(2)}) async-start(f32[32,16,128]{2,1,0:T(8,128)} %shard_map.77), calls=%async_computation | async-start | bytes 524288 | tf_op jit(solution)/shard_map/all_to_all | solution.py:485
  22.0 3.5 %collective-permute-start = (f32[8,1024]{1,0:T(8,128)S(1)}, f32[8,1024]{1,0:T(8,128)S(1)}, u32[]{:S(2)}, u32[]{:S(2)}) collective-permute-start(f32[8,1024]{1,0:T(8,128)S(1)} %get-tuple-element.52), channel_id=1, source_target_pairs={{0,16},{16,32},{32,48},{48,64},{64,80},{80,96},{96,112},{112,128},... | collective-permute-start | bytes 98312 | tf_op jit(solution)/shard_map/ppermute | solution.py:499
  25.5 1.9 collective-permute-start.1
  27.4 1.5 collective-permute-done
  28.9 6.2 %collective-permute-done.1 = f32[8,1024]{1,0:T(8,128)S(1)} collective-permute-done((f32[8,1024]{1,0:T(8,128)S(1)}, f32[8,1024]{1,0:T(8,128)S(1)}, u32[]{:S(2)}, u32[]{:S(2)}) %collective-permute-start.1) | collective-permute-done | bytes 32800 | tf_op jit(solution)/shard_map/ppermute | solution.py:500
  35.1 8.6 %all-to-all-done.refs_1_ = f32[32,16,128]{2,1,0:T(8,128)S(1)} async-done(((f32[32,16,128]{2,1,0:T(8,128)}), f32[32,16,128]{2,1,0:T(8,128)S(1)}, u32[]{:S(2)}, u32[]{:S(2)}) %all-to-all-start) | async-done | bytes 262176 | tf_op jit(solution)/shard_map/all_to_all | solution.py:485
  43.8 2.2 shard_map.78
  46.7 32.0 %all_to_all.35.refs_1_ = f32[32,24,128]{2,1,0:T(8,128)S(1)} all-to-all(f32[32,24,128]{2,1,0:T(8,128)S(1)} %get-tuple-element.28), channel_id=1, replica_groups=mesh['gy'=32,'gz_0'=4,'gz_1'=4] {'gy'}, dimensions={0} | all-to-all | bytes 786432 | tf_op jit(solution)/shard_map/all_to_all | solution.py:485
  78.7 0.9 shard_map.79
  79.6 1.3 collective-permute-start.5
  80.9 1.3 collective-permute-start.4
  82.2 4.0 %collective-permute-start.3 = (f32[48,1024]{1,0:T(8,128)S(1)}, f32[48,1024]{1,0:T(8,128)S(1)}, u32[]{:S(2)}, u32[]{:S(2)}) collective-permute-start(f32[48,1024]{1,0:T(8,128)S(1)} %get-tuple-element.30.refs_6_.refs_2_), channel_id=1, source_target_pairs={{0,1},{1,2},{2,3},{3,4},{4,5},{5,6},{6,7},{7,8},{8,9},{9,10},{10,1... | collective-permute-start | bytes 589832 | tf_op jit(solution)/shard_map/ppermute | solution.py:490
  86.2 6.5 %collective-permute-start.2 = (f32[48,1024]{1,0:T(8,128)S(1)}, f32[48,1024]{1,0:T(8,128)}, u32[]{:S(2)}, u32[]{:S(2)}) collective-permute-start(f32[48,1024]{1,0:T(8,128)S(1)} %get-tuple-element.30.refs_6_.refs_2_), channel_id=1, source_target_pairs={{0,2},{1,3},{2,4},{3,5},{4,6},{5,7},{6,8},{7,9},{8,10},{9,11},{10,... | collective-permute-start | bytes 589832 | tf_op jit(solution)/shard_map/ppermute | solution.py:490
  92.9 2.2 collective-permute-done.2.refs_4_
  95.1 4.6 %shard_map.80 = (f32[48,1024]{1,0:T(8,128)S(1)}, f32[32,1024]{1,0:T(8,128)S(1)}, f32[32,8,128]{2,1,0:T(8,128)}, f32[1,128]{1,0:T(1,128)S(1)}) custom-call(f32[27]{0:T(128)S(1)} %reshape.14.refs_0_.weights_ref, bf16[2048,512]{1,0:T(8,128)(2,1)S(1)} %copy-done, f32[48,1024]{1,0:T(8,128)S(1)} %get-tuple-element.29.refs_2_, f32[32,1024]{1,0:T(8,128)S(1)} %bitcast.9, ...), custom_call_target="tpu_custom_call" | custom-call | flops 400000000 | bytes 4000000 | tf_op jit(solution)/shard_map/pallas_call | solution.py:473
  101.0 6.2 %all-to-all-start.2 = ((f32[32,8,128]{2,1,0:T(8,128)}), f32[32,8,128]{2,1,0:T(8,128)}, u32[]{:S(2)}, u32[]{:S(2)}) async-start(f32[32,8,128]{2,1,0:T(8,128)} %get-tuple-element.32), calls=%async_computation.2 | async-start | bytes 262144 | tf_op jit(solution)/shard_map/all_to_all | solution.py:485
  107.2 1.3 collective-permute-start.7
  108.5 5.5 %collective-permute-start.6 = (f32[48,1024]{1,0:T(8,128)}, f32[48,1024]{1,0:T(8,128)S(1)}, u32[]{:S(2)}, u32[]{:S(2)}) collective-permute-start(f32[48,1024]{1,0:T(8,128)} %copy-done.8), channel_id=1, source_target_pairs={{0,1},{1,2},{2,3},{3,4},{4,5},{5,6},{6,7},{7,8},{8,9},{9,10},{10,1... | collective-permute-start | bytes 589832 | tf_op jit(solution)/shard_map/ppermute | solution.py:490
  114.0 9.4 %all-to-all-done.2.refs_1_ = f32[32,8,128]{2,1,0:T(8,128)} async-done(((f32[32,8,128]{2,1,0:T(8,128)}), f32[32,8,128]{2,1,0:T(8,128)}, u32[]{:S(2)}, u32[]{:S(2)}) %all-to-all-start.2) | async-done | bytes 131104 | tf_op jit(solution)/shard_map/all_to_all | solution.py:485
  123.5 1.0 copy-done.18
  124.4 2.3 shard_map.81
  126.9 1.1 copy-done.9
  127.9 2.0 shard_map.82
  130.0 4.9 %all-to-all-start.3 = ((f32[32,16,128]{2,1,0:T(8,128)}), f32[32,16,128]{2,1,0:T(8,128)S(1)}, u32[]{:S(2)}, u32[]{:S(2)}) async-start(f32[32,16,128]{2,1,0:T(8,128)} %get-tuple-element.37), calls=%async_computation.3 | async-start | bytes 524288 | tf_op jit(solution)/shard_map/all_to_all | solution.py:485
  134.9 1.3 collective-permute-start.9
  136.2 5.5 %collective-permute-start.8 = (f32[48,1024]{1,0:T(8,128)S(1)}, f32[48,1024]{1,0:T(8,128)S(1)}, u32[]{:S(2)}, u32[]{:S(2)}) collective-permute-start(f32[48,1024]{1,0:T(8,128)S(1)} %get-tuple-element.38.refs_2_.refs_11_), channel_id=1, source_target_pairs={{0,1},{1,2},{2,3},{3,4},{4,5},{5,6},{6,7},{7,8},{8,9},{9,10},{10,1... | collective-permute-start | bytes 589832 | tf_op jit(solution)/shard_map/ppermute | solution.py:490
  141.7 3.0 %collective-permute-done.9.refs_3_ = f32[48,1024]{1,0:T(8,128)S(1)} collective-permute-done((f32[48,1024]{1,0:T(8,128)S(1)}, f32[48,1024]{1,0:T(8,128)S(1)}, u32[]{:S(2)}, u32[]{:S(2)}) %collective-permute-start.9) | collective-permute-done | bytes 196640 | tf_op jit(solution)/shard_map/ppermute | solution.py:490
  144.7 0.9 collective-permute-done.8.refs_1_
  145.6 1.1 shard_map.83.refs_2_
  146.7 10.2 %all-to-all-done.3.refs_1_ = f32[32,16,128]{2,1,0:T(8,128)S(1)} async-done(((f32[32,16,128]{2,1,0:T(8,128)}), f32[32,16,128]{2,1,0:T(8,128)S(1)}, u32[]{:S(2)}, u32[]{:S(2)}) %all-to-all-start.3) | async-done | bytes 262176 | tf_op jit(solution)/shard_map/all_to_all | solution.py:485
  157.5 17.5 %all_to_all.36.rows = f32[16,1,128]{2,1,0:T(1,128)S(1)} all-to-all(f32[16,1,128]{2,1,0:T(1,128)S(1)} %broadcast_in_dim.12), channel_id=1, replica_groups=mesh['gy'=32,'gz_0'=4,'gz_1'=4] {'gz_0','gz_1'}, dimensions={0} | all-to-all | bytes 16384 | tf_op jit(solution)/shard_map/all_to_all | solution.py:506
  175.0 1.3 shard_map.85
  176.3 1.3 collective-permute-start.13
  177.6 1.3 collective-permute-start.12
  178.9 4.0 %collective-permute-start.11 = (f32[48,1024]{1,0:T(8,128)S(1)}, f32[48,1024]{1,0:T(8,128)S(1)}, u32[]{:S(2)}, u32[]{:S(2)}) collective-permute-start(f32[48,1024]{1,0:T(8,128)S(1)} %get-tuple-element.45.refs_6_.refs_8_), channel_id=1, source_target_pairs={{0,1},{1,2},{2,3},{3,4},{4,5},{5,6},{6,7},{7,8},{8,9},{9,10},{10,1... | collective-permute-start | bytes 589832 | tf_op jit(solution)/shard_map/ppermute | solution.py:490
  183.0 5.5 %collective-permute-start.10 = (f32[48,1024]{1,0:T(8,128)S(1)}, f32[48,1024]{1,0:T(8,128)S(1)}, u32[]{:S(2)}, u32[]{:S(2)}) collective-permute-start(f32[48,1024]{1,0:T(8,128)S(1)} %get-tuple-element.45.refs_6_.refs_8_), channel_id=1, source_target_pairs={{0,2},{1,3},{2,4},{3,5},{4,6},{5,7},{6,8},{7,9},{8,10},{9,11},{10,... | collective-permute-start | bytes 589832 | tf_op jit(solution)/shard_map/ppermute | solution.py:490
  188.5 2.6 collective-permute-done.10.refs_4_
  191.1 5.0 %shard_map.86 = (f32[32,1024]{1,0:T(8,128)S(1)}, f32[32,16,128]{2,1,0:T(8,128)}) custom-call(f32[34]{0:T(128)S(1)} %get-tuple-element.44.refs_0_, bf16[2048,512]{1,0:T(8,128)(2,1)S(1)} %copy-done, f32[48,1024]{1,0:T(8,128)S(1)} %shard_map.83.refs_2_, f32[32,1024]{1,0:T(8,128)S(1)} %bitcast.10, f32[48,1024]{1,0:T(8,128)S(1)} %collective-permute-done.10.refs_4_, ...), custom_call_target="tpu_custom_call" | custom-call | flops 400000000 | bytes 4000000 | tf_op jit(solution)/shard_map/pallas_call | solution.py:473
  196.7 7.6 %all-to-all-start.5 = ((f32[32,16,128]{2,1,0:T(8,128)}), f32[32,16,128]{2,1,0:T(8,128)S(1)}, u32[]{:S(2)}, u32[]{:S(2)}) async-start(f32[32,16,128]{2,1,0:T(8,128)} %get-tuple-element.46), calls=%async_computation.5 | async-start | bytes 524288 | tf_op jit(solution)/shard_map/all_to_all | solution.py:485
  204.4 4.4 %shard_map.87 = f32[1,128]{1,0:T(1,128)} custom-call(f32[34]{0:T(128)} %copy-done.15, f32[48,1024]{1,0:T(8,128)} %copy-done.4, f32[48,1024]{1,0:T(8,128)} %copy-done.2, f32[48,1024]{1,0:T(8,128)} %copy-done.3, f32[48,1024]{1,0:T(8,128)} %copy-done.11, f32[48,1024]{1,0:T(8,128)} %copy-done.8, f32[48,1024]{1,0:T(8,128)} %copy-done.10, f32[48,1024]{1,0:T(8,128)} %copy-done.7, ...), custom_call_target="tpu_custom_call" | custom-call | flops 400000000 | bytes 4000000 | tf_op jit(solution)/shard_map/pallas_call | solution.py:473
  208.8 12.6 %psum.14.refs_5_ = f32[1,128]{1,0:T(1,128)} all-reduce(f32[1,128]{1,0:T(1,128)} %shard_map.87), channel_id=1, replica_groups=mesh['gy'=32,'gz_0'=4,'gz_1'=4] {'gz_1'}, use_global_device_ids=true, to_apply=%region_0.0 | all-reduce | flops 128 | bytes 1024 | tf_op jit(solution)/shard_map/psum | solution.py:596
  221.4 5.0 %all-to-all-done.5.refs_2_ = f32[32,16,128]{2,1,0:T(8,128)S(1)} async-done(((f32[32,16,128]{2,1,0:T(8,128)}), f32[32,16,128]{2,1,0:T(8,128)S(1)}, u32[]{:S(2)}, u32[]{:S(2)}) %all-to-all-start.5) | async-done | bytes 262176 | tf_op jit(solution)/shard_map/all_to_all | solution.py:485
  226.3 0.7 copy-done.20
  227.0 4.6 %shard_map.88 = f32[32,16,128]{2,1,0:T(8,128)} custom-call(f32[34]{0:T(128)} %copy-done.15, f32[256,128]{1,0:T(8,128)} %constant.8.clone.refs_0_.refs_1_, f32[32,16,128]{2,1,0:T(8,128)} %copy-done.20, f32[2,288,128]{2,1,0:T(8,128)} %copy-done.17, f32[288,128]{1,0:T(8,128)} %copy-done.19, f32[1,128]{1,0:T(1,128)} %psum.14.refs_5_), custom_call_target="tpu_custom_call" | custom-call | flops 400000000 | bytes 4000000 | tf_op jit(solution)/shard_map/pallas_call | solution.py:473
  231.6 30.8 %all_to_all.37.refs_1_ = f32[32,16,128]{2,1,0:T(8,128)S(1)} all-to-all(f32[32,16,128]{2,1,0:T(8,128)} %shard_map.88), channel_id=1, replica_groups=mesh['gy'=32,'gz_0'=4,'gz_1'=4] {'gy'}, dimensions={0} | all-to-all | bytes 524288 | tf_op jit(solution)/shard_map/all_to_all | solution.py:485
  262.4 1.2 shard_map.89
  263.5 7.0 %psum.15 = f32[1,128]{1,0:T(1,128)S(1)} all-reduce(f32[1,128]{1,0:T(1,128)S(1)} %get-tuple-element.51), channel_id=1, replica_groups=mesh['gy'=32,'gz_0'=4,'gz_1'=4] {'gz_0'}, use_global_device_ids=true, to_apply=%region_1.0 | all-reduce | flops 128 | bytes 1024 | tf_op jit(solution)/shard_map/psum | solution.py:607
  (56 shorter events, 4.3 us)
Async XLA Ops:
  0.6 43.1 %copy-start.16 = (f32[256,128]{1,0:T(8,128)S(1)}, f32[256,128]{1,0:T(8,128)}, u32[]{:S(2)}) copy-start(f32[256,128]{1,0:T(8,128)} %constant.8.clone.refs_0_.refs_1_) | copy-start | bytes 393220
  0.6 21.3 %copy-start.1 = (f32[1,32,1024]{2,1,0:T(8,128)S(1)}, f32[1,32,1024]{2,1,0:T(8,128)}, u32[]{:S(2)}) copy-start(f32[1,32,1024]{2,1,0:T(8,128)} %param.9) | copy-start | bytes 393220
  5.0 73.7 %copy-start = (bf16[2048,512]{1,0:T(8,128)(2,1)S(1)}, bf16[2048,512]{1,0:T(8,128)(2,1)}, u32[]{:S(2)}) copy-start(bf16[2048,512]{1,0:T(8,128)(2,1)} %constant.7.clone.refs_0_.refs_1_) | copy-start | bytes 6291460
  5.0 38.7 %all-to-all-start = ((f32[32,16,128]{2,1,0:T(8,128)}), f32[32,16,128]{2,1,0:T(8,128)S(1)}, u32[]{:S(2)}, u32[]{:S(2)}) async-start(f32[32,16,128]{2,1,0:T(8,128)} %shard_map.77), calls=%async_computation | async-start | bytes 524288 | tf_op jit(solution)/shard_map/all_to_all | solution.py:485
  22.0 7.0 %collective-permute-start = (f32[8,1024]{1,0:T(8,128)S(1)}, f32[8,1024]{1,0:T(8,128)S(1)}, u32[]{:S(2)}, u32[]{:S(2)}) collective-permute-start(f32[8,1024]{1,0:T(8,128)S(1)} %get-tuple-element.52), channel_id=1, source_target_pairs={{0,16},{16,32},{32,48},{48,64},{64,80},{80,96},{96,112},{112,128},... | collective-permute-start | bytes 98312 | tf_op jit(solution)/shard_map/ppermute | solution.py:499
  25.5 9.6 %collective-permute-start.1 = (f32[8,1024]{1,0:T(8,128)S(1)}, f32[8,1024]{1,0:T(8,128)S(1)}, u32[]{:S(2)}, u32[]{:S(2)}) collective-permute-start(f32[8,1024]{1,0:T(8,128)S(1)} %get-tuple-element.53), channel_id=1, source_target_pairs={{16,0},{32,16},{48,32},{64,48},{80,64},{96,80},{112,96},{128,112},... | collective-permute-start | bytes 98312 | tf_op jit(solution)/shard_map/ppermute | solution.py:500
  35.1 57.6 %copy-start.21 = (f32[3,3,3]{2,1,0:T(4,128)S(1)}, f32[3,3,3]{2,1,0:T(4,128)}, u32[]{:S(2)}) copy-start(f32[3,3,3]{2,1,0:T(4,128)} %param.8) | copy-start | bytes 328
  46.0 0.7 copy-start.17
  79.6 47.2 %copy-start.2 = (f32[48,1024]{1,0:T(8,128)}, f32[48,1024]{1,0:T(8,128)S(1)}, u32[]{:S(2)}) copy-start(f32[48,1024]{1,0:T(8,128)S(1)} %get-tuple-element.30.refs_6_.refs_2_) | copy-start | bytes 589828
  79.6 13.2 %collective-permute-start.5 = (f32[48,1024]{1,0:T(8,128)S(1)}, f32[48,1024]{1,0:T(8,128)S(1)}, u32[]{:S(2)}, u32[]{:S(2)}) collective-permute-start(f32[48,1024]{1,0:T(8,128)S(1)} %get-tuple-element.30.refs_6_.refs_2_), channel_id=1, source_target_pairs={{2,0},{3,1},{4,2},{5,3},{6,4},{7,5},{8,6},{9,7},{10,8},{11,9},{12,... | collective-permute-start | bytes 589832 | tf_op jit(solution)/shard_map/ppermute | solution.py:490
  80.9 11.9 %collective-permute-start.4 = (f32[48,1024]{1,0:T(8,128)S(1)}, f32[48,1024]{1,0:T(8,128)S(1)}, u32[]{:S(2)}, u32[]{:S(2)}) collective-permute-start(f32[48,1024]{1,0:T(8,128)S(1)} %get-tuple-element.30.refs_6_.refs_2_), channel_id=1, source_target_pairs={{1,0},{2,1},{3,2},{4,3},{5,4},{6,5},{7,6},{8,7},{9,8},{10,9},{11,1... | collective-permute-start | bytes 589832 | tf_op jit(solution)/shard_map/ppermute | solution.py:490
  82.2 10.7 %collective-permute-start.3 = (f32[48,1024]{1,0:T(8,128)S(1)}, f32[48,1024]{1,0:T(8,128)S(1)}, u32[]{:S(2)}, u32[]{:S(2)}) collective-permute-start(f32[48,1024]{1,0:T(8,128)S(1)} %get-tuple-element.30.refs_6_.refs_2_), channel_id=1, source_target_pairs={{0,1},{1,2},{2,3},{3,4},{4,5},{5,6},{6,7},{7,8},{8,9},{9,10},{10,1... | collective-permute-start | bytes 589832 | tf_op jit(solution)/shard_map/ppermute | solution.py:490
  86.2 8.9 %collective-permute-start.2 = (f32[48,1024]{1,0:T(8,128)S(1)}, f32[48,1024]{1,0:T(8,128)}, u32[]{:S(2)}, u32[]{:S(2)}) collective-permute-start(f32[48,1024]{1,0:T(8,128)S(1)} %get-tuple-element.30.refs_6_.refs_2_), channel_id=1, source_target_pairs={{0,2},{1,3},{2,4},{3,5},{4,6},{5,7},{6,8},{7,9},{8,10},{9,11},{10,... | collective-permute-start | bytes 589832 | tf_op jit(solution)/shard_map/ppermute | solution.py:490
  92.8 33.9 %copy-start.3 = (f32[48,1024]{1,0:T(8,128)}, f32[48,1024]{1,0:T(8,128)S(1)}, u32[]{:S(2)}) copy-start(f32[48,1024]{1,0:T(8,128)S(1)} %collective-permute-done.4.refs_7_.refs_3_) | copy-start | bytes 589828
  92.9 33.9 %copy-start.4 = (f32[48,1024]{1,0:T(8,128)}, f32[48,1024]{1,0:T(8,128)S(1)}, u32[]{:S(2)}) copy-start(f32[48,1024]{1,0:T(8,128)S(1)} %collective-permute-done.3.refs_5_.refs_1_) | copy-start | bytes 589828
  99.6 0.7 copy-start.8
  100.3 0.7 copy-start.13
  101.0 22.5 %all-to-all-start.2 = ((f32[32,8,128]{2,1,0:T(8,128)}), f32[32,8,128]{2,1,0:T(8,128)}, u32[]{:S(2)}, u32[]{:S(2)}) async-start(f32[32,8,128]{2,1,0:T(8,128)} %get-tuple-element.32), calls=%async_computation.2 | async-start | bytes 262144 | tf_op jit(solution)/shard_map/all_to_all | solution.py:485
  107.2 19.6 %collective-permute-start.7 = (f32[48,1024]{1,0:T(8,128)}, f32[48,1024]{1,0:T(8,128)S(1)}, u32[]{:S(2)}, u32[]{:S(2)}) collective-permute-start(f32[48,1024]{1,0:T(8,128)} %copy-done.8), channel_id=1, source_target_pairs={{1,0},{2,1},{3,2},{4,3},{5,4},{6,5},{7,6},{8,7},{9,8},{10,9},{11,1... | collective-permute-start | bytes 589832 | tf_op jit(solution)/shard_map/ppermute | solution.py:490
  108.5 18.3 %collective-permute-start.6 = (f32[48,1024]{1,0:T(8,128)}, f32[48,1024]{1,0:T(8,128)S(1)}, u32[]{:S(2)}, u32[]{:S(2)}) collective-permute-start(f32[48,1024]{1,0:T(8,128)} %copy-done.8), channel_id=1, source_target_pairs={{0,1},{1,2},{2,3},{3,4},{4,5},{5,6},{6,7},{7,8},{8,9},{9,10},{10,1... | collective-permute-start | bytes 589832 | tf_op jit(solution)/shard_map/ppermute | solution.py:490
  123.5 1.0 copy-start.18
  126.8 3.2 %copy-start.19 = (f32[288,128]{1,0:T(8,128)}, f32[288,128]{1,0:T(8,128)S(1)}, u32[]{:S(2)}) copy-start(f32[288,128]{1,0:T(8,128)S(1)} %get-tuple-element.47.refs_4_) | copy-start | bytes 442372
  126.8 3.2 %copy-start.10 = (f32[48,1024]{1,0:T(8,128)}, f32[48,1024]{1,0:T(8,128)S(1)}, u32[]{:S(2)}) copy-start(f32[48,1024]{1,0:T(8,128)S(1)} %collective-permute-done.7.refs_6_) | copy-start | bytes 589828
  126.8 3.1 %copy-start.11 = (f32[48,1024]{1,0:T(8,128)}, f32[48,1024]{1,0:T(8,128)S(1)}, u32[]{:S(2)}) copy-start(f32[48,1024]{1,0:T(8,128)S(1)} %collective-permute-done.6.refs_4_) | copy-start | bytes 589828
  126.8 1.1 copy-start.9
  130.0 27.5 %copy-start.12 = (f32[48,1024]{1,0:T(8,128)}, f32[48,1024]{1,0:T(8,128)S(1)}, u32[]{:S(2)}) copy-start(f32[48,1024]{1,0:T(8,128)S(1)} %get-tuple-element.38.refs_2_.refs_11_) | copy-start | bytes 589828
  130.0 26.9 %all-to-all-start.3 = ((f32[32,16,128]{2,1,0:T(8,128)}), f32[32,16,128]{2,1,0:T(8,128)S(1)}, u32[]{:S(2)}, u32[]{:S(2)}) async-start(f32[32,16,128]{2,1,0:T(8,128)} %get-tuple-element.37), calls=%async_computation.3 | async-start | bytes 524288 | tf_op jit(solution)/shard_map/all_to_all | solution.py:485
  134.9 9.8 %collective-permute-start.9 = (f32[48,1024]{1,0:T(8,128)S(1)}, f32[48,1024]{1,0:T(8,128)S(1)}, u32[]{:S(2)}, u32[]{:S(2)}) collective-permute-start(f32[48,1024]{1,0:T(8,128)S(1)} %get-tuple-element.38.refs_2_.refs_11_), channel_id=1, source_target_pairs={{1,0},{2,1},{3,2},{4,3},{5,4},{6,5},{7,6},{8,7},{9,8},{10,9},{11,1... | collective-permute-start | bytes 589832 | tf_op jit(solution)/shard_map/ppermute | solution.py:490
  136.2 9.4 %collective-permute-start.8 = (f32[48,1024]{1,0:T(8,128)S(1)}, f32[48,1024]{1,0:T(8,128)S(1)}, u32[]{:S(2)}, u32[]{:S(2)}) collective-permute-start(f32[48,1024]{1,0:T(8,128)S(1)} %get-tuple-element.38.refs_2_.refs_11_), channel_id=1, source_target_pairs={{0,1},{1,2},{2,3},{3,4},{4,5},{5,6},{6,7},{7,8},{8,9},{9,10},{10,1... | collective-permute-start | bytes 589832 | tf_op jit(solution)/shard_map/ppermute | solution.py:490
  176.3 28.0 %copy-start.5 = (f32[48,1024]{1,0:T(8,128)}, f32[48,1024]{1,0:T(8,128)S(1)}, u32[]{:S(2)}) copy-start(f32[48,1024]{1,0:T(8,128)S(1)} %get-tuple-element.45.refs_6_.refs_8_) | copy-start | bytes 589828
  176.3 28.0 %copy-start.15 = (f32[34]{0:T(128)}, f32[34]{0:T(128)S(1)}, u32[]{:S(2)}) copy-start(f32[34]{0:T(128)S(1)} %get-tuple-element.44.refs_0_) | copy-start | bytes 412
  176.3 12.1 %collective-permute-start.13 = (f32[48,1024]{1,0:T(8,128)S(1)}, f32[48,1024]{1,0:T(8,128)S(1)}, u32[]{:S(2)}, u32[]{:S(2)}) collective-permute-start(f32[48,1024]{1,0:T(8,128)S(1)} %get-tuple-element.45.refs_6_.refs_8_), channel_id=1, source_target_pairs={{2,0},{3,1},{4,2},{5,3},{6,4},{7,5},{8,6},{9,7},{10,8},{11,9},{12,... | collective-permute-start | bytes 589832 | tf_op jit(solution)/shard_map/ppermute | solution.py:490
  177.6 10.8 %collective-permute-start.12 = (f32[48,1024]{1,0:T(8,128)S(1)}, f32[48,1024]{1,0:T(8,128)S(1)}, u32[]{:S(2)}, u32[]{:S(2)}) collective-permute-start(f32[48,1024]{1,0:T(8,128)S(1)} %get-tuple-element.45.refs_6_.refs_8_), channel_id=1, source_target_pairs={{1,0},{2,1},{3,2},{4,3},{5,4},{6,5},{7,6},{8,7},{9,8},{10,9},{11,1... | collective-permute-start | bytes 589832 | tf_op jit(solution)/shard_map/ppermute | solution.py:490
  178.9 9.5 %collective-permute-start.11 = (f32[48,1024]{1,0:T(8,128)S(1)}, f32[48,1024]{1,0:T(8,128)S(1)}, u32[]{:S(2)}, u32[]{:S(2)}) collective-permute-start(f32[48,1024]{1,0:T(8,128)S(1)} %get-tuple-element.45.refs_6_.refs_8_), channel_id=1, source_target_pairs={{0,1},{1,2},{2,3},{3,4},{4,5},{5,6},{6,7},{7,8},{8,9},{9,10},{10,1... | collective-permute-start | bytes 589832 | tf_op jit(solution)/shard_map/ppermute | solution.py:490
  183.0 8.1 %collective-permute-start.10 = (f32[48,1024]{1,0:T(8,128)S(1)}, f32[48,1024]{1,0:T(8,128)S(1)}, u32[]{:S(2)}, u32[]{:S(2)}) collective-permute-start(f32[48,1024]{1,0:T(8,128)S(1)} %get-tuple-element.45.refs_6_.refs_8_), channel_id=1, source_target_pairs={{0,2},{1,3},{2,4},{3,5},{4,6},{5,7},{6,8},{7,9},{8,10},{9,11},{10,... | collective-permute-start | bytes 589832 | tf_op jit(solution)/shard_map/ppermute | solution.py:490
  188.5 15.9 %copy-start.6 = (f32[48,1024]{1,0:T(8,128)}, f32[48,1024]{1,0:T(8,128)S(1)}, u32[]{:S(2)}) copy-start(f32[48,1024]{1,0:T(8,128)S(1)} %collective-permute-done.12.refs_7_.refs_9_) | copy-start | bytes 589828
  188.5 15.8 %copy-start.7 = (f32[48,1024]{1,0:T(8,128)}, f32[48,1024]{1,0:T(8,128)S(1)}, u32[]{:S(2)}) copy-start(f32[48,1024]{1,0:T(8,128)S(1)} %collective-permute-done.11.refs_5_.refs_7_) | copy-start | bytes 589828
  196.1 0.7 copy-start.14
  196.7 29.6 %all-to-all-start.5 = ((f32[32,16,128]{2,1,0:T(8,128)}), f32[32,16,128]{2,1,0:T(8,128)S(1)}, u32[]{:S(2)}, u32[]{:S(2)}) async-start(f32[32,16,128]{2,1,0:T(8,128)} %get-tuple-element.46), calls=%async_computation.5 | async-start | bytes 524288 | tf_op jit(solution)/shard_map/all_to_all | solution.py:485
  226.3 0.7 copy-start.20
